TPU v7x, 32 devices: a whole 2x2x4 slice. The times are simulated.
32 devices in a mesh: grp: 2 (over x), clu: 16 (over z, y, core).
Axes of the slice: x: 2, y: 2, z: 4, core: 2. Of those that a mesh axis runs over, the one named last changes fastest.
Arguments:
- raw_rows: bfloat16 [262144, 256], P(('grp', 'clu')), parts along dimension 0, may hold values from -6 to 6
- enc_weight: bfloat16 [256, 256], replicated, may hold values from -0.375 to 0.375
- counts: int32 [32, 256], P(('grp', 'clu')), parts along dimension 0, may hold values from 1 to 64, 8192 in all within a row
- member_rows: int32 [32, 8192], P(('grp', 'clu')), parts along dimension 0, may hold values from 0 to 8191, each once within a row
- pool: int32 [32, 1024], P(('grp', 'clu')), parts along dimension 0, may hold values from 0 to 4095, as said below
- picks: int32 [4096, 100], P(('grp', 'clu')), parts along dimension 0, may hold values from 0 to 1023, all different within a row
- queries: bfloat16 [4096, 256], P(('grp', 'clu')), parts along dimension 0, may hold values from -6 to 6
- attn_weights: bfloat16 [4, 256, 256], replicated, may hold values from -0.375 to 0.375
- out_grad: bfloat16 [4096, 256], P(('grp', 'clu')), parts along dimension 0, may hold values from -6 to 6
Outputs:
- grad_query: bfloat16 [4096, 256], P(('grp', 'clu')), parts along dimension 0
- grad_rows: bfloat16 [262144, 256], P(('grp', 'clu')), parts along dimension 0
- grad_attn: float32 [8, 256, 256], P('grp'), parts along dimension 0
- grad_encoder: float32 [512, 256], P('grp'), parts along dimension 0
There are 2 independent parts, one for each index of `grp`. A program takes and returns all parts, laid end to end along the dimension named above; an argument that names none is the same for every part. Nothing has to cross between parts.
Inputs may be any that keep to these rules, and one draw needn't show every extreme that they name: `counts`: row o sums to 8192. `member_rows`: each row holds every number of 0 to 8191 once. `pool`: in each row, entries 64 * o to 64 * o + 63 are 64 different clusters of owner o, that is of o * 256 to o * 256 + 255. `picks`: the 100 entries of a row are different.
All inputs are finite; a program needn't handle non-finite values.
Results may differ from a plain program's by a relative error of at most 0.012.
Values may be sent and summed in bfloat16 or wider, within the bound.
No kernel may reach another device: no remote copies, remote signals or barrier semaphores. Data moves between devices by JAX's collectives and lax.ppermute only.
A program may use at most 128 MiB of HBM per device.

v0:
```python
import math

import jax
import jax.numpy as jnp
from jax import lax
from jax.sharding import PartitionSpec as P

HEADS = 4


highest = lax.Precision.HIGHEST


def dense_backward(query_rows, key_pool, value_pool, pick_mask, grad_out, weights):
    targets = query_rows.shape[0]
    pooled = key_pool.shape[0]
    width = query_rows.shape[1]
    head_size = width // HEADS
    scale = 1.0 / math.sqrt(head_size)
    query_proj = jnp.dot(query_rows, weights[0], preferred_element_type=jnp.float32).astype(
        jnp.bfloat16
    )
    query_heads = query_proj.reshape(targets, HEADS, head_size)
    key_heads = key_pool.reshape(pooled, HEADS, head_size)
    value_heads = value_pool.reshape(pooled, HEADS, head_size)
    scores = (
        jnp.einsum("thd,jhd->thj", query_heads, key_heads, preferred_element_type=jnp.float32)
        * scale
    )
    live = pick_mask[:, None, :]
    masked = jnp.where(live, scores, -jnp.inf)
    top = jnp.max(masked, axis=-1, keepdims=True)
    raised = jnp.where(live, jnp.exp(masked - top), 0.0)
    attend = raised / jnp.sum(raised, axis=-1, keepdims=True)
    attend_low = attend.astype(jnp.bfloat16)
    mixed = jnp.einsum("thj,jhd->thd", attend_low, value_heads, preferred_element_type=jnp.float32)
    mixed = mixed.reshape(targets, width).astype(jnp.bfloat16)
    grad_wo = jnp.dot(mixed.T, grad_out, preferred_element_type=jnp.float32)
    grad_mixed = jnp.dot(grad_out, weights[3].T, preferred_element_type=jnp.float32).astype(
        jnp.bfloat16
    )
    mixed_heads = grad_mixed.reshape(targets, HEADS, head_size)
    grad_attend = jnp.einsum(
        "thd,jhd->thj", mixed_heads, value_heads, preferred_element_type=jnp.float32
    )
    grad_scores = attend * (grad_attend - jnp.sum(attend * grad_attend, axis=-1, keepdims=True))
    score_low = (grad_scores * scale).astype(jnp.bfloat16)
    grad_qproj = jnp.einsum(
        "thj,jhd->thd", score_low, key_heads, preferred_element_type=jnp.float32
    )
    grad_qproj = grad_qproj.reshape(targets, width).astype(jnp.bfloat16)
    key_grad = jnp.einsum(
        "thj,thd->jhd", score_low, query_heads, preferred_element_type=jnp.float32
    )
    value_grad = jnp.einsum(
        "thj,thd->jhd", attend_low, mixed_heads, preferred_element_type=jnp.float32
    )
    grad_wq = jnp.dot(query_rows.T, grad_qproj, preferred_element_type=jnp.float32)
    grad_query = jnp.dot(grad_qproj, weights[0].T, preferred_element_type=jnp.float32).astype(
        jnp.bfloat16
    )
    return (
        grad_query,
        key_grad.reshape(pooled, width),
        value_grad.reshape(pooled, width),
        grad_wq,
        grad_wo,
    )


def local(raw_rows, enc_weight, counts, member_rows, pool, picks, queries, attn_weights, out_grad):
    counts_row = counts[0]
    members = member_rows[0]
    pool_row = pool[0]
    cluster_count = counts_row.shape[0]
    row_count = members.shape[0]
    width = enc_weight.shape[1]
    owners = lax.axis_size("clu")
    per_owner = pool_row.shape[0] // owners
    asked_total = owners * per_owner
    behavior = jnp.dot(raw_rows, enc_weight, preferred_element_type=jnp.float32).astype(
        jnp.bfloat16
    )
    position_of = (
        jnp.zeros((row_count,), jnp.int32).at[members].set(jnp.arange(row_count, dtype=jnp.int32))
    )
    cluster_ends = jnp.cumsum(counts_row)
    row_cluster = jnp.sum((position_of[:, None] >= cluster_ends[None, :]).astype(jnp.int32), axis=1)
    cluster_iota = jnp.arange(cluster_count, dtype=jnp.int32)
    membership = row_cluster[:, None] == cluster_iota[None, :]
    member_total = jnp.dot(
        membership.astype(jnp.bfloat16).T, behavior, preferred_element_type=jnp.float32
    )
    count_wide = counts_row[:, None].astype(jnp.float32)
    cluster_emb = (member_total / count_wide).astype(jnp.bfloat16)
    wanted = lax.all_to_all(
        pool_row.reshape(owners, per_owner), "clu", split_axis=0, concat_axis=0, tiled=True
    )
    local_ids = (wanted % cluster_count).reshape(-1)
    request_table = local_ids[:, None] == cluster_iota[None, :]
    request_low = request_table.astype(jnp.bfloat16)
    request_wide = request_table.astype(jnp.float32)
    key_local = jnp.dot(cluster_emb, attn_weights[1], preferred_element_type=jnp.float32).astype(
        jnp.bfloat16
    )
    value_local = jnp.dot(cluster_emb, attn_weights[2], preferred_element_type=jnp.float32).astype(
        jnp.bfloat16
    )
    key_sent = jnp.dot(request_low, key_local, preferred_element_type=jnp.float32).astype(
        jnp.bfloat16
    )
    value_sent = jnp.dot(request_low, value_local, preferred_element_type=jnp.float32).astype(
        jnp.bfloat16
    )
    key_pool, value_pool = (
        lax.all_to_all(
            key_sent.reshape(owners, per_owner, width),
            "clu",
            split_axis=0,
            concat_axis=0,
            tiled=True,
        ),
        lax.all_to_all(
            value_sent.reshape(owners, per_owner, width),
            "clu",
            split_axis=0,
            concat_axis=0,
            tiled=True,
        ),
    )
    key_pool = key_pool.reshape(asked_total, width)
    value_pool = value_pool.reshape(asked_total, width)
    pool_iota = jnp.arange(asked_total, dtype=jnp.int32)
    pick_mask = jnp.any(picks[:, :, None] == pool_iota[None, None, :], axis=1)
    grad_query, key_grad, value_grad, grad_wq, grad_wo = dense_backward(
        queries, key_pool, value_pool, pick_mask, out_grad, attn_weights
    )
    key_weight = attn_weights[1].astype(jnp.float32).T
    value_weight = attn_weights[2].astype(jnp.float32).T
    key_back, value_back = (
        lax.all_to_all(
            key_grad.reshape(owners, per_owner, width),
            "clu",
            split_axis=0,
            concat_axis=0,
            tiled=True,
        ),
        lax.all_to_all(
            value_grad.reshape(owners, per_owner, width),
            "clu",
            split_axis=0,
            concat_axis=0,
            tiled=True,
        ),
    )
    key_local_grad = jnp.dot(
        request_wide.T, key_back.reshape(asked_total, width), precision=highest
    )
    value_local_grad = jnp.dot(
        request_wide.T, value_back.reshape(asked_total, width), precision=highest
    )
    emb_wide = cluster_emb.astype(jnp.float32)
    grad_wk = jnp.dot(emb_wide.T, key_local_grad, precision=highest)
    grad_wv = jnp.dot(emb_wide.T, value_local_grad, precision=highest)
    cluster_grad = jnp.dot(key_local_grad, key_weight, precision=highest) + jnp.dot(
        value_local_grad, value_weight, precision=highest
    )
    grad_attn = lax.psum(jnp.stack([grad_wq, grad_wk, grad_wv, grad_wo]), "clu")
    per_member = cluster_grad / count_wide
    grad_rows = jnp.dot(membership.astype(jnp.float32), per_member, precision=highest).astype(
        jnp.bfloat16
    )
    encoder_terms = jnp.dot(raw_rows.T, grad_rows, preferred_element_type=jnp.float32)
    grad_encoder = lax.psum(encoder_terms, "clu")
    return (grad_query, grad_rows, grad_attn, grad_encoder)


def solution(mesh):
    in_specs = (
        P(("grp", "clu"), None),
        P(),
        P(("grp", "clu"), None),
        P(("grp", "clu"), None),
        P(("grp", "clu"), None),
        P(("grp", "clu"), None),
        P(("grp", "clu"), None),
        P(),
        P(("grp", "clu"), None),
    )
    out_specs = (
        P(("grp", "clu"), None),
        P(("grp", "clu"), None),
        P("grp", None, None),
        P("grp", None),
    )
    return jax.shard_map(local, mesh=mesh, in_specs=in_specs, out_specs=out_specs, check_vma=False)
```

profile of v0, /device:TPU:0, one launch (start us, length us, event | category | flops | bytes accessed | tf_op | source)
XLA Modules:
  0.0 289.2 jit_solution(7991384179787058738)
XLA Ops:
  9.7 7.4 %all-to-all-start = ((s32[16,1,64]{2,1,0:T(1,128)}), s32[16,1,64]{2,1,0:T(1,128)S(1)}, u32[]{:S(2)}, u32[]{:S(2)}) async-start(s32[16,1,64]{2,1,0:T(1,128)} %all_to_all.20), calls=%async_computation | async-start | bytes 16384 | tf_op jit(solution)/shard_map/all_to_all | solution.py:96
  19.9 30.5 %scatter_custom_fusion = s32[8192]{0:T(1024)S(1)} fusion(s32[8192]{0:T(1024)S(1)} %bitcast.134, s32[8192]{0:T(1024)S(1)} %iota.12, s32[]{:T(128)} %constant.11.clone.1), kind=kCustom, calls=%fused_computation.72 | custom fusion | bytes 32772 | tf_op jit(solution)/shard_map/scatter | solution.py:85
  50.4 2.6 convert_reduce_fusion
  53.0 3.4 %convolution_convert_fusion.1.clone.9 = bf16[8192,256]{1,0:T(8,128)(2,1)S(1)} fusion(bf16[8192,256]{1,0:T(8,128)(2,1)} %param.9, bf16[256,256]{1,0:T(8,128)(2,1)S(1)} %copy-done), kind=kOutput, calls=%fused_computation.6.clone.clone.clone.clone.clone.clone.clone.2 | convolution fusion | flops 1075838976 | bytes 8519680 | tf_op jit(solution)/shard_map/dot_general | solution.py:81
  56.4 3.6 %fusion.12 = bf16[256,256]{1,0:T(8,128)(2,1)S(1)} fusion(s32[8192]{0:T(1024)S(1)} %convert_reduce_fusion, f32[256]{0:T(256)S(1)} %bitcast.136, bf16[8192,256]{1,0:T(8,128)(2,1)S(1)} %convolution_convert_fusion.1.clone.9), kind=kOutput, calls=%fused_computation.34 | convolution fusion | flops 1075970048 | bytes 4359168 | tf_op jit(solution)/shard_map/dot_general | solution.py:91
  62.2 6.1 %all-to-all-start.2 = ((bf16[16,64,256]{2,1,0:T(8,128)(2,1)}), bf16[16,64,256]{2,1,0:T(8,128)(2,1)S(1)}, u32[]{:S(2)}, u32[]{:S(2)}) async-start(bf16[16,64,256]{2,1,0:T(8,128)(2,1)} %bitcast.11), calls=%async_computation.2 | async-start | bytes 1048576 | tf_op jit(solution)/shard_map/all_to_all | solution.py:123
  69.6 13.1 %all-to-all-done.2 = bf16[16,64,256]{2,1,0:T(8,128)(2,1)S(1)} async-done(((bf16[16,64,256]{2,1,0:T(8,128)(2,1)}), bf16[16,64,256]{2,1,0:T(8,128)(2,1)S(1)}, u32[]{:S(2)}, u32[]{:S(2)}) %all-to-all-start.2) | async-done | bytes 524320 | tf_op jit(solution)/shard_map/all_to_all | solution.py:123
  82.8 4.1 %all-to-all-start.1 = ((bf16[16,64,256]{2,1,0:T(8,128)(2,1)}), bf16[16,64,256]{2,1,0:T(8,128)(2,1)S(1)}, u32[]{:S(2)}, u32[]{:S(2)}) async-start(bf16[16,64,256]{2,1,0:T(8,128)(2,1)} %bitcast.6), calls=%async_computation.1 | async-start | bytes 1048576 | tf_op jit(solution)/shard_map/all_to_all | solution.py:116
  88.7 9.6 %fusion.2 = pred[128,1024]{1,0:T(8,128)(4,1)S(1)} fusion(s32[128,100]{0,1:T(8,128)S(1)} %copy-done.14), kind=kLoop, calls=%fused_computation.4 | loop fusion | flops 26083328 | bytes 182272 | tf_op jit(solution)/shard_map/reduce_or | solution.py:134
  103.9 3.8 %fusion.55 = (f32[128,4]{0,1:T(4,128)S(1)}, f32[128,4,1024]{0,2,1:T(8,128)}) fusion(pred[128,1024]{0,1:T(8,128)(4,1)} %copy.62, bf16[1024,4,64]{0,2,1:T(8,128)(2,1)S(1)} %copy.84, bf16[128,4,64]{0,2,1:T(8,128)(2,1)} %bitcast.131), kind=kOutput, calls=%fused_computation.86 | convolution fusion | flops 69731328 | bytes 2820096 | tf_op jit(solution)/shard_map/sub | solution.py:33
  107.7 3.1 %convolution_bitcast_fusion.1 = f32[1024,4,64]{0,2,1:T(8,128)S(1)} fusion(bf16[128,4,64]{0,2,1:T(8,128)(2,1)} %bitcast.132, f32[4,1024,128]{2,1,0:T(8,128)S(1)} %fusion.56, f32[128,4,1024]{0,2,1:T(8,128)} %get-tuple-element.23, f32[128,4]{0,1:T(4,128)S(1)} %get-tuple-element.22), kind=kOutput, calls=%fused_computation.21 | convolution fusion | flops 70780416 | bytes 5310464 | tf_op jit(solution)/shard_map/thj,thd->jhd/dot_general | solution.py:52
  111.3 2.0 copy.68
  113.3 4.9 %all-to-all-start.3 = ((f32[16,64,256]{2,1,0:T(8,128)}), f32[16,64,256]{2,1,0:T(8,128)S(1)}, u32[]{:S(2)}, u32[]{:S(2)}) async-start(f32[16,64,256]{2,1,0:T(8,128)} %copy.68), calls=%async_computation.3 | async-start | bytes 2097152 | tf_op jit(solution)/shard_map/all_to_all | solution.py:141
  118.3 3.1 %convolution_bitcast_fusion = f32[1024,4,64]{0,2,1:T(8,128)} fusion(bf16[128,4,64]{0,2,1:T(8,128)(2,1)S(1)} %bitcast.130, f32[128,4,1024]{0,2,1:T(8,128)} %get-tuple-element.23, f32[128,4]{0,1:T(4,128)S(1)} %get-tuple-element.22), kind=kOutput, calls=%fused_computation.20 | convolution fusion | flops 68157440 | bytes 3213312 | tf_op jit(solution)/shard_map/thj,thd->jhd/dot_general | solution.py:55
  123.0 2.0 copy.70
  125.0 16.2 %all-to-all-done.3 = f32[16,64,256]{2,1,0:T(8,128)S(1)} async-done(((f32[16,64,256]{2,1,0:T(8,128)}), f32[16,64,256]{2,1,0:T(8,128)S(1)}, u32[]{:S(2)}, u32[]{:S(2)}) %all-to-all-start.3) | async-done | bytes 1048608 | tf_op jit(solution)/shard_map/all_to_all | solution.py:141
  141.2 6.9 %all-to-all-start.4 = ((f32[16,64,256]{2,1,0:T(8,128)}), f32[16,64,256]{2,1,0:T(8,128)S(1)}, u32[]{:S(2)}, u32[]{:S(2)}) async-start(f32[16,64,256]{2,1,0:T(8,128)} %copy.70), calls=%async_computation.4 | async-start | bytes 2097152 | tf_op jit(solution)/shard_map/all_to_all | solution.py:148
  148.4 1.9 convolution_convert_fusion.6
  150.5 4.3 %convolution_convert_fusion.7 = bf16[4,64,128]{2,1,0:T(8,128)(2,1)S(1)} fusion(bf16[1024,4,64]{0,2,1:T(8,128)(2,1)S(1)} %copy-done.7, f32[4,1024,128]{2,1,0:T(8,128)} %copy-done.3, f32[128,4,1024]{0,2,1:T(8,128)} %get-tuple-element.23, f32[128,4]{0,1:T(4,128)S(1)} %get-tuple-element.22), kind=kOutput, calls=%fused_computation.36 | convolution fusion | flops 70813184 | bytes 4786176 | tf_op jit(solution)/shard_map/thj,jhd->thd/dot_general | solution.py:48
  157.0 14.0 %all-to-all-done.4 = f32[16,64,256]{2,1,0:T(8,128)S(1)} async-done(((f32[16,64,256]{2,1,0:T(8,128)}), f32[16,64,256]{2,1,0:T(8,128)S(1)}, u32[]{:S(2)}, u32[]{:S(2)}) %all-to-all-start.4) | async-done | bytes 1048608 | tf_op jit(solution)/shard_map/all_to_all | solution.py:148
  173.0 6.7 %convolution_convert_fusion = bf16[8192,256]{1,0:T(8,128)(2,1)S(1)} fusion(f32[256,256]{1,0:T(8,128)S(1)} %fusion.10, s32[8192]{0:T(1024)S(1)} %copy-done.16), kind=kOutput, calls=%fused_computation.5 | convolution fusion | flops 6446645248 | bytes 4489216 | tf_op jit(solution)/shard_map/dot_general | solution.py:170
  179.7 2.1 convolution_bitcast_fusion.6
  183.7 95.2 %all-reduce.3.cloned.1.call-done = (f32[4,256,256]{1,2,0:T(8,128)}, f32[256,256]{0,1:T(8,128)}) async-done(((f32[4,256,256]{1,2,0:T(8,128)}, f32[256,256]{0,1:T(8,128)}), (f32[4,256,256]{1,2,0:T(8,128)}, f32[256,256]{0,1:T(8,128)})) %all-reduce.3.cloned.1.call-update) | async-done | bytes 1310736 | tf_op jit(solution)/shard_map/psum | solution.py:168
  278.9 2.6 copy.75
  (77 shorter events, 25.5 us)
Async XLA Ops:
  7.2 45.8 %copy-start = (bf16[256,256]{1,0:T(8,128)(2,1)S(1)}, bf16[256,256]{1,0:T(8,128)(2,1)}, u32[]{:S(2)}) copy-start(bf16[256,256]{1,0:T(8,128)(2,1)} %param.10) | copy-start | bytes 393220
  9.7 50.3 %all-to-all-start = ((s32[16,1,64]{2,1,0:T(1,128)}), s32[16,1,64]{2,1,0:T(1,128)S(1)}, u32[]{:S(2)}, u32[]{:S(2)}) async-start(s32[16,1,64]{2,1,0:T(1,128)} %all_to_all.20), calls=%async_computation | async-start | bytes 16384 | tf_op jit(solution)/shard_map/all_to_all | solution.py:96
  52.9 3.5 %copy-start.15 = (s32[8192]{0:T(1024)}, s32[8192]{0:T(1024)S(1)}, u32[]{:S(2)}) copy-start(s32[8192]{0:T(1024)S(1)} %convert_reduce_fusion) | copy-start | bytes 98308
  56.4 4.4 %copy-start.8 = (bf16[4,256,256]{2,1,0:T(8,128)(2,1)S(1)}, bf16[4,256,256]{2,1,0:T(8,128)(2,1)}, u32[]{:S(2)}) copy-start(bf16[4,256,256]{2,1,0:T(8,128)(2,1)} %param.16) | copy-start | bytes 1572868
  60.0 26.9 %copy-start.12 = (bf16[128,256]{1,0:T(8,128)(2,1)S(1)}, bf16[128,256]{1,0:T(8,128)(2,1)}, u32[]{:S(2)}) copy-start(bf16[128,256]{1,0:T(8,128)(2,1)} %param.15) | copy-start | bytes 196612
  60.8 27.0 %copy-start.11 = (bf16[128,256]{1,0:T(8,128)(2,1)S(1)}, bf16[128,256]{1,0:T(8,128)(2,1)}, u32[]{:S(2)}) copy-start(bf16[128,256]{1,0:T(8,128)(2,1)} %param.17) | copy-start | bytes 196612
  62.2 26.6 %copy-start.14 = (s32[128,100]{0,1:T(8,128)S(1)}, s32[128,100]{0,1:T(8,128)}, u32[]{:S(2)}) copy-start(s32[128,100]{0,1:T(8,128)} %param.14) | copy-start | bytes 153604
  62.2 20.6 %all-to-all-start.2 = ((bf16[16,64,256]{2,1,0:T(8,128)(2,1)}), bf16[16,64,256]{2,1,0:T(8,128)(2,1)S(1)}, u32[]{:S(2)}, u32[]{:S(2)}) async-start(bf16[16,64,256]{2,1,0:T(8,128)(2,1)} %bitcast.11), calls=%async_computation.2 | async-start | bytes 1048576 | tf_op jit(solution)/shard_map/all_to_all | solution.py:123
  82.8 18.6 %all-to-all-start.1 = ((bf16[16,64,256]{2,1,0:T(8,128)(2,1)}), bf16[16,64,256]{2,1,0:T(8,128)(2,1)S(1)}, u32[]{:S(2)}, u32[]{:S(2)}) async-start(bf16[16,64,256]{2,1,0:T(8,128)(2,1)} %bitcast.6), calls=%async_computation.1 | async-start | bytes 1048576 | tf_op jit(solution)/shard_map/all_to_all | solution.py:116
  100.3 3.6 %copy-start.4 = (bf16[1024,4,64]{0,2,1:T(8,128)(2,1)}, bf16[1024,4,64]{0,2,1:T(8,128)(2,1)S(1)}, u32[]{:S(2)}) copy-start(bf16[1024,4,64]{0,2,1:T(8,128)(2,1)S(1)} %copy.85) | copy-start | bytes 1572868
  102.4 5.3 %copy-start.6 = (bf16[1024,4,64]{0,2,1:T(8,128)(2,1)}, bf16[1024,4,64]{0,2,1:T(8,128)(2,1)S(1)}, u32[]{:S(2)}) copy-start(bf16[1024,4,64]{0,2,1:T(8,128)(2,1)S(1)} %copy.84) | copy-start | bytes 1572868
  103.9 3.8 %copy-start.3 = (f32[4,1024,128]{2,1,0:T(8,128)}, f32[4,1024,128]{2,1,0:T(8,128)S(1)}, u32[]{:S(2)}) copy-start(f32[4,1024,128]{2,1,0:T(8,128)S(1)} %fusion.56) | copy-start | bytes 6291460
  111.3 7.0 %copy-start.13 = (bf16[128,256]{0,1:T(8,128)(2,1)S(1)}, bf16[128,256]{0,1:T(8,128)(2,1)}, u32[]{:S(2)}) copy-start(bf16[128,256]{0,1:T(8,128)(2,1)} %copy.65) | copy-start | bytes 196612
  113.3 27.9 %all-to-all-start.3 = ((f32[16,64,256]{2,1,0:T(8,128)}), f32[16,64,256]{2,1,0:T(8,128)S(1)}, u32[]{:S(2)}, u32[]{:S(2)}) async-start(f32[16,64,256]{2,1,0:T(8,128)} %copy.68), calls=%async_computation.3 | async-start | bytes 2097152 | tf_op jit(solution)/shard_map/all_to_all | solution.py:141
  125.0 23.3 %copy-start.5 = (bf16[1024,4,64]{0,2,1:T(8,128)(2,1)S(1)}, bf16[1024,4,64]{0,2,1:T(8,128)(2,1)}, u32[]{:S(2)}) copy-start(bf16[1024,4,64]{0,2,1:T(8,128)(2,1)} %copy-done.4) | copy-start | bytes 1572868
  141.2 29.8 %all-to-all-start.4 = ((f32[16,64,256]{2,1,0:T(8,128)}), f32[16,64,256]{2,1,0:T(8,128)S(1)}, u32[]{:S(2)}, u32[]{:S(2)}) async-start(f32[16,64,256]{2,1,0:T(8,128)} %copy.70), calls=%async_computation.4 | async-start | bytes 2097152 | tf_op jit(solution)/shard_map/all_to_all | solution.py:148
  148.1 2.4 copy-start.7
  148.1 130.8 %all-reduce.3.cloned.1.call-start = ((), (), s32[]{:S(2)}) async-start(), calls=%async_computation.5 | async-start | bytes 2621440 | tf_op jit(solution)/shard_map/psum | solution.py:168
  154.8 1.8 copy-start.9
  156.2 16.7 %copy-start.16 = (s32[8192]{0:T(1024)S(1)}, s32[8192]{0:T(1024)}, u32[]{:S(2)}) copy-start(s32[8192]{0:T(1024)} %copy-done.15) | copy-start | bytes 98308
  173.0 6.7 %copy-start.1 = (bf16[8192,256]{1,0:T(8,128)(2,1)S(1)}, bf16[8192,256]{1,0:T(8,128)(2,1)}, u32[]{:S(2)}) copy-start(bf16[8192,256]{1,0:T(8,128)(2,1)} %param.9) | copy-start | bytes 12582916
  179.7 2.1 copy-start.2
  278.9 2.6 copy-start.10
Sparse Core Ops, SparseCore 0:
  183.0 95.9 all-reduce.2
where the time goes:
time: 290 us; the launch traced here: 289 us
  waiting for transfers between devices  140 us (48%)
  local copies, waits for them, and re-layouts  46.1 us (16%)
  matrix products  41.4 us (14%)
  starting transfers between devices  29.7 us (10%)
  other arithmetic  17.8 us (6%)
  between operations  14.5 us (5%)
    psum x1, waiting for transfers between devices, local(): grad_attn = lax.psum(jnp.stack([grad_wq, grad_wk, grad_wv, grad_wo]), 'clu')  95.2 us
    scatter x1, local copies, waits for them, and re-layouts, local(): jnp.zeros((row_count,), jnp.int32).at[members]  30.5 us
    all_to_all x1, waiting for transfers between devices, local(): lax.all_to_all(key_grad.reshape(owners, per_owner, width), 'clu', split_a...  16.2 us
    all_to_all x1, waiting for transfers between devices, local(): lax.all_to_all(value_grad.reshape(owners, per_owner, width), 'clu', split...  14 us
    all_to_all x1, waiting for transfers between devices, local(): lax.all_to_all(value_sent.reshape(owners, per_owner, width), 'clu', split...  13.1 us
    reduce_or x1, other arithmetic, local(): pick_mask = jnp.any(picks[:, :, None] == pool_iota[None, None, :], axis=1)  9.62 us
    all_to_all x1, starting transfers between devices, local(): lax.all_to_all(pool_row.reshape(owners, per_owner), 'clu', split_axis=0,...  7.39 us
    all_to_all x1, starting transfers between devices, local(): lax.all_to_all(value_grad.reshape(owners, per_owner, width), 'clu', split...  6.86 us
  transfers between devices with their start and end apart: 6, of which 5 were waited for; matrix products, arithmetic and copies ran while one was open for 25% of the time, Pallas kernels for 0%

commit v1 on v0

v1 whole, which is shorter than its diff:
```python
import functools

import jax
import jax.numpy as jnp
from jax import lax
from jax.experimental import pallas as pl
from jax.experimental.pallas import tpu as pltpu
from jax.sharding import PartitionSpec as P

HEADS = 4
LANES = 128
F32 = jnp.float32
BF16 = jnp.bfloat16
VMEM_LIMIT = 48 * 1024 * 1024


def dot(a, b):
    return jnp.dot(a, b, preferred_element_type=F32)


def dot_nt(a, b):
    return lax.dot_general(a, b, (((1,), (1,)), ((), ())), preferred_element_type=F32)


def dot_tn(a, b):
    return lax.dot_general(a, b, (((0,), (0,)), ((), ())), preferred_element_type=F32)


def iota(shape, dim):
    return lax.broadcasted_iota(jnp.int32, shape, dim)


def ones_where(cond):
    return jnp.where(cond, 1.0, 0.0).astype(BF16)


def column_of(row):
    n = row.shape[1]
    wide = jnp.where(iota((n, n), 0) == iota((n, n), 1), row, 0.0)
    return jnp.sum(wide, axis=1, keepdims=True)


def member_onehot(table_ref, at, clusters):
    sub = iota((clusters, LANES), 0).astype(F32)
    parts = [ones_where(table_ref[pl.ds(at + k, 1), :] == sub) for k in range(2)]
    return jnp.concatenate(parts, axis=1)


def means_kernel(counts_s, counts_v, members, raw, mean_out, table, acc):
    step = pl.program_id(0)
    clusters = counts_v.shape[1]
    groups = members.shape[0]

    @pl.when(step == 0)
    def _():
        place = iota((groups, LANES), 0) * LANES + iota((groups, LANES), 1)

        def body(j, carry):
            end, cluster = carry
            end = end + counts_s[0, j]
            return end, cluster + jnp.where(place >= end, 1, 0)

        _, cluster = lax.fori_loop(
            0, clusters, body, (jnp.int32(0), jnp.zeros((groups, LANES), jnp.int32)), unroll=8
        )
        cluster = cluster.astype(F32)
        rows = members[...]
        high = rows // LANES
        low = rows % LANES
        total = jnp.zeros((groups, LANES), F32)
        high_iota = iota((groups, LANES), 0)
        low_iota = iota((LANES, LANES), 0)
        for k in range(0, groups, 2):
            a_parts, b_parts = [], []
            for m in (k, k + 1):
                a_parts.append(
                    jnp.where(high[m : m + 1] == high_iota, cluster[m : m + 1], 0.0).astype(BF16)
                )
                b_parts.append(ones_where(low[m : m + 1] == low_iota))
            total = total + dot_nt(
                jnp.concatenate(a_parts, axis=1), jnp.concatenate(b_parts, axis=1)
            )
        table[...] = total
        acc[...] = jnp.zeros_like(acc)

    blocks = raw.shape[0] // 256
    total = acc[...]
    for k in range(blocks):
        onehot = member_onehot(table, (step * blocks + k) * 2, clusters)
        total = total + dot(onehot, raw[k * 256 : k * 256 + 256, :])
    acc[...] = total

    @pl.when(step == pl.num_programs(0) - 1)
    def _():
        mean_out[...] = (acc[...] / column_of(counts_v[...].astype(F32))).astype(BF16)


def cluster_means(counts, members, raw_rows):
    clusters = counts.shape[1]
    rows, width = raw_rows.shape
    groups = rows // LANES
    block = 1024
    return pl.pallas_call(
        means_kernel,
        grid=(rows // block,),
        in_specs=[
            pl.BlockSpec(memory_space=pltpu.SMEM),
            pl.BlockSpec((1, clusters), lambda i: (0, 0)),
            pl.BlockSpec((groups, LANES), lambda i: (0, 0)),
            pl.BlockSpec((block, width), lambda i: (i, 0)),
        ],
        out_specs=[
            pl.BlockSpec((clusters, width), lambda i: (0, 0)),
            pl.BlockSpec((groups, LANES), lambda i: (0, 0)),
        ],
        out_shape=[
            jax.ShapeDtypeStruct((clusters, width), BF16),
            jax.ShapeDtypeStruct((groups, LANES), F32),
        ],
        scratch_shapes=[pltpu.VMEM((clusters, width), F32)],
        compiler_params=pltpu.CompilerParams(vmem_limit_bytes=VMEM_LIMIT),
        cost_estimate=pl.CostEstimate(
            flops=2 * rows * clusters * width, bytes_accessed=2 * rows * width, transcendentals=0
        ),
    )(counts, counts, members.reshape(groups, LANES), raw_rows)


def spread_heads(rows):
    head = iota(rows.shape, 1) // (rows.shape[1] // HEADS)
    return jnp.concatenate([jnp.where(head == h, rows, 0.0) for h in range(HEADS)], axis=0).astype(
        BF16
    )


def targets_kernel(scale, picks, queries, out_grad, weights, bias, query_heads, mixed_heads):
    query_proj = dot(queries[...], weights[0]).astype(BF16)
    query_heads[...] = spread_heads(query_proj.astype(F32) * scale)
    grad_mixed = dot_nt(out_grad[...], weights[3]).astype(BF16)
    mixed_heads[...] = spread_heads(grad_mixed.astype(F32))
    count, targets = picks.shape
    block = 128

    def body(b, carry):
        at = pl.multiple_of(b * block, block)
        slot = iota((block, targets), 0) + at
        found = jnp.zeros((block, targets), F32)
        for i in range(count):
            found = jnp.where(picks[i : i + 1, :] == slot, 1.0, found)
        bias[pl.ds(at, block), :] = jnp.where(found > 0.5, 0.0, -1e30)
        return carry

    lax.fori_loop(0, bias.shape[0] // block, body, 0)


def target_terms(scale, picks_t, queries, out_grad, weights, pooled):
    targets, width = queries.shape
    return pl.pallas_call(
        functools.partial(targets_kernel, scale),
        out_shape=[
            jax.ShapeDtypeStruct((pooled, targets), F32),
            jax.ShapeDtypeStruct((HEADS * targets, width), BF16),
            jax.ShapeDtypeStruct((HEADS * targets, width), BF16),
        ],
        compiler_params=pltpu.CompilerParams(vmem_limit_bytes=VMEM_LIMIT),
        cost_estimate=pl.CostEstimate(
            flops=4 * targets * pooled * picks_t.shape[0],
            bytes_accessed=4 * pooled * targets,
            transcendentals=0,
        ),
    )(picks_t, queries, out_grad, weights)


def attention_kernel(
    scale, owners, raw, enc, weights, queries, out_grad, bias, query_heads, mixed_heads, send, grad_query, grads
):
    pooled, width = raw.shape
    targets = queries.shape[0]
    raw_pool = raw[...]
    emb = dot(raw_pool, enc[...]).astype(BF16)
    key = dot(emb, weights[1]).astype(BF16)
    value = dot(emb, weights[2]).astype(BF16)
    key_t = dot_nt(weights[1].T, emb).astype(BF16)
    value_t = dot_nt(weights[2].T, emb).astype(BF16)
    pair_bias = jnp.concatenate([bias[...], bias[...]], axis=1)
    head_of_row = iota((width, targets), 0) // (width // HEADS)
    key_grad = jnp.zeros((pooled, width), F32)
    value_grad = jnp.zeros((pooled, width), F32)
    mixed_t = jnp.zeros((width, targets), F32)
    qproj_t = jnp.zeros((width, targets), F32)
    for pair in range(HEADS // 2):
        rows = slice(pair * 2 * targets, (pair + 1) * 2 * targets)
        query_pair = query_heads[rows, :]
        mixed_pair = mixed_heads[rows, :]
        scores = dot_nt(key, query_pair) + pair_bias
        raised = jnp.exp(scores - jnp.max(scores, axis=0, keepdims=True))
        attend = raised * (1.0 / jnp.sum(raised, axis=0, keepdims=True))
        attend_low = attend.astype(BF16)
        weighted = attend * dot_nt(value, mixed_pair)
        score_low = (weighted - attend * jnp.sum(weighted, axis=0, keepdims=True)).astype(BF16)
        value_grad = value_grad + dot(attend_low, mixed_pair)
        key_grad = key_grad + dot(score_low, query_pair)
        mixed_both = dot(value_t, attend_low)
        qproj_both = dot(key_t, score_low)
        for k in range(2):
            own = head_of_row == pair * 2 + k
            cols = slice(k * targets, (k + 1) * targets)
            mixed_t = jnp.where(own, mixed_both[:, cols], mixed_t)
            qproj_t = jnp.where(own, qproj_both[:, cols], qproj_t)
    grad_qproj = (qproj_t * scale).T.astype(BF16)
    grad_query[...] = dot_nt(grad_qproj, weights[0]).astype(BF16)
    key_low = key_grad.astype(BF16)
    value_low = value_grad.astype(BF16)
    emb_grad = (dot_nt(key_low, weights[1]) + dot_nt(value_low, weights[2])).astype(BF16)
    grads[0:width, :] = dot_tn(queries[...], grad_qproj)
    grads[width : 2 * width, :] = dot_tn(emb, key_low)
    grads[2 * width : 3 * width, :] = dot_tn(emb, value_low)
    grads[3 * width : 4 * width, :] = dot(mixed_t.astype(BF16), out_grad[...])
    grads[4 * width : 5 * width, :] = dot_tn(raw_pool, emb_grad)
    if grads.shape[0] > 5 * width:
        grads[5 * width :, :] = jnp.zeros((grads.shape[0] - 5 * width, width), F32)
    per_owner = pooled // owners
    chunk = grads.shape[0] // owners
    for o in range(owners):
        send[o, 0:per_owner, :] = emb_grad[o * per_owner : (o + 1) * per_owner, :]
        send[o, per_owner:, :] = grads[o * chunk : (o + 1) * chunk, :].astype(BF16)


def attention(scale, owners, chunk, raw_pool, enc, weights, queries, out_grad, bias, query_heads, mixed_heads):
    pooled, width = raw_pool.shape
    return pl.pallas_call(
        functools.partial(attention_kernel, scale, owners),
        out_shape=[
            jax.ShapeDtypeStruct((owners, pooled // owners + chunk, width), BF16),
            jax.ShapeDtypeStruct(queries.shape, BF16),
        ],
        scratch_shapes=[pltpu.VMEM((owners * chunk, width), F32)],
        compiler_params=pltpu.CompilerParams(vmem_limit_bytes=VMEM_LIMIT),
    )(raw_pool, enc, weights, queries, out_grad, bias, query_heads, mixed_heads)


def rows_kernel(counts, ids, table, back, out, share):
    step = pl.program_id(0)
    clusters = counts.shape[1]
    owners, _, width = back.shape
    per_owner = ids.shape[1] // owners

    @pl.when(step == 0)
    def _():
        total = jnp.zeros((clusters, width), F32)
        many = 256 // per_owner
        for o in range(0, owners, many):
            at = o * per_owner
            onehot = ones_where(ids[:, at : at + 256] == iota((clusters, 256), 0))
            terms = jnp.concatenate([back[o + k, 0:per_owner, :] for k in range(many)], axis=0)
            total = total + dot(onehot, terms)
        share[...] = (total / column_of(counts[...].astype(F32))).astype(BF16)

    blocks = out.shape[0] // 256
    for k in range(blocks):
        onehot = member_onehot(table, (step * blocks + k) * 2, clusters)
        out[k * 256 : k * 256 + 256, :] = dot_tn(onehot, share[...]).astype(BF16)


def member_grads(counts, ids, table, back, rows):
    clusters = counts.shape[1]
    width = back.shape[2]
    block = 1024
    return pl.pallas_call(
        rows_kernel,
        grid=(rows // block,),
        in_specs=[
            pl.BlockSpec((1, clusters), lambda i: (0, 0)),
            pl.BlockSpec(ids.shape, lambda i: (0, 0)),
            pl.BlockSpec(table.shape, lambda i: (0, 0)),
            pl.BlockSpec(back.shape, lambda i: (0, 0, 0)),
        ],
        out_specs=pl.BlockSpec((block, width), lambda i: (i, 0)),
        out_shape=jax.ShapeDtypeStruct((rows, width), BF16),
        scratch_shapes=[pltpu.VMEM((clusters, width), BF16)],
        compiler_params=pltpu.CompilerParams(vmem_limit_bytes=VMEM_LIMIT),
        cost_estimate=pl.CostEstimate(
            flops=2 * rows * clusters * width, bytes_accessed=2 * rows * width, transcendentals=0
        ),
    )(counts, ids, table, back)


def swap(blocks):
    return lax.all_to_all(blocks, "clu", split_axis=0, concat_axis=0, tiled=True)


def local(raw_rows, enc_weight, counts, member_rows, pool, picks, queries, attn_weights, out_grad):
    clusters = counts.shape[1]
    rows, width = raw_rows.shape
    owners = lax.axis_size("clu")
    pooled = pool.shape[1]
    per_owner = pooled // owners
    scale = (width // HEADS) ** -0.5
    chunk = -(-5 * width // (owners * 16)) * 16

    wanted = swap(pool.reshape(owners, per_owner))
    ids = (wanted % clusters).reshape(1, pooled)
    means, table = cluster_means(counts, member_rows, raw_rows)
    asked = (ids[0][:, None] == jnp.arange(clusters, dtype=jnp.int32)[None, :]).astype(BF16)
    sent = jnp.dot(asked, means, preferred_element_type=F32).astype(BF16)
    raw_pool = swap(sent.reshape(owners, per_owner, width)).reshape(pooled, width)
    bias, query_heads, mixed_heads = target_terms(
        scale, picks.T, queries, out_grad, attn_weights, pooled
    )
    send, grad_query = attention(
        scale, owners, chunk, raw_pool, enc_weight, attn_weights, queries, out_grad, bias, query_heads, mixed_heads
    )
    back = swap(send)
    summed = jnp.sum(back[:, per_owner:, :].astype(F32), axis=0).astype(BF16)
    grads = swap(jnp.broadcast_to(summed[None], (owners, chunk, width)))
    grads = grads.reshape(owners * chunk, width)[: 5 * width].astype(F32)
    grad_rows = member_grads(counts, ids, table, back, rows)
    grad_attn = grads[: 4 * width].reshape(4, width, width)
    return grad_query, grad_rows, grad_attn, grads[4 * width :]


def solution(mesh):
    split = P(("grp", "clu"), None)
    in_specs = (split, P(), split, split, split, split, split, P(), split)
    out_specs = (split, split, P("grp", None, None), P("grp", None))
    return jax.shard_map(local, mesh=mesh, in_specs=in_specs, out_specs=out_specs, check_vma=False)
```

time: 290 us -> 103 us (0.36)
  waiting for transfers between devices: 140 us -> 21.7 us
  matrix products: 41.4 us -> 1.15 us
  local copies, waits for them, and re-layouts: 46.1 us -> 7.63 us
  blocking collectives: 0 us -> 33.4 us
  Pallas kernels: 0 us -> 18.8 us
  other arithmetic: 17.8 us -> 2.33 us
  between operations: 14.5 us -> 0.8 us
  starting transfers between devices: 29.7 us -> 17 us
    psum x1 -> x0, waiting for transfers between devices: 95.2 us -> none  [local(): grad_attn = lax.psum(jnp.stack([grad_wq, grad_wk, grad_wv, grad_wo]), 'clu')]
    dot_general x22 -> x1, matrix products: 37.6 us -> 1.15 us  [local(): sent = jnp.dot(asked, means, preferred_element_type=F32).astype(BF16)]
    all_to_all x0 -> x1, blocking collectives: none -> 33.4 us  [swap(): lax.all_to_all(blocks, 'clu', split_axis=0, concat_axis=0, tiled=True)]
    scatter x1 -> x0, local copies, waits for them, and re-layouts: 30.5 us -> none  [local(): jnp.zeros((row_count,), jnp.int32).at[members]]
    all_to_all x5 -> x3, waiting for transfers between devices: 44.4 us -> 21.7 us  [swap(): lax.all_to_all(blocks, 'clu', split_axis=0, concat_axis=0, tiled=True)]
    pallas_call x0 -> x4, Pallas kernels: none -> 18.8 us  [the longest x1 5.31 us: member_grads(): pl.pallas_call(rows_kernel, grid=(rows // block,), in_specs=[pl.BlockSpec...]
    all_to_all x5 -> x3, starting transfers between devices: 29.4 us -> 17 us  [swap(): lax.all_to_all(blocks, 'clu', split_axis=0, concat_axis=0, tiled=True)]
    reduce_or x1 -> x0, other arithmetic: 9.62 us -> none  [local(): pick_mask = jnp.any(picks[:, :, None] == pool_iota[None, None, :], axis=1)]
  transfers between devices with their start and end apart: 6 -> 3, of which waited for: 5 -> 2; matrix products, arithmetic and copies ran while one was open for 25% -> 0% of each run, Pallas kernels for 0% -> 14%
where the time goes in v1:
time: 103 us
  blocking collectives  33.4 us (32%)
  waiting for transfers between devices  21.7 us (21%)
  Pallas kernels  18.8 us (18%)
  starting transfers between devices  17 us (17%)
  local copies, waits for them, and re-layouts  7.63 us (7%)
  other arithmetic  2.33 us (2%)
  matrix products  1.15 us (1%)
    all_to_all x1, blocking collectives, swap(): lax.all_to_all(blocks, 'clu', split_axis=0, concat_axis=0, tiled=True)  33.4 us
    all_to_all x3, waiting for transfers between devices, swap(): lax.all_to_all(blocks, 'clu', split_axis=0, concat_axis=0, tiled=True)  21.7 us
    all_to_all x3, starting transfers between devices, swap(): lax.all_to_all(blocks, 'clu', split_axis=0, concat_axis=0, tiled=True)  17 us
    pallas_call x1, Pallas kernels, member_grads(): pl.pallas_call(rows_kernel, grid=(rows // block,), in_specs=[pl.BlockSpec...  5.31 us
    pallas_call x1, Pallas kernels, cluster_means(): pl.pallas_call(means_kernel, grid=(rows // block,), in_specs=[pl.BlockSpe...  5.16 us
    pallas_call x1, Pallas kernels, attention(): pl.pallas_call(functools.partial(attention_kernel, scale, owners), out_sh...  4.5 us
    unnamed x19, local copies, waits for them, and re-layouts  4.17 us
    pallas_call x1, Pallas kernels, target_terms(): pl.pallas_call(functools.partial(targets_kernel, scale), out_shape=[jax.S...  3.87 us
  transfers between devices with their start and end apart: 3, of which 2 were waited for; matrix products, arithmetic and copies ran while one was open for 0% of the time, Pallas kernels for 14%

profile of v1, /device:TPU:0, one launch (start us, length us, event | category | flops | bytes accessed | tf_op | source)
XLA Modules:
  0.0 102.8 jit_solution(16980402082484255138)
XLA Ops:
  0.6 0.5 broadcast.76
  1.1 1.3 %reduce.9 = s32[1024]{0:T(1024)S(1)} reduce(s32[1,1024]{1,0:T(1,128)} %param.13, s32[]{:T(128)} %broadcast.76), dimensions={0}, to_apply=%param.13.reduce_sub_computation.3 | reduce | bytes 8196 | tf_op args[4]
  2.5 0.7 all_to_all.19
  3.2 7.4 %all-to-all-start = ((s32[16,1,64]{2,1,0:T(1,128)}), s32[16,1,64]{2,1,0:T(1,128)S(1)}, u32[]{:S(2)}, u32[]{:S(2)}) async-start(s32[16,1,64]{2,1,0:T(1,128)} %all_to_all.19), calls=%async_computation | async-start | bytes 16384 | tf_op jit(solution)/shard_map/all_to_all | solution.py:288
  10.6 2.2 %copy-done = bf16[8192,256]{1,0:T(8,128)(2,1)S(1)} copy-done((bf16[8192,256]{1,0:T(8,128)(2,1)S(1)}, bf16[8192,256]{1,0:T(8,128)(2,1)}, u32[]{:S(2)}) %copy-start) | copy-done | bytes 4194328
  12.8 0.8 copy-done.6
  13.5 0.7 copy-done.7
  14.2 5.2 %shard_map.120 = (bf16[256,256]{1,0:T(8,128)(2,1)S(1)}, f32[64,128]{1,0:T(8,128)S(1)}) custom-call(s32[1,256]{1,0:T(1,128)S(1)} %copy-done.7, s32[1,256]{1,0:T(1,128)S(1)} %copy-done.7, s32[64,128]{1,0:T(8,128)S(1)} %bitcast.12, bf16[8192,256]{1,0:T(8,128)(2,1)S(1)} %copy-done), custom_call_target="tpu_custom_call" | custom-call | flops 1073741824 | bytes 4194304 | tf_op jit(solution)/shard_map/pallas_call | solution.py:103
  19.4 0.7 reduce.10
  20.3 1.1 %convolution_convert_fusion = bf16[1024,256]{1,0:T(8,128)(2,1)} fusion(bf16[256,256]{1,0:T(8,128)(2,1)S(1)} %get-tuple-element.11, s32[1024]{0:T(1024)S(1)} %add_select_fusion), kind=kOutput, calls=%fused_computation | convolution fusion | flops 134742016 | bytes 659456 | tf_op jit(solution)/shard_map/dot_general | solution.py:304
  21.4 6.0 %all-to-all-start.1 = ((bf16[16,64,256]{2,1,0:T(8,128)(2,1)}), bf16[16,64,256]{2,1,0:T(8,128)(2,1)S(1)}, u32[]{:S(2)}, u32[]{:S(2)}) async-start(bf16[16,64,256]{2,1,0:T(8,128)(2,1)} %bitcast.1), calls=%async_computation.1 | async-start | bytes 1048576 | tf_op jit(solution)/shard_map/all_to_all | solution.py:288
  27.5 3.9 %shard_map.121 = (f32[1024,128]{1,0:T(8,128)S(1)}, bf16[512,256]{1,0:T(8,128)(2,1)S(1)}, bf16[512,256]{1,0:T(8,128)(2,1)S(1)}) custom-call(s32[100,128]{1,0:T(8,128)S(1)} %bitcast.11, bf16[128,256]{1,0:T(8,128)(2,1)S(1)} %copy-done.2, bf16[128,256]{1,0:T(8,128)(2,1)S(1)} %copy-done.3, bf16[4,256,256]{2,1,0:T(8,128)(2,1)S(1)} %copy-done.1), custom_call_target="tpu_custom_call" | custom-call | flops 52428800 | bytes 524288 | tf_op jit(solution)/shard_map/pallas_call | solution.py:157
  31.3 10.6 %all-to-all-done.1 = bf16[16,64,256]{2,1,0:T(8,128)(2,1)S(1)} async-done(((bf16[16,64,256]{2,1,0:T(8,128)(2,1)}), bf16[16,64,256]{2,1,0:T(8,128)(2,1)S(1)}, u32[]{:S(2)}, u32[]{:S(2)}) %all-to-all-start.1) | async-done | bytes 524320 | tf_op jit(solution)/shard_map/all_to_all | solution.py:288
  41.9 4.5 %shard_map.122 = (bf16[16,144,256]{2,1,0:T(8,128)(2,1)S(1)}, bf16[128,256]{1,0:T(8,128)(2,1)}) custom-call(bf16[1024,256]{1,0:T(8,128)(2,1)S(1)} %bitcast.10, bf16[256,256]{1,0:T(8,128)(2,1)S(1)} %copy-done.4, bf16[4,256,256]{2,1,0:T(8,128)(2,1)S(1)} %copy-done.1, bf16[128,256]{1,0:T(8,128)(2,1)S(1)} %copy-done.2, bf16[128,256]{1,0:T(8,128)(2,1)S(1)} %copy-done.3, ...), custom_call_target="tpu_custom_call" | custom-call | tf_op jit(solution)/shard_map/pallas_call | solution.py:230
  46.4 33.4 %all_to_all.30.back = bf16[16,144,256]{2,1,0:T(8,128)(2,1)S(1)} all-to-all(bf16[16,144,256]{2,1,0:T(8,128)(2,1)S(1)} %get-tuple-element.17), channel_id=1, replica_groups=mesh['grp'=2,'clu'=16] {'clu'}, dimensions={0} | all-to-all | bytes 2359296 | tf_op jit(solution)/shard_map/all_to_all | solution.py:288
  79.8 0.1 slice_reduce_fusion
  79.9 0.9 broadcast_in_dim.2
  80.8 3.6 %all-to-all-start.3 = ((bf16[16,80,256]{2,1,0:T(8,128)(2,1)}), bf16[16,80,256]{2,1,0:T(8,128)(2,1)S(1)}, u32[]{:S(2)}, u32[]{:S(2)}) async-start(bf16[16,80,256]{2,1,0:T(8,128)(2,1)} %broadcast_in_dim.2), calls=%async_computation.3 | async-start | bytes 1310720 | tf_op jit(solution)/shard_map/all_to_all | solution.py:288
  84.4 0.1 all_to_all.23
  84.5 5.3 %shard_map.123 = bf16[8192,256]{1,0:T(8,128)(2,1)} custom-call(s32[1,256]{1,0:T(1,128)S(1)} %copy-done.8, s32[1,1024]{1,0:T(1,128)S(1)} %and_select_fusion.ids, f32[64,128]{1,0:T(8,128)S(1)} %get-tuple-element.16.table, bf16[16,144,256]{2,1,0:T(8,128)(2,1)S(1)} %all_to_all.30.back), custom_call_target="tpu_custom_call" | custom-call | flops 1073741824 | bytes 4194304 | tf_op jit(solution)/shard_map/pallas_call | solution.py:268
  89.8 11.1 %all-to-all-done.3 = bf16[16,80,256]{2,1,0:T(8,128)(2,1)S(1)} async-done(((bf16[16,80,256]{2,1,0:T(8,128)(2,1)}), bf16[16,80,256]{2,1,0:T(8,128)(2,1)S(1)}, u32[]{:S(2)}, u32[]{:S(2)}) %all-to-all-start.3) | async-done | bytes 655392 | tf_op jit(solution)/shard_map/all_to_all | solution.py:288
  100.9 0.1 bitcast_convert_fusion
  101.1 0.7 slice.14
  101.8 1.0 %slice.13 = f32[1024,256]{1,0:T(8,128)} slice(f32[1280,256]{1,0:T(8,128)S(1)} %bitcast_convert_fusion), slice={[0:1024], [0:256]} | slice | bytes 2097152 | tf_op jit(solution)/shard_map/slice | solution.py:317
  (19 shorter events, 0.1 us)
Async XLA Ops:
  3.2 16.3 %all-to-all-start = ((s32[16,1,64]{2,1,0:T(1,128)}), s32[16,1,64]{2,1,0:T(1,128)S(1)}, u32[]{:S(2)}, u32[]{:S(2)}) async-start(s32[16,1,64]{2,1,0:T(1,128)} %all_to_all.19), calls=%async_computation | async-start | bytes 16384 | tf_op jit(solution)/shard_map/all_to_all | solution.py:288
  10.6 2.2 %copy-start = (bf16[8192,256]{1,0:T(8,128)(2,1)S(1)}, bf16[8192,256]{1,0:T(8,128)(2,1)}, u32[]{:S(2)}) copy-start(bf16[8192,256]{1,0:T(8,128)(2,1)} %raw.1) | copy-start | bytes 12582916
  12.8 0.8 copy-start.6
  13.5 0.7 copy-start.7
  19.4 8.1 %copy-start.1 = (bf16[4,256,256]{2,1,0:T(8,128)(2,1)S(1)}, bf16[4,256,256]{2,1,0:T(8,128)(2,1)}, u32[]{:S(2)}) copy-start(bf16[4,256,256]{2,1,0:T(8,128)(2,1)} %weights.3) | copy-start | bytes 1572868
  19.4 8.1 %copy-start.2 = (bf16[128,256]{1,0:T(8,128)(2,1)S(1)}, bf16[128,256]{1,0:T(8,128)(2,1)}, u32[]{:S(2)}) copy-start(bf16[128,256]{1,0:T(8,128)(2,1)} %queries.3) | copy-start | bytes 196612
  19.4 8.1 %copy-start.3 = (bf16[128,256]{1,0:T(8,128)(2,1)S(1)}, bf16[128,256]{1,0:T(8,128)(2,1)}, u32[]{:S(2)}) copy-start(bf16[128,256]{1,0:T(8,128)(2,1)} %out_grad.3) | copy-start | bytes 196612
  19.4 8.1 %copy-start.5 = (s32[128,100]{0,1:T(8,128)S(1)}, s32[128,100]{0,1:T(8,128)}, u32[]{:S(2)}) copy-start(s32[128,100]{0,1:T(8,128)} %param.14) | copy-start | bytes 153604
  19.4 22.5 %copy-start.4 = (bf16[256,256]{1,0:T(8,128)(2,1)S(1)}, bf16[256,256]{1,0:T(8,128)(2,1)}, u32[]{:S(2)}) copy-start(bf16[256,256]{1,0:T(8,128)(2,1)} %enc.1) | copy-start | bytes 393220
  21.4 20.5 %all-to-all-start.1 = ((bf16[16,64,256]{2,1,0:T(8,128)(2,1)}), bf16[16,64,256]{2,1,0:T(8,128)(2,1)S(1)}, u32[]{:S(2)}, u32[]{:S(2)}) async-start(bf16[16,64,256]{2,1,0:T(8,128)(2,1)} %bitcast.1), calls=%async_computation.1 | async-start | bytes 1048576 | tf_op jit(solution)/shard_map/all_to_all | solution.py:288
  79.8 4.7 %copy-start.8 = (s32[1,256]{1,0:T(1,128)S(1)}, s32[1,256]{1,0:T(1,128)}, u32[]{:S(2)}) copy-start(s32[1,256]{1,0:T(1,128)} %counts.1) | copy-start | bytes 3076
  80.8 20.2 %all-to-all-start.3 = ((bf16[16,80,256]{2,1,0:T(8,128)(2,1)}), bf16[16,80,256]{2,1,0:T(8,128)(2,1)S(1)}, u32[]{:S(2)}, u32[]{:S(2)}) async-start(bf16[16,80,256]{2,1,0:T(8,128)(2,1)} %broadcast_in_dim.2), calls=%async_computation.3 | async-start | bytes 1310720 | tf_op jit(solution)/shard_map/all_to_all | solution.py:288

commit v2 on v1

v2 whole, which is shorter than its diff:
```python
import functools

import jax
import jax.numpy as jnp
from jax import lax
from jax.experimental import pallas as pl
from jax.experimental.pallas import tpu as pltpu
from jax.sharding import PartitionSpec as P

HEADS = 4
MATRICES = 5
LANES = 128
F32 = jnp.float32
BF16 = jnp.bfloat16
VMEM_LIMIT = 48 * 1024 * 1024


def dot(a, b):
    return jnp.dot(a, b, preferred_element_type=F32)


def dot_nt(a, b):
    return lax.dot_general(a, b, (((1,), (1,)), ((), ())), preferred_element_type=F32)


def dot_tn(a, b):
    return lax.dot_general(a, b, (((0,), (0,)), ((), ())), preferred_element_type=F32)


def iota(shape, dim):
    return lax.broadcasted_iota(jnp.int32, shape, dim)


def ones_where(cond):
    return jnp.where(cond, 1.0, 0.0).astype(BF16)


def column_of(row):
    n = row.shape[1]
    wide = jnp.where(iota((n, n), 0) == iota((n, n), 1), row, 0.0)
    return jnp.sum(wide, axis=1, keepdims=True)


def member_onehot(table_ref, at, clusters):
    sub = iota((clusters, LANES), 0).astype(F32)
    parts = [ones_where(table_ref[pl.ds(at + k, 1), :] == sub) for k in range(2)]
    return jnp.concatenate(parts, axis=1)


def means_kernel(
    counts_h, members_h, raw_h, mean_out, table, counts_s, counts_v, members, raw, small_sem, raw_sem
):
    clusters = counts_v.shape[1]
    groups = members.shape[0]
    parts = raw_sem.shape[0]
    part = raw.shape[0] // parts
    small = [
        pltpu.make_async_copy(counts_h, counts_s, small_sem.at[0]),
        pltpu.make_async_copy(members_h, members, small_sem.at[1]),
        pltpu.make_async_copy(counts_h, counts_v, small_sem.at[2]),
    ]
    large = [
        pltpu.make_async_copy(
            raw_h.at[pl.ds(k * part, part)], raw.at[pl.ds(k * part, part)], raw_sem.at[k]
        )
        for k in range(parts)
    ]
    for copy in small + large:
        copy.start()
    place = iota((groups, LANES), 0) * LANES + iota((groups, LANES), 1)
    small[0].wait()

    def body(j, carry):
        end, cluster = carry
        end = end + counts_s[0, j]
        return end, cluster + jnp.where(place >= end, 1, 0)

    _, cluster = lax.fori_loop(
        0, clusters, body, (jnp.int32(0), jnp.zeros((groups, LANES), jnp.int32)), unroll=8
    )
    cluster = cluster.astype(F32)
    small[1].wait()
    rows = members[...]
    high = rows // LANES
    low = rows % LANES
    total = jnp.zeros((groups, LANES), F32)
    high_iota = iota((groups, LANES), 0)
    low_iota = iota((LANES, LANES), 0)
    for k in range(0, groups, 2):
        a_parts, b_parts = [], []
        for m in (k, k + 1):
            a_parts.append(
                jnp.where(high[m : m + 1] == high_iota, cluster[m : m + 1], 0.0).astype(BF16)
            )
            b_parts.append(ones_where(low[m : m + 1] == low_iota))
        total = total + dot_nt(jnp.concatenate(a_parts, axis=1), jnp.concatenate(b_parts, axis=1))
    table[...] = total
    small[2].wait()
    count_column = column_of(counts_v[...].astype(F32))
    sums = jnp.zeros((clusters, raw.shape[1]), F32)
    for p in range(parts):
        large[p].wait()
        for k in range(part // 256):
            at = p * part + k * 256
            onehot = member_onehot(table, at // LANES, clusters)
            sums = sums + dot(onehot, raw[at : at + 256, :])
    mean_out[...] = (sums / count_column).astype(BF16)


def cluster_means(counts, members, raw_rows):
    clusters = counts.shape[1]
    rows, width = raw_rows.shape
    groups = rows // LANES
    parts = 8
    return pl.pallas_call(
        means_kernel,
        in_specs=[pl.BlockSpec(memory_space=pltpu.HBM)] * 3,
        out_shape=[
            jax.ShapeDtypeStruct((clusters, width), BF16),
            jax.ShapeDtypeStruct((groups, LANES), F32),
        ],
        scratch_shapes=[
            pltpu.SMEM((1, clusters), jnp.int32),
            pltpu.VMEM((1, clusters), jnp.int32),
            pltpu.VMEM((groups, LANES), jnp.int32),
            pltpu.VMEM((rows, width), BF16),
            pltpu.SemaphoreType.DMA((3,)),
            pltpu.SemaphoreType.DMA((parts,)),
        ],
        compiler_params=pltpu.CompilerParams(vmem_limit_bytes=VMEM_LIMIT),
        cost_estimate=pl.CostEstimate(
            flops=2 * rows * clusters * width, bytes_accessed=2 * rows * width, transcendentals=0
        ),
    )(counts, members.reshape(groups, LANES), raw_rows)


def select_kernel(got, means, onehot_t, sent):
    clusters = means.shape[0]
    parity = lax.axis_index("clu") % 2
    half = LANES // 2
    wanted = lax.rem(got[...], clusters)
    turned = pltpu.roll(wanted, half, 1)
    first = jnp.where(parity == 0, wanted, turned)
    second = jnp.where(parity == 0, turned, wanted)
    left = iota((1, LANES), 1) < half
    for k in range(got.shape[0] // 2):
        row = jnp.where(left, first[2 * k : 2 * k + 1], second[2 * k + 1 : 2 * k + 2])
        onehot_t[:, k * LANES : (k + 1) * LANES] = ones_where(row == iota((clusters, LANES), 0))
    sent[...] = dot_tn(onehot_t[...], means[...]).astype(BF16)


def select_rows(got, means, pooled):
    clusters, width = means.shape
    return pl.pallas_call(
        select_kernel,
        out_shape=[
            jax.ShapeDtypeStruct((clusters, pooled), BF16),
            jax.ShapeDtypeStruct((pooled, width), BF16),
        ],
        compiler_params=pltpu.CompilerParams(vmem_limit_bytes=VMEM_LIMIT),
    )(got, means)


def spread_heads(rows):
    head = iota(rows.shape, 1) // (rows.shape[1] // HEADS)
    return jnp.concatenate([jnp.where(head == h, rows, 0.0) for h in range(HEADS)], axis=0).astype(
        BF16
    )


def targets_kernel(scale, picks, queries, out_grad, weights, bias, query_heads, mixed_heads):
    query_proj = dot(queries[...], weights[0]).astype(BF16)
    query_heads[...] = spread_heads(query_proj.astype(F32) * scale)
    grad_mixed = dot_nt(out_grad[...], weights[3]).astype(BF16)
    mixed_heads[...] = spread_heads(grad_mixed.astype(F32))
    count, targets = picks.shape
    block = 128

    def body(b, carry):
        at = pl.multiple_of(b * block, block)
        slot = iota((block, targets), 0) + at
        found = jnp.zeros((block, targets), F32)
        for i in range(count):
            found = jnp.where(picks[i : i + 1, :] == slot, 1.0, found)
        bias[pl.ds(at, block), :] = jnp.where(found > 0.5, 0.0, -1e30)
        return carry

    lax.fori_loop(0, bias.shape[0] // block, body, 0)


def target_terms(scale, picks_t, queries, out_grad, weights, pooled):
    targets, width = queries.shape
    return pl.pallas_call(
        functools.partial(targets_kernel, scale),
        out_shape=[
            jax.ShapeDtypeStruct((pooled, targets), F32),
            jax.ShapeDtypeStruct((HEADS * targets, width), BF16),
            jax.ShapeDtypeStruct((HEADS * targets, width), BF16),
        ],
        compiler_params=pltpu.CompilerParams(vmem_limit_bytes=VMEM_LIMIT),
        cost_estimate=pl.CostEstimate(
            flops=4 * targets * pooled * picks_t.shape[0],
            bytes_accessed=4 * pooled * targets,
            transcendentals=0,
        ),
    )(picks_t, queries, out_grad, weights)


def attention_kernel(
    scale, owners, raw, enc, weights, queries, out_grad, bias, query_heads, mixed_heads, back, grad_query, keep, send, grads
):
    pooled, width = raw.shape
    targets = queries.shape[0]
    raw_pool = raw[...]
    emb = dot(raw_pool, enc[...]).astype(BF16)
    key = dot(emb, weights[1]).astype(BF16)
    value = dot(emb, weights[2]).astype(BF16)
    key_t = dot_nt(weights[1].T, emb).astype(BF16)
    value_t = dot_nt(weights[2].T, emb).astype(BF16)
    pair_bias = jnp.concatenate([bias[...], bias[...]], axis=1)
    head_of_row = iota((width, targets), 0) // (width // HEADS)
    key_grad = jnp.zeros((pooled, width), F32)
    value_grad = jnp.zeros((pooled, width), F32)
    mixed_t = jnp.zeros((width, targets), F32)
    qproj_t = jnp.zeros((width, targets), F32)
    for pair in range(HEADS // 2):
        rows = slice(pair * 2 * targets, (pair + 1) * 2 * targets)
        query_pair = query_heads[rows, :]
        mixed_pair = mixed_heads[rows, :]
        scores = dot_nt(key, query_pair) + pair_bias
        raised = jnp.exp(scores - jnp.max(scores, axis=0, keepdims=True))
        attend = raised * (1.0 / jnp.sum(raised, axis=0, keepdims=True))
        attend_low = attend.astype(BF16)
        weighted = attend * dot_nt(value, mixed_pair)
        score_low = (weighted - attend * jnp.sum(weighted, axis=0, keepdims=True)).astype(BF16)
        value_grad = value_grad + dot(attend_low, mixed_pair)
        key_grad = key_grad + dot(score_low, query_pair)
        mixed_both = dot(value_t, attend_low)
        qproj_both = dot(key_t, score_low)
        for k in range(2):
            own = head_of_row == pair * 2 + k
            cols = slice(k * targets, (k + 1) * targets)
            mixed_t = jnp.where(own, mixed_both[:, cols], mixed_t)
            qproj_t = jnp.where(own, qproj_both[:, cols], qproj_t)
    grad_qproj = (qproj_t * scale).T.astype(BF16)
    grad_query[...] = dot_nt(grad_qproj, weights[0]).astype(BF16)
    key_low = key_grad.astype(BF16)
    value_low = value_grad.astype(BF16)
    emb_grad = (dot_nt(key_low, weights[1]) + dot_nt(value_low, weights[2])).astype(BF16)
    grads[0:width, :] = dot_tn(queries[...], grad_qproj)
    grads[width : 2 * width, :] = dot_tn(emb, key_low)
    grads[2 * width : 3 * width, :] = dot_tn(emb, value_low)
    grads[3 * width : 4 * width, :] = dot(mixed_t.astype(BF16), out_grad[...])
    grads[4 * width : 5 * width, :] = dot_tn(raw_pool, emb_grad)
    back[...] = emb_grad
    core = lax.axis_index("clu") % 2
    part = width // owners
    deep = owners // 4
    for y in range(2):
        for z in range(deep):
            for m in range(MATRICES):
                at = m * width + (z * 4 + y * 2) * part
                kept = pl.ds(pl.multiple_of(at + core * part, part), part)
                given = pl.ds(pl.multiple_of(at + (1 - core) * part, part), part)
                keep[y * deep + z, m] = grads[kept, :].astype(BF16)
                send[y * deep + z, m] = grads[given, :].astype(BF16)


def attention(scale, owners, raw_pool, enc, weights, queries, out_grad, bias, query_heads, mixed_heads):
    pooled, width = raw_pool.shape
    half = jax.ShapeDtypeStruct((owners // 2, MATRICES, width // owners, width), BF16)
    return pl.pallas_call(
        functools.partial(attention_kernel, scale, owners),
        out_shape=[
            jax.ShapeDtypeStruct((pooled, width), BF16),
            jax.ShapeDtypeStruct(queries.shape, BF16),
            half,
            half,
        ],
        scratch_shapes=[pltpu.VMEM((MATRICES * width, width), F32)],
        compiler_params=pltpu.CompilerParams(vmem_limit_bytes=VMEM_LIMIT),
    )(raw_pool, enc, weights, queries, out_grad, bias, query_heads, mixed_heads)


def add_low(a, b):
    return (a.astype(F32) + b.astype(F32)).astype(BF16)


def split_y_kernel(keep, got, kept, given):
    y = lax.axis_index("clu") // 2 % 2
    deep = kept.shape[0]
    for i in range(deep):
        own = y * deep + i
        other = (1 - y) * deep + i
        kept[i] = add_low(keep[own], got[own])
        given[i] = add_low(keep[other], got[other])


def split_y(keep, got):
    half = jax.ShapeDtypeStruct((keep.shape[0] // 2,) + keep.shape[1:], BF16)
    return pl.pallas_call(split_y_kernel, out_shape=[half, half])(keep, got)


def split_z_kernel(keep, got, *outs):
    z = lax.axis_index("clu") // 4
    deep = keep.shape[0]
    for k in range(deep):
        at = lax.rem(z + k, deep)
        outs[k][...] = add_low(keep[at], got[at])


def split_z(keep, got):
    one = jax.ShapeDtypeStruct(keep.shape[1:], BF16)
    return pl.pallas_call(split_z_kernel, out_shape=[one] * keep.shape[0])(keep, got)


def place_kernel(own, beside, own_core, beside_core, attn, enc):
    me = lax.axis_index("clu")
    deep, matrices, part, _ = own.shape
    for k in range(deep):
        z = lax.rem(me // 4 + deep - k, deep)
        low = me % 4
        for source, flip in ((own, 0), (beside, 2), (own_core, 1), (beside_core, 3)):
            at = pl.multiple_of((z * 4 + (low ^ flip)) * part, part)
            for m in range(matrices - 1):
                attn[m, pl.ds(at, part), :] = source[k, m].astype(F32)
            enc[pl.ds(at, part), :] = source[k, matrices - 1].astype(F32)


def place(own, beside, own_core, beside_core):
    width = own.shape[3]
    return pl.pallas_call(
        place_kernel,
        out_shape=[
            jax.ShapeDtypeStruct((MATRICES - 1, width, width), F32),
            jax.ShapeDtypeStruct((width, width), F32),
        ],
    )(own, beside, own_core, beside_core)


def rows_kernel(counts, onehot_t, table, back, out, share):
    step = pl.program_id(0)
    clusters = counts.shape[1]

    @pl.when(step == 0)
    def _():
        total = dot(onehot_t[...], back[...])
        share[...] = (total / column_of(counts[...].astype(F32))).astype(BF16)

    blocks = out.shape[0] // 256
    for k in range(blocks):
        onehot = member_onehot(table, (step * blocks + k) * 2, clusters)
        out[k * 256 : k * 256 + 256, :] = dot_tn(onehot, share[...]).astype(BF16)


def member_grads(counts, onehot_t, table, back, rows):
    clusters = counts.shape[1]
    width = back.shape[1]
    block = 1024
    return pl.pallas_call(
        rows_kernel,
        grid=(rows // block,),
        in_specs=[
            pl.BlockSpec((1, clusters), lambda i: (0, 0)),
            pl.BlockSpec(onehot_t.shape, lambda i: (0, 0)),
            pl.BlockSpec(table.shape, lambda i: (0, 0)),
            pl.BlockSpec(back.shape, lambda i: (0, 0)),
        ],
        out_specs=pl.BlockSpec((block, width), lambda i: (i, 0)),
        out_shape=jax.ShapeDtypeStruct((rows, width), BF16),
        scratch_shapes=[pltpu.VMEM((clusters, width), BF16)],
        compiler_params=pltpu.CompilerParams(vmem_limit_bytes=VMEM_LIMIT),
        cost_estimate=pl.CostEstimate(
            flops=2 * rows * clusters * width, bytes_accessed=2 * rows * width, transcendentals=0
        ),
    )(counts, onehot_t, table, back)


def swap(blocks):
    return lax.all_to_all(blocks, "clu", split_axis=0, concat_axis=0, tiled=True)


def local(raw_rows, enc_weight, counts, member_rows, pool, picks, queries, attn_weights, out_grad):
    rows, width = raw_rows.shape
    owners = lax.axis_size("clu")
    deep = owners // 4
    pooled = pool.shape[1]
    scale = (width // HEADS) ** -0.5

    def permute(block, target):
        return lax.ppermute(block, "clu", [(d, target(d)) for d in range(owners)])

    def along_z(k):
        return lambda d: (d // 4 + k) % deep * 4 + d % 4

    def flip(bit):
        return lambda d: d ^ bit

    pairs = pool.reshape(owners // 2, 1, 1, LANES)
    asking = jnp.broadcast_to(pairs, (owners // 2, 2, 1, LANES)).reshape(owners, 1, LANES)
    got = swap(asking).reshape(owners, LANES)
    means, table = cluster_means(counts, member_rows, raw_rows)
    onehot_t, sent = select_rows(got, means, pooled)
    raw_pool = swap(sent.reshape(owners, pooled // owners, width)).reshape(pooled, width)
    bias, query_heads, mixed_heads = target_terms(
        scale, picks.T, queries, out_grad, attn_weights, pooled
    )
    back, grad_query, keep, given = attention(
        scale, owners, raw_pool, enc_weight, attn_weights, queries, out_grad, bias, query_heads, mixed_heads
    )
    keep, given = split_y(keep, permute(given, flip(1)))
    back = swap(back.reshape(owners, pooled // owners, width)).reshape(pooled, width)
    terms = split_z(keep, permute(given, flip(2)))
    total = terms[0].astype(F32)
    for k in range(1, deep):
        total = total + permute(terms[k], along_z(k)).astype(F32)
    total = total.astype(BF16)
    own = jnp.stack([total] + [permute(total, along_z(k)) for k in range(1, deep)])
    beside = permute(own, flip(2))
    grad_attn, grad_encoder = place(own, beside, permute(own, flip(1)), permute(beside, flip(1)))
    grad_rows = member_grads(counts, onehot_t, table, back, rows)
    return grad_query, grad_rows, grad_attn, grad_encoder


def solution(mesh):
    split = P(("grp", "clu"), None)
    in_specs = (split, P(), split, split, split, split, split, P(), split)
    out_specs = (split, split, P("grp", None, None), P("grp", None))
    return jax.shard_map(local, mesh=mesh, in_specs=in_specs, out_specs=out_specs, check_vma=False)
```

time: 103 us -> 98.3 us (0.954)
  blocking collectives: 33.4 us -> 0 us
  starting transfers between devices: 17 us -> 29.3 us
  waiting for transfers between devices: 21.7 us -> 31.6 us
  Pallas kernels: 18.8 us -> 27.4 us
  other arithmetic: 2.33 us -> 0.83 us
  matrix products: 1.15 us -> 0 us
    all_to_all x1 -> x0, blocking collectives: 33.4 us -> none  [swap(): lax.all_to_all(blocks, 'clu', split_axis=0, concat_axis=0, tiled=True)]
    ppermute x0 -> x11, waiting for transfers between devices: none -> 21.1 us  [permute(): return lax.ppermute(block, 'clu', [(d, target(d)) for d in range(owners)])]
    ppermute x0 -> x11, starting transfers between devices: none -> 11.5 us  [permute(): return lax.ppermute(block, 'clu', [(d, target(d)) for d in range(owners)])]
    all_to_all x3, waiting for transfers between devices: 21.7 us -> 10.6 us  [swap(): lax.all_to_all(blocks, 'clu', split_axis=0, concat_axis=0, tiled=True)]
    pallas_call x1 -> x5, Pallas kernels: 5.16 us -> 12.8 us  [the longest x1 5.66 us: cluster_means(): pl.pallas_call(means_kernel, in_specs=[pl.BlockSpec(memory_space=pltpu.HB...]
    unnamed x19 -> x32, local copies, waits for them, and re-layouts: 4.17 us -> 6.42 us
    slice x2 -> x0, local copies, waits for them, and re-layouts: 1.76 us -> none  [the longest x1 1.04 us: local(): grad_attn = grads[:4 * width].reshape(4, width, width)]
    unnamed x1 -> x0, other arithmetic: 1.35 us -> none
  transfers between devices with their start and end apart: 3 -> 14, of which waited for: 2 -> 10; matrix products, arithmetic and copies ran while one was open for 0% -> 1% of each run, Pallas kernels for 14% -> 16%
where the time goes in v2:
time: 98.3 us; the launch traced here: 97.7 us
  waiting for transfers between devices  31.6 us (32%)
  starting transfers between devices  29.3 us (30%)
  Pallas kernels  27.4 us (28%)
  local copies, waits for them, and re-layouts  7.71 us (8%)
    ppermute x11, waiting for transfers between devices, permute(): return lax.ppermute(block, 'clu', [(d, target(d)) for d in range(owners)])  21.1 us
    all_to_all x3, starting transfers between devices, swap(): lax.all_to_all(blocks, 'clu', split_axis=0, concat_axis=0, tiled=True)  17.8 us
    ppermute x11, starting transfers between devices, permute(): return lax.ppermute(block, 'clu', [(d, target(d)) for d in range(owners)])  11.5 us
    all_to_all x3, waiting for transfers between devices, swap(): lax.all_to_all(blocks, 'clu', split_axis=0, concat_axis=0, tiled=True)  10.6 us
    unnamed x32, local copies, waits for them, and re-layouts  6.42 us
    pallas_call x1, Pallas kernels, cluster_means(): pl.pallas_call(means_kernel, in_specs=[pl.BlockSpec(memory_space=pltpu.HB...  5.66 us
    pallas_call x1, Pallas kernels, attention(): pl.pallas_call(functools.partial(attention_kernel, scale, owners), out_sh...  5.44 us
    pallas_call x1, Pallas kernels, member_grads(): pl.pallas_call(rows_kernel, grid=(rows // block,), in_specs=[pl.BlockSpec...  5.31 us
  transfers between devices with their start and end apart: 14, of which 10 were waited for; matrix products, arithmetic and copies ran while one was open for 1% of the time, Pallas kernels for 16%

profile of v2, /device:TPU:0, one launch (start us, length us, event | category | flops | bytes accessed | tf_op | source)
XLA Modules:
  0.0 97.7 jit_solution(6564875701595046018)
XLA Ops:
  0.6 1.3 %broadcast_in_dim.10 = s32[8,2,128]{2,1,0:T(2,128)} broadcast(s32[8,128]{1,0:T(8,128)} %bitcast.22), dimensions={0,2} | broadcast | bytes 12288 | tf_op jit(solution)/shard_map/broadcast_in_dim | solution.py:400
  1.9 7.4 %all-to-all-start = ((s32[16,1,128]{2,1,0:T(1,128)}), s32[16,1,128]{2,1,0:T(1,128)S(1)}, u32[]{:S(2)}, u32[]{:S(2)}) async-start(s32[16,1,128]{2,1,0:T(1,128)} %bitcast.1), calls=%async_computation | async-start | bytes 16384 | tf_op jit(solution)/shard_map/all_to_all | solution.py:380
  9.3 2.2 %copy-done = bf16[8192,256]{1,0:T(8,128)(2,1)S(1)} copy-done((bf16[8192,256]{1,0:T(8,128)(2,1)S(1)}, bf16[8192,256]{1,0:T(8,128)(2,1)}, u32[]{:S(2)}) %copy-start) | copy-done | bytes 4194328
  13.0 5.7 %shard_map.120 = (bf16[256,256]{1,0:T(8,128)(2,1)S(1)}, f32[64,128]{1,0:T(8,128)S(1)}) custom-call(s32[1,256]{1,0:T(1,128)S(1)} %copy-done.8, s32[64,128]{1,0:T(8,128)S(1)} %bitcast.16, bf16[8192,256]{1,0:T(8,128)(2,1)S(1)} %copy-done), custom_call_target="tpu_custom_call" | custom-call | flops 1073741824 | bytes 4194304 | tf_op jit(solution)/shard_map/pallas_call | solution.py:115
  18.7 1.3 %shard_map.121 = (bf16[256,1024]{1,0:T(8,128)(2,1)S(1)}, bf16[1024,256]{1,0:T(8,128)(2,1)}) custom-call(s32[16,128]{1,0:T(8,128)S(1)} %bitcast.17, bf16[256,256]{1,0:T(8,128)(2,1)S(1)} %get-tuple-element.23.means), custom_call_target="tpu_custom_call" | custom-call | tf_op jit(solution)/shard_map/pallas_call | solution.py:154
  19.9 6.0 %all-to-all-start.1 = ((bf16[16,64,256]{2,1,0:T(8,128)(2,1)}), bf16[16,64,256]{2,1,0:T(8,128)(2,1)S(1)}, u32[]{:S(2)}, u32[]{:S(2)}) async-start(bf16[16,64,256]{2,1,0:T(8,128)(2,1)} %bitcast.4), calls=%async_computation.1 | async-start | bytes 1048576 | tf_op jit(solution)/shard_map/all_to_all | solution.py:380
  26.0 3.9 %shard_map.122 = (f32[1024,128]{1,0:T(8,128)S(1)}, bf16[512,256]{1,0:T(8,128)(2,1)S(1)}, bf16[512,256]{1,0:T(8,128)(2,1)S(1)}) custom-call(s32[100,128]{1,0:T(8,128)S(1)} %bitcast.15, bf16[128,256]{1,0:T(8,128)(2,1)S(1)} %copy-done.3, bf16[128,256]{1,0:T(8,128)(2,1)S(1)} %copy-done.4, bf16[4,256,256]{2,1,0:T(8,128)(2,1)S(1)} %copy-done.1), custom_call_target="tpu_custom_call" | custom-call | flops 52428800 | bytes 524288 | tf_op jit(solution)/shard_map/pallas_call | solution.py:193
  29.9 10.6 %all-to-all-done.1 = bf16[16,64,256]{2,1,0:T(8,128)(2,1)S(1)} async-done(((bf16[16,64,256]{2,1,0:T(8,128)(2,1)}), bf16[16,64,256]{2,1,0:T(8,128)(2,1)S(1)}, u32[]{:S(2)}, u32[]{:S(2)}) %all-to-all-start.1) | async-done | bytes 524320 | tf_op jit(solution)/shard_map/all_to_all | solution.py:380
  40.4 5.4 %shard_map.123 = (bf16[1024,256]{1,0:T(8,128)(2,1)}, bf16[128,256]{1,0:T(8,128)(2,1)}, bf16[8,5,16,256]{3,2,1,0:T(8,128)(2,1)S(1)}, bf16[8,5,16,256]{3,2,1,0:T(8,128)(2,1)S(1)}) custom-call(bf16[1024,256]{1,0:T(8,128)(2,1)S(1)} %bitcast.14, bf16[256,256]{1,0:T(8,128)(2,1)S(1)} %copy-done.5, bf16[4,256,256]{2,1,0:T(8,128)(2,1)S(1)} %copy-done.1, ...), custom_call_target="tpu_custom_call" | custom-call | tf_op jit(solution)/shard_map/pallas_call | solution.py:272
  46.6 4.4 %all-to-all-start.2 = ((bf16[16,64,256]{2,1,0:T(8,128)(2,1)}), bf16[16,64,256]{2,1,0:T(8,128)(2,1)S(1)}, u32[]{:S(2)}, u32[]{:S(2)}) async-start(bf16[16,64,256]{2,1,0:T(8,128)(2,1)} %bitcast.7), calls=%async_computation.2 | async-start | bytes 1048576 | tf_op jit(solution)/shard_map/all_to_all | solution.py:380
  51.7 1.9 %shard_map.125 = (bf16[4,5,16,256]{3,2,1,0:T(8,128)(2,1)}, bf16[4,5,16,256]{3,2,1,0:T(8,128)(2,1)}) custom-call(bf16[8,5,16,256]{3,2,1,0:T(8,128)(2,1)} %copy-done.2, bf16[8,5,16,256]{3,2,1,0:T(8,128)(2,1)} %copy-done.11), custom_call_target="tpu_custom_call" | custom-call | tf_op jit(solution)/shard_map/pallas_call | solution.py:301
  53.6 1.9 %collective-permute-start.1 = (bf16[4,5,16,256]{3,2,1,0:T(8,128)(2,1)}, bf16[4,5,16,256]{3,2,1,0:T(8,128)(2,1)S(1)}, u32[]{:S(2)}, u32[]{:S(2)}) collective-permute-start(bf16[4,5,16,256]{3,2,1,0:T(8,128)(2,1)} %get-tuple-element.35), channel_id=1, source_target_pairs={{0,2},{1,3},{2,0},{3,1},{4,6},{5,7},{6,4},{7,5},{8,10},{9,11},{10,... | collective-permute-start | bytes 491528 | tf_op jit(solution)/shard_map/ppermute | solution.py:391
  55.5 6.6 %collective-permute-done.1.got = bf16[4,5,16,256]{3,2,1,0:T(8,128)(2,1)S(1)} collective-permute-done((bf16[4,5,16,256]{3,2,1,0:T(8,128)(2,1)}, bf16[4,5,16,256]{3,2,1,0:T(8,128)(2,1)S(1)}, u32[]{:S(2)}, u32[]{:S(2)}) %collective-permute-start.1) | collective-permute-done | bytes 163872 | tf_op jit(solution)/shard_map/ppermute | solution.py:391
  62.7 1.7 %shard_map.126 = (bf16[5,16,256]{2,1,0:T(8,128)(2,1)}, bf16[5,16,256]{2,1,0:T(8,128)(2,1)}, bf16[5,16,256]{2,1,0:T(8,128)(2,1)}, bf16[5,16,256]{2,1,0:T(8,128)(2,1)}) custom-call(bf16[4,5,16,256]{3,2,1,0:T(8,128)(2,1)} %get-tuple-element.34.keep, bf16[4,5,16,256]{3,2,1,0:T(8,128)(2,1)} %copy-done.15), custom_call_target="tpu_custom_call" | custom-call | tf_op jit(solution)/shard_map/pallas_call | solution.py:314
  64.4 3.7 %collective-permute-start.4 = (bf16[5,16,256]{2,1,0:T(8,128)(2,1)}, bf16[5,16,256]{2,1,0:T(8,128)(2,1)S(1)}, u32[]{:S(2)}, u32[]{:S(2)}) collective-permute-start(bf16[5,16,256]{2,1,0:T(8,128)(2,1)} %get-tuple-element.39), channel_id=1, source_target_pairs={{0,12},{1,13},{2,14},{3,15},{4,0},{5,1},{6,2},{7,3},{8,4},{9,5},{1... | collective-permute-start | bytes 122888 | tf_op jit(solution)/shard_map/ppermute | solution.py:391
  70.2 3.5 %collective-permute-done.3 = bf16[5,16,256]{2,1,0:T(8,128)(2,1)S(1)} collective-permute-done((bf16[5,16,256]{2,1,0:T(8,128)(2,1)}, bf16[5,16,256]{2,1,0:T(8,128)(2,1)S(1)}, u32[]{:S(2)}, u32[]{:S(2)}) %collective-permute-start.3) | collective-permute-done | bytes 40992 | tf_op jit(solution)/shard_map/ppermute | solution.py:391
  73.7 1.3 %collective-permute-done.2 = bf16[5,16,256]{2,1,0:T(8,128)(2,1)S(1)} collective-permute-done((bf16[5,16,256]{2,1,0:T(8,128)(2,1)}, bf16[5,16,256]{2,1,0:T(8,128)(2,1)S(1)}, u32[]{:S(2)}, u32[]{:S(2)}) %collective-permute-start.2) | collective-permute-done | bytes 40992 | tf_op jit(solution)/shard_map/ppermute | solution.py:391
  76.5 1.7 %collective-permute-start.5 = (bf16[5,16,256]{2,1,0:T(8,128)(2,1)S(1)}, bf16[5,16,256]{2,1,0:T(8,128)(2,1)S(1)}, u32[]{:S(2)}, u32[]{:S(2)}) collective-permute-start(bf16[5,16,256]{2,1,0:T(8,128)(2,1)S(1)} %add_convert_fusion), channel_id=1, source_target_pairs={{0,4},{1,5},{2,6},{3,7},{4,8},{5,9},{6,10},{7,11},{8,12},{9,13},{1... | collective-permute-start | bytes 122888 | tf_op jit(solution)/shard_map/ppermute | solution.py:391
  78.2 2.0 %collective-permute-done.7 = bf16[5,16,256]{2,1,0:T(8,128)(2,1)S(1)} collective-permute-done((bf16[5,16,256]{2,1,0:T(8,128)(2,1)S(1)}, bf16[5,16,256]{2,1,0:T(8,128)(2,1)S(1)}, u32[]{:S(2)}, u32[]{:S(2)}) %collective-permute-start.7) | collective-permute-done | bytes 40992 | tf_op jit(solution)/shard_map/ppermute | solution.py:391
  82.6 1.6 %collective-permute-start.8 = (bf16[4,5,16,256]{3,2,1,0:T(8,128)(2,1)S(1)}, bf16[4,5,16,256]{3,2,1,0:T(8,128)(2,1)S(1)}, u32[]{:S(2)}, u32[]{:S(2)}) collective-permute-start(bf16[4,5,16,256]{3,2,1,0:T(8,128)(2,1)S(1)} %pad_maximum_fusion.own), channel_id=1, source_target_pairs={{0,2},{1,3},{2,0},{3,1},{4,6},{5,7},{6,4},{7,5},{8,10},{9,11},{10,... | collective-permute-start | bytes 491528 | tf_op jit(solution)/shard_map/ppermute | solution.py:391
  84.2 3.7 %collective-permute-done.8.beside = bf16[4,5,16,256]{3,2,1,0:T(8,128)(2,1)S(1)} collective-permute-done((bf16[4,5,16,256]{3,2,1,0:T(8,128)(2,1)S(1)}, bf16[4,5,16,256]{3,2,1,0:T(8,128)(2,1)S(1)}, u32[]{:S(2)}, u32[]{:S(2)}) %collective-permute-start.8) | collective-permute-done | bytes 163872 | tf_op jit(solution)/shard_map/ppermute | solution.py:391
  88.0 1.4 %collective-permute-done.10.beside_core = bf16[4,5,16,256]{3,2,1,0:T(8,128)(2,1)S(1)} collective-permute-done((bf16[4,5,16,256]{3,2,1,0:T(8,128)(2,1)S(1)}, bf16[4,5,16,256]{3,2,1,0:T(8,128)(2,1)S(1)}, u32[]{:S(2)}, u32[]{:S(2)}) %collective-permute-start.10) | collective-permute-done | bytes 163872 | tf_op jit(solution)/shard_map/ppermute | solution.py:391
  90.1 2.3 %shard_map.127 = (f32[4,256,256]{2,1,0:T(8,128)}, f32[256,256]{1,0:T(8,128)}) custom-call(bf16[4,5,16,256]{3,2,1,0:T(8,128)(2,1)} %copy-done.10, bf16[4,5,16,256]{3,2,1,0:T(8,128)(2,1)} %copy-done.12, bf16[4,5,16,256]{3,2,1,0:T(8,128)(2,1)} %copy-done.13, bf16[4,5,16,256]{3,2,1,0:T(8,128)(2,1)} %copy-done.14), custom_call_target="tpu_custom_call" | custom-call | tf_op jit(solution)/shard_map/pallas_call | solution.py:332
  92.4 5.3 %shard_map.124 = bf16[8192,256]{1,0:T(8,128)(2,1)} custom-call(s32[1,256]{1,0:T(1,128)S(1)} %copy-done.9, bf16[256,1024]{1,0:T(8,128)(2,1)S(1)} %get-tuple-element.29.onehot_t, f32[64,128]{1,0:T(8,128)S(1)} %get-tuple-element.30.table, bf16[1024,256]{1,0:T(8,128)(2,1)S(1)} %bitcast.13), custom_call_target="tpu_custom_call" | custom-call | flops 1073741824 | bytes 4194304 | tf_op jit(solution)/shard_map/pallas_call | solution.py:360
  (47 shorter events, 10.3 us)
Async XLA Ops:
  1.9 16.7 %all-to-all-start = ((s32[16,1,128]{2,1,0:T(1,128)}), s32[16,1,128]{2,1,0:T(1,128)S(1)}, u32[]{:S(2)}, u32[]{:S(2)}) async-start(s32[16,1,128]{2,1,0:T(1,128)} %bitcast.1), calls=%async_computation | async-start | bytes 16384 | tf_op jit(solution)/shard_map/all_to_all | solution.py:380
  9.3 2.2 %copy-start = (bf16[8192,256]{1,0:T(8,128)(2,1)S(1)}, bf16[8192,256]{1,0:T(8,128)(2,1)}, u32[]{:S(2)}) copy-start(bf16[8192,256]{1,0:T(8,128)(2,1)} %raw_h.1) | copy-start | bytes 12582916
  12.9 13.0 %copy-start.1 = (bf16[4,256,256]{2,1,0:T(8,128)(2,1)S(1)}, bf16[4,256,256]{2,1,0:T(8,128)(2,1)}, u32[]{:S(2)}) copy-start(bf16[4,256,256]{2,1,0:T(8,128)(2,1)} %weights.3) | copy-start | bytes 1572868
  12.9 13.0 %copy-start.3 = (bf16[128,256]{1,0:T(8,128)(2,1)S(1)}, bf16[128,256]{1,0:T(8,128)(2,1)}, u32[]{:S(2)}) copy-start(bf16[128,256]{1,0:T(8,128)(2,1)} %queries.3) | copy-start | bytes 196612
  12.9 13.0 %copy-start.4 = (bf16[128,256]{1,0:T(8,128)(2,1)S(1)}, bf16[128,256]{1,0:T(8,128)(2,1)}, u32[]{:S(2)}) copy-start(bf16[128,256]{1,0:T(8,128)(2,1)} %out_grad.3) | copy-start | bytes 196612
  12.9 13.0 %copy-start.6 = (s32[128,100]{0,1:T(8,128)S(1)}, s32[128,100]{0,1:T(8,128)}, u32[]{:S(2)}) copy-start(s32[128,100]{0,1:T(8,128)} %param.14) | copy-start | bytes 153604
  13.0 27.5 %copy-start.5 = (bf16[256,256]{1,0:T(8,128)(2,1)S(1)}, bf16[256,256]{1,0:T(8,128)(2,1)}, u32[]{:S(2)}) copy-start(bf16[256,256]{1,0:T(8,128)(2,1)} %enc.1) | copy-start | bytes 393220
  18.6 73.7 %copy-start.9 = (s32[1,256]{1,0:T(1,128)S(1)}, s32[1,256]{1,0:T(1,128)}, u32[]{:S(2)}) copy-start(s32[1,256]{1,0:T(1,128)} %counts.1) | copy-start | bytes 3076
  19.9 20.5 %all-to-all-start.1 = ((bf16[16,64,256]{2,1,0:T(8,128)(2,1)}), bf16[16,64,256]{2,1,0:T(8,128)(2,1)S(1)}, u32[]{:S(2)}, u32[]{:S(2)}) async-start(bf16[16,64,256]{2,1,0:T(8,128)(2,1)} %bitcast.4), calls=%async_computation.1 | async-start | bytes 1048576 | tf_op jit(solution)/shard_map/all_to_all | solution.py:380
  46.6 4.4 %collective-permute-start = (bf16[8,5,16,256]{3,2,1,0:T(8,128)(2,1)S(1)}, bf16[8,5,16,256]{3,2,1,0:T(8,128)(2,1)S(1)}, u32[]{:S(2)}, u32[]{:S(2)}) collective-permute-start(bf16[8,5,16,256]{3,2,1,0:T(8,128)(2,1)S(1)} %get-tuple-element.33), channel_id=1, source_target_pairs={{0,1},{1,0},{2,3},{3,2},{4,5},{5,4},{6,7},{7,6},{8,9},{9,8},{10,11... | collective-permute-start | bytes 983048 | tf_op jit(solution)/shard_map/ppermute | solution.py:391
  46.6 45.8 %all-to-all-start.2 = ((bf16[16,64,256]{2,1,0:T(8,128)(2,1)}), bf16[16,64,256]{2,1,0:T(8,128)(2,1)S(1)}, u32[]{:S(2)}, u32[]{:S(2)}) async-start(bf16[16,64,256]{2,1,0:T(8,128)(2,1)} %bitcast.7), calls=%async_computation.2 | async-start | bytes 1048576 | tf_op jit(solution)/shard_map/all_to_all | solution.py:380
  53.6 8.5 %collective-permute-start.1 = (bf16[4,5,16,256]{3,2,1,0:T(8,128)(2,1)}, bf16[4,5,16,256]{3,2,1,0:T(8,128)(2,1)S(1)}, u32[]{:S(2)}, u32[]{:S(2)}) collective-permute-start(bf16[4,5,16,256]{3,2,1,0:T(8,128)(2,1)} %get-tuple-element.35), channel_id=1, source_target_pairs={{0,2},{1,3},{2,0},{3,1},{4,6},{5,7},{6,4},{7,5},{8,10},{9,11},{10,... | collective-permute-start | bytes 491528 | tf_op jit(solution)/shard_map/ppermute | solution.py:391
  64.4 5.8 %collective-permute-start.4 = (bf16[5,16,256]{2,1,0:T(8,128)(2,1)}, bf16[5,16,256]{2,1,0:T(8,128)(2,1)S(1)}, u32[]{:S(2)}, u32[]{:S(2)}) collective-permute-start(bf16[5,16,256]{2,1,0:T(8,128)(2,1)} %get-tuple-element.39), channel_id=1, source_target_pairs={{0,12},{1,13},{2,14},{3,15},{4,0},{5,1},{6,2},{7,3},{8,4},{9,5},{1... | collective-permute-start | bytes 122888 | tf_op jit(solution)/shard_map/ppermute | solution.py:391
  68.1 5.5 %collective-permute-start.3 = (bf16[5,16,256]{2,1,0:T(8,128)(2,1)}, bf16[5,16,256]{2,1,0:T(8,128)(2,1)S(1)}, u32[]{:S(2)}, u32[]{:S(2)}) collective-permute-start(bf16[5,16,256]{2,1,0:T(8,128)(2,1)} %get-tuple-element.38), channel_id=1, source_target_pairs={{0,8},{1,9},{2,10},{3,11},{4,12},{5,13},{6,14},{7,15},{8,0},{9,1},... | collective-permute-start | bytes 122888 | tf_op jit(solution)/shard_map/ppermute | solution.py:391
  68.9 6.0 %collective-permute-start.2 = (bf16[5,16,256]{2,1,0:T(8,128)(2,1)}, bf16[5,16,256]{2,1,0:T(8,128)(2,1)S(1)}, u32[]{:S(2)}, u32[]{:S(2)}) collective-permute-start(bf16[5,16,256]{2,1,0:T(8,128)(2,1)} %get-tuple-element.37), channel_id=1, source_target_pairs={{0,4},{1,5},{2,6},{3,7},{4,8},{5,9},{6,10},{7,11},{8,12},{9,13},{1... | collective-permute-start | bytes 122888 | tf_op jit(solution)/shard_map/ppermute | solution.py:391
  75.7 4.5 %collective-permute-start.7 = (bf16[5,16,256]{2,1,0:T(8,128)(2,1)S(1)}, bf16[5,16,256]{2,1,0:T(8,128)(2,1)S(1)}, u32[]{:S(2)}, u32[]{:S(2)}) collective-permute-start(bf16[5,16,256]{2,1,0:T(8,128)(2,1)S(1)} %add_convert_fusion), channel_id=1, source_target_pairs={{0,12},{1,13},{2,14},{3,15},{4,0},{5,1},{6,2},{7,3},{8,4},{9,5},{1... | collective-permute-start | bytes 122888 | tf_op jit(solution)/shard_map/ppermute | solution.py:391
  76.4 4.9 %collective-permute-start.6 = (bf16[5,16,256]{2,1,0:T(8,128)(2,1)S(1)}, bf16[5,16,256]{2,1,0:T(8,128)(2,1)S(1)}, u32[]{:S(2)}, u32[]{:S(2)}) collective-permute-start(bf16[5,16,256]{2,1,0:T(8,128)(2,1)S(1)} %add_convert_fusion), channel_id=1, source_target_pairs={{0,8},{1,9},{2,10},{3,11},{4,12},{5,13},{6,14},{7,15},{8,0},{9,1},... | collective-permute-start | bytes 122888 | tf_op jit(solution)/shard_map/ppermute | solution.py:391
  76.5 6.1 %collective-permute-start.5 = (bf16[5,16,256]{2,1,0:T(8,128)(2,1)S(1)}, bf16[5,16,256]{2,1,0:T(8,128)(2,1)S(1)}, u32[]{:S(2)}, u32[]{:S(2)}) collective-permute-start(bf16[5,16,256]{2,1,0:T(8,128)(2,1)S(1)} %add_convert_fusion), channel_id=1, source_target_pairs={{0,4},{1,5},{2,6},{3,7},{4,8},{5,9},{6,10},{7,11},{8,12},{9,13},{1... | collective-permute-start | bytes 122888 | tf_op jit(solution)/shard_map/ppermute | solution.py:391
  82.6 6.8 %copy-start.10 = (bf16[4,5,16,256]{3,2,1,0:T(8,128)(2,1)}, bf16[4,5,16,256]{3,2,1,0:T(8,128)(2,1)S(1)}, u32[]{:S(2)}) copy-start(bf16[4,5,16,256]{3,2,1,0:T(8,128)(2,1)S(1)} %pad_maximum_fusion.own) | copy-start | bytes 491524
  82.6 5.4 %collective-permute-start.8 = (bf16[4,5,16,256]{3,2,1,0:T(8,128)(2,1)S(1)}, bf16[4,5,16,256]{3,2,1,0:T(8,128)(2,1)S(1)}, u32[]{:S(2)}, u32[]{:S(2)}) collective-permute-start(bf16[4,5,16,256]{3,2,1,0:T(8,128)(2,1)S(1)} %pad_maximum_fusion.own), channel_id=1, source_target_pairs={{0,2},{1,3},{2,0},{3,1},{4,6},{5,7},{6,4},{7,5},{8,10},{9,11},{10,... | collective-permute-start | bytes 491528 | tf_op jit(solution)/shard_map/ppermute | solution.py:391
  84.2 3.8 %collective-permute-start.9 = (bf16[4,5,16,256]{3,2,1,0:T(8,128)(2,1)S(1)}, bf16[4,5,16,256]{3,2,1,0:T(8,128)(2,1)S(1)}, u32[]{:S(2)}, u32[]{:S(2)}) collective-permute-start(bf16[4,5,16,256]{3,2,1,0:T(8,128)(2,1)S(1)} %pad_maximum_fusion.own), channel_id=1, source_target_pairs={{0,1},{1,0},{2,3},{3,2},{4,5},{5,4},{6,7},{7,6},{8,9},{9,8},{10,11... | collective-permute-start | bytes 491528 | tf_op jit(solution)/shard_map/ppermute | solution.py:391
  88.0 1.4 %copy-start.12 = (bf16[4,5,16,256]{3,2,1,0:T(8,128)(2,1)}, bf16[4,5,16,256]{3,2,1,0:T(8,128)(2,1)S(1)}, u32[]{:S(2)}) copy-start(bf16[4,5,16,256]{3,2,1,0:T(8,128)(2,1)S(1)} %collective-permute-done.8.beside) | copy-start | bytes 491524
  88.0 1.4 %collective-permute-start.10 = (bf16[4,5,16,256]{3,2,1,0:T(8,128)(2,1)S(1)}, bf16[4,5,16,256]{3,2,1,0:T(8,128)(2,1)S(1)}, u32[]{:S(2)}, u32[]{:S(2)}) collective-permute-start(bf16[4,5,16,256]{3,2,1,0:T(8,128)(2,1)S(1)} %collective-permute-done.8.beside), channel_id=1, source_target_pairs={{0,1},{1,0},{2,3},{3,2},{4,5},{5,4},{6,7},{7,6},{8,9},{9,8},{10,11... | collective-permute-start | bytes 491528 | tf_op jit(solution)/shard_map/ppermute | solution.py:391
  88.0 1.4 %copy-start.13 = (bf16[4,5,16,256]{3,2,1,0:T(8,128)(2,1)}, bf16[4,5,16,256]{3,2,1,0:T(8,128)(2,1)S(1)}, u32[]{:S(2)}) copy-start(bf16[4,5,16,256]{3,2,1,0:T(8,128)(2,1)S(1)} %collective-permute-done.9.own_core) | copy-start | bytes 491524
  (6 other events, 4.2 us)

commit v3 on v2

--- a/solution.py
+++ b/solution.py
@@ -12,7 +12,8 @@
 LANES = 128
 F32 = jnp.float32
 BF16 = jnp.bfloat16
-VMEM_LIMIT = 48 * 1024 * 1024
+VMEM_LIMIT = 32 * 1024 * 1024
+SMALL = pltpu.CompilerParams(vmem_limit_bytes=8 * 1024 * 1024)
 
 
 def dot(a, b):
@@ -127,7 +128,7 @@
             pltpu.SemaphoreType.DMA((3,)),
             pltpu.SemaphoreType.DMA((parts,)),
         ],
-        compiler_params=pltpu.CompilerParams(vmem_limit_bytes=VMEM_LIMIT),
+        compiler_params=pltpu.CompilerParams(vmem_limit_bytes=51 * 1024 * 1024),
         cost_estimate=pl.CostEstimate(
             flops=2 * rows * clusters * width, bytes_accessed=2 * rows * width, transcendentals=0
         ),
@@ -298,7 +299,7 @@
 
 def split_y(keep, got):
     half = jax.ShapeDtypeStruct((keep.shape[0] // 2,) + keep.shape[1:], BF16)
-    return pl.pallas_call(split_y_kernel, out_shape=[half, half])(keep, got)
+    return pl.pallas_call(split_y_kernel, out_shape=[half, half], compiler_params=SMALL)(keep, got)
 
 
 def split_z_kernel(keep, got, *outs):
@@ -311,7 +312,9 @@
 
 def split_z(keep, got):
     one = jax.ShapeDtypeStruct(keep.shape[1:], BF16)
-    return pl.pallas_call(split_z_kernel, out_shape=[one] * keep.shape[0])(keep, got)
+    return pl.pallas_call(
+        split_z_kernel, out_shape=[one] * keep.shape[0], compiler_params=SMALL
+    )(keep, got)
 
 
 def place_kernel(own, beside, own_core, beside_core, attn, enc):
@@ -335,45 +338,84 @@
             jax.ShapeDtypeStruct((MATRICES - 1, width, width), F32),
             jax.ShapeDtypeStruct((width, width), F32),
         ],
+        compiler_params=SMALL,
     )(own, beside, own_core, beside_core)
 
 
-def rows_kernel(counts, onehot_t, table, back, out, share):
-    step = pl.program_id(0)
-    clusters = counts.shape[1]
-
-    @pl.when(step == 0)
+def fill_rows(table, share, out, first):
+    clusters = share.shape[0]
+    blocks = out.shape[0] // 256
+    for k in range(blocks):
+        at = (first + pl.program_id(0)) * blocks + k
+        onehot = member_onehot(table, at * 2, clusters)
+        out[k * 256 : k * 256 + 256, :] = dot_tn(onehot, share[...]).astype(BF16)
+
+
+def early_rows_kernel(counts, onehot_t, table, back, out, share):
+    @pl.when(pl.program_id(0) == 0)
     def _():
         total = dot(onehot_t[...], back[...])
         share[...] = (total / column_of(counts[...].astype(F32))).astype(BF16)
 
-    blocks = out.shape[0] // 256
-    for k in range(blocks):
-        onehot = member_onehot(table, (step * blocks + k) * 2, clusters)
-        out[k * 256 : k * 256 + 256, :] = dot_tn(onehot, share[...]).astype(BF16)
-
-
-def member_grads(counts, onehot_t, table, back, rows):
+    fill_rows(table, share, out, 0)
+
+
+def late_rows_kernel(first, table, share, early, out):
+    del early
+    fill_rows(table, share, out, first)
+
+
+ROW_BLOCK = 1024
+
+
+def rows_cost(rows, clusters, width):
+    return pl.CostEstimate(
+        flops=2 * rows * clusters * width, bytes_accessed=2 * rows * width, transcendentals=0
+    )
+
+
+def early_rows(counts, onehot_t, table, back, rows, steps):
     clusters = counts.shape[1]
     width = back.shape[1]
-    block = 1024
-    return pl.pallas_call(
-        rows_kernel,
-        grid=(rows // block,),
+    return pl.pallas_call(
+        early_rows_kernel,
+        grid=(steps,),
         in_specs=[
             pl.BlockSpec((1, clusters), lambda i: (0, 0)),
             pl.BlockSpec(onehot_t.shape, lambda i: (0, 0)),
             pl.BlockSpec(table.shape, lambda i: (0, 0)),
             pl.BlockSpec(back.shape, lambda i: (0, 0)),
         ],
-        out_specs=pl.BlockSpec((block, width), lambda i: (i, 0)),
+        out_specs=[
+            pl.BlockSpec((ROW_BLOCK, width), lambda i: (i, 0)),
+            pl.BlockSpec((clusters, width), lambda i: (0, 0)),
+        ],
+        out_shape=[
+            jax.ShapeDtypeStruct((rows, width), BF16),
+            jax.ShapeDtypeStruct((clusters, width), BF16),
+        ],
+        compiler_params=pltpu.CompilerParams(vmem_limit_bytes=VMEM_LIMIT),
+        cost_estimate=rows_cost(steps * ROW_BLOCK, clusters, width),
+    )(counts, onehot_t, table, back)
+
+
+def late_rows(table, share, early, first):
+    rows, width = early.shape
+    steps = rows // ROW_BLOCK - first
+    return pl.pallas_call(
+        functools.partial(late_rows_kernel, first),
+        grid=(steps,),
+        in_specs=[
+            pl.BlockSpec(table.shape, lambda i: (0, 0)),
+            pl.BlockSpec(share.shape, lambda i: (0, 0)),
+            pl.BlockSpec(memory_space=pl.ANY),
+        ],
+        out_specs=pl.BlockSpec((ROW_BLOCK, width), lambda i: (first + i, 0)),
         out_shape=jax.ShapeDtypeStruct((rows, width), BF16),
-        scratch_shapes=[pltpu.VMEM((clusters, width), BF16)],
+        input_output_aliases={2: 0},
         compiler_params=pltpu.CompilerParams(vmem_limit_bytes=VMEM_LIMIT),
-        cost_estimate=pl.CostEstimate(
-            flops=2 * rows * clusters * width, bytes_accessed=2 * rows * width, transcendentals=0
-        ),
-    )(counts, onehot_t, table, back)
+        cost_estimate=rows_cost(steps * ROW_BLOCK, share.shape[0], width),
+    )(table, share, early)
 
 
 def swap(blocks):
@@ -415,10 +457,16 @@
     for k in range(1, deep):
         total = total + permute(terms[k], along_z(k)).astype(F32)
     total = total.astype(BF16)
-    own = jnp.stack([total] + [permute(total, along_z(k)) for k in range(1, deep)])
+    passed = [permute(total, along_z(k)) for k in range(1, deep)]
+    steps = rows // ROW_BLOCK // 2
+    early, share = early_rows(counts, onehot_t, table, back, rows, steps)
+    passed, share = lax.optimization_barrier((passed, share))
+    own = jnp.stack([total] + passed)
     beside = permute(own, flip(2))
-    grad_attn, grad_encoder = place(own, beside, permute(own, flip(1)), permute(beside, flip(1)))
-    grad_rows = member_grads(counts, onehot_t, table, back, rows)
+    own_core = permute(own, flip(1))
+    grad_rows = late_rows(table, share, early, steps)
+    beside, own_core, grad_rows = lax.optimization_barrier((beside, own_core, grad_rows))
+    grad_attn, grad_encoder = place(own, beside, own_core, permute(beside, flip(1)))
     return grad_query, grad_rows, grad_attn, grad_encoder
 
 

time: 98.3 us -> 86.2 us (0.88)
  Pallas kernels: 27.4 us -> 23.2 us
  local copies, waits for them, and re-layouts: 7.71 us -> 3.54 us
  waiting for transfers between devices: 31.6 us -> 28.7 us
    unnamed x32 -> x18, local copies, waits for them, and re-layouts: 6.42 us -> 2.18 us
    pallas_call x3 -> x4, Pallas kernels: 8.84 us -> 5.78 us  [the longest x1 2.99 us: early_rows(): pl.pallas_call(early_rows_kernel, grid=(steps,), in_specs=[pl.BlockSpec((...]
    ppermute x11, waiting for transfers between devices: 21.1 us -> 18.1 us  [permute(): return lax.ppermute(block, 'clu', [(d, target(d)) for d in range(owners)])]
    pallas_call x1, Pallas kernels: 2.3 us -> 1.15 us  [place(): pl.pallas_call(place_kernel, out_shape=[jax.ShapeDtypeStruct((MATRICES -...]
  transfers between devices with their start and end apart: 14 -> 14, of which waited for: 10 -> 10; matrix products, arithmetic and copies ran while one was open for 1% -> 0% of each run, Pallas kernels for 16% -> 18%
where the time goes in v3:
time: 86.2 us; the launch traced here: 85.7 us
  starting transfers between devices  29.5 us (34%)
  waiting for transfers between devices  28.7 us (33%)
  Pallas kernels  23.2 us (27%)
  local copies, waits for them, and re-layouts  3.54 us (4%)
    ppermute x11, waiting for transfers between devices, permute(): return lax.ppermute(block, 'clu', [(d, target(d)) for d in range(owners)])  18.1 us
    all_to_all x3, starting transfers between devices, swap(): lax.all_to_all(blocks, 'clu', split_axis=0, concat_axis=0, tiled=True)  17.5 us
    ppermute x11, starting transfers between devices, permute(): return lax.ppermute(block, 'clu', [(d, target(d)) for d in range(owners)])  12 us
    all_to_all x3, waiting for transfers between devices, swap(): lax.all_to_all(blocks, 'clu', split_axis=0, concat_axis=0, tiled=True)  10.6 us
    pallas_call x1, Pallas kernels, cluster_means(): pl.pallas_call(means_kernel, in_specs=[pl.BlockSpec(memory_space=pltpu.HB...  5.65 us
    pallas_call x1, Pallas kernels, attention(): pl.pallas_call(functools.partial(attention_kernel, scale, owners), out_sh...  5.45 us
    pallas_call x1, Pallas kernels, target_terms(): pl.pallas_call(functools.partial(targets_kernel, scale), out_shape=[jax.S...  3.87 us
    pallas_call x1, Pallas kernels, early_rows(): pl.pallas_call(early_rows_kernel, grid=(steps,), in_specs=[pl.BlockSpec((...  2.99 us
  transfers between devices with their start and end apart: 14, of which 10 were waited for; matrix products, arithmetic and copies ran while one was open for 0% of the time, Pallas kernels for 18%

profile of v3, /device:TPU:0, one launch (start us, length us, event | category | flops | bytes accessed | tf_op | source)
XLA Modules:
  0.0 85.7 jit_solution(16197277037621389066)
XLA Ops:
  0.7 1.4 %broadcast_in_dim.10 = s32[8,2,128]{2,1,0:T(2,128)} broadcast(s32[8,128]{1,0:T(8,128)} %bitcast.22), dimensions={0,2} | broadcast | bytes 12288 | tf_op jit(solution)/shard_map/broadcast_in_dim | solution.py:442
  2.0 7.4 %all-to-all-start = ((s32[16,1,128]{2,1,0:T(1,128)}), s32[16,1,128]{2,1,0:T(1,128)S(1)}, u32[]{:S(2)}, u32[]{:S(2)}) async-start(s32[16,1,128]{2,1,0:T(1,128)} %bitcast.1), calls=%async_computation | async-start | bytes 16384 | tf_op jit(solution)/shard_map/all_to_all | solution.py:422
  10.9 5.7 %shard_map.120 = (bf16[256,256]{1,0:T(8,128)(2,1)S(1)}, f32[64,128]{1,0:T(8,128)S(1)}) custom-call(s32[1,256]{1,0:T(1,128)S(1)} %copy-done.6, s32[64,128]{1,0:T(8,128)S(1)} %bitcast.16, bf16[8192,256]{1,0:T(8,128)(2,1)} %raw_h.1), custom_call_target="tpu_custom_call" | custom-call | flops 1073741824 | bytes 4194304 | tf_op jit(solution)/shard_map/pallas_call | solution.py:116
  16.6 1.3 %shard_map.121 = (bf16[256,1024]{1,0:T(8,128)(2,1)S(1)}, bf16[1024,256]{1,0:T(8,128)(2,1)}) custom-call(s32[16,128]{1,0:T(8,128)S(1)} %bitcast.17, bf16[256,256]{1,0:T(8,128)(2,1)S(1)} %get-tuple-element.32.means), custom_call_target="tpu_custom_call" | custom-call | tf_op jit(solution)/shard_map/pallas_call | solution.py:155
  17.8 6.0 %all-to-all-start.1 = ((bf16[16,64,256]{2,1,0:T(8,128)(2,1)}), bf16[16,64,256]{2,1,0:T(8,128)(2,1)S(1)}, u32[]{:S(2)}, u32[]{:S(2)}) async-start(bf16[16,64,256]{2,1,0:T(8,128)(2,1)} %bitcast.4), calls=%async_computation.1 | async-start | bytes 1048576 | tf_op jit(solution)/shard_map/all_to_all | solution.py:422
  23.9 3.9 %shard_map.122 = (f32[1024,128]{1,0:T(8,128)S(1)}, bf16[512,256]{1,0:T(8,128)(2,1)S(1)}, bf16[512,256]{1,0:T(8,128)(2,1)S(1)}) custom-call(s32[100,128]{1,0:T(8,128)S(1)} %bitcast.15, bf16[128,256]{1,0:T(8,128)(2,1)S(1)} %copy-done.1, bf16[128,256]{1,0:T(8,128)(2,1)S(1)} %copy-done.2, bf16[4,256,256]{2,1,0:T(8,128)(2,1)S(1)} %copy-done), custom_call_target="tpu_custom_call" | custom-call | flops 52428800 | bytes 524288 | tf_op jit(solution)/shard_map/pallas_call | solution.py:194
  27.8 10.6 %all-to-all-done.1 = bf16[16,64,256]{2,1,0:T(8,128)(2,1)S(1)} async-done(((bf16[16,64,256]{2,1,0:T(8,128)(2,1)}), bf16[16,64,256]{2,1,0:T(8,128)(2,1)S(1)}, u32[]{:S(2)}, u32[]{:S(2)}) %all-to-all-start.1) | async-done | bytes 524320 | tf_op jit(solution)/shard_map/all_to_all | solution.py:422
  38.3 5.4 %shard_map.123 = (bf16[1024,256]{1,0:T(8,128)(2,1)}, bf16[128,256]{1,0:T(8,128)(2,1)}, bf16[8,5,16,256]{3,2,1,0:T(8,128)(2,1)S(1)}, bf16[8,5,16,256]{3,2,1,0:T(8,128)(2,1)S(1)}) custom-call(bf16[1024,256]{1,0:T(8,128)(2,1)S(1)} %bitcast.13, bf16[256,256]{1,0:T(8,128)(2,1)S(1)} %copy-done.3, bf16[4,256,256]{2,1,0:T(8,128)(2,1)S(1)} %copy-done, ...), custom_call_target="tpu_custom_call" | custom-call | tf_op jit(solution)/shard_map/pallas_call | solution.py:273
  44.5 4.1 %all-to-all-start.2 = ((bf16[16,64,256]{2,1,0:T(8,128)(2,1)}), bf16[16,64,256]{2,1,0:T(8,128)(2,1)S(1)}, u32[]{:S(2)}, u32[]{:S(2)}) async-start(bf16[16,64,256]{2,1,0:T(8,128)(2,1)} %bitcast.8), calls=%async_computation.2 | async-start | bytes 1048576 | tf_op jit(solution)/shard_map/all_to_all | solution.py:422
  49.0 1.5 %collective-permute-done.got = bf16[8,5,16,256]{3,2,1,0:T(8,128)(2,1)S(1)} collective-permute-done((bf16[8,5,16,256]{3,2,1,0:T(8,128)(2,1)}, bf16[8,5,16,256]{3,2,1,0:T(8,128)(2,1)S(1)}, u32[]{:S(2)}, u32[]{:S(2)}) %collective-permute-start) | collective-permute-done | bytes 327712 | tf_op jit(solution)/shard_map/ppermute | solution.py:433
  50.6 1.9 %collective-permute-start.1 = (bf16[4,5,16,256]{3,2,1,0:T(8,128)(2,1)S(1)}, bf16[4,5,16,256]{3,2,1,0:T(8,128)(2,1)S(1)}, u32[]{:S(2)}, u32[]{:S(2)}) collective-permute-start(bf16[4,5,16,256]{3,2,1,0:T(8,128)(2,1)S(1)} %get-tuple-element.41), channel_id=1, source_target_pairs={{0,2},{1,3},{2,0},{3,1},{4,6},{5,7},{6,4},{7,5},{8,10},{9,11},{10,... | collective-permute-start | bytes 491528 | tf_op jit(solution)/shard_map/ppermute | solution.py:433
  52.5 7.0 %collective-permute-done.1.got = bf16[4,5,16,256]{3,2,1,0:T(8,128)(2,1)S(1)} collective-permute-done((bf16[4,5,16,256]{3,2,1,0:T(8,128)(2,1)S(1)}, bf16[4,5,16,256]{3,2,1,0:T(8,128)(2,1)S(1)}, u32[]{:S(2)}, u32[]{:S(2)}) %collective-permute-start.1) | collective-permute-done | bytes 163872 | tf_op jit(solution)/shard_map/ppermute | solution.py:433
  59.6 2.8 %collective-permute-start.2 = (bf16[5,16,256]{2,1,0:T(8,128)(2,1)S(1)}, bf16[5,16,256]{2,1,0:T(8,128)(2,1)S(1)}, u32[]{:S(2)}, u32[]{:S(2)}) collective-permute-start(bf16[5,16,256]{2,1,0:T(8,128)(2,1)S(1)} %get-tuple-element.43), channel_id=1, source_target_pairs={{0,4},{1,5},{2,6},{3,7},{4,8},{5,9},{6,10},{7,11},{8,12},{9,13},{1... | collective-permute-start | bytes 122888 | tf_op jit(solution)/shard_map/ppermute | solution.py:433
  62.3 1.7 %collective-permute-start.3 = (bf16[5,16,256]{2,1,0:T(8,128)(2,1)S(1)}, bf16[5,16,256]{2,1,0:T(8,128)(2,1)S(1)}, u32[]{:S(2)}, u32[]{:S(2)}) collective-permute-start(bf16[5,16,256]{2,1,0:T(8,128)(2,1)S(1)} %get-tuple-element.44), channel_id=1, source_target_pairs={{0,8},{1,9},{2,10},{3,11},{4,12},{5,13},{6,14},{7,15},{8,0},{9,1},... | collective-permute-start | bytes 122888 | tf_op jit(solution)/shard_map/ppermute | solution.py:433
  64.8 1.3 %collective-permute-done.2 = bf16[5,16,256]{2,1,0:T(8,128)(2,1)S(1)} collective-permute-done((bf16[5,16,256]{2,1,0:T(8,128)(2,1)S(1)}, bf16[5,16,256]{2,1,0:T(8,128)(2,1)S(1)}, u32[]{:S(2)}, u32[]{:S(2)}) %collective-permute-start.2) | collective-permute-done | bytes 40992 | tf_op jit(solution)/shard_map/ppermute | solution.py:433
  66.1 1.6 %collective-permute-done.3 = bf16[5,16,256]{2,1,0:T(8,128)(2,1)S(1)} collective-permute-done((bf16[5,16,256]{2,1,0:T(8,128)(2,1)S(1)}, bf16[5,16,256]{2,1,0:T(8,128)(2,1)S(1)}, u32[]{:S(2)}, u32[]{:S(2)}) %collective-permute-start.3) | collective-permute-done | bytes 40992 | tf_op jit(solution)/shard_map/ppermute | solution.py:433
  68.1 2.6 %collective-permute-start.7 = (bf16[5,16,256]{2,1,0:T(8,128)(2,1)S(1)}, bf16[5,16,256]{2,1,0:T(8,128)(2,1)S(1)}, u32[]{:S(2)}, u32[]{:S(2)}) collective-permute-start(bf16[5,16,256]{2,1,0:T(8,128)(2,1)S(1)} %add_convert_fusion), channel_id=1, source_target_pairs={{0,12},{1,13},{2,14},{3,15},{4,0},{5,1},{6,2},{7,3},{8,4},{9,5},{1... | collective-permute-start | bytes 122888 | tf_op jit(solution)/shard_map/ppermute | solution.py:433
  71.4 3.0 %shard_map.126 = (bf16[8192,256]{1,0:T(8,128)(2,1)}, bf16[256,256]{1,0:T(8,128)(2,1)S(1)}) custom-call(s32[1,256]{1,0:T(1,128)S(1)} %copy-done.7, bf16[256,1024]{1,0:T(8,128)(2,1)S(1)} %get-tuple-element.46.onehot_t, f32[64,128]{1,0:T(8,128)S(1)} %get-tuple-element.47.table, bf16[1024,256]{1,0:T(8,128)(2,1)S(1)} %bitcast.14), custom_call_target="tpu_custom_call" | custom-call | flops 536870912 | bytes 2097152 | tf_op jit(solution)/shard_map/pallas_call | solution.py:380
  74.4 1.2 %collective-permute-done.6 = bf16[5,16,256]{2,1,0:T(8,128)(2,1)S(1)} collective-permute-done((bf16[5,16,256]{2,1,0:T(8,128)(2,1)S(1)}, bf16[5,16,256]{2,1,0:T(8,128)(2,1)S(1)}, u32[]{:S(2)}, u32[]{:S(2)}) %collective-permute-start.6) | collective-permute-done | bytes 40992 | tf_op jit(solution)/shard_map/ppermute | solution.py:433
  76.6 1.1 %collective-permute-start.8 = (bf16[4,5,16,256]{3,2,1,0:T(8,128)(2,1)S(1)}, bf16[4,5,16,256]{3,2,1,0:T(8,128)(2,1)S(1)}, u32[]{:S(2)}, u32[]{:S(2)}) collective-permute-start(bf16[4,5,16,256]{3,2,1,0:T(8,128)(2,1)S(1)} %pad_maximum_fusion.own), channel_id=1, source_target_pairs={{0,2},{1,3},{2,0},{3,1},{4,6},{5,7},{6,4},{7,5},{8,10},{9,11},{10,... | collective-permute-start | bytes 491528 | tf_op jit(solution)/shard_map/ppermute | solution.py:433
  77.7 2.7 %shard_map.127 = bf16[8192,256]{1,0:T(8,128)(2,1)} custom-call(f32[64,128]{1,0:T(8,128)S(1)} %get-tuple-element.47.table, bf16[256,256]{1,0:T(8,128)(2,1)S(1)} %get-tuple-element.53.share, bf16[8192,256]{1,0:T(8,128)(2,1)} %get-tuple-element.54.early), custom_call_target="tpu_custom_call", output_to_operand_aliasing={{}: (2, {})} | custom-call | flops 536870912 | bytes 2097152 | tf_op jit(solution)/shard_map/pallas_call | solution.py:405
  80.4 2.8 %collective-permute-done.8.beside = bf16[4,5,16,256]{3,2,1,0:T(8,128)(2,1)S(1)} collective-permute-done((bf16[4,5,16,256]{3,2,1,0:T(8,128)(2,1)S(1)}, bf16[4,5,16,256]{3,2,1,0:T(8,128)(2,1)S(1)}, u32[]{:S(2)}, u32[]{:S(2)}) %collective-permute-start.8) | collective-permute-done | bytes 163872 | tf_op jit(solution)/shard_map/ppermute | solution.py:433
  83.2 1.4 %collective-permute-done.10.beside_core = bf16[4,5,16,256]{3,2,1,0:T(8,128)(2,1)S(1)} collective-permute-done((bf16[4,5,16,256]{3,2,1,0:T(8,128)(2,1)S(1)}, bf16[4,5,16,256]{3,2,1,0:T(8,128)(2,1)S(1)}, u32[]{:S(2)}, u32[]{:S(2)}) %collective-permute-start.10) | collective-permute-done | bytes 163872 | tf_op jit(solution)/shard_map/ppermute | solution.py:433
  84.6 1.2 %shard_map.128 = (f32[4,256,256]{2,1,0:T(8,128)}, f32[256,256]{1,0:T(8,128)}) custom-call(bf16[4,5,16,256]{3,2,1,0:T(8,128)(2,1)S(1)} %pad_maximum_fusion.own, bf16[4,5,16,256]{3,2,1,0:T(8,128)(2,1)S(1)} %collective-permute-done.8.beside, bf16[4,5,16,256]{3,2,1,0:T(8,128)(2,1)S(1)} %collective-permute-done.9.own_core, ...), custom_call_target="tpu_custom_call" | custom-call | tf_op jit(solution)/shard_map/pallas_call | solution.py:335
  (34 shorter events, 5.6 us)
Async XLA Ops:
  0.6 23.2 %copy-start.2 = (bf16[128,256]{1,0:T(8,128)(2,1)S(1)}, bf16[128,256]{1,0:T(8,128)(2,1)}, u32[]{:S(2)}) copy-start(bf16[128,256]{1,0:T(8,128)(2,1)} %out_grad.3) | copy-start | bytes 196612
  0.6 23.2 %copy-start = (bf16[4,256,256]{2,1,0:T(8,128)(2,1)S(1)}, bf16[4,256,256]{2,1,0:T(8,128)(2,1)}, u32[]{:S(2)}) copy-start(bf16[4,256,256]{2,1,0:T(8,128)(2,1)} %weights.3) | copy-start | bytes 1572868
  0.7 23.2 %copy-start.1 = (bf16[128,256]{1,0:T(8,128)(2,1)S(1)}, bf16[128,256]{1,0:T(8,128)(2,1)}, u32[]{:S(2)}) copy-start(bf16[128,256]{1,0:T(8,128)(2,1)} %queries.3) | copy-start | bytes 196612
  0.7 23.2 %copy-start.4 = (s32[128,100]{0,1:T(8,128)S(1)}, s32[128,100]{0,1:T(8,128)}, u32[]{:S(2)}) copy-start(s32[128,100]{0,1:T(8,128)} %param.14) | copy-start | bytes 153604
  0.7 37.6 %copy-start.3 = (bf16[256,256]{1,0:T(8,128)(2,1)S(1)}, bf16[256,256]{1,0:T(8,128)(2,1)}, u32[]{:S(2)}) copy-start(bf16[256,256]{1,0:T(8,128)(2,1)} %enc.1) | copy-start | bytes 393220
  2.0 14.5 %all-to-all-start = ((s32[16,1,128]{2,1,0:T(1,128)}), s32[16,1,128]{2,1,0:T(1,128)S(1)}, u32[]{:S(2)}, u32[]{:S(2)}) async-start(s32[16,1,128]{2,1,0:T(1,128)} %bitcast.1), calls=%async_computation | async-start | bytes 16384 | tf_op jit(solution)/shard_map/all_to_all | solution.py:422
  9.4 0.8 copy-start.5
  10.2 0.7 copy-start.6
  16.5 54.8 %copy-start.7 = (s32[1,256]{1,0:T(1,128)S(1)}, s32[1,256]{1,0:T(1,128)}, u32[]{:S(2)}) copy-start(s32[1,256]{1,0:T(1,128)} %counts.1) | copy-start | bytes 3076
  17.8 20.5 %all-to-all-start.1 = ((bf16[16,64,256]{2,1,0:T(8,128)(2,1)}), bf16[16,64,256]{2,1,0:T(8,128)(2,1)S(1)}, u32[]{:S(2)}, u32[]{:S(2)}) async-start(bf16[16,64,256]{2,1,0:T(8,128)(2,1)} %bitcast.4), calls=%async_computation.1 | async-start | bytes 1048576 | tf_op jit(solution)/shard_map/all_to_all | solution.py:422
  43.8 0.7 copy-start.8
  44.5 26.9 %all-to-all-start.2 = ((bf16[16,64,256]{2,1,0:T(8,128)(2,1)}), bf16[16,64,256]{2,1,0:T(8,128)(2,1)S(1)}, u32[]{:S(2)}, u32[]{:S(2)}) async-start(bf16[16,64,256]{2,1,0:T(8,128)(2,1)} %bitcast.8), calls=%async_computation.2 | async-start | bytes 1048576 | tf_op jit(solution)/shard_map/all_to_all | solution.py:422
  48.6 1.9 %collective-permute-start = (bf16[8,5,16,256]{3,2,1,0:T(8,128)(2,1)}, bf16[8,5,16,256]{3,2,1,0:T(8,128)(2,1)S(1)}, u32[]{:S(2)}, u32[]{:S(2)}) collective-permute-start(bf16[8,5,16,256]{3,2,1,0:T(8,128)(2,1)} %copy-done.8), channel_id=1, source_target_pairs={{0,1},{1,0},{2,3},{3,2},{4,5},{5,4},{6,7},{7,6},{8,9},{9,8},{10,11... | collective-permute-start | bytes 983048 | tf_op jit(solution)/shard_map/ppermute | solution.py:433
  50.6 8.9 %collective-permute-start.1 = (bf16[4,5,16,256]{3,2,1,0:T(8,128)(2,1)S(1)}, bf16[4,5,16,256]{3,2,1,0:T(8,128)(2,1)S(1)}, u32[]{:S(2)}, u32[]{:S(2)}) collective-permute-start(bf16[4,5,16,256]{3,2,1,0:T(8,128)(2,1)S(1)} %get-tuple-element.41), channel_id=1, source_target_pairs={{0,2},{1,3},{2,0},{3,1},{4,6},{5,7},{6,4},{7,5},{8,10},{9,11},{10,... | collective-permute-start | bytes 491528 | tf_op jit(solution)/shard_map/ppermute | solution.py:433
  59.6 6.5 %collective-permute-start.2 = (bf16[5,16,256]{2,1,0:T(8,128)(2,1)S(1)}, bf16[5,16,256]{2,1,0:T(8,128)(2,1)S(1)}, u32[]{:S(2)}, u32[]{:S(2)}) collective-permute-start(bf16[5,16,256]{2,1,0:T(8,128)(2,1)S(1)} %get-tuple-element.43), channel_id=1, source_target_pairs={{0,4},{1,5},{2,6},{3,7},{4,8},{5,9},{6,10},{7,11},{8,12},{9,13},{1... | collective-permute-start | bytes 122888 | tf_op jit(solution)/shard_map/ppermute | solution.py:433
  62.3 5.3 %collective-permute-start.3 = (bf16[5,16,256]{2,1,0:T(8,128)(2,1)S(1)}, bf16[5,16,256]{2,1,0:T(8,128)(2,1)S(1)}, u32[]{:S(2)}, u32[]{:S(2)}) collective-permute-start(bf16[5,16,256]{2,1,0:T(8,128)(2,1)S(1)} %get-tuple-element.44), channel_id=1, source_target_pairs={{0,8},{1,9},{2,10},{3,11},{4,12},{5,13},{6,14},{7,15},{8,0},{9,1},... | collective-permute-start | bytes 122888 | tf_op jit(solution)/shard_map/ppermute | solution.py:433
  64.1 4.0 %collective-permute-start.4 = (bf16[5,16,256]{2,1,0:T(8,128)(2,1)S(1)}, bf16[5,16,256]{2,1,0:T(8,128)(2,1)S(1)}, u32[]{:S(2)}, u32[]{:S(2)}) collective-permute-start(bf16[5,16,256]{2,1,0:T(8,128)(2,1)S(1)} %get-tuple-element.45), channel_id=1, source_target_pairs={{0,12},{1,13},{2,14},{3,15},{4,0},{5,1},{6,2},{7,3},{8,4},{9,5},{1... | collective-permute-start | bytes 122888 | tf_op jit(solution)/shard_map/ppermute | solution.py:433
  68.1 6.3 %collective-permute-start.7 = (bf16[5,16,256]{2,1,0:T(8,128)(2,1)S(1)}, bf16[5,16,256]{2,1,0:T(8,128)(2,1)S(1)}, u32[]{:S(2)}, u32[]{:S(2)}) collective-permute-start(bf16[5,16,256]{2,1,0:T(8,128)(2,1)S(1)} %add_convert_fusion), channel_id=1, source_target_pairs={{0,12},{1,13},{2,14},{3,15},{4,0},{5,1},{6,2},{7,3},{8,4},{9,5},{1... | collective-permute-start | bytes 122888 | tf_op jit(solution)/shard_map/ppermute | solution.py:433
  70.7 4.9 %collective-permute-start.6 = (bf16[5,16,256]{2,1,0:T(8,128)(2,1)S(1)}, bf16[5,16,256]{2,1,0:T(8,128)(2,1)S(1)}, u32[]{:S(2)}, u32[]{:S(2)}) collective-permute-start(bf16[5,16,256]{2,1,0:T(8,128)(2,1)S(1)} %add_convert_fusion), channel_id=1, source_target_pairs={{0,8},{1,9},{2,10},{3,11},{4,12},{5,13},{6,14},{7,15},{8,0},{9,1},... | collective-permute-start | bytes 122888 | tf_op jit(solution)/shard_map/ppermute | solution.py:433
  70.7 5.8 %collective-permute-start.5 = (bf16[5,16,256]{2,1,0:T(8,128)(2,1)S(1)}, bf16[5,16,256]{2,1,0:T(8,128)(2,1)S(1)}, u32[]{:S(2)}, u32[]{:S(2)}) collective-permute-start(bf16[5,16,256]{2,1,0:T(8,128)(2,1)S(1)} %add_convert_fusion), channel_id=1, source_target_pairs={{0,4},{1,5},{2,6},{3,7},{4,8},{5,9},{6,10},{7,11},{8,12},{9,13},{1... | collective-permute-start | bytes 122888 | tf_op jit(solution)/shard_map/ppermute | solution.py:433
  76.5 3.9 %collective-permute-start.9 = (bf16[4,5,16,256]{3,2,1,0:T(8,128)(2,1)S(1)}, bf16[4,5,16,256]{3,2,1,0:T(8,128)(2,1)S(1)}, u32[]{:S(2)}, u32[]{:S(2)}) collective-permute-start(bf16[4,5,16,256]{3,2,1,0:T(8,128)(2,1)S(1)} %pad_maximum_fusion.own), channel_id=1, source_target_pairs={{0,1},{1,0},{2,3},{3,2},{4,5},{5,4},{6,7},{7,6},{8,9},{9,8},{10,11... | collective-permute-start | bytes 491528 | tf_op jit(solution)/shard_map/ppermute | solution.py:433
  76.6 6.6 %collective-permute-start.8 = (bf16[4,5,16,256]{3,2,1,0:T(8,128)(2,1)S(1)}, bf16[4,5,16,256]{3,2,1,0:T(8,128)(2,1)S(1)}, u32[]{:S(2)}, u32[]{:S(2)}) collective-permute-start(bf16[4,5,16,256]{3,2,1,0:T(8,128)(2,1)S(1)} %pad_maximum_fusion.own), channel_id=1, source_target_pairs={{0,2},{1,3},{2,0},{3,1},{4,6},{5,7},{6,4},{7,5},{8,10},{9,11},{10,... | collective-permute-start | bytes 491528 | tf_op jit(solution)/shard_map/ppermute | solution.py:433
  83.2 1.4 %collective-permute-start.10 = (bf16[4,5,16,256]{3,2,1,0:T(8,128)(2,1)S(1)}, bf16[4,5,16,256]{3,2,1,0:T(8,128)(2,1)S(1)}, u32[]{:S(2)}, u32[]{:S(2)}) collective-permute-start(bf16[4,5,16,256]{3,2,1,0:T(8,128)(2,1)S(1)} %collective-permute-done.8.beside), channel_id=1, source_target_pairs={{0,1},{1,0},{2,3},{3,2},{4,5},{5,4},{6,7},{7,6},{8,9},{9,8},{10,11... | collective-permute-start | bytes 491528 | tf_op jit(solution)/shard_map/ppermute | solution.py:433

commit v4 on v2

--- a/solution.py
+++ b/solution.py
@@ -9,10 +9,13 @@
 
 HEADS = 4
 MATRICES = 5
+WEIGHT = 10**11
 LANES = 128
 F32 = jnp.float32
 BF16 = jnp.bfloat16
-VMEM_LIMIT = 48 * 1024 * 1024
+VMEM_LIMIT = 32 * 1024 * 1024
+MOST_VMEM = 51 * 1024 * 1024
+SMALL = pltpu.CompilerParams(vmem_limit_bytes=8 * 1024 * 1024)
 
 
 def dot(a, b):
@@ -127,7 +130,7 @@
             pltpu.SemaphoreType.DMA((3,)),
             pltpu.SemaphoreType.DMA((parts,)),
         ],
-        compiler_params=pltpu.CompilerParams(vmem_limit_bytes=VMEM_LIMIT),
+        compiler_params=pltpu.CompilerParams(vmem_limit_bytes=MOST_VMEM),
         cost_estimate=pl.CostEstimate(
             flops=2 * rows * clusters * width, bytes_accessed=2 * rows * width, transcendentals=0
         ),
@@ -168,7 +171,9 @@
     )
 
 
-def targets_kernel(scale, picks, queries, out_grad, weights, bias, query_heads, mixed_heads):
+def targets_kernel(
+    scale, picks, queries, out_grad, weights, table, bias, query_heads, mixed_heads, members
+):
     query_proj = dot(queries[...], weights[0]).astype(BF16)
     query_heads[...] = spread_heads(query_proj.astype(F32) * scale)
     grad_mixed = dot_nt(out_grad[...], weights[3]).astype(BF16)
@@ -186,24 +191,45 @@
         return carry
 
     lax.fori_loop(0, bias.shape[0] // block, body, 0)
-
-
-def target_terms(scale, picks_t, queries, out_grad, weights, pooled):
+    clusters = members.shape[1]
+    unit = ones_where(iota((clusters, clusters), 0) == iota((clusters, clusters), 1))
+
+    def turn(b, carry):
+        onehot = member_onehot(table, b * 2, clusters)
+        at = pl.multiple_of(b * 256, 256)
+        members[pl.ds(at, 256), :] = dot_tn(onehot, unit).astype(BF16)
+        return carry
+
+    lax.fori_loop(0, members.shape[0] // 256, turn, 0, unroll=4)
+
+
+def target_terms(scale, picks_t, queries, out_grad, weights, table, pooled, clusters):
     targets, width = queries.shape
+    rows = table.shape[0] * LANES
     return pl.pallas_call(
         functools.partial(targets_kernel, scale),
         out_shape=[
             jax.ShapeDtypeStruct((pooled, targets), F32),
             jax.ShapeDtypeStruct((HEADS * targets, width), BF16),
             jax.ShapeDtypeStruct((HEADS * targets, width), BF16),
-        ],
-        compiler_params=pltpu.CompilerParams(vmem_limit_bytes=VMEM_LIMIT),
+            jax.ShapeDtypeStruct((rows, clusters), BF16),
+        ],
+        compiler_params=pltpu.CompilerParams(vmem_limit_bytes=MOST_VMEM),
         cost_estimate=pl.CostEstimate(
             flops=4 * targets * pooled * picks_t.shape[0],
             bytes_accessed=4 * pooled * targets,
             transcendentals=0,
         ),
-    )(picks_t, queries, out_grad, weights)
+    )(picks_t, queries, out_grad, weights, table)
+
+
+def mirrored(number, count):
+    out, size = 0, 1
+    while size < count:
+        out = out * 2 + number % 2
+        number //= 2
+        size *= 2
+    return out
 
 
 def attention_kernel(
@@ -255,15 +281,14 @@
     back[...] = emb_grad
     core = lax.axis_index("clu") % 2
     part = width // owners
-    deep = owners // 4
-    for y in range(2):
-        for z in range(deep):
-            for m in range(MATRICES):
-                at = m * width + (z * 4 + y * 2) * part
-                kept = pl.ds(pl.multiple_of(at + core * part, part), part)
-                given = pl.ds(pl.multiple_of(at + (1 - core) * part, part), part)
-                keep[y * deep + z, m] = grads[kept, :].astype(BF16)
-                send[y * deep + z, m] = grads[given, :].astype(BF16)
+    for q in range(owners // 2):
+        base = 2 * mirrored(q, owners // 2)
+        for m in range(MATRICES):
+            at = m * width + base * part
+            kept = pl.ds(pl.multiple_of(at + core * part, part), part)
+            given = pl.ds(pl.multiple_of(at + (1 - core) * part, part), part)
+            keep[q, m] = grads[kept, :].astype(BF16)
+            send[q, m] = grads[given, :].astype(BF16)
 
 
 def attention(scale, owners, raw_pool, enc, weights, queries, out_grad, bias, query_heads, mixed_heads):
@@ -286,75 +311,62 @@
     return (a.astype(F32) + b.astype(F32)).astype(BF16)
 
 
-def split_y_kernel(keep, got, kept, given):
-    y = lax.axis_index("clu") // 2 % 2
-    deep = kept.shape[0]
-    for i in range(deep):
-        own = y * deep + i
-        other = (1 - y) * deep + i
+def split_kernel(bit, keep, got, kept, given):
+    side = lax.shift_right_logical(lax.axis_index("clu"), bit) & 1
+    half = kept.shape[0]
+    for i in range(half):
+        own = side * half + i
+        other = (1 - side) * half + i
         kept[i] = add_low(keep[own], got[own])
         given[i] = add_low(keep[other], got[other])
 
 
-def split_y(keep, got):
+def split(bit, keep, got, flops):
     half = jax.ShapeDtypeStruct((keep.shape[0] // 2,) + keep.shape[1:], BF16)
-    return pl.pallas_call(split_y_kernel, out_shape=[half, half])(keep, got)
-
-
-def split_z_kernel(keep, got, *outs):
-    z = lax.axis_index("clu") // 4
-    deep = keep.shape[0]
-    for k in range(deep):
-        at = lax.rem(z + k, deep)
-        outs[k][...] = add_low(keep[at], got[at])
-
-
-def split_z(keep, got):
-    one = jax.ShapeDtypeStruct(keep.shape[1:], BF16)
-    return pl.pallas_call(split_z_kernel, out_shape=[one] * keep.shape[0])(keep, got)
-
-
-def place_kernel(own, beside, own_core, beside_core, attn, enc):
+    return pl.pallas_call(
+        functools.partial(split_kernel, bit),
+        out_shape=[half, half],
+        compiler_params=SMALL,
+        cost_estimate=pl.CostEstimate(
+            flops=flops, bytes_accessed=4 * keep.size, transcendentals=0
+        ),
+    )(keep, got)
+
+
+def place_kernel(masks, own, beside, own_core, beside_core, attn, enc):
     me = lax.axis_index("clu")
-    deep, matrices, part, _ = own.shape
-    for k in range(deep):
-        z = lax.rem(me // 4 + deep - k, deep)
-        low = me % 4
+    _, matrices, part, _ = own.shape
+    for k, mask in enumerate(masks):
         for source, flip in ((own, 0), (beside, 2), (own_core, 1), (beside_core, 3)):
-            at = pl.multiple_of((z * 4 + (low ^ flip)) * part, part)
+            at = pl.multiple_of((me ^ (mask ^ flip)) * part, part)
             for m in range(matrices - 1):
                 attn[m, pl.ds(at, part), :] = source[k, m].astype(F32)
             enc[pl.ds(at, part), :] = source[k, matrices - 1].astype(F32)
 
 
-def place(own, beside, own_core, beside_core):
+def place(masks, own, beside, own_core, beside_core):
     width = own.shape[3]
     return pl.pallas_call(
-        place_kernel,
+        functools.partial(place_kernel, masks),
         out_shape=[
             jax.ShapeDtypeStruct((MATRICES - 1, width, width), F32),
             jax.ShapeDtypeStruct((width, width), F32),
         ],
+        compiler_params=SMALL,
     )(own, beside, own_core, beside_core)
 
 
-def rows_kernel(counts, onehot_t, table, back, out, share):
-    step = pl.program_id(0)
-    clusters = counts.shape[1]
-
-    @pl.when(step == 0)
+def rows_kernel(counts, onehot_t, back, members, out, share):
+    @pl.when(pl.program_id(0) == 0)
     def _():
         total = dot(onehot_t[...], back[...])
         share[...] = (total / column_of(counts[...].astype(F32))).astype(BF16)
 
-    blocks = out.shape[0] // 256
-    for k in range(blocks):
-        onehot = member_onehot(table, (step * blocks + k) * 2, clusters)
-        out[k * 256 : k * 256 + 256, :] = dot_tn(onehot, share[...]).astype(BF16)
-
-
-def member_grads(counts, onehot_t, table, back, rows):
-    clusters = counts.shape[1]
+    out[...] = dot(members[...], share[...]).astype(BF16)
+
+
+def member_grads(counts, onehot_t, back, members):
+    rows, clusters = members.shape
     width = back.shape[1]
     block = 1024
     return pl.pallas_call(
@@ -363,17 +375,17 @@
         in_specs=[
             pl.BlockSpec((1, clusters), lambda i: (0, 0)),
             pl.BlockSpec(onehot_t.shape, lambda i: (0, 0)),
-            pl.BlockSpec(table.shape, lambda i: (0, 0)),
             pl.BlockSpec(back.shape, lambda i: (0, 0)),
+            pl.BlockSpec((block, clusters), lambda i: (i, 0)),
         ],
         out_specs=pl.BlockSpec((block, width), lambda i: (i, 0)),
         out_shape=jax.ShapeDtypeStruct((rows, width), BF16),
         scratch_shapes=[pltpu.VMEM((clusters, width), BF16)],
-        compiler_params=pltpu.CompilerParams(vmem_limit_bytes=VMEM_LIMIT),
+        compiler_params=pltpu.CompilerParams(vmem_limit_bytes=MOST_VMEM),
         cost_estimate=pl.CostEstimate(
-            flops=2 * rows * clusters * width, bytes_accessed=2 * rows * width, transcendentals=0
+            flops=2 * rows * clusters * width, bytes_accessed=4 * rows * width, transcendentals=0
         ),
-    )(counts, onehot_t, table, back)
+    )(counts, onehot_t, back, members)
 
 
 def swap(blocks):
@@ -383,18 +395,13 @@
 def local(raw_rows, enc_weight, counts, member_rows, pool, picks, queries, attn_weights, out_grad):
     rows, width = raw_rows.shape
     owners = lax.axis_size("clu")
-    deep = owners // 4
     pooled = pool.shape[1]
+    clusters = counts.shape[1]
     scale = (width // HEADS) ** -0.5
-
-    def permute(block, target):
-        return lax.ppermute(block, "clu", [(d, target(d)) for d in range(owners)])
-
-    def along_z(k):
-        return lambda d: (d // 4 + k) % deep * 4 + d % 4
-
-    def flip(bit):
-        return lambda d: d ^ bit
+    bits = owners.bit_length() - 1
+
+    def exchange(bit, block):
+        return lax.ppermute(block, "clu", [(d, d ^ (1 << bit)) for d in range(owners)])
 
     pairs = pool.reshape(owners // 2, 1, 1, LANES)
     asking = jnp.broadcast_to(pairs, (owners // 2, 2, 1, LANES)).reshape(owners, 1, LANES)
@@ -402,23 +409,29 @@
     means, table = cluster_means(counts, member_rows, raw_rows)
     onehot_t, sent = select_rows(got, means, pooled)
     raw_pool = swap(sent.reshape(owners, pooled // owners, width)).reshape(pooled, width)
-    bias, query_heads, mixed_heads = target_terms(
-        scale, picks.T, queries, out_grad, attn_weights, pooled
+    bias, query_heads, mixed_heads, members = target_terms(
+        scale, picks.T, queries, out_grad, attn_weights, table, pooled, clusters
     )
     back, grad_query, keep, given = attention(
         scale, owners, raw_pool, enc_weight, attn_weights, queries, out_grad, bias, query_heads, mixed_heads
     )
-    keep, given = split_y(keep, permute(given, flip(1)))
+    keep, given = split(1, keep, exchange(0, given), keep.size)
+    given, back = lax.optimization_barrier((given, back))
+    got = exchange(1, given)
     back = swap(back.reshape(owners, pooled // owners, width)).reshape(pooled, width)
-    terms = split_z(keep, permute(given, flip(2)))
-    total = terms[0].astype(F32)
-    for k in range(1, deep):
-        total = total + permute(terms[k], along_z(k)).astype(F32)
-    total = total.astype(BF16)
-    own = jnp.stack([total] + [permute(total, along_z(k)) for k in range(1, deep)])
-    beside = permute(own, flip(2))
-    grad_attn, grad_encoder = place(own, beside, permute(own, flip(1)), permute(beside, flip(1)))
-    grad_rows = member_grads(counts, onehot_t, table, back, rows)
+    keep, given = split(2, keep, got, WEIGHT)
+    for bit in range(2, bits - 1):
+        keep, given = split(bit + 1, keep, exchange(bit, given), keep.size)
+    own = add_low(keep, exchange(bits - 1, given))
+    masks = [0]
+    for bit in range(bits - 1, 1, -1):
+        own = jnp.concatenate([own, exchange(bit, own)])
+        masks = masks + [mask ^ (1 << bit) for mask in masks]
+    beside = exchange(1, own)
+    own_core = exchange(0, own)
+    grad_rows = member_grads(counts, onehot_t, back, members)
+    beside, own_core, grad_rows = lax.optimization_barrier((beside, own_core, grad_rows))
+    grad_attn, grad_encoder = place(masks, own, beside, own_core, exchange(0, beside))
     return grad_query, grad_rows, grad_attn, grad_encoder
 
 

time: 98.3 us -> 90.6 us (0.922)
  local copies, waits for them, and re-layouts: 7.71 us -> 2.81 us
  waiting for transfers between devices: 31.6 us -> 28.5 us
  Pallas kernels: 27.4 us -> 30.1 us
  starting transfers between devices: 29.3 us -> 27.8 us
    unnamed x32 -> x16, local copies, waits for them, and re-layouts: 6.42 us -> 1.46 us
    pallas_call x1, Pallas kernels: 3.87 us -> 8.62 us  [target_terms(): pl.pallas_call(functools.partial(targets_kernel, scale), out_shape=[jax.S...]
    all_to_all x3, waiting for transfers between devices: 10.6 us -> 5.81 us  [swap(): lax.all_to_all(blocks, 'clu', split_axis=0, concat_axis=0, tiled=True)]
    pallas_call x3 -> x4, Pallas kernels: 5.83 us -> 1.3 us  [the longest x1 1.16 us: place(): pl.pallas_call(functools.partial(place_kernel, masks), out_shape=[jax.Sha...]
    pallas_call x1, Pallas kernels: 5.31 us -> 7.76 us  [member_grads(): pl.pallas_call(rows_kernel, grid=(rows // block,), in_specs=[pl.BlockSpec...]
    ppermute x11 -> x9, waiting for transfers between devices: 21.1 us -> 22.7 us  [exchange(): lax.ppermute(block, 'clu', [(d, d ^ 1 << bit) for d in range(owners)])]
    ppermute x11 -> x9, starting transfers between devices: 11.5 us -> 10.1 us  [exchange(): lax.ppermute(block, 'clu', [(d, d ^ 1 << bit) for d in range(owners)])]
  transfers between devices with their start and end apart: 14 -> 12, of which waited for: 10 -> 8; matrix products, arithmetic and copies ran while one was open for 1% -> 0% of each run, Pallas kernels for 16% -> 25%
where the time goes in v4:
time: 90.6 us; the launch traced here: 90 us
  Pallas kernels  30.1 us (33%)
  waiting for transfers between devices  28.5 us (31%)
  starting transfers between devices  27.8 us (31%)
  local copies, waits for them, and re-layouts  2.81 us (3%)
    ppermute x9, waiting for transfers between devices, exchange(): lax.ppermute(block, 'clu', [(d, d ^ 1 << bit) for d in range(owners)])  22.7 us
    all_to_all x3, starting transfers between devices, swap(): lax.all_to_all(blocks, 'clu', split_axis=0, concat_axis=0, tiled=True)  17.7 us
    ppermute x9, starting transfers between devices, exchange(): lax.ppermute(block, 'clu', [(d, d ^ 1 << bit) for d in range(owners)])  10.1 us
    pallas_call x1, Pallas kernels, target_terms(): pl.pallas_call(functools.partial(targets_kernel, scale), out_shape=[jax.S...  8.62 us
    pallas_call x1, Pallas kernels, member_grads(): pl.pallas_call(rows_kernel, grid=(rows // block,), in_specs=[pl.BlockSpec...  7.76 us
    all_to_all x3, waiting for transfers between devices, swap(): lax.all_to_all(blocks, 'clu', split_axis=0, concat_axis=0, tiled=True)  5.81 us
    pallas_call x1, Pallas kernels, cluster_means(): pl.pallas_call(means_kernel, in_specs=[pl.BlockSpec(memory_space=pltpu.HB...  5.65 us
    pallas_call x1, Pallas kernels, attention(): pl.pallas_call(functools.partial(attention_kernel, scale, owners), out_sh...  5.45 us
  transfers between devices with their start and end apart: 12, of which 8 were waited for; matrix products, arithmetic and copies ran while one was open for 0% of the time, Pallas kernels for 25%

profile of v4, /device:TPU:0, one launch (start us, length us, event | category | flops | bytes accessed | tf_op | source)
XLA Modules:
  0.0 90.0 jit_solution(12333542280105261191)
XLA Ops:
  0.7 1.4 %broadcast_in_dim.10 = s32[8,2,128]{2,1,0:T(2,128)} broadcast(s32[8,128]{1,0:T(8,128)} %bitcast.14), dimensions={0,2} | broadcast | bytes 12288 | tf_op jit(solution)/shard_map/broadcast_in_dim | solution.py:407
  2.0 7.4 %all-to-all-start = ((s32[16,1,128]{2,1,0:T(1,128)}), s32[16,1,128]{2,1,0:T(1,128)S(1)}, u32[]{:S(2)}, u32[]{:S(2)}) async-start(s32[16,1,128]{2,1,0:T(1,128)} %bitcast.1), calls=%async_computation | async-start | bytes 16384 | tf_op jit(solution)/shard_map/all_to_all | solution.py:392
  9.4 0.7 copy-done.5
  10.2 0.7 copy-done.6
  10.9 5.7 %shard_map.120 = (bf16[256,256]{1,0:T(8,128)(2,1)S(1)}, f32[64,128]{1,0:T(8,128)S(1)}) custom-call(s32[1,256]{1,0:T(1,128)S(1)} %copy-done.6, s32[64,128]{1,0:T(8,128)S(1)} %bitcast.12, bf16[8192,256]{1,0:T(8,128)(2,1)} %raw_h.1), custom_call_target="tpu_custom_call" | custom-call | flops 1073741824 | bytes 4194304 | tf_op jit(solution)/shard_map/pallas_call | solution.py:118
  16.5 1.3 %shard_map.121 = (bf16[256,1024]{1,0:T(8,128)(2,1)S(1)}, bf16[1024,256]{1,0:T(8,128)(2,1)}) custom-call(s32[16,128]{1,0:T(8,128)S(1)} %bitcast.13, bf16[256,256]{1,0:T(8,128)(2,1)S(1)} %get-tuple-element.29.means), custom_call_target="tpu_custom_call" | custom-call | tf_op jit(solution)/shard_map/pallas_call | solution.py:157
  17.8 6.0 %all-to-all-start.1 = ((bf16[16,64,256]{2,1,0:T(8,128)(2,1)}), bf16[16,64,256]{2,1,0:T(8,128)(2,1)S(1)}, u32[]{:S(2)}, u32[]{:S(2)}) async-start(bf16[16,64,256]{2,1,0:T(8,128)(2,1)} %bitcast.4), calls=%async_computation.1 | async-start | bytes 1048576 | tf_op jit(solution)/shard_map/all_to_all | solution.py:392
  23.9 8.6 %shard_map.122 = (f32[1024,128]{1,0:T(8,128)S(1)}, bf16[512,256]{1,0:T(8,128)(2,1)S(1)}, bf16[512,256]{1,0:T(8,128)(2,1)S(1)}, bf16[8192,256]{1,0:T(8,128)(2,1)}) custom-call(s32[100,128]{1,0:T(8,128)S(1)} %bitcast.11, bf16[128,256]{1,0:T(8,128)(2,1)S(1)} %copy-done.1, bf16[128,256]{1,0:T(8,128)(2,1)S(1)} %copy-done.2, bf16[4,256,256]{2,1,0:T(8,128)(2,1)S(1)} %copy-done, ...), custom_call_target="tpu_custom_call" | custom-call | flops 52428800 | bytes 524288 | tf_op jit(solution)/shard_map/pallas_call | solution.py:209
  32.5 5.8 %all-to-all-done.1 = bf16[16,64,256]{2,1,0:T(8,128)(2,1)S(1)} async-done(((bf16[16,64,256]{2,1,0:T(8,128)(2,1)}), bf16[16,64,256]{2,1,0:T(8,128)(2,1)S(1)}, u32[]{:S(2)}, u32[]{:S(2)}) %all-to-all-start.1) | async-done | bytes 524320 | tf_op jit(solution)/shard_map/all_to_all | solution.py:392
  38.3 5.4 %shard_map.123 = (bf16[1024,256]{1,0:T(8,128)(2,1)}, bf16[128,256]{1,0:T(8,128)(2,1)}, bf16[8,5,16,256]{3,2,1,0:T(8,128)(2,1)S(1)}, bf16[8,5,16,256]{3,2,1,0:T(8,128)(2,1)S(1)}) custom-call(bf16[1024,256]{1,0:T(8,128)(2,1)S(1)} %bitcast.10, bf16[256,256]{1,0:T(8,128)(2,1)S(1)} %copy-done.3, bf16[4,256,256]{2,1,0:T(8,128)(2,1)S(1)} %copy-done, ...), custom_call_target="tpu_custom_call" | custom-call | tf_op jit(solution)/shard_map/pallas_call | solution.py:297
  43.8 1.6 %collective-permute-done.got = bf16[8,5,16,256]{3,2,1,0:T(8,128)(2,1)S(1)} collective-permute-done((bf16[8,5,16,256]{3,2,1,0:T(8,128)(2,1)S(1)}, bf16[8,5,16,256]{3,2,1,0:T(8,128)(2,1)S(1)}, u32[]{:S(2)}, u32[]{:S(2)}) %collective-permute-start) | collective-permute-done | bytes 327712 | tf_op jit(solution)/shard_map/ppermute | solution.py:404
  45.5 0.9 collective-permute-start.1
  46.3 4.3 %all-to-all-start.2 = ((bf16[16,64,256]{2,1,0:T(8,128)(2,1)}), bf16[16,64,256]{2,1,0:T(8,128)(2,1)S(1)}, u32[]{:S(2)}, u32[]{:S(2)}) async-start(bf16[16,64,256]{2,1,0:T(8,128)(2,1)} %bitcast.7), calls=%async_computation.2 | async-start | bytes 1048576 | tf_op jit(solution)/shard_map/all_to_all | solution.py:392
  50.6 1.1 %collective-permute-done.1.got = bf16[4,5,16,256]{3,2,1,0:T(8,128)(2,1)S(1)} collective-permute-done((bf16[4,5,16,256]{3,2,1,0:T(8,128)(2,1)S(1)}, bf16[4,5,16,256]{3,2,1,0:T(8,128)(2,1)S(1)}, u32[]{:S(2)}, u32[]{:S(2)}) %collective-permute-start.1) | collective-permute-done | bytes 163872 | tf_op jit(solution)/shard_map/ppermute | solution.py:404
  51.8 1.7 %collective-permute-start.2 = (bf16[2,5,16,256]{3,2,1,0:T(8,128)(2,1)S(1)}, bf16[2,5,16,256]{3,2,1,0:T(8,128)(2,1)S(1)}, u32[]{:S(2)}, u32[]{:S(2)}) collective-permute-start(bf16[2,5,16,256]{3,2,1,0:T(8,128)(2,1)S(1)} %get-tuple-element.43), channel_id=1, source_target_pairs={{0,4},{1,5},{2,6},{3,7},{4,0},{5,1},{6,2},{7,3},{8,12},{9,13},{10,... | collective-permute-start | bytes 245768 | tf_op jit(solution)/shard_map/ppermute | solution.py:404
  53.5 9.2 %collective-permute-done.2.got = bf16[2,5,16,256]{3,2,1,0:T(8,128)(2,1)S(1)} collective-permute-done((bf16[2,5,16,256]{3,2,1,0:T(8,128)(2,1)S(1)}, bf16[2,5,16,256]{3,2,1,0:T(8,128)(2,1)S(1)}, u32[]{:S(2)}, u32[]{:S(2)}) %collective-permute-start.2) | collective-permute-done | bytes 81952 | tf_op jit(solution)/shard_map/ppermute | solution.py:404
  62.7 3.8 %collective-permute-start.3 = (bf16[1,5,16,256]{3,2,1,0:T(8,128)(2,1)S(1)}, bf16[1,5,16,256]{3,2,1,0:T(8,128)(2,1)S(1)}, u32[]{:S(2)}, u32[]{:S(2)}) collective-permute-start(bf16[1,5,16,256]{3,2,1,0:T(8,128)(2,1)S(1)} %get-tuple-element.45), channel_id=1, source_target_pairs={{0,8},{1,9},{2,10},{3,11},{4,12},{5,13},{6,14},{7,15},{8,0},{9,1},... | collective-permute-start | bytes 122888 | tf_op jit(solution)/shard_map/ppermute | solution.py:404
  66.5 2.4 %collective-permute-done.3 = bf16[1,5,16,256]{3,2,1,0:T(8,128)(2,1)S(1)} collective-permute-done((bf16[1,5,16,256]{3,2,1,0:T(8,128)(2,1)S(1)}, bf16[1,5,16,256]{3,2,1,0:T(8,128)(2,1)S(1)}, u32[]{:S(2)}, u32[]{:S(2)}) %collective-permute-start.3) | collective-permute-done | bytes 40992 | tf_op jit(solution)/shard_map/ppermute | solution.py:404
  69.0 2.5 %collective-permute-start.4 = (bf16[1,5,16,256]{3,2,1,0:T(8,128)(2,1)S(1)}, bf16[1,5,16,256]{3,2,1,0:T(8,128)(2,1)S(1)}, u32[]{:S(2)}, u32[]{:S(2)}) collective-permute-start(bf16[1,5,16,256]{3,2,1,0:T(8,128)(2,1)S(1)} %add_convert_fusion), channel_id=1, source_target_pairs={{0,8},{1,9},{2,10},{3,11},{4,12},{5,13},{6,14},{7,15},{8,0},{9,1},... | collective-permute-start | bytes 122888 | tf_op jit(solution)/shard_map/ppermute | solution.py:404
  71.5 2.8 %collective-permute-done.4 = bf16[1,5,16,256]{3,2,1,0:T(8,128)(2,1)S(1)} collective-permute-done((bf16[1,5,16,256]{3,2,1,0:T(8,128)(2,1)S(1)}, bf16[1,5,16,256]{3,2,1,0:T(8,128)(2,1)S(1)}, u32[]{:S(2)}, u32[]{:S(2)}) %collective-permute-start.4) | collective-permute-done | bytes 40992 | tf_op jit(solution)/shard_map/ppermute | solution.py:404
  74.6 4.3 %collective-permute-done.5 = bf16[2,5,16,256]{3,2,1,0:T(8,128)(2,1)S(1)} collective-permute-done((bf16[2,5,16,256]{3,2,1,0:T(8,128)(2,1)S(1)}, bf16[2,5,16,256]{3,2,1,0:T(8,128)(2,1)S(1)}, u32[]{:S(2)}, u32[]{:S(2)}) %collective-permute-start.5) | collective-permute-done | bytes 81952 | tf_op jit(solution)/shard_map/ppermute | solution.py:404
  79.6 7.8 %shard_map.127 = bf16[8192,256]{1,0:T(8,128)(2,1)} custom-call(s32[1,256]{1,0:T(1,128)S(1)} %copy-done.7, bf16[256,1024]{1,0:T(8,128)(2,1)S(1)} %get-tuple-element.46.onehot_t, bf16[1024,256]{1,0:T(8,128)(2,1)S(1)} %bitcast.9, bf16[8192,256]{1,0:T(8,128)(2,1)} %get-tuple-element.48.members), custom_call_target="tpu_custom_call" | custom-call | flops 1073741824 | bytes 8388608 | tf_op jit(solution)/shard_map/pallas_call | solution.py:372
  87.7 1.2 %collective-permute-done.8.beside_core = bf16[4,5,16,256]{3,2,1,0:T(8,128)(2,1)S(1)} collective-permute-done((bf16[4,5,16,256]{3,2,1,0:T(8,128)(2,1)S(1)}, bf16[4,5,16,256]{3,2,1,0:T(8,128)(2,1)S(1)}, u32[]{:S(2)}, u32[]{:S(2)}) %collective-permute-start.8) | collective-permute-done | bytes 163872 | tf_op jit(solution)/shard_map/ppermute | solution.py:404
  88.9 1.2 %shard_map.128 = (f32[4,256,256]{2,1,0:T(8,128)}, f32[256,256]{1,0:T(8,128)}) custom-call(bf16[4,5,16,256]{3,2,1,0:T(8,128)(2,1)S(1)} %pad_maximum_fusion.own, bf16[4,5,16,256]{3,2,1,0:T(8,128)(2,1)S(1)} %collective-permute-done.6.beside, bf16[4,5,16,256]{3,2,1,0:T(8,128)(2,1)S(1)} %collective-permute-done.7.own_core, ...), custom_call_target="tpu_custom_call" | custom-call | tf_op jit(solution)/shard_map/pallas_call | solution.py:349
  (29 shorter events, 1.4 us)
Async XLA Ops:
  0.6 23.2 %copy-start.2 = (bf16[128,256]{1,0:T(8,128)(2,1)S(1)}, bf16[128,256]{1,0:T(8,128)(2,1)}, u32[]{:S(2)}) copy-start(bf16[128,256]{1,0:T(8,128)(2,1)} %out_grad.3) | copy-start | bytes 196612
  0.6 23.2 %copy-start = (bf16[4,256,256]{2,1,0:T(8,128)(2,1)S(1)}, bf16[4,256,256]{2,1,0:T(8,128)(2,1)}, u32[]{:S(2)}) copy-start(bf16[4,256,256]{2,1,0:T(8,128)(2,1)} %weights.3) | copy-start | bytes 1572868
  0.7 23.2 %copy-start.1 = (bf16[128,256]{1,0:T(8,128)(2,1)S(1)}, bf16[128,256]{1,0:T(8,128)(2,1)}, u32[]{:S(2)}) copy-start(bf16[128,256]{1,0:T(8,128)(2,1)} %queries.3) | copy-start | bytes 196612
  0.7 23.2 %copy-start.4 = (s32[128,100]{0,1:T(8,128)S(1)}, s32[128,100]{0,1:T(8,128)}, u32[]{:S(2)}) copy-start(s32[128,100]{0,1:T(8,128)} %param.14) | copy-start | bytes 153604
  0.7 37.6 %copy-start.3 = (bf16[256,256]{1,0:T(8,128)(2,1)S(1)}, bf16[256,256]{1,0:T(8,128)(2,1)}, u32[]{:S(2)}) copy-start(bf16[256,256]{1,0:T(8,128)(2,1)} %enc.1) | copy-start | bytes 393220
  2.0 14.5 %all-to-all-start = ((s32[16,1,128]{2,1,0:T(1,128)}), s32[16,1,128]{2,1,0:T(1,128)S(1)}, u32[]{:S(2)}, u32[]{:S(2)}) async-start(s32[16,1,128]{2,1,0:T(1,128)} %bitcast.1), calls=%async_computation | async-start | bytes 16384 | tf_op jit(solution)/shard_map/all_to_all | solution.py:392
  9.4 0.8 copy-start.5
  10.2 0.7 copy-start.6
  17.8 20.5 %all-to-all-start.1 = ((bf16[16,64,256]{2,1,0:T(8,128)(2,1)}), bf16[16,64,256]{2,1,0:T(8,128)(2,1)S(1)}, u32[]{:S(2)}, u32[]{:S(2)}) async-start(bf16[16,64,256]{2,1,0:T(8,128)(2,1)} %bitcast.4), calls=%async_computation.1 | async-start | bytes 1048576 | tf_op jit(solution)/shard_map/all_to_all | solution.py:392
  43.8 1.6 %collective-permute-start = (bf16[8,5,16,256]{3,2,1,0:T(8,128)(2,1)S(1)}, bf16[8,5,16,256]{3,2,1,0:T(8,128)(2,1)S(1)}, u32[]{:S(2)}, u32[]{:S(2)}) collective-permute-start(bf16[8,5,16,256]{3,2,1,0:T(8,128)(2,1)S(1)} %get-tuple-element.37), channel_id=1, source_target_pairs={{0,1},{1,0},{2,3},{3,2},{4,5},{5,4},{6,7},{7,6},{8,9},{9,8},{10,11... | collective-permute-start | bytes 983048 | tf_op jit(solution)/shard_map/ppermute | solution.py:404
  45.5 6.3 %collective-permute-start.1 = (bf16[4,5,16,256]{3,2,1,0:T(8,128)(2,1)S(1)}, bf16[4,5,16,256]{3,2,1,0:T(8,128)(2,1)S(1)}, u32[]{:S(2)}, u32[]{:S(2)}) collective-permute-start(bf16[4,5,16,256]{3,2,1,0:T(8,128)(2,1)S(1)} %get-tuple-element.41), channel_id=1, source_target_pairs={{0,2},{1,3},{2,0},{3,1},{4,6},{5,7},{6,4},{7,5},{8,10},{9,11},{10,... | collective-permute-start | bytes 491528 | tf_op jit(solution)/shard_map/ppermute | solution.py:404
  46.3 33.3 %all-to-all-start.2 = ((bf16[16,64,256]{2,1,0:T(8,128)(2,1)}), bf16[16,64,256]{2,1,0:T(8,128)(2,1)S(1)}, u32[]{:S(2)}, u32[]{:S(2)}) async-start(bf16[16,64,256]{2,1,0:T(8,128)(2,1)} %bitcast.7), calls=%async_computation.2 | async-start | bytes 1048576 | tf_op jit(solution)/shard_map/all_to_all | solution.py:392
  51.8 27.9 %copy-start.7 = (s32[1,256]{1,0:T(1,128)S(1)}, s32[1,256]{1,0:T(1,128)}, u32[]{:S(2)}) copy-start(s32[1,256]{1,0:T(1,128)} %counts.1) | copy-start | bytes 3076
  51.8 10.9 %collective-permute-start.2 = (bf16[2,5,16,256]{3,2,1,0:T(8,128)(2,1)S(1)}, bf16[2,5,16,256]{3,2,1,0:T(8,128)(2,1)S(1)}, u32[]{:S(2)}, u32[]{:S(2)}) collective-permute-start(bf16[2,5,16,256]{3,2,1,0:T(8,128)(2,1)S(1)} %get-tuple-element.43), channel_id=1, source_target_pairs={{0,4},{1,5},{2,6},{3,7},{4,0},{5,1},{6,2},{7,3},{8,12},{9,13},{10,... | collective-permute-start | bytes 245768 | tf_op jit(solution)/shard_map/ppermute | solution.py:404
  62.7 6.2 %collective-permute-start.3 = (bf16[1,5,16,256]{3,2,1,0:T(8,128)(2,1)S(1)}, bf16[1,5,16,256]{3,2,1,0:T(8,128)(2,1)S(1)}, u32[]{:S(2)}, u32[]{:S(2)}) collective-permute-start(bf16[1,5,16,256]{3,2,1,0:T(8,128)(2,1)S(1)} %get-tuple-element.45), channel_id=1, source_target_pairs={{0,8},{1,9},{2,10},{3,11},{4,12},{5,13},{6,14},{7,15},{8,0},{9,1},... | collective-permute-start | bytes 122888 | tf_op jit(solution)/shard_map/ppermute | solution.py:404
  69.0 5.4 %collective-permute-start.4 = (bf16[1,5,16,256]{3,2,1,0:T(8,128)(2,1)S(1)}, bf16[1,5,16,256]{3,2,1,0:T(8,128)(2,1)S(1)}, u32[]{:S(2)}, u32[]{:S(2)}) collective-permute-start(bf16[1,5,16,256]{3,2,1,0:T(8,128)(2,1)S(1)} %add_convert_fusion), channel_id=1, source_target_pairs={{0,8},{1,9},{2,10},{3,11},{4,12},{5,13},{6,14},{7,15},{8,0},{9,1},... | collective-permute-start | bytes 122888 | tf_op jit(solution)/shard_map/ppermute | solution.py:404
  74.4 4.5 %collective-permute-start.5 = (bf16[2,5,16,256]{3,2,1,0:T(8,128)(2,1)S(1)}, bf16[2,5,16,256]{3,2,1,0:T(8,128)(2,1)S(1)}, u32[]{:S(2)}, u32[]{:S(2)}) collective-permute-start(bf16[2,5,16,256]{3,2,1,0:T(8,128)(2,1)S(1)} %pad_maximum_fusion.1), channel_id=1, source_target_pairs={{0,4},{1,5},{2,6},{3,7},{4,0},{5,1},{6,2},{7,3},{8,12},{9,13},{10,... | collective-permute-start | bytes 245768 | tf_op jit(solution)/shard_map/ppermute | solution.py:404
  78.9 8.5 %collective-permute-start.7 = (bf16[4,5,16,256]{3,2,1,0:T(8,128)(2,1)S(1)}, bf16[4,5,16,256]{3,2,1,0:T(8,128)(2,1)S(1)}, u32[]{:S(2)}, u32[]{:S(2)}) collective-permute-start(bf16[4,5,16,256]{3,2,1,0:T(8,128)(2,1)S(1)} %pad_maximum_fusion.own), channel_id=1, source_target_pairs={{0,1},{1,0},{2,3},{3,2},{4,5},{5,4},{6,7},{7,6},{8,9},{9,8},{10,11... | collective-permute-start | bytes 491528 | tf_op jit(solution)/shard_map/ppermute | solution.py:404
  79.0 8.4 %collective-permute-start.6 = (bf16[4,5,16,256]{3,2,1,0:T(8,128)(2,1)S(1)}, bf16[4,5,16,256]{3,2,1,0:T(8,128)(2,1)S(1)}, u32[]{:S(2)}, u32[]{:S(2)}) collective-permute-start(bf16[4,5,16,256]{3,2,1,0:T(8,128)(2,1)S(1)} %pad_maximum_fusion.own), channel_id=1, source_target_pairs={{0,2},{1,3},{2,0},{3,1},{4,6},{5,7},{6,4},{7,5},{8,10},{9,11},{10,... | collective-permute-start | bytes 491528 | tf_op jit(solution)/shard_map/ppermute | solution.py:404
  87.4 1.5 %collective-permute-start.8 = (bf16[4,5,16,256]{3,2,1,0:T(8,128)(2,1)S(1)}, bf16[4,5,16,256]{3,2,1,0:T(8,128)(2,1)S(1)}, u32[]{:S(2)}, u32[]{:S(2)}) collective-permute-start(bf16[4,5,16,256]{3,2,1,0:T(8,128)(2,1)S(1)} %collective-permute-done.6.beside), channel_id=1, source_target_pairs={{0,1},{1,0},{2,3},{3,2},{4,5},{5,4},{6,7},{7,6},{8,9},{9,8},{10,11... | collective-permute-start | bytes 491528 | tf_op jit(solution)/shard_map/ppermute | solution.py:404

commit v5 on v2

--- a/solution.py
+++ b/solution.py
@@ -9,10 +9,13 @@
 
 HEADS = 4
 MATRICES = 5
+WEIGHT = 10**11
 LANES = 128
 F32 = jnp.float32
 BF16 = jnp.bfloat16
-VMEM_LIMIT = 48 * 1024 * 1024
+VMEM_LIMIT = 32 * 1024 * 1024
+MOST_VMEM = 51 * 1024 * 1024
+SMALL = pltpu.CompilerParams(vmem_limit_bytes=8 * 1024 * 1024)
 
 
 def dot(a, b):
@@ -127,30 +130,33 @@
             pltpu.SemaphoreType.DMA((3,)),
             pltpu.SemaphoreType.DMA((parts,)),
         ],
-        compiler_params=pltpu.CompilerParams(vmem_limit_bytes=VMEM_LIMIT),
+        compiler_params=pltpu.CompilerParams(vmem_limit_bytes=MOST_VMEM),
         cost_estimate=pl.CostEstimate(
             flops=2 * rows * clusters * width, bytes_accessed=2 * rows * width, transcendentals=0
         ),
     )(counts, members.reshape(groups, LANES), raw_rows)
 
 
-def select_kernel(got, means, onehot_t, sent):
+def select_kernel(asked, means, onehot_t, sent):
     clusters = means.shape[0]
-    parity = lax.axis_index("clu") % 2
+    me = lax.axis_index("clu")
+    parity = me % 2
     half = LANES // 2
-    wanted = lax.rem(got[...], clusters)
+    columns = pl.ds(pl.multiple_of(me // 2 * LANES, LANES), LANES)
+    wanted = lax.rem(asked[:, columns], clusters)
     turned = pltpu.roll(wanted, half, 1)
     first = jnp.where(parity == 0, wanted, turned)
     second = jnp.where(parity == 0, turned, wanted)
     left = iota((1, LANES), 1) < half
-    for k in range(got.shape[0] // 2):
+    for k in range(asked.shape[0] // 2):
         row = jnp.where(left, first[2 * k : 2 * k + 1], second[2 * k + 1 : 2 * k + 2])
         onehot_t[:, k * LANES : (k + 1) * LANES] = ones_where(row == iota((clusters, LANES), 0))
     sent[...] = dot_tn(onehot_t[...], means[...]).astype(BF16)
 
 
-def select_rows(got, means, pooled):
+def select_rows(asked, means):
     clusters, width = means.shape
+    pooled = asked.shape[1]
     return pl.pallas_call(
         select_kernel,
         out_shape=[
@@ -158,7 +164,7 @@
             jax.ShapeDtypeStruct((pooled, width), BF16),
         ],
         compiler_params=pltpu.CompilerParams(vmem_limit_bytes=VMEM_LIMIT),
-    )(got, means)
+    )(asked, means)
 
 
 def spread_heads(rows):
@@ -207,7 +213,7 @@
 
 
 def attention_kernel(
-    scale, owners, raw, enc, weights, queries, out_grad, bias, query_heads, mixed_heads, back, grad_query, keep, send, grads
+    scale, raw, enc, weights, queries, out_grad, bias, query_heads, mixed_heads, back, grad_query, keep, send, grads
 ):
     pooled, width = raw.shape
     targets = queries.shape[0]
@@ -254,23 +260,21 @@
     grads[4 * width : 5 * width, :] = dot_tn(raw_pool, emb_grad)
     back[...] = emb_grad
     core = lax.axis_index("clu") % 2
-    part = width // owners
-    deep = owners // 4
+    part = width // 4
     for y in range(2):
-        for z in range(deep):
-            for m in range(MATRICES):
-                at = m * width + (z * 4 + y * 2) * part
-                kept = pl.ds(pl.multiple_of(at + core * part, part), part)
-                given = pl.ds(pl.multiple_of(at + (1 - core) * part, part), part)
-                keep[y * deep + z, m] = grads[kept, :].astype(BF16)
-                send[y * deep + z, m] = grads[given, :].astype(BF16)
-
-
-def attention(scale, owners, raw_pool, enc, weights, queries, out_grad, bias, query_heads, mixed_heads):
+        for m in range(MATRICES):
+            at = m * width + 2 * y * part
+            kept = pl.ds(pl.multiple_of(at + core * part, part), part)
+            given = pl.ds(pl.multiple_of(at + (1 - core) * part, part), part)
+            keep[y, m] = grads[kept, :].astype(BF16)
+            send[y, m] = grads[given, :].astype(BF16)
+
+
+def attention(scale, raw_pool, enc, weights, queries, out_grad, bias, query_heads, mixed_heads):
     pooled, width = raw_pool.shape
-    half = jax.ShapeDtypeStruct((owners // 2, MATRICES, width // owners, width), BF16)
-    return pl.pallas_call(
-        functools.partial(attention_kernel, scale, owners),
+    half = jax.ShapeDtypeStruct((2, MATRICES, width // 4, width), BF16)
+    return pl.pallas_call(
+        functools.partial(attention_kernel, scale),
         out_shape=[
             jax.ShapeDtypeStruct((pooled, width), BF16),
             jax.ShapeDtypeStruct(queries.shape, BF16),
@@ -286,55 +290,51 @@
     return (a.astype(F32) + b.astype(F32)).astype(BF16)
 
 
-def split_y_kernel(keep, got, kept, given):
-    y = lax.axis_index("clu") // 2 % 2
-    deep = kept.shape[0]
-    for i in range(deep):
-        own = y * deep + i
-        other = (1 - y) * deep + i
-        kept[i] = add_low(keep[own], got[own])
-        given[i] = add_low(keep[other], got[other])
-
-
-def split_y(keep, got):
-    half = jax.ShapeDtypeStruct((keep.shape[0] // 2,) + keep.shape[1:], BF16)
-    return pl.pallas_call(split_y_kernel, out_shape=[half, half])(keep, got)
-
-
-def split_z_kernel(keep, got, *outs):
-    z = lax.axis_index("clu") // 4
-    deep = keep.shape[0]
-    for k in range(deep):
-        at = lax.rem(z + k, deep)
-        outs[k][...] = add_low(keep[at], got[at])
-
-
-def split_z(keep, got):
-    one = jax.ShapeDtypeStruct(keep.shape[1:], BF16)
-    return pl.pallas_call(split_z_kernel, out_shape=[one] * keep.shape[0])(keep, got)
+def split_kernel(keep, got, kept, given):
+    side = lax.axis_index("clu") // 2 % 2
+    kept[...] = add_low(keep[side], got[side])
+    given[...] = add_low(keep[1 - side], got[1 - side])
+
+
+def split(keep, got):
+    half = jax.ShapeDtypeStruct(keep.shape[1:], BF16)
+    return pl.pallas_call(split_kernel, out_shape=[half, half], compiler_params=SMALL)(keep, got)
+
+
+def sum_kernel(a, b, out):
+    out[...] = add_low(a[...], b[...])
+
+
+def sum_rows(a, b, flops):
+    return pl.pallas_call(
+        sum_kernel,
+        out_shape=jax.ShapeDtypeStruct(a.shape, BF16),
+        compiler_params=SMALL,
+        cost_estimate=pl.CostEstimate(
+            flops=flops, bytes_accessed=6 * a.size, transcendentals=0
+        ),
+    )(a, b)
 
 
 def place_kernel(own, beside, own_core, beside_core, attn, enc):
-    me = lax.axis_index("clu")
-    deep, matrices, part, _ = own.shape
-    for k in range(deep):
-        z = lax.rem(me // 4 + deep - k, deep)
-        low = me % 4
-        for source, flip in ((own, 0), (beside, 2), (own_core, 1), (beside_core, 3)):
-            at = pl.multiple_of((z * 4 + (low ^ flip)) * part, part)
-            for m in range(matrices - 1):
-                attn[m, pl.ds(at, part), :] = source[k, m].astype(F32)
-            enc[pl.ds(at, part), :] = source[k, matrices - 1].astype(F32)
+    quarter = lax.axis_index("clu") % 4
+    matrices, part, _ = own.shape
+    for source, flip in ((own, 0), (beside, 2), (own_core, 1), (beside_core, 3)):
+        rows = pl.ds(pl.multiple_of((quarter ^ flip) * part, part), part)
+        for m in range(matrices - 1):
+            attn[m, rows, :] = source[m].astype(F32)
+        enc[rows, :] = source[matrices - 1].astype(F32)
 
 
 def place(own, beside, own_core, beside_core):
-    width = own.shape[3]
+    width = own.shape[2]
     return pl.pallas_call(
         place_kernel,
         out_shape=[
             jax.ShapeDtypeStruct((MATRICES - 1, width, width), F32),
             jax.ShapeDtypeStruct((width, width), F32),
         ],
+        compiler_params=SMALL,
     )(own, beside, own_core, beside_core)
 
 
@@ -383,42 +383,38 @@
 def local(raw_rows, enc_weight, counts, member_rows, pool, picks, queries, attn_weights, out_grad):
     rows, width = raw_rows.shape
     owners = lax.axis_size("clu")
-    deep = owners // 4
     pooled = pool.shape[1]
+    clusters = counts.shape[1]
     scale = (width // HEADS) ** -0.5
-
-    def permute(block, target):
-        return lax.ppermute(block, "clu", [(d, target(d)) for d in range(owners)])
-
-    def along_z(k):
-        return lambda d: (d // 4 + k) % deep * 4 + d % 4
-
-    def flip(bit):
-        return lambda d: d ^ bit
-
-    pairs = pool.reshape(owners // 2, 1, 1, LANES)
-    asking = jnp.broadcast_to(pairs, (owners // 2, 2, 1, LANES)).reshape(owners, 1, LANES)
-    got = swap(asking).reshape(owners, LANES)
+    bits = owners.bit_length() - 1
+
+    def exchange(bit, block):
+        return lax.ppermute(block, "clu", [(d, d ^ (1 << bit)) for d in range(owners)])
+
+    asked = lax.all_gather(pool, "clu", axis=0, tiled=True)
     means, table = cluster_means(counts, member_rows, raw_rows)
-    onehot_t, sent = select_rows(got, means, pooled)
+    onehot_t, sent = select_rows(asked, means)
     raw_pool = swap(sent.reshape(owners, pooled // owners, width)).reshape(pooled, width)
     bias, query_heads, mixed_heads = target_terms(
         scale, picks.T, queries, out_grad, attn_weights, pooled
     )
     back, grad_query, keep, given = attention(
-        scale, owners, raw_pool, enc_weight, attn_weights, queries, out_grad, bias, query_heads, mixed_heads
+        scale, raw_pool, enc_weight, attn_weights, queries, out_grad, bias, query_heads, mixed_heads
     )
-    keep, given = split_y(keep, permute(given, flip(1)))
+    own, given = split(keep, exchange(0, given))
+    given, back = lax.optimization_barrier((given, back))
+    got = exchange(1, given)
     back = swap(back.reshape(owners, pooled // owners, width)).reshape(pooled, width)
-    terms = split_z(keep, permute(given, flip(2)))
-    total = terms[0].astype(F32)
-    for k in range(1, deep):
-        total = total + permute(terms[k], along_z(k)).astype(F32)
-    total = total.astype(BF16)
-    own = jnp.stack([total] + [permute(total, along_z(k)) for k in range(1, deep)])
-    beside = permute(own, flip(2))
-    grad_attn, grad_encoder = place(own, beside, permute(own, flip(1)), permute(beside, flip(1)))
+    own = sum_rows(own, got, WEIGHT)
+    for bit in range(2, bits - 1):
+        own = sum_rows(own, exchange(bit, own), own.size)
+    got = exchange(bits - 1, own)
     grad_rows = member_grads(counts, onehot_t, table, back, rows)
+    got, grad_rows = lax.optimization_barrier((got, grad_rows))
+    own = sum_rows(own, got, own.size)
+    beside = exchange(1, own)
+    own_core = exchange(0, own)
+    grad_attn, grad_encoder = place(own, beside, own_core, exchange(0, beside))
     return grad_query, grad_rows, grad_attn, grad_encoder
 
 

time: 98.3 us -> 97 us (0.987)
  blocking collectives: 0 us -> 23.6 us
  starting transfers between devices: 29.3 us -> 14.4 us
  local copies, waits for them, and re-layouts: 7.71 us -> 1.47 us
  Pallas kernels: 27.4 us -> 22.5 us
  waiting for transfers between devices: 31.6 us -> 33.7 us
    all_gather x0 -> x1, blocking collectives: none -> 23.6 us  [local(): asked = lax.all_gather(pool, 'clu', axis=0, tiled=True)]
    all_to_all x3 -> x2, starting transfers between devices: 17.8 us -> 7.84 us  [swap(): lax.all_to_all(blocks, 'clu', split_axis=0, concat_axis=0, tiled=True)]
    unnamed x32 -> x17, local copies, waits for them, and re-layouts: 6.42 us -> 1.47 us
    ppermute x11 -> x7, starting transfers between devices: 11.5 us -> 6.61 us  [exchange(): lax.ppermute(block, 'clu', [(d, d ^ 1 << bit) for d in range(owners)])]
    pallas_call x3 -> x5, Pallas kernels: 8.97 us -> 5.28 us  [the longest x1 5.08 us: attention(): pl.pallas_call(functools.partial(attention_kernel, scale), out_shape=[jax...]
    ppermute x11 -> x7, waiting for transfers between devices: 21.1 us -> 23.2 us  [exchange(): lax.ppermute(block, 'clu', [(d, d ^ 1 << bit) for d in range(owners)])]
    broadcast_in_dim x1 -> x0, local copies, waits for them, and re-layouts: 1.29 us -> none  [local(): jnp.broadcast_to(pairs, (owners // 2, 2, 1, LANES))]
    pallas_call x1, Pallas kernels: 2.3 us -> 1.14 us  [place(): pl.pallas_call(place_kernel, out_shape=[jax.ShapeDtypeStruct((MATRICES -...]
  transfers between devices with their start and end apart: 14 -> 9, of which waited for: 10 -> 7; matrix products, arithmetic and copies ran while one was open for 1% -> 0% of each run, Pallas kernels for 16% -> 10%
where the time goes in v5:
time: 97 us; the launch traced here: 96.6 us
  waiting for transfers between devices  33.7 us (35%)
  blocking collectives  23.6 us (24%)
  Pallas kernels  22.5 us (23%)
  starting transfers between devices  14.4 us (15%)
  local copies, waits for them, and re-layouts  1.47 us (2%)
    all_gather x1, blocking collectives, local(): asked = lax.all_gather(pool, 'clu', axis=0, tiled=True)  23.6 us
    ppermute x7, waiting for transfers between devices, exchange(): lax.ppermute(block, 'clu', [(d, d ^ 1 << bit) for d in range(owners)])  23.2 us
    all_to_all x2, waiting for transfers between devices, swap(): lax.all_to_all(blocks, 'clu', split_axis=0, concat_axis=0, tiled=True)  10.5 us
    all_to_all x2, starting transfers between devices, swap(): lax.all_to_all(blocks, 'clu', split_axis=0, concat_axis=0, tiled=True)  7.84 us
    ppermute x7, starting transfers between devices, exchange(): lax.ppermute(block, 'clu', [(d, d ^ 1 << bit) for d in range(owners)])  6.61 us
    pallas_call x1, Pallas kernels, cluster_means(): pl.pallas_call(means_kernel, in_specs=[pl.BlockSpec(memory_space=pltpu.HB...  5.66 us
    pallas_call x1, Pallas kernels, member_grads(): pl.pallas_call(rows_kernel, grid=(rows // block,), in_specs=[pl.BlockSpec...  5.29 us
    pallas_call x1, Pallas kernels, attention(): pl.pallas_call(functools.partial(attention_kernel, scale), out_shape=[jax...  5.08 us
  transfers between devices with their start and end apart: 9, of which 7 were waited for; matrix products, arithmetic and copies ran while one was open for 0% of the time, Pallas kernels for 10%

profile of v5, /device:TPU:0, one launch (start us, length us, event | category | flops | bytes accessed | tf_op | source)
XLA Modules:
  0.0 96.6 jit_solution(11067870249282541892)
XLA Ops:
  0.7 23.6 %all-gather = s32[16,1,1024]{2,1,0:T(1,128)S(1)} all-gather(s32[1,1,1024]{2,1,0:T(1,128)} %bitcast.15), channel_id=1, replica_groups=mesh['grp'=2,'clu'=16] {'clu'}, dimensions={0}, use_global_device_ids=true | all-gather | bytes 69632 | tf_op jit(solution)/shard_map/all_gather | solution.py:394
  24.4 0.7 copy-done.5
  25.1 0.7 copy-done.6
  25.8 5.7 %shard_map.120 = (bf16[256,256]{1,0:T(8,128)(2,1)S(1)}, f32[64,128]{1,0:T(8,128)S(1)}) custom-call(s32[1,256]{1,0:T(1,128)S(1)} %copy-done.6, s32[64,128]{1,0:T(8,128)S(1)} %bitcast.14, bf16[8192,256]{1,0:T(8,128)(2,1)} %raw_h.1), custom_call_target="tpu_custom_call" | custom-call | flops 1073741824 | bytes 4194304 | tf_op jit(solution)/shard_map/pallas_call | solution.py:118
  31.4 1.3 %shard_map.121 = (bf16[256,1024]{1,0:T(8,128)(2,1)S(1)}, bf16[1024,256]{1,0:T(8,128)(2,1)}) custom-call(s32[16,1024]{1,0:T(8,128)S(1)} %bitcast.12, bf16[256,256]{1,0:T(8,128)(2,1)S(1)} %get-tuple-element.23.means), custom_call_target="tpu_custom_call" | custom-call | tf_op jit(solution)/shard_map/pallas_call | solution.py:160
  32.7 3.6 %all-to-all-start = ((bf16[16,64,256]{2,1,0:T(8,128)(2,1)}), bf16[16,64,256]{2,1,0:T(8,128)(2,1)S(1)}, u32[]{:S(2)}, u32[]{:S(2)}) async-start(bf16[16,64,256]{2,1,0:T(8,128)(2,1)} %bitcast.2), calls=%async_computation | async-start | bytes 1048576 | tf_op jit(solution)/shard_map/all_to_all | solution.py:380
  36.4 3.9 %shard_map.122 = (f32[1024,128]{1,0:T(8,128)S(1)}, bf16[512,256]{1,0:T(8,128)(2,1)S(1)}, bf16[512,256]{1,0:T(8,128)(2,1)S(1)}) custom-call(s32[100,128]{1,0:T(8,128)S(1)} %bitcast.13, bf16[128,256]{1,0:T(8,128)(2,1)S(1)} %copy-done.1, bf16[128,256]{1,0:T(8,128)(2,1)S(1)} %copy-done.2, bf16[4,256,256]{2,1,0:T(8,128)(2,1)S(1)} %copy-done), custom_call_target="tpu_custom_call" | custom-call | flops 52428800 | bytes 524288 | tf_op jit(solution)/shard_map/pallas_call | solution.py:199
  40.2 10.5 %all-to-all-done = bf16[16,64,256]{2,1,0:T(8,128)(2,1)S(1)} async-done(((bf16[16,64,256]{2,1,0:T(8,128)(2,1)}), bf16[16,64,256]{2,1,0:T(8,128)(2,1)S(1)}, u32[]{:S(2)}, u32[]{:S(2)}) %all-to-all-start) | async-done | bytes 524320 | tf_op jit(solution)/shard_map/all_to_all | solution.py:380
  50.7 5.1 %shard_map.123 = (bf16[1024,256]{1,0:T(8,128)(2,1)}, bf16[128,256]{1,0:T(8,128)(2,1)}, bf16[2,5,64,256]{3,2,1,0:T(8,128)(2,1)S(1)}, bf16[2,5,64,256]{3,2,1,0:T(8,128)(2,1)S(1)}) custom-call(bf16[1024,256]{1,0:T(8,128)(2,1)S(1)} %bitcast.11, bf16[256,256]{1,0:T(8,128)(2,1)S(1)} %copy-done.3, bf16[4,256,256]{2,1,0:T(8,128)(2,1)S(1)} %copy-done, ...), custom_call_target="tpu_custom_call" | custom-call | tf_op jit(solution)/shard_map/pallas_call | solution.py:276
  55.8 0.0 collective-permute-start
  55.8 1.6 %collective-permute-done.got = bf16[2,5,64,256]{3,2,1,0:T(8,128)(2,1)S(1)} collective-permute-done((bf16[2,5,64,256]{3,2,1,0:T(8,128)(2,1)S(1)}, bf16[2,5,64,256]{3,2,1,0:T(8,128)(2,1)S(1)}, u32[]{:S(2)}, u32[]{:S(2)}) %collective-permute-start) | collective-permute-done | bytes 327712 | tf_op jit(solution)/shard_map/ppermute | solution.py:392
  57.5 0.1 shard_map.124
  57.5 0.9 collective-permute-start.1
  58.4 4.3 %all-to-all-start.1 = ((bf16[16,64,256]{2,1,0:T(8,128)(2,1)}), bf16[16,64,256]{2,1,0:T(8,128)(2,1)S(1)}, u32[]{:S(2)}, u32[]{:S(2)}) async-start(bf16[16,64,256]{2,1,0:T(8,128)(2,1)} %bitcast.5), calls=%async_computation.1 | async-start | bytes 1048576 | tf_op jit(solution)/shard_map/all_to_all | solution.py:380
  62.7 1.2 %collective-permute-done.1.b = bf16[5,64,256]{2,1,0:T(8,128)(2,1)S(1)} collective-permute-done((bf16[5,64,256]{2,1,0:T(8,128)(2,1)S(1)}, bf16[5,64,256]{2,1,0:T(8,128)(2,1)S(1)}, u32[]{:S(2)}, u32[]{:S(2)}) %collective-permute-start.1) | collective-permute-done | bytes 163872 | tf_op jit(solution)/shard_map/ppermute | solution.py:392
  63.9 1.7 %collective-permute-start.2 = (bf16[5,64,256]{2,1,0:T(8,128)(2,1)S(1)}, bf16[5,64,256]{2,1,0:T(8,128)(2,1)S(1)}, u32[]{:S(2)}, u32[]{:S(2)}) collective-permute-start(bf16[5,64,256]{2,1,0:T(8,128)(2,1)S(1)} %shard_map.125.a), channel_id=1, source_target_pairs={{0,4},{1,5},{2,6},{3,7},{4,0},{5,1},{6,2},{7,3},{8,12},{9,13},{10,... | collective-permute-start | bytes 491528 | tf_op jit(solution)/shard_map/ppermute | solution.py:392
  65.6 12.2 %collective-permute-done.2.b = bf16[5,64,256]{2,1,0:T(8,128)(2,1)S(1)} collective-permute-done((bf16[5,64,256]{2,1,0:T(8,128)(2,1)S(1)}, bf16[5,64,256]{2,1,0:T(8,128)(2,1)S(1)}, u32[]{:S(2)}, u32[]{:S(2)}) %collective-permute-start.2) | collective-permute-done | bytes 163872 | tf_op jit(solution)/shard_map/ppermute | solution.py:392
  77.8 2.5 %collective-permute-start.3 = (bf16[5,64,256]{2,1,0:T(8,128)(2,1)S(1)}, bf16[5,64,256]{2,1,0:T(8,128)(2,1)S(1)}, u32[]{:S(2)}, u32[]{:S(2)}) collective-permute-start(bf16[5,64,256]{2,1,0:T(8,128)(2,1)S(1)} %shard_map.126.a), channel_id=1, source_target_pairs={{0,8},{1,9},{2,10},{3,11},{4,12},{5,13},{6,14},{7,15},{8,0},{9,1},... | collective-permute-start | bytes 491528 | tf_op jit(solution)/shard_map/ppermute | solution.py:392
  80.3 5.3 %shard_map.127 = bf16[8192,256]{1,0:T(8,128)(2,1)} custom-call(s32[1,256]{1,0:T(1,128)S(1)} %copy-done.7, bf16[256,1024]{1,0:T(8,128)(2,1)S(1)} %get-tuple-element.35.onehot_t, f32[64,128]{1,0:T(8,128)S(1)} %get-tuple-element.36.table, bf16[1024,256]{1,0:T(8,128)(2,1)S(1)} %bitcast.10), custom_call_target="tpu_custom_call" | custom-call | flops 1073741824 | bytes 4194304 | tf_op jit(solution)/shard_map/pallas_call | solution.py:360
  85.6 2.4 %collective-permute-done.3.b = bf16[5,64,256]{2,1,0:T(8,128)(2,1)S(1)} collective-permute-done((bf16[5,64,256]{2,1,0:T(8,128)(2,1)S(1)}, bf16[5,64,256]{2,1,0:T(8,128)(2,1)S(1)}, u32[]{:S(2)}, u32[]{:S(2)}) %collective-permute-start.3) | collective-permute-done | bytes 163872 | tf_op jit(solution)/shard_map/ppermute | solution.py:392
  88.0 1.5 %collective-permute-start.4 = (bf16[5,64,256]{2,1,0:T(8,128)(2,1)S(1)}, bf16[5,64,256]{2,1,0:T(8,128)(2,1)S(1)}, u32[]{:S(2)}, u32[]{:S(2)}) collective-permute-start(bf16[5,64,256]{2,1,0:T(8,128)(2,1)S(1)} %shard_map.128.own), channel_id=1, source_target_pairs={{0,2},{1,3},{2,0},{3,1},{4,6},{5,7},{6,4},{7,5},{8,10},{9,11},{10,... | collective-permute-start | bytes 491528 | tf_op jit(solution)/shard_map/ppermute | solution.py:392
  89.6 4.5 %collective-permute-done.4.beside = bf16[5,64,256]{2,1,0:T(8,128)(2,1)S(1)} collective-permute-done((bf16[5,64,256]{2,1,0:T(8,128)(2,1)S(1)}, bf16[5,64,256]{2,1,0:T(8,128)(2,1)S(1)}, u32[]{:S(2)}, u32[]{:S(2)}) %collective-permute-start.4) | collective-permute-done | bytes 163872 | tf_op jit(solution)/shard_map/ppermute | solution.py:392
  94.1 1.4 %collective-permute-done.6.beside_core = bf16[5,64,256]{2,1,0:T(8,128)(2,1)S(1)} collective-permute-done((bf16[5,64,256]{2,1,0:T(8,128)(2,1)S(1)}, bf16[5,64,256]{2,1,0:T(8,128)(2,1)S(1)}, u32[]{:S(2)}, u32[]{:S(2)}) %collective-permute-start.6) | collective-permute-done | bytes 163872 | tf_op jit(solution)/shard_map/ppermute | solution.py:392
  95.5 1.1 %shard_map.129 = (f32[4,256,256]{2,1,0:T(8,128)}, f32[256,256]{1,0:T(8,128)}) custom-call(bf16[5,64,256]{2,1,0:T(8,128)(2,1)S(1)} %shard_map.128.own, bf16[5,64,256]{2,1,0:T(8,128)(2,1)S(1)} %collective-permute-done.4.beside, bf16[5,64,256]{2,1,0:T(8,128)(2,1)S(1)} %collective-permute-done.5.own_core, bf16[5,64,256]{2,1,0:T(8,128)(2,1)S(1)} %collective-permute-done.6.beside_core), custom_call_target="tpu_custom_call" | custom-call | tf_op jit(solution)/shard_map/pallas_call | solution.py:331
  (22 shorter events, 0.2 us)
Async XLA Ops:
  0.6 35.7 %copy-start.2 = (bf16[128,256]{1,0:T(8,128)(2,1)S(1)}, bf16[128,256]{1,0:T(8,128)(2,1)}, u32[]{:S(2)}) copy-start(bf16[128,256]{1,0:T(8,128)(2,1)} %out_grad.3) | copy-start | bytes 196612
  0.6 35.7 %copy-start = (bf16[4,256,256]{2,1,0:T(8,128)(2,1)S(1)}, bf16[4,256,256]{2,1,0:T(8,128)(2,1)}, u32[]{:S(2)}) copy-start(bf16[4,256,256]{2,1,0:T(8,128)(2,1)} %weights.3) | copy-start | bytes 1572868
  0.7 35.7 %copy-start.1 = (bf16[128,256]{1,0:T(8,128)(2,1)S(1)}, bf16[128,256]{1,0:T(8,128)(2,1)}, u32[]{:S(2)}) copy-start(bf16[128,256]{1,0:T(8,128)(2,1)} %queries.3) | copy-start | bytes 196612
  0.7 35.7 %copy-start.4 = (s32[128,100]{0,1:T(8,128)S(1)}, s32[128,100]{0,1:T(8,128)}, u32[]{:S(2)}) copy-start(s32[128,100]{0,1:T(8,128)} %param.14) | copy-start | bytes 153604
  0.7 50.1 %copy-start.3 = (bf16[256,256]{1,0:T(8,128)(2,1)S(1)}, bf16[256,256]{1,0:T(8,128)(2,1)}, u32[]{:S(2)}) copy-start(bf16[256,256]{1,0:T(8,128)(2,1)} %enc.1) | copy-start | bytes 393220
  24.3 0.8 copy-start.5
  25.1 0.7 copy-start.6
  32.7 18.0 %all-to-all-start = ((bf16[16,64,256]{2,1,0:T(8,128)(2,1)}), bf16[16,64,256]{2,1,0:T(8,128)(2,1)S(1)}, u32[]{:S(2)}, u32[]{:S(2)}) async-start(bf16[16,64,256]{2,1,0:T(8,128)(2,1)} %bitcast.2), calls=%async_computation | async-start | bytes 1048576 | tf_op jit(solution)/shard_map/all_to_all | solution.py:380
  55.8 1.6 %collective-permute-start = (bf16[2,5,64,256]{3,2,1,0:T(8,128)(2,1)S(1)}, bf16[2,5,64,256]{3,2,1,0:T(8,128)(2,1)S(1)}, u32[]{:S(2)}, u32[]{:S(2)}) collective-permute-start(bf16[2,5,64,256]{3,2,1,0:T(8,128)(2,1)S(1)} %get-tuple-element.30), channel_id=1, source_target_pairs={{0,1},{1,0},{2,3},{3,2},{4,5},{5,4},{6,7},{7,6},{8,9},{9,8},{10,11... | collective-permute-start | bytes 983048 | tf_op jit(solution)/shard_map/ppermute | solution.py:392
  57.5 6.3 %collective-permute-start.1 = (bf16[5,64,256]{2,1,0:T(8,128)(2,1)S(1)}, bf16[5,64,256]{2,1,0:T(8,128)(2,1)S(1)}, u32[]{:S(2)}, u32[]{:S(2)}) collective-permute-start(bf16[5,64,256]{2,1,0:T(8,128)(2,1)S(1)} %get-tuple-element.34), channel_id=1, source_target_pairs={{0,2},{1,3},{2,0},{3,1},{4,6},{5,7},{6,4},{7,5},{8,10},{9,11},{10,... | collective-permute-start | bytes 491528 | tf_op jit(solution)/shard_map/ppermute | solution.py:392
  58.4 21.9 %all-to-all-start.1 = ((bf16[16,64,256]{2,1,0:T(8,128)(2,1)}), bf16[16,64,256]{2,1,0:T(8,128)(2,1)S(1)}, u32[]{:S(2)}, u32[]{:S(2)}) async-start(bf16[16,64,256]{2,1,0:T(8,128)(2,1)} %bitcast.5), calls=%async_computation.1 | async-start | bytes 1048576 | tf_op jit(solution)/shard_map/all_to_all | solution.py:380
  63.8 16.5 %copy-start.7 = (s32[1,256]{1,0:T(1,128)S(1)}, s32[1,256]{1,0:T(1,128)}, u32[]{:S(2)}) copy-start(s32[1,256]{1,0:T(1,128)} %counts.1) | copy-start | bytes 3076
  63.9 13.8 %collective-permute-start.2 = (bf16[5,64,256]{2,1,0:T(8,128)(2,1)S(1)}, bf16[5,64,256]{2,1,0:T(8,128)(2,1)S(1)}, u32[]{:S(2)}, u32[]{:S(2)}) collective-permute-start(bf16[5,64,256]{2,1,0:T(8,128)(2,1)S(1)} %shard_map.125.a), channel_id=1, source_target_pairs={{0,4},{1,5},{2,6},{3,7},{4,0},{5,1},{6,2},{7,3},{8,12},{9,13},{10,... | collective-permute-start | bytes 491528 | tf_op jit(solution)/shard_map/ppermute | solution.py:392
  77.8 10.2 %collective-permute-start.3 = (bf16[5,64,256]{2,1,0:T(8,128)(2,1)S(1)}, bf16[5,64,256]{2,1,0:T(8,128)(2,1)S(1)}, u32[]{:S(2)}, u32[]{:S(2)}) collective-permute-start(bf16[5,64,256]{2,1,0:T(8,128)(2,1)S(1)} %shard_map.126.a), channel_id=1, source_target_pairs={{0,8},{1,9},{2,10},{3,11},{4,12},{5,13},{6,14},{7,15},{8,0},{9,1},... | collective-permute-start | bytes 491528 | tf_op jit(solution)/shard_map/ppermute | solution.py:392
  88.0 6.0 %collective-permute-start.4 = (bf16[5,64,256]{2,1,0:T(8,128)(2,1)S(1)}, bf16[5,64,256]{2,1,0:T(8,128)(2,1)S(1)}, u32[]{:S(2)}, u32[]{:S(2)}) collective-permute-start(bf16[5,64,256]{2,1,0:T(8,128)(2,1)S(1)} %shard_map.128.own), channel_id=1, source_target_pairs={{0,2},{1,3},{2,0},{3,1},{4,6},{5,7},{6,4},{7,5},{8,10},{9,11},{10,... | collective-permute-start | bytes 491528 | tf_op jit(solution)/shard_map/ppermute | solution.py:392
  89.6 4.5 %collective-permute-start.5 = (bf16[5,64,256]{2,1,0:T(8,128)(2,1)S(1)}, bf16[5,64,256]{2,1,0:T(8,128)(2,1)S(1)}, u32[]{:S(2)}, u32[]{:S(2)}) collective-permute-start(bf16[5,64,256]{2,1,0:T(8,128)(2,1)S(1)} %shard_map.128.own), channel_id=1, source_target_pairs={{0,1},{1,0},{2,3},{3,2},{4,5},{5,4},{6,7},{7,6},{8,9},{9,8},{10,11... | collective-permute-start | bytes 491528 | tf_op jit(solution)/shard_map/ppermute | solution.py:392
  94.1 1.4 %collective-permute-start.6 = (bf16[5,64,256]{2,1,0:T(8,128)(2,1)S(1)}, bf16[5,64,256]{2,1,0:T(8,128)(2,1)S(1)}, u32[]{:S(2)}, u32[]{:S(2)}) collective-permute-start(bf16[5,64,256]{2,1,0:T(8,128)(2,1)S(1)} %collective-permute-done.4.beside), channel_id=1, source_target_pairs={{0,1},{1,0},{2,3},{3,2},{4,5},{5,4},{6,7},{7,6},{8,9},{9,8},{10,11... | collective-permute-start | bytes 491528 | tf_op jit(solution)/shard_map/ppermute | solution.py:392

commit v6 on v4

--- a/solution.py
+++ b/solution.py
@@ -50,17 +50,37 @@
     return jnp.concatenate(parts, axis=1)
 
 
+def running(rows, cols, strict):
+    gap = iota((rows, cols), 1) - iota((rows, cols), 0)
+    return ones_where(gap > 0 if strict else gap >= 0)
+
+
+def position_clusters(counts_row, groups):
+    clusters = counts_row.shape[1]
+    padded = jnp.broadcast_to(counts_row.astype(F32), (16, clusters)).astype(BF16)
+    ends = dot(padded, running(clusters, clusters, False))[0:1].astype(jnp.int32)
+    high = ones_where(ends // LANES == iota((groups, clusters), 0))
+    low = ones_where(ends % LANES == iota((LANES, clusters), 0))
+    marks = dot_nt(high, low).astype(BF16)
+    within = dot(marks, running(LANES, LANES, False))
+    totals = jnp.sum(marks.astype(F32), axis=1, keepdims=True)
+    wide = jnp.broadcast_to(totals, (groups, LANES)).astype(BF16)
+    before = lax.dot_general(
+        running(groups, groups, True), wide, (((0,), (0,)), ((), ())), preferred_element_type=F32
+    )
+    return within + before
+
+
 def means_kernel(
-    counts_h, members_h, raw_h, mean_out, table, counts_s, counts_v, members, raw, small_sem, raw_sem
+    counts_h, members_h, raw_h, mean_out, table, counts_v, members, raw, small_sem, raw_sem
 ):
     clusters = counts_v.shape[1]
     groups = members.shape[0]
     parts = raw_sem.shape[0]
     part = raw.shape[0] // parts
     small = [
-        pltpu.make_async_copy(counts_h, counts_s, small_sem.at[0]),
+        pltpu.make_async_copy(counts_h, counts_v, small_sem.at[0]),
         pltpu.make_async_copy(members_h, members, small_sem.at[1]),
-        pltpu.make_async_copy(counts_h, counts_v, small_sem.at[2]),
     ]
     large = [
         pltpu.make_async_copy(
@@ -70,19 +90,9 @@
     ]
     for copy in small + large:
         copy.start()
-    place = iota((groups, LANES), 0) * LANES + iota((groups, LANES), 1)
-    small[0].wait()
-
-    def body(j, carry):
-        end, cluster = carry
-        end = end + counts_s[0, j]
-        return end, cluster + jnp.where(place >= end, 1, 0)
-
-    _, cluster = lax.fori_loop(
-        0, clusters, body, (jnp.int32(0), jnp.zeros((groups, LANES), jnp.int32)), unroll=8
-    )
-    cluster = cluster.astype(F32)
-    small[1].wait()
+    for copy in small:
+        copy.wait()
+    cluster = position_clusters(counts_v[...], groups)
     rows = members[...]
     high = rows // LANES
     low = rows % LANES
@@ -98,7 +108,6 @@
             b_parts.append(ones_where(low[m : m + 1] == low_iota))
         total = total + dot_nt(jnp.concatenate(a_parts, axis=1), jnp.concatenate(b_parts, axis=1))
     table[...] = total
-    small[2].wait()
     count_column = column_of(counts_v[...].astype(F32))
     sums = jnp.zeros((clusters, raw.shape[1]), F32)
     for p in range(parts):
@@ -123,11 +132,10 @@
             jax.ShapeDtypeStruct((groups, LANES), F32),
         ],
         scratch_shapes=[
-            pltpu.SMEM((1, clusters), jnp.int32),
             pltpu.VMEM((1, clusters), jnp.int32),
             pltpu.VMEM((groups, LANES), jnp.int32),
             pltpu.VMEM((rows, width), BF16),
-            pltpu.SemaphoreType.DMA((3,)),
+            pltpu.SemaphoreType.DMA((2,)),
             pltpu.SemaphoreType.DMA((parts,)),
         ],
         compiler_params=pltpu.CompilerParams(vmem_limit_bytes=MOST_VMEM),
@@ -171,9 +179,7 @@
     )
 
 
-def targets_kernel(
-    scale, picks, queries, out_grad, weights, table, bias, query_heads, mixed_heads, members
-):
+def targets_kernel(scale, picks, queries, out_grad, weights, bias, query_heads, mixed_heads):
     query_proj = dot(queries[...], weights[0]).astype(BF16)
     query_heads[...] = spread_heads(query_proj.astype(F32) * scale)
     grad_mixed = dot_nt(out_grad[...], weights[3]).astype(BF16)
@@ -191,36 +197,24 @@
         return carry
 
     lax.fori_loop(0, bias.shape[0] // block, body, 0)
-    clusters = members.shape[1]
-    unit = ones_where(iota((clusters, clusters), 0) == iota((clusters, clusters), 1))
-
-    def turn(b, carry):
-        onehot = member_onehot(table, b * 2, clusters)
-        at = pl.multiple_of(b * 256, 256)
-        members[pl.ds(at, 256), :] = dot_tn(onehot, unit).astype(BF16)
-        return carry
-
-    lax.fori_loop(0, members.shape[0] // 256, turn, 0, unroll=4)
-
-
-def target_terms(scale, picks_t, queries, out_grad, weights, table, pooled, clusters):
+
+
+def target_terms(scale, picks_t, queries, out_grad, weights, pooled):
     targets, width = queries.shape
-    rows = table.shape[0] * LANES
     return pl.pallas_call(
         functools.partial(targets_kernel, scale),
         out_shape=[
             jax.ShapeDtypeStruct((pooled, targets), F32),
             jax.ShapeDtypeStruct((HEADS * targets, width), BF16),
             jax.ShapeDtypeStruct((HEADS * targets, width), BF16),
-            jax.ShapeDtypeStruct((rows, clusters), BF16),
-        ],
-        compiler_params=pltpu.CompilerParams(vmem_limit_bytes=MOST_VMEM),
+        ],
+        compiler_params=pltpu.CompilerParams(vmem_limit_bytes=VMEM_LIMIT),
         cost_estimate=pl.CostEstimate(
             flops=4 * targets * pooled * picks_t.shape[0],
             bytes_accessed=4 * pooled * targets,
             transcendentals=0,
         ),
-    )(picks_t, queries, out_grad, weights, table)
+    )(picks_t, queries, out_grad, weights)
 
 
 def mirrored(number, count):
@@ -233,7 +227,7 @@
 
 
 def attention_kernel(
-    scale, owners, raw, enc, weights, queries, out_grad, bias, query_heads, mixed_heads, back, grad_query, keep, send, grads
+    scale, raw, enc, weights, queries, out_grad, bias, query_heads, mixed_heads, back, grad_query, keep, send, grads
 ):
     pooled, width = raw.shape
     targets = queries.shape[0]
@@ -244,11 +238,11 @@
     key_t = dot_nt(weights[1].T, emb).astype(BF16)
     value_t = dot_nt(weights[2].T, emb).astype(BF16)
     pair_bias = jnp.concatenate([bias[...], bias[...]], axis=1)
-    head_of_row = iota((width, targets), 0) // (width // HEADS)
+    head_size = width // HEADS
+    upper = iota((2 * head_size, targets), 0) < head_size
+    mixed_parts, qproj_parts = [], []
     key_grad = jnp.zeros((pooled, width), F32)
     value_grad = jnp.zeros((pooled, width), F32)
-    mixed_t = jnp.zeros((width, targets), F32)
-    qproj_t = jnp.zeros((width, targets), F32)
     for pair in range(HEADS // 2):
         rows = slice(pair * 2 * targets, (pair + 1) * 2 * targets)
         query_pair = query_heads[rows, :]
@@ -261,13 +255,13 @@
         score_low = (weighted - attend * jnp.sum(weighted, axis=0, keepdims=True)).astype(BF16)
         value_grad = value_grad + dot(attend_low, mixed_pair)
         key_grad = key_grad + dot(score_low, query_pair)
-        mixed_both = dot(value_t, attend_low)
-        qproj_both = dot(key_t, score_low)
-        for k in range(2):
-            own = head_of_row == pair * 2 + k
-            cols = slice(k * targets, (k + 1) * targets)
-            mixed_t = jnp.where(own, mixed_both[:, cols], mixed_t)
-            qproj_t = jnp.where(own, qproj_both[:, cols], qproj_t)
+        wide = slice(pair * 2 * head_size, (pair + 1) * 2 * head_size)
+        mixed_both = dot(value_t[wide], attend_low)
+        qproj_both = dot(key_t[wide], score_low)
+        mixed_parts.append(jnp.where(upper, mixed_both[:, :targets], mixed_both[:, targets:]))
+        qproj_parts.append(jnp.where(upper, qproj_both[:, :targets], qproj_both[:, targets:]))
+    mixed_t = jnp.concatenate(mixed_parts, axis=0)
+    qproj_t = jnp.concatenate(qproj_parts, axis=0)
     grad_qproj = (qproj_t * scale).T.astype(BF16)
     grad_query[...] = dot_nt(grad_qproj, weights[0]).astype(BF16)
     key_low = key_grad.astype(BF16)
@@ -280,9 +274,9 @@
     grads[4 * width : 5 * width, :] = dot_tn(raw_pool, emb_grad)
     back[...] = emb_grad
     core = lax.axis_index("clu") % 2
-    part = width // owners
-    for q in range(owners // 2):
-        base = 2 * mirrored(q, owners // 2)
+    pieces, _, part, _ = keep.shape
+    for q in range(pieces):
+        base = 2 * mirrored(q, pieces)
         for m in range(MATRICES):
             at = m * width + base * part
             kept = pl.ds(pl.multiple_of(at + core * part, part), part)
@@ -293,9 +287,9 @@
 
 def attention(scale, owners, raw_pool, enc, weights, queries, out_grad, bias, query_heads, mixed_heads):
     pooled, width = raw_pool.shape
-    half = jax.ShapeDtypeStruct((owners // 2, MATRICES, width // owners, width), BF16)
-    return pl.pallas_call(
-        functools.partial(attention_kernel, scale, owners),
+    half = jax.ShapeDtypeStruct((owners // 4, MATRICES, 2 * width // owners, width), BF16)
+    return pl.pallas_call(
+        functools.partial(attention_kernel, scale),
         out_shape=[
             jax.ShapeDtypeStruct((pooled, width), BF16),
             jax.ShapeDtypeStruct(queries.shape, BF16),
@@ -327,46 +321,61 @@
         functools.partial(split_kernel, bit),
         out_shape=[half, half],
         compiler_params=SMALL,
-        cost_estimate=pl.CostEstimate(
-            flops=flops, bytes_accessed=4 * keep.size, transcendentals=0
-        ),
+        cost_estimate=pl.CostEstimate(flops=flops, bytes_accessed=4 * keep.size, transcendentals=0),
     )(keep, got)
 
 
-def place_kernel(masks, own, beside, own_core, beside_core, attn, enc):
-    me = lax.axis_index("clu")
-    _, matrices, part, _ = own.shape
-    for k, mask in enumerate(masks):
-        for source, flip in ((own, 0), (beside, 2), (own_core, 1), (beside_core, 3)):
-            at = pl.multiple_of((me ^ (mask ^ flip)) * part, part)
+def sum_kernel(a, b, out):
+    out[...] = add_low(a[...], b[...])
+
+
+def sum_rows(a, b):
+    return pl.pallas_call(
+        sum_kernel, out_shape=jax.ShapeDtypeStruct(a.shape, BF16), compiler_params=SMALL
+    )(a, b)
+
+
+def place_kernel(masks, *refs):
+    *sources, attn, enc = refs
+    _, matrices, part, _ = sources[0].shape
+    place_of = lax.rem(lax.axis_index("clu"), enc.shape[0] // part)
+    for source, flips in zip(sources, masks):
+        for k, flip in enumerate(flips):
+            rows = pl.ds(pl.multiple_of((place_of ^ flip) * part, part), part)
             for m in range(matrices - 1):
-                attn[m, pl.ds(at, part), :] = source[k, m].astype(F32)
-            enc[pl.ds(at, part), :] = source[k, matrices - 1].astype(F32)
-
-
-def place(masks, own, beside, own_core, beside_core):
-    width = own.shape[3]
-    return pl.pallas_call(
-        functools.partial(place_kernel, masks),
+                attn[m, rows, :] = source[k, m].astype(F32)
+            enc[rows, :] = source[k, matrices - 1].astype(F32)
+
+
+def place(pieces):
+    width = pieces[0][0].shape[3]
+    return pl.pallas_call(
+        functools.partial(place_kernel, [flips for _, flips in pieces]),
         out_shape=[
             jax.ShapeDtypeStruct((MATRICES - 1, width, width), F32),
             jax.ShapeDtypeStruct((width, width), F32),
         ],
         compiler_params=SMALL,
-    )(own, beside, own_core, beside_core)
-
-
-def rows_kernel(counts, onehot_t, back, members, out, share):
-    @pl.when(pl.program_id(0) == 0)
+    )(*[piece for piece, _ in pieces])
+
+
+def rows_kernel(counts, onehot_t, table, back, out, share):
+    step = pl.program_id(0)
+    clusters = counts.shape[1]
+
+    @pl.when(step == 0)
     def _():
         total = dot(onehot_t[...], back[...])
         share[...] = (total / column_of(counts[...].astype(F32))).astype(BF16)
 
-    out[...] = dot(members[...], share[...]).astype(BF16)
-
-
-def member_grads(counts, onehot_t, back, members):
-    rows, clusters = members.shape
+    blocks = out.shape[0] // 256
+    for k in range(blocks):
+        onehot = member_onehot(table, (step * blocks + k) * 2, clusters)
+        out[k * 256 : k * 256 + 256, :] = dot_tn(onehot, share[...]).astype(BF16)
+
+
+def member_grads(counts, onehot_t, table, back, rows):
+    clusters = counts.shape[1]
     width = back.shape[1]
     block = 1024
     return pl.pallas_call(
@@ -375,17 +384,17 @@
         in_specs=[
             pl.BlockSpec((1, clusters), lambda i: (0, 0)),
             pl.BlockSpec(onehot_t.shape, lambda i: (0, 0)),
+            pl.BlockSpec(table.shape, lambda i: (0, 0)),
             pl.BlockSpec(back.shape, lambda i: (0, 0)),
-            pl.BlockSpec((block, clusters), lambda i: (i, 0)),
         ],
         out_specs=pl.BlockSpec((block, width), lambda i: (i, 0)),
         out_shape=jax.ShapeDtypeStruct((rows, width), BF16),
         scratch_shapes=[pltpu.VMEM((clusters, width), BF16)],
-        compiler_params=pltpu.CompilerParams(vmem_limit_bytes=MOST_VMEM),
+        compiler_params=pltpu.CompilerParams(vmem_limit_bytes=VMEM_LIMIT),
         cost_estimate=pl.CostEstimate(
-            flops=2 * rows * clusters * width, bytes_accessed=4 * rows * width, transcendentals=0
+            flops=2 * rows * clusters * width, bytes_accessed=2 * rows * width, transcendentals=0
         ),
-    )(counts, onehot_t, back, members)
+    )(counts, onehot_t, table, back)
 
 
 def swap(blocks):
@@ -409,8 +418,8 @@
     means, table = cluster_means(counts, member_rows, raw_rows)
     onehot_t, sent = select_rows(got, means, pooled)
     raw_pool = swap(sent.reshape(owners, pooled // owners, width)).reshape(pooled, width)
-    bias, query_heads, mixed_heads, members = target_terms(
-        scale, picks.T, queries, out_grad, attn_weights, table, pooled, clusters
+    bias, query_heads, mixed_heads = target_terms(
+        scale, picks.T, queries, out_grad, attn_weights, pooled
     )
     back, grad_query, keep, given = attention(
         scale, owners, raw_pool, enc_weight, attn_weights, queries, out_grad, bias, query_heads, mixed_heads
@@ -420,18 +429,36 @@
     got = exchange(1, given)
     back = swap(back.reshape(owners, pooled // owners, width)).reshape(pooled, width)
     keep, given = split(2, keep, got, WEIGHT)
-    for bit in range(2, bits - 1):
+    for bit in range(2, bits - 2):
         keep, given = split(bit + 1, keep, exchange(bit, given), keep.size)
-    own = add_low(keep, exchange(bits - 1, given))
+    own = sum_rows(keep, exchange(bits - 2, given))
+    got = exchange(bits - 1, own)
+    grad_rows = member_grads(counts, onehot_t, table, back, rows)
+    got, grad_rows = lax.optimization_barrier((got, grad_rows))
+    own = sum_rows(own, got)
     masks = [0]
-    for bit in range(bits - 1, 1, -1):
+    for bit in range(bits - 2, 2, -1):
         own = jnp.concatenate([own, exchange(bit, own)])
         masks = masks + [mask ^ (1 << bit) for mask in masks]
+    deep = exchange(2, own)
     beside = exchange(1, own)
-    own_core = exchange(0, own)
-    grad_rows = member_grads(counts, onehot_t, back, members)
-    beside, own_core, grad_rows = lax.optimization_barrier((beside, own_core, grad_rows))
-    grad_attn, grad_encoder = place(masks, own, beside, own_core, exchange(0, beside))
+    deep_beside = exchange(1, deep)
+    near = exchange(0, jnp.concatenate([own, beside]))
+    far = exchange(0, jnp.concatenate([deep, deep_beside]))
+
+    def flipped(*flips):
+        return [mask ^ flip for flip in flips for mask in masks]
+
+    grad_attn, grad_encoder = place(
+        [
+            (own, flipped(0)),
+            (deep, flipped(4)),
+            (beside, flipped(2)),
+            (deep_beside, flipped(6)),
+            (near, flipped(1, 3)),
+            (far, flipped(5, 7)),
+        ]
+    )
     return grad_query, grad_rows, grad_attn, grad_encoder
 
 

time: 90.6 us -> 82.5 us (0.911)
  Pallas kernels: 30.1 us -> 21.5 us
  waiting for transfers between devices: 28.5 us -> 30 us
    all_to_all x3, waiting for transfers between devices: 5.81 us -> 10.9 us  [swap(): lax.all_to_all(blocks, 'clu', split_axis=0, concat_axis=0, tiled=True)]
    pallas_call x1, Pallas kernels: 8.62 us -> 3.87 us  [target_terms(): pl.pallas_call(functools.partial(targets_kernel, scale), out_shape=[jax.S...]
    ppermute x9, waiting for transfers between devices: 22.7 us -> 19.1 us  [exchange(): lax.ppermute(block, 'clu', [(d, d ^ 1 << bit) for d in range(owners)])]
    pallas_call x1, Pallas kernels: 7.76 us -> 5.29 us  [member_grads(): pl.pallas_call(rows_kernel, grid=(rows // block,), in_specs=[pl.BlockSpec...]
    pallas_call x1, Pallas kernels: 5.65 us -> 4.49 us  [cluster_means(): pl.pallas_call(means_kernel, in_specs=[pl.BlockSpec(memory_space=pltpu.HB...]
    pallas_call x2 -> x4, Pallas kernels: 6.6 us -> 6.41 us  [the longest x1 5.22 us: attention(): pl.pallas_call(functools.partial(attention_kernel, scale), out_shape=[jax...]
  transfers between devices with their start and end apart: 12 -> 12, of which waited for: 8 -> 8; matrix products, arithmetic and copies ran while one was open for 0% -> 0% of each run, Pallas kernels for 25% -> 17%
where the time goes in v6:
time: 82.5 us; the launch traced here: 82 us
  waiting for transfers between devices  30 us (36%)
  starting transfers between devices  26.9 us (33%)
  Pallas kernels  21.5 us (26%)
  local copies, waits for them, and re-layouts  2.81 us (3%)
    ppermute x9, waiting for transfers between devices, exchange(): lax.ppermute(block, 'clu', [(d, d ^ 1 << bit) for d in range(owners)])  19.1 us
    all_to_all x3, starting transfers between devices, swap(): lax.all_to_all(blocks, 'clu', split_axis=0, concat_axis=0, tiled=True)  17.3 us
    all_to_all x3, waiting for transfers between devices, swap(): lax.all_to_all(blocks, 'clu', split_axis=0, concat_axis=0, tiled=True)  10.9 us
    ppermute x9, starting transfers between devices, exchange(): lax.ppermute(block, 'clu', [(d, d ^ 1 << bit) for d in range(owners)])  9.57 us
    pallas_call x1, Pallas kernels, member_grads(): pl.pallas_call(rows_kernel, grid=(rows // block,), in_specs=[pl.BlockSpec...  5.29 us
    pallas_call x1, Pallas kernels, attention(): pl.pallas_call(functools.partial(attention_kernel, scale), out_shape=[jax...  5.22 us
    pallas_call x1, Pallas kernels, cluster_means(): pl.pallas_call(means_kernel, in_specs=[pl.BlockSpec(memory_space=pltpu.HB...  4.49 us
    pallas_call x1, Pallas kernels, target_terms(): pl.pallas_call(functools.partial(targets_kernel, scale), out_shape=[jax.S...  3.87 us
  transfers between devices with their start and end apart: 12, of which 8 were waited for; matrix products, arithmetic and copies ran while one was open for 0% of the time, Pallas kernels for 17%

profile of v6, /device:TPU:0, one launch (start us, length us, event | category | flops | bytes accessed | tf_op | source)
XLA Modules:
  0.0 82.0 jit_solution(940132692595895440)
XLA Ops:
  0.7 1.4 %broadcast_in_dim.10 = s32[8,2,128]{2,1,0:T(2,128)} broadcast(s32[8,128]{1,0:T(8,128)} %bitcast.14), dimensions={0,2} | broadcast | bytes 12288 | tf_op jit(solution)/shard_map/broadcast_in_dim | solution.py:416
  2.0 7.4 %all-to-all-start = ((s32[16,1,128]{2,1,0:T(1,128)}), s32[16,1,128]{2,1,0:T(1,128)S(1)}, u32[]{:S(2)}, u32[]{:S(2)}) async-start(s32[16,1,128]{2,1,0:T(1,128)} %bitcast.1), calls=%async_computation | async-start | bytes 16384 | tf_op jit(solution)/shard_map/all_to_all | solution.py:401
  9.4 0.7 copy-done.5
  10.2 0.7 copy-done.6
  10.9 4.5 %shard_map.120 = (bf16[256,256]{1,0:T(8,128)(2,1)S(1)}, f32[64,128]{1,0:T(8,128)S(1)}) custom-call(s32[1,256]{1,0:T(1,128)S(1)} %copy-done.6, s32[64,128]{1,0:T(8,128)S(1)} %bitcast.12, bf16[8192,256]{1,0:T(8,128)(2,1)} %raw_h.1), custom_call_target="tpu_custom_call" | custom-call | flops 1073741824 | bytes 4194304 | tf_op jit(solution)/shard_map/pallas_call | solution.py:127
  15.8 1.3 %shard_map.121 = (bf16[256,1024]{1,0:T(8,128)(2,1)S(1)}, bf16[1024,256]{1,0:T(8,128)(2,1)}) custom-call(s32[16,128]{1,0:T(8,128)S(1)} %bitcast.13, bf16[256,256]{1,0:T(8,128)(2,1)S(1)} %get-tuple-element.25.means), custom_call_target="tpu_custom_call" | custom-call | tf_op jit(solution)/shard_map/pallas_call | solution.py:165
  17.0 5.6 %all-to-all-start.1 = ((bf16[16,64,256]{2,1,0:T(8,128)(2,1)}), bf16[16,64,256]{2,1,0:T(8,128)(2,1)S(1)}, u32[]{:S(2)}, u32[]{:S(2)}) async-start(bf16[16,64,256]{2,1,0:T(8,128)(2,1)} %bitcast.4), calls=%async_computation.1 | async-start | bytes 1048576 | tf_op jit(solution)/shard_map/all_to_all | solution.py:401
  22.7 3.9 %shard_map.122 = (f32[1024,128]{1,0:T(8,128)S(1)}, bf16[512,256]{1,0:T(8,128)(2,1)S(1)}, bf16[512,256]{1,0:T(8,128)(2,1)S(1)}) custom-call(s32[100,128]{1,0:T(8,128)S(1)} %bitcast.11, bf16[128,256]{1,0:T(8,128)(2,1)S(1)} %copy-done.1, bf16[128,256]{1,0:T(8,128)(2,1)S(1)} %copy-done.2, bf16[4,256,256]{2,1,0:T(8,128)(2,1)S(1)} %copy-done), custom_call_target="tpu_custom_call" | custom-call | flops 52428800 | bytes 524288 | tf_op jit(solution)/shard_map/pallas_call | solution.py:204
  26.6 10.6 %all-to-all-done.1 = bf16[16,64,256]{2,1,0:T(8,128)(2,1)S(1)} async-done(((bf16[16,64,256]{2,1,0:T(8,128)(2,1)}), bf16[16,64,256]{2,1,0:T(8,128)(2,1)S(1)}, u32[]{:S(2)}, u32[]{:S(2)}) %all-to-all-start.1) | async-done | bytes 524320 | tf_op jit(solution)/shard_map/all_to_all | solution.py:401
  37.1 5.2 %shard_map.123 = (bf16[1024,256]{1,0:T(8,128)(2,1)}, bf16[128,256]{1,0:T(8,128)(2,1)}, bf16[4,5,32,256]{3,2,1,0:T(8,128)(2,1)S(1)}, bf16[4,5,32,256]{3,2,1,0:T(8,128)(2,1)S(1)}) custom-call(bf16[1024,256]{1,0:T(8,128)(2,1)S(1)} %bitcast.10, bf16[256,256]{1,0:T(8,128)(2,1)S(1)} %copy-done.3, bf16[4,256,256]{2,1,0:T(8,128)(2,1)S(1)} %copy-done, ...), custom_call_target="tpu_custom_call" | custom-call | tf_op jit(solution)/shard_map/pallas_call | solution.py:291
  42.4 1.6 %collective-permute-done.got = bf16[4,5,32,256]{3,2,1,0:T(8,128)(2,1)S(1)} collective-permute-done((bf16[4,5,32,256]{3,2,1,0:T(8,128)(2,1)S(1)}, bf16[4,5,32,256]{3,2,1,0:T(8,128)(2,1)S(1)}, u32[]{:S(2)}, u32[]{:S(2)}) %collective-permute-start) | collective-permute-done | bytes 327712 | tf_op jit(solution)/shard_map/ppermute | solution.py:413
  44.1 0.9 %collective-permute-start.1 = (bf16[2,5,32,256]{3,2,1,0:T(8,128)(2,1)S(1)}, bf16[2,5,32,256]{3,2,1,0:T(8,128)(2,1)S(1)}, u32[]{:S(2)}, u32[]{:S(2)}) collective-permute-start(bf16[2,5,32,256]{3,2,1,0:T(8,128)(2,1)S(1)} %get-tuple-element.36), channel_id=1, source_target_pairs={{0,2},{1,3},{2,0},{3,1},{4,6},{5,7},{6,4},{7,5},{8,10},{9,11},{10,... | collective-permute-start | bytes 491528 | tf_op jit(solution)/shard_map/ppermute | solution.py:413
  44.9 4.3 %all-to-all-start.2 = ((bf16[16,64,256]{2,1,0:T(8,128)(2,1)}), bf16[16,64,256]{2,1,0:T(8,128)(2,1)S(1)}, u32[]{:S(2)}, u32[]{:S(2)}) async-start(bf16[16,64,256]{2,1,0:T(8,128)(2,1)} %bitcast.7), calls=%async_computation.2 | async-start | bytes 1048576 | tf_op jit(solution)/shard_map/all_to_all | solution.py:401
  49.2 1.1 %collective-permute-done.1.got = bf16[2,5,32,256]{3,2,1,0:T(8,128)(2,1)S(1)} collective-permute-done((bf16[2,5,32,256]{3,2,1,0:T(8,128)(2,1)S(1)}, bf16[2,5,32,256]{3,2,1,0:T(8,128)(2,1)S(1)}, u32[]{:S(2)}, u32[]{:S(2)}) %collective-permute-start.1) | collective-permute-done | bytes 163872 | tf_op jit(solution)/shard_map/ppermute | solution.py:413
  50.4 1.7 %collective-permute-start.2 = (bf16[1,5,32,256]{3,2,1,0:T(8,128)(2,1)S(1)}, bf16[1,5,32,256]{3,2,1,0:T(8,128)(2,1)S(1)}, u32[]{:S(2)}, u32[]{:S(2)}) collective-permute-start(bf16[1,5,32,256]{3,2,1,0:T(8,128)(2,1)S(1)} %get-tuple-element.38), channel_id=1, source_target_pairs={{0,4},{1,5},{2,6},{3,7},{4,0},{5,1},{6,2},{7,3},{8,12},{9,13},{10,... | collective-permute-start | bytes 245768 | tf_op jit(solution)/shard_map/ppermute | solution.py:413
  52.1 9.2 %collective-permute-done.2.b = bf16[1,5,32,256]{3,2,1,0:T(8,128)(2,1)S(1)} collective-permute-done((bf16[1,5,32,256]{3,2,1,0:T(8,128)(2,1)S(1)}, bf16[1,5,32,256]{3,2,1,0:T(8,128)(2,1)S(1)}, u32[]{:S(2)}, u32[]{:S(2)}) %collective-permute-start.2) | collective-permute-done | bytes 81952 | tf_op jit(solution)/shard_map/ppermute | solution.py:413
  61.3 3.8 %collective-permute-start.3 = (bf16[1,5,32,256]{3,2,1,0:T(8,128)(2,1)S(1)}, bf16[1,5,32,256]{3,2,1,0:T(8,128)(2,1)S(1)}, u32[]{:S(2)}, u32[]{:S(2)}) collective-permute-start(bf16[1,5,32,256]{3,2,1,0:T(8,128)(2,1)S(1)} %shard_map.126.a), channel_id=1, source_target_pairs={{0,8},{1,9},{2,10},{3,11},{4,12},{5,13},{6,14},{7,15},{8,0},{9,1},... | collective-permute-start | bytes 245768 | tf_op jit(solution)/shard_map/ppermute | solution.py:413
  65.1 5.3 %shard_map.127 = bf16[8192,256]{1,0:T(8,128)(2,1)} custom-call(s32[1,256]{1,0:T(1,128)S(1)} %copy-done.7, bf16[256,1024]{1,0:T(8,128)(2,1)S(1)} %get-tuple-element.39.onehot_t, f32[64,128]{1,0:T(8,128)S(1)} %get-tuple-element.40.table, bf16[1024,256]{1,0:T(8,128)(2,1)S(1)} %bitcast.9), custom_call_target="tpu_custom_call" | custom-call | flops 1073741824 | bytes 4194304 | tf_op jit(solution)/shard_map/pallas_call | solution.py:381
  70.5 1.5 %collective-permute-start.5 = (bf16[1,5,32,256]{3,2,1,0:T(8,128)(2,1)S(1)}, bf16[1,5,32,256]{3,2,1,0:T(8,128)(2,1)S(1)}, u32[]{:S(2)}, u32[]{:S(2)}) collective-permute-start(bf16[1,5,32,256]{3,2,1,0:T(8,128)(2,1)S(1)} %shard_map.128.refs_0_), channel_id=1, source_target_pairs={{0,2},{1,3},{2,0},{3,1},{4,6},{5,7},{6,4},{7,5},{8,10},{9,11},{10,... | collective-permute-start | bytes 245768 | tf_op jit(solution)/shard_map/ppermute | solution.py:413
  72.1 2.9 %collective-permute-done.4.refs_1_ = bf16[1,5,32,256]{3,2,1,0:T(8,128)(2,1)S(1)} collective-permute-done((bf16[1,5,32,256]{3,2,1,0:T(8,128)(2,1)S(1)}, bf16[1,5,32,256]{3,2,1,0:T(8,128)(2,1)S(1)}, u32[]{:S(2)}, u32[]{:S(2)}) %collective-permute-start.4) | collective-permute-done | bytes 81952 | tf_op jit(solution)/shard_map/ppermute | solution.py:413
  75.0 1.5 %collective-permute-start.6 = (bf16[1,5,32,256]{3,2,1,0:T(8,128)(2,1)S(1)}, bf16[1,5,32,256]{3,2,1,0:T(8,128)(2,1)S(1)}, u32[]{:S(2)}, u32[]{:S(2)}) collective-permute-start(bf16[1,5,32,256]{3,2,1,0:T(8,128)(2,1)S(1)} %collective-permute-done.4.refs_1_), channel_id=1, source_target_pairs={{0,2},{1,3},{2,0},{3,1},{4,6},{5,7},{6,4},{7,5},{8,10},{9,11},{10,... | collective-permute-start | bytes 245768 | tf_op jit(solution)/shard_map/ppermute | solution.py:413
  76.5 2.9 %collective-permute-done.6.refs_3_ = bf16[1,5,32,256]{3,2,1,0:T(8,128)(2,1)S(1)} collective-permute-done((bf16[1,5,32,256]{3,2,1,0:T(8,128)(2,1)S(1)}, bf16[1,5,32,256]{3,2,1,0:T(8,128)(2,1)S(1)}, u32[]{:S(2)}, u32[]{:S(2)}) %collective-permute-start.6) | collective-permute-done | bytes 81952 | tf_op jit(solution)/shard_map/ppermute | solution.py:413
  79.5 1.4 %collective-permute-done.8.refs_5_ = bf16[2,5,32,256]{3,2,1,0:T(8,128)(2,1)S(1)} collective-permute-done((bf16[2,5,32,256]{3,2,1,0:T(8,128)(2,1)S(1)}, bf16[2,5,32,256]{3,2,1,0:T(8,128)(2,1)S(1)}, u32[]{:S(2)}, u32[]{:S(2)}) %collective-permute-start.8) | collective-permute-done | bytes 163872 | tf_op jit(solution)/shard_map/ppermute | solution.py:413
  80.9 1.1 %shard_map.129 = (f32[4,256,256]{2,1,0:T(8,128)}, f32[256,256]{1,0:T(8,128)}) custom-call(bf16[1,5,32,256]{3,2,1,0:T(8,128)(2,1)S(1)} %shard_map.128.refs_0_, bf16[1,5,32,256]{3,2,1,0:T(8,128)(2,1)S(1)} %collective-permute-done.4.refs_1_, bf16[1,5,32,256]{3,2,1,0:T(8,128)(2,1)S(1)} %collective-permute-done.5.refs_2_, ...), custom_call_target="tpu_custom_call" | custom-call | tf_op jit(solution)/shard_map/pallas_call | solution.py:352
  (29 shorter events, 0.9 us)
Async XLA Ops:
  0.6 22.0 %copy-start.2 = (bf16[128,256]{1,0:T(8,128)(2,1)S(1)}, bf16[128,256]{1,0:T(8,128)(2,1)}, u32[]{:S(2)}) copy-start(bf16[128,256]{1,0:T(8,128)(2,1)} %out_grad.3) | copy-start | bytes 196612
  0.6 22.0 %copy-start = (bf16[4,256,256]{2,1,0:T(8,128)(2,1)S(1)}, bf16[4,256,256]{2,1,0:T(8,128)(2,1)}, u32[]{:S(2)}) copy-start(bf16[4,256,256]{2,1,0:T(8,128)(2,1)} %weights.3) | copy-start | bytes 1572868
  0.7 22.0 %copy-start.1 = (bf16[128,256]{1,0:T(8,128)(2,1)S(1)}, bf16[128,256]{1,0:T(8,128)(2,1)}, u32[]{:S(2)}) copy-start(bf16[128,256]{1,0:T(8,128)(2,1)} %queries.3) | copy-start | bytes 196612
  0.7 22.0 %copy-start.4 = (s32[128,100]{0,1:T(8,128)S(1)}, s32[128,100]{0,1:T(8,128)}, u32[]{:S(2)}) copy-start(s32[128,100]{0,1:T(8,128)} %param.14) | copy-start | bytes 153604
  0.7 36.5 %copy-start.3 = (bf16[256,256]{1,0:T(8,128)(2,1)S(1)}, bf16[256,256]{1,0:T(8,128)(2,1)}, u32[]{:S(2)}) copy-start(bf16[256,256]{1,0:T(8,128)(2,1)} %enc.1) | copy-start | bytes 393220
  2.0 13.7 %all-to-all-start = ((s32[16,1,128]{2,1,0:T(1,128)}), s32[16,1,128]{2,1,0:T(1,128)S(1)}, u32[]{:S(2)}, u32[]{:S(2)}) async-start(s32[16,1,128]{2,1,0:T(1,128)} %bitcast.1), calls=%async_computation | async-start | bytes 16384 | tf_op jit(solution)/shard_map/all_to_all | solution.py:401
  9.4 0.8 copy-start.5
  10.2 0.7 copy-start.6
  17.0 20.1 %all-to-all-start.1 = ((bf16[16,64,256]{2,1,0:T(8,128)(2,1)}), bf16[16,64,256]{2,1,0:T(8,128)(2,1)S(1)}, u32[]{:S(2)}, u32[]{:S(2)}) async-start(bf16[16,64,256]{2,1,0:T(8,128)(2,1)} %bitcast.4), calls=%async_computation.1 | async-start | bytes 1048576 | tf_op jit(solution)/shard_map/all_to_all | solution.py:401
  42.4 1.6 %collective-permute-start = (bf16[4,5,32,256]{3,2,1,0:T(8,128)(2,1)S(1)}, bf16[4,5,32,256]{3,2,1,0:T(8,128)(2,1)S(1)}, u32[]{:S(2)}, u32[]{:S(2)}) collective-permute-start(bf16[4,5,32,256]{3,2,1,0:T(8,128)(2,1)S(1)} %get-tuple-element.32), channel_id=1, source_target_pairs={{0,1},{1,0},{2,3},{3,2},{4,5},{5,4},{6,7},{7,6},{8,9},{9,8},{10,11... | collective-permute-start | bytes 983048 | tf_op jit(solution)/shard_map/ppermute | solution.py:413
  44.1 6.3 %collective-permute-start.1 = (bf16[2,5,32,256]{3,2,1,0:T(8,128)(2,1)S(1)}, bf16[2,5,32,256]{3,2,1,0:T(8,128)(2,1)S(1)}, u32[]{:S(2)}, u32[]{:S(2)}) collective-permute-start(bf16[2,5,32,256]{3,2,1,0:T(8,128)(2,1)S(1)} %get-tuple-element.36), channel_id=1, source_target_pairs={{0,2},{1,3},{2,0},{3,1},{4,6},{5,7},{6,4},{7,5},{8,10},{9,11},{10,... | collective-permute-start | bytes 491528 | tf_op jit(solution)/shard_map/ppermute | solution.py:413
  44.9 20.2 %all-to-all-start.2 = ((bf16[16,64,256]{2,1,0:T(8,128)(2,1)}), bf16[16,64,256]{2,1,0:T(8,128)(2,1)S(1)}, u32[]{:S(2)}, u32[]{:S(2)}) async-start(bf16[16,64,256]{2,1,0:T(8,128)(2,1)} %bitcast.7), calls=%async_computation.2 | async-start | bytes 1048576 | tf_op jit(solution)/shard_map/all_to_all | solution.py:401
  50.4 14.7 %copy-start.7 = (s32[1,256]{1,0:T(1,128)S(1)}, s32[1,256]{1,0:T(1,128)}, u32[]{:S(2)}) copy-start(s32[1,256]{1,0:T(1,128)} %counts.1) | copy-start | bytes 3076
  50.4 10.9 %collective-permute-start.2 = (bf16[1,5,32,256]{3,2,1,0:T(8,128)(2,1)S(1)}, bf16[1,5,32,256]{3,2,1,0:T(8,128)(2,1)S(1)}, u32[]{:S(2)}, u32[]{:S(2)}) collective-permute-start(bf16[1,5,32,256]{3,2,1,0:T(8,128)(2,1)S(1)} %get-tuple-element.38), channel_id=1, source_target_pairs={{0,4},{1,5},{2,6},{3,7},{4,0},{5,1},{6,2},{7,3},{8,12},{9,13},{10,... | collective-permute-start | bytes 245768 | tf_op jit(solution)/shard_map/ppermute | solution.py:413
  61.3 9.1 %collective-permute-start.3 = (bf16[1,5,32,256]{3,2,1,0:T(8,128)(2,1)S(1)}, bf16[1,5,32,256]{3,2,1,0:T(8,128)(2,1)S(1)}, u32[]{:S(2)}, u32[]{:S(2)}) collective-permute-start(bf16[1,5,32,256]{3,2,1,0:T(8,128)(2,1)S(1)} %shard_map.126.a), channel_id=1, source_target_pairs={{0,8},{1,9},{2,10},{3,11},{4,12},{5,13},{6,14},{7,15},{8,0},{9,1},... | collective-permute-start | bytes 245768 | tf_op jit(solution)/shard_map/ppermute | solution.py:413
  70.4 4.5 %collective-permute-start.4 = (bf16[1,5,32,256]{3,2,1,0:T(8,128)(2,1)S(1)}, bf16[1,5,32,256]{3,2,1,0:T(8,128)(2,1)S(1)}, u32[]{:S(2)}, u32[]{:S(2)}) collective-permute-start(bf16[1,5,32,256]{3,2,1,0:T(8,128)(2,1)S(1)} %shard_map.128.refs_0_), channel_id=1, source_target_pairs={{0,4},{1,5},{2,6},{3,7},{4,0},{5,1},{6,2},{7,3},{8,12},{9,13},{10,... | collective-permute-start | bytes 245768 | tf_op jit(solution)/shard_map/ppermute | solution.py:413
  70.5 5.9 %collective-permute-start.5 = (bf16[1,5,32,256]{3,2,1,0:T(8,128)(2,1)S(1)}, bf16[1,5,32,256]{3,2,1,0:T(8,128)(2,1)S(1)}, u32[]{:S(2)}, u32[]{:S(2)}) collective-permute-start(bf16[1,5,32,256]{3,2,1,0:T(8,128)(2,1)S(1)} %shard_map.128.refs_0_), channel_id=1, source_target_pairs={{0,2},{1,3},{2,0},{3,1},{4,6},{5,7},{6,4},{7,5},{8,10},{9,11},{10,... | collective-permute-start | bytes 245768 | tf_op jit(solution)/shard_map/ppermute | solution.py:413
  75.0 4.4 %collective-permute-start.6 = (bf16[1,5,32,256]{3,2,1,0:T(8,128)(2,1)S(1)}, bf16[1,5,32,256]{3,2,1,0:T(8,128)(2,1)S(1)}, u32[]{:S(2)}, u32[]{:S(2)}) collective-permute-start(bf16[1,5,32,256]{3,2,1,0:T(8,128)(2,1)S(1)} %collective-permute-done.4.refs_1_), channel_id=1, source_target_pairs={{0,2},{1,3},{2,0},{3,1},{4,6},{5,7},{6,4},{7,5},{8,10},{9,11},{10,... | collective-permute-start | bytes 245768 | tf_op jit(solution)/shard_map/ppermute | solution.py:413
  76.4 3.1 %collective-permute-start.7 = (bf16[2,5,32,256]{3,2,1,0:T(8,128)(2,1)S(1)}, bf16[2,5,32,256]{3,2,1,0:T(8,128)(2,1)S(1)}, u32[]{:S(2)}, u32[]{:S(2)}) collective-permute-start(bf16[2,5,32,256]{3,2,1,0:T(8,128)(2,1)S(1)} %pad_maximum_fusion), channel_id=1, source_target_pairs={{0,1},{1,0},{2,3},{3,2},{4,5},{5,4},{6,7},{7,6},{8,9},{9,8},{10,11... | collective-permute-start | bytes 491528 | tf_op jit(solution)/shard_map/ppermute | solution.py:413
  79.4 1.5 %collective-permute-start.8 = (bf16[2,5,32,256]{3,2,1,0:T(8,128)(2,1)S(1)}, bf16[2,5,32,256]{3,2,1,0:T(8,128)(2,1)S(1)}, u32[]{:S(2)}, u32[]{:S(2)}) collective-permute-start(bf16[2,5,32,256]{3,2,1,0:T(8,128)(2,1)S(1)} %pad_maximum_fusion.1), channel_id=1, source_target_pairs={{0,1},{1,0},{2,3},{3,2},{4,5},{5,4},{6,7},{7,6},{8,9},{9,8},{10,11... | collective-permute-start | bytes 491528 | tf_op jit(solution)/shard_map/ppermute | solution.py:413

commit v7 on v6

--- a/solution.py
+++ b/solution.py
@@ -359,37 +359,43 @@
     )(*[piece for piece, _ in pieces])
 
 
-def rows_kernel(counts, onehot_t, table, back, out, share):
-    step = pl.program_id(0)
+def rows_kernel(counts, onehot_t, table, back, out, share, filled, sem):
     clusters = counts.shape[1]
-
-    @pl.when(step == 0)
-    def _():
-        total = dot(onehot_t[...], back[...])
-        share[...] = (total / column_of(counts[...].astype(F32))).astype(BF16)
+    total = dot(onehot_t[...], back[...])
+    share[...] = (total / column_of(counts[...].astype(F32))).astype(BF16)
+
+    def block(k):
+        rows = pl.ds(pl.multiple_of(k * 256, 256), 256)
+        return pltpu.make_async_copy(filled.at[rows], out.at[rows], sem.at[k])
+
+    def fill(k, carry):
+        onehot = member_onehot(table, k * 2, clusters)
+        rows = pl.ds(pl.multiple_of(k * 256, 256), 256)
+        filled[rows, :] = dot_tn(onehot, share[...]).astype(BF16)
+        block(k).start()
+        return carry
+
+    def finish(k, carry):
+        block(k).wait()
+        return carry
 
     blocks = out.shape[0] // 256
-    for k in range(blocks):
-        onehot = member_onehot(table, (step * blocks + k) * 2, clusters)
-        out[k * 256 : k * 256 + 256, :] = dot_tn(onehot, share[...]).astype(BF16)
+    lax.fori_loop(0, blocks, fill, 0, unroll=4)
+    lax.fori_loop(0, blocks, finish, 0)
 
 
 def member_grads(counts, onehot_t, table, back, rows):
     clusters = counts.shape[1]
     width = back.shape[1]
-    block = 1024
     return pl.pallas_call(
         rows_kernel,
-        grid=(rows // block,),
-        in_specs=[
-            pl.BlockSpec((1, clusters), lambda i: (0, 0)),
-            pl.BlockSpec(onehot_t.shape, lambda i: (0, 0)),
-            pl.BlockSpec(table.shape, lambda i: (0, 0)),
-            pl.BlockSpec(back.shape, lambda i: (0, 0)),
-        ],
-        out_specs=pl.BlockSpec((block, width), lambda i: (i, 0)),
+        out_specs=pl.BlockSpec(memory_space=pltpu.HBM),
         out_shape=jax.ShapeDtypeStruct((rows, width), BF16),
-        scratch_shapes=[pltpu.VMEM((clusters, width), BF16)],
+        scratch_shapes=[
+            pltpu.VMEM((clusters, width), BF16),
+            pltpu.VMEM((rows, width), BF16),
+            pltpu.SemaphoreType.DMA((rows // 256,)),
+        ],
         compiler_params=pltpu.CompilerParams(vmem_limit_bytes=VMEM_LIMIT),
         cost_estimate=pl.CostEstimate(
             flops=2 * rows * clusters * width, bytes_accessed=2 * rows * width, transcendentals=0
@@ -409,8 +415,8 @@
     scale = (width // HEADS) ** -0.5
     bits = owners.bit_length() - 1
 
-    def exchange(bit, block):
-        return lax.ppermute(block, "clu", [(d, d ^ (1 << bit)) for d in range(owners)])
+    def exchange(flip, block):
+        return lax.ppermute(block, "clu", [(d, d ^ flip) for d in range(owners)])
 
     pairs = pool.reshape(owners // 2, 1, 1, LANES)
     asking = jnp.broadcast_to(pairs, (owners // 2, 2, 1, LANES)).reshape(owners, 1, LANES)
@@ -424,41 +430,26 @@
     back, grad_query, keep, given = attention(
         scale, owners, raw_pool, enc_weight, attn_weights, queries, out_grad, bias, query_heads, mixed_heads
     )
-    keep, given = split(1, keep, exchange(0, given), keep.size)
+    keep, given = split(1, keep, exchange(1, given), keep.size)
     given, back = lax.optimization_barrier((given, back))
-    got = exchange(1, given)
+    got = exchange(2, given)
     back = swap(back.reshape(owners, pooled // owners, width)).reshape(pooled, width)
     keep, given = split(2, keep, got, WEIGHT)
     for bit in range(2, bits - 2):
-        keep, given = split(bit + 1, keep, exchange(bit, given), keep.size)
-    own = sum_rows(keep, exchange(bits - 2, given))
-    got = exchange(bits - 1, own)
+        keep, given = split(bit + 1, keep, exchange(1 << bit, given), keep.size)
+    own = sum_rows(keep, exchange(owners // 4, given))
+    got = exchange(owners // 2, own)
     grad_rows = member_grads(counts, onehot_t, table, back, rows)
     got, grad_rows = lax.optimization_barrier((got, grad_rows))
     own = sum_rows(own, got)
     masks = [0]
     for bit in range(bits - 2, 2, -1):
-        own = jnp.concatenate([own, exchange(bit, own)])
+        own = jnp.concatenate([own, exchange(1 << bit, own)])
         masks = masks + [mask ^ (1 << bit) for mask in masks]
-    deep = exchange(2, own)
-    beside = exchange(1, own)
-    deep_beside = exchange(1, deep)
-    near = exchange(0, jnp.concatenate([own, beside]))
-    far = exchange(0, jnp.concatenate([deep, deep_beside]))
-
-    def flipped(*flips):
-        return [mask ^ flip for flip in flips for mask in masks]
-
-    grad_attn, grad_encoder = place(
-        [
-            (own, flipped(0)),
-            (deep, flipped(4)),
-            (beside, flipped(2)),
-            (deep_beside, flipped(6)),
-            (near, flipped(1, 3)),
-            (far, flipped(5, 7)),
-        ]
-    )
+    chip = jnp.concatenate([own] + [exchange(flip, own) for flip in (4, 2, 6)])
+    masks = [mask ^ flip for flip in (0, 4, 2, 6) for mask in masks]
+    beside = exchange(1, chip)
+    grad_attn, grad_encoder = place([(chip, masks), (beside, [mask ^ 1 for mask in masks])])
     return grad_query, grad_rows, grad_attn, grad_encoder
 
 

time: 82.5 us -> 79.4 us (0.962)
  waiting for transfers between devices: 30 us -> 27.7 us
  Pallas kernels: 21.5 us -> 20.3 us
    ppermute x9 -> x8, waiting for transfers between devices: 19.1 us -> 16.8 us  [exchange(): return lax.ppermute(block, 'clu', [(d, d ^ flip) for d in range(owners)])]
    pallas_call x1, Pallas kernels: 5.29 us -> 4.08 us  [member_grads(): pl.pallas_call(rows_kernel, out_specs=pl.BlockSpec(memory_space=pltpu.HBM...]
    ppermute x9 -> x8, starting transfers between devices: 9.57 us -> 9.99 us  [exchange(): return lax.ppermute(block, 'clu', [(d, d ^ flip) for d in range(owners)])]
  transfers between devices with their start and end apart: 12 -> 11, of which waited for: 8 -> 9; matrix products, arithmetic and copies ran while one was open for 0% -> 0% of each run, Pallas kernels for 17% -> 16%
where the time goes in v7:
time: 79.4 us; the launch traced here: 78.9 us
  waiting for transfers between devices  27.7 us (35%)
  starting transfers between devices  27.3 us (34%)
  Pallas kernels  20.3 us (26%)
  local copies, waits for them, and re-layouts  2.81 us (4%)
  between operations  0.81 us (1%)
    all_to_all x3, starting transfers between devices, swap(): lax.all_to_all(blocks, 'clu', split_axis=0, concat_axis=0, tiled=True)  17.3 us
    ppermute x8, waiting for transfers between devices, exchange(): return lax.ppermute(block, 'clu', [(d, d ^ flip) for d in range(owners)])  16.8 us
    all_to_all x3, waiting for transfers between devices, swap(): lax.all_to_all(blocks, 'clu', split_axis=0, concat_axis=0, tiled=True)  10.9 us
    ppermute x8, starting transfers between devices, exchange(): return lax.ppermute(block, 'clu', [(d, d ^ flip) for d in range(owners)])  9.99 us
    pallas_call x1, Pallas kernels, attention(): pl.pallas_call(functools.partial(attention_kernel, scale), out_shape=[jax...  5.22 us
    pallas_call x1, Pallas kernels, cluster_means(): pl.pallas_call(means_kernel, in_specs=[pl.BlockSpec(memory_space=pltpu.HB...  4.49 us
    pallas_call x1, Pallas kernels, member_grads(): pl.pallas_call(rows_kernel, out_specs=pl.BlockSpec(memory_space=pltpu.HBM...  4.08 us
    pallas_call x1, Pallas kernels, target_terms(): pl.pallas_call(functools.partial(targets_kernel, scale), out_shape=[jax.S...  3.87 us
  transfers between devices with their start and end apart: 11, of which 9 were waited for; matrix products, arithmetic and copies ran while one was open for 0% of the time, Pallas kernels for 16%

profile of v7, /device:TPU:0, one launch (start us, length us, event | category | flops | bytes accessed | tf_op | source)
XLA Modules:
  0.0 78.9 jit_solution(3598473387165515956)
XLA Ops:
  0.7 1.4 %broadcast_in_dim.10 = s32[8,2,128]{2,1,0:T(2,128)} broadcast(s32[8,128]{1,0:T(8,128)} %bitcast.14), dimensions={0,2} | broadcast | bytes 12288 | tf_op jit(solution)/shard_map/broadcast_in_dim | solution.py:422
  2.0 7.4 %all-to-all-start = ((s32[16,1,128]{2,1,0:T(1,128)}), s32[16,1,128]{2,1,0:T(1,128)S(1)}, u32[]{:S(2)}, u32[]{:S(2)}) async-start(s32[16,1,128]{2,1,0:T(1,128)} %bitcast.1), calls=%async_computation | async-start | bytes 16384 | tf_op jit(solution)/shard_map/all_to_all | solution.py:407
  9.4 0.7 copy-done.5
  10.2 0.7 copy-done.6
  10.9 4.5 %shard_map.120 = (bf16[256,256]{1,0:T(8,128)(2,1)S(1)}, f32[64,128]{1,0:T(8,128)S(1)}) custom-call(s32[1,256]{1,0:T(1,128)S(1)} %copy-done.6, s32[64,128]{1,0:T(8,128)S(1)} %bitcast.12, bf16[8192,256]{1,0:T(8,128)(2,1)} %raw_h.1), custom_call_target="tpu_custom_call" | custom-call | flops 1073741824 | bytes 4194304 | tf_op jit(solution)/shard_map/pallas_call | solution.py:127
  15.8 1.3 %shard_map.121 = (bf16[256,1024]{1,0:T(8,128)(2,1)S(1)}, bf16[1024,256]{1,0:T(8,128)(2,1)}) custom-call(s32[16,128]{1,0:T(8,128)S(1)} %bitcast.13, bf16[256,256]{1,0:T(8,128)(2,1)S(1)} %get-tuple-element.25.means), custom_call_target="tpu_custom_call" | custom-call | tf_op jit(solution)/shard_map/pallas_call | solution.py:165
  17.0 5.6 %all-to-all-start.1 = ((bf16[16,64,256]{2,1,0:T(8,128)(2,1)}), bf16[16,64,256]{2,1,0:T(8,128)(2,1)S(1)}, u32[]{:S(2)}, u32[]{:S(2)}) async-start(bf16[16,64,256]{2,1,0:T(8,128)(2,1)} %bitcast.4), calls=%async_computation.1 | async-start | bytes 1048576 | tf_op jit(solution)/shard_map/all_to_all | solution.py:407
  22.7 3.9 %shard_map.122 = (f32[1024,128]{1,0:T(8,128)S(1)}, bf16[512,256]{1,0:T(8,128)(2,1)S(1)}, bf16[512,256]{1,0:T(8,128)(2,1)S(1)}) custom-call(s32[100,128]{1,0:T(8,128)S(1)} %bitcast.11, bf16[128,256]{1,0:T(8,128)(2,1)S(1)} %copy-done.1, bf16[128,256]{1,0:T(8,128)(2,1)S(1)} %copy-done.2, bf16[4,256,256]{2,1,0:T(8,128)(2,1)S(1)} %copy-done), custom_call_target="tpu_custom_call" | custom-call | flops 52428800 | bytes 524288 | tf_op jit(solution)/shard_map/pallas_call | solution.py:204
  26.6 10.6 %all-to-all-done.1 = bf16[16,64,256]{2,1,0:T(8,128)(2,1)S(1)} async-done(((bf16[16,64,256]{2,1,0:T(8,128)(2,1)}), bf16[16,64,256]{2,1,0:T(8,128)(2,1)S(1)}, u32[]{:S(2)}, u32[]{:S(2)}) %all-to-all-start.1) | async-done | bytes 524320 | tf_op jit(solution)/shard_map/all_to_all | solution.py:407
  37.1 5.2 %shard_map.123 = (bf16[1024,256]{1,0:T(8,128)(2,1)}, bf16[128,256]{1,0:T(8,128)(2,1)}, bf16[4,5,32,256]{3,2,1,0:T(8,128)(2,1)S(1)}, bf16[4,5,32,256]{3,2,1,0:T(8,128)(2,1)S(1)}) custom-call(bf16[1024,256]{1,0:T(8,128)(2,1)S(1)} %bitcast.10, bf16[256,256]{1,0:T(8,128)(2,1)S(1)} %copy-done.3, bf16[4,256,256]{2,1,0:T(8,128)(2,1)S(1)} %copy-done, ...), custom_call_target="tpu_custom_call" | custom-call | tf_op jit(solution)/shard_map/pallas_call | solution.py:291
  42.4 1.6 %collective-permute-done.got = bf16[4,5,32,256]{3,2,1,0:T(8,128)(2,1)S(1)} collective-permute-done((bf16[4,5,32,256]{3,2,1,0:T(8,128)(2,1)S(1)}, bf16[4,5,32,256]{3,2,1,0:T(8,128)(2,1)S(1)}, u32[]{:S(2)}, u32[]{:S(2)}) %collective-permute-start) | collective-permute-done | bytes 327712 | tf_op jit(solution)/shard_map/ppermute | solution.py:419
  44.1 0.9 %collective-permute-start.1 = (bf16[2,5,32,256]{3,2,1,0:T(8,128)(2,1)S(1)}, bf16[2,5,32,256]{3,2,1,0:T(8,128)(2,1)S(1)}, u32[]{:S(2)}, u32[]{:S(2)}) collective-permute-start(bf16[2,5,32,256]{3,2,1,0:T(8,128)(2,1)S(1)} %get-tuple-element.36), channel_id=1, source_target_pairs={{0,2},{1,3},{2,0},{3,1},{4,6},{5,7},{6,4},{7,5},{8,10},{9,11},{10,... | collective-permute-start | bytes 491528 | tf_op jit(solution)/shard_map/ppermute | solution.py:419
  44.9 4.3 %all-to-all-start.2 = ((bf16[16,64,256]{2,1,0:T(8,128)(2,1)}), bf16[16,64,256]{2,1,0:T(8,128)(2,1)S(1)}, u32[]{:S(2)}, u32[]{:S(2)}) async-start(bf16[16,64,256]{2,1,0:T(8,128)(2,1)} %bitcast.7), calls=%async_computation.2 | async-start | bytes 1048576 | tf_op jit(solution)/shard_map/all_to_all | solution.py:407
  49.2 1.1 %collective-permute-done.1.got = bf16[2,5,32,256]{3,2,1,0:T(8,128)(2,1)S(1)} collective-permute-done((bf16[2,5,32,256]{3,2,1,0:T(8,128)(2,1)S(1)}, bf16[2,5,32,256]{3,2,1,0:T(8,128)(2,1)S(1)}, u32[]{:S(2)}, u32[]{:S(2)}) %collective-permute-start.1) | collective-permute-done | bytes 163872 | tf_op jit(solution)/shard_map/ppermute | solution.py:419
  50.4 1.7 %collective-permute-start.2 = (bf16[1,5,32,256]{3,2,1,0:T(8,128)(2,1)S(1)}, bf16[1,5,32,256]{3,2,1,0:T(8,128)(2,1)S(1)}, u32[]{:S(2)}, u32[]{:S(2)}) collective-permute-start(bf16[1,5,32,256]{3,2,1,0:T(8,128)(2,1)S(1)} %get-tuple-element.38), channel_id=1, source_target_pairs={{0,4},{1,5},{2,6},{3,7},{4,0},{5,1},{6,2},{7,3},{8,12},{9,13},{10,... | collective-permute-start | bytes 245768 | tf_op jit(solution)/shard_map/ppermute | solution.py:419
  52.1 9.2 %collective-permute-done.2.b = bf16[1,5,32,256]{3,2,1,0:T(8,128)(2,1)S(1)} collective-permute-done((bf16[1,5,32,256]{3,2,1,0:T(8,128)(2,1)S(1)}, bf16[1,5,32,256]{3,2,1,0:T(8,128)(2,1)S(1)}, u32[]{:S(2)}, u32[]{:S(2)}) %collective-permute-start.2) | collective-permute-done | bytes 81952 | tf_op jit(solution)/shard_map/ppermute | solution.py:419
  61.3 3.8 %collective-permute-start.3 = (bf16[1,5,32,256]{3,2,1,0:T(8,128)(2,1)S(1)}, bf16[1,5,32,256]{3,2,1,0:T(8,128)(2,1)S(1)}, u32[]{:S(2)}, u32[]{:S(2)}) collective-permute-start(bf16[1,5,32,256]{3,2,1,0:T(8,128)(2,1)S(1)} %shard_map.126.a), channel_id=1, source_target_pairs={{0,8},{1,9},{2,10},{3,11},{4,12},{5,13},{6,14},{7,15},{8,0},{9,1},... | collective-permute-start | bytes 245768 | tf_op jit(solution)/shard_map/ppermute | solution.py:419
  65.1 4.1 %shard_map.127 = bf16[8192,256]{1,0:T(8,128)(2,1)} custom-call(s32[1,256]{1,0:T(1,128)S(1)} %copy-done.7, bf16[256,1024]{1,0:T(8,128)(2,1)S(1)} %get-tuple-element.39.onehot_t, f32[64,128]{1,0:T(8,128)S(1)} %get-tuple-element.40.table, bf16[1024,256]{1,0:T(8,128)(2,1)S(1)} %bitcast.9), custom_call_target="tpu_custom_call" | custom-call | flops 1073741824 | bytes 4194304 | tf_op jit(solution)/shard_map/pallas_call | solution.py:390
  69.3 0.5 collective-permute-start.6
  69.8 1.1 %collective-permute-start.5 = (bf16[1,5,32,256]{3,2,1,0:T(8,128)(2,1)S(1)}, bf16[1,5,32,256]{3,2,1,0:T(8,128)(2,1)S(1)}, u32[]{:S(2)}, u32[]{:S(2)}) collective-permute-start(bf16[1,5,32,256]{3,2,1,0:T(8,128)(2,1)S(1)} %shard_map.128), channel_id=1, source_target_pairs={{0,2},{1,3},{2,0},{3,1},{4,6},{5,7},{6,4},{7,5},{8,10},{9,11},{10,... | collective-permute-start | bytes 245768 | tf_op jit(solution)/shard_map/ppermute | solution.py:419
  70.9 1.9 %collective-permute-start.4 = (bf16[1,5,32,256]{3,2,1,0:T(8,128)(2,1)S(1)}, bf16[1,5,32,256]{3,2,1,0:T(8,128)(2,1)S(1)}, u32[]{:S(2)}, u32[]{:S(2)}) collective-permute-start(bf16[1,5,32,256]{3,2,1,0:T(8,128)(2,1)S(1)} %shard_map.128), channel_id=1, source_target_pairs={{0,4},{1,5},{2,6},{3,7},{4,0},{5,1},{6,2},{7,3},{8,12},{9,13},{10,... | collective-permute-start | bytes 245768 | tf_op jit(solution)/shard_map/ppermute | solution.py:419
  72.8 2.7 %collective-permute-done.6 = bf16[1,5,32,256]{3,2,1,0:T(8,128)(2,1)S(1)} collective-permute-done((bf16[1,5,32,256]{3,2,1,0:T(8,128)(2,1)S(1)}, bf16[1,5,32,256]{3,2,1,0:T(8,128)(2,1)S(1)}, u32[]{:S(2)}, u32[]{:S(2)}) %collective-permute-start.6) | collective-permute-done | bytes 81952 | tf_op jit(solution)/shard_map/ppermute | solution.py:419
  76.2 1.6 %collective-permute-done.7.refs_1_ = bf16[4,5,32,256]{3,2,1,0:T(8,128)(2,1)S(1)} collective-permute-done((bf16[4,5,32,256]{3,2,1,0:T(8,128)(2,1)S(1)}, bf16[4,5,32,256]{3,2,1,0:T(8,128)(2,1)S(1)}, u32[]{:S(2)}, u32[]{:S(2)}) %collective-permute-start.7) | collective-permute-done | bytes 327712 | tf_op jit(solution)/shard_map/ppermute | solution.py:419
  77.8 1.1 %shard_map.129 = (f32[4,256,256]{2,1,0:T(8,128)}, f32[256,256]{1,0:T(8,128)}) custom-call(bf16[4,5,32,256]{3,2,1,0:T(8,128)(2,1)S(1)} %pad_maximum_fusion.refs_0_, bf16[4,5,32,256]{3,2,1,0:T(8,128)(2,1)S(1)} %collective-permute-done.7.refs_1_), custom_call_target="tpu_custom_call" | custom-call | tf_op jit(solution)/shard_map/pallas_call | solution.py:352
  (26 shorter events, 1.3 us)
Async XLA Ops:
  0.6 22.0 %copy-start.2 = (bf16[128,256]{1,0:T(8,128)(2,1)S(1)}, bf16[128,256]{1,0:T(8,128)(2,1)}, u32[]{:S(2)}) copy-start(bf16[128,256]{1,0:T(8,128)(2,1)} %out_grad.3) | copy-start | bytes 196612
  0.6 22.0 %copy-start = (bf16[4,256,256]{2,1,0:T(8,128)(2,1)S(1)}, bf16[4,256,256]{2,1,0:T(8,128)(2,1)}, u32[]{:S(2)}) copy-start(bf16[4,256,256]{2,1,0:T(8,128)(2,1)} %weights.3) | copy-start | bytes 1572868
  0.7 22.0 %copy-start.1 = (bf16[128,256]{1,0:T(8,128)(2,1)S(1)}, bf16[128,256]{1,0:T(8,128)(2,1)}, u32[]{:S(2)}) copy-start(bf16[128,256]{1,0:T(8,128)(2,1)} %queries.3) | copy-start | bytes 196612
  0.7 22.0 %copy-start.4 = (s32[128,100]{0,1:T(8,128)S(1)}, s32[128,100]{0,1:T(8,128)}, u32[]{:S(2)}) copy-start(s32[128,100]{0,1:T(8,128)} %param.14) | copy-start | bytes 153604
  0.7 36.5 %copy-start.3 = (bf16[256,256]{1,0:T(8,128)(2,1)S(1)}, bf16[256,256]{1,0:T(8,128)(2,1)}, u32[]{:S(2)}) copy-start(bf16[256,256]{1,0:T(8,128)(2,1)} %enc.1) | copy-start | bytes 393220
  2.0 13.7 %all-to-all-start = ((s32[16,1,128]{2,1,0:T(1,128)}), s32[16,1,128]{2,1,0:T(1,128)S(1)}, u32[]{:S(2)}, u32[]{:S(2)}) async-start(s32[16,1,128]{2,1,0:T(1,128)} %bitcast.1), calls=%async_computation | async-start | bytes 16384 | tf_op jit(solution)/shard_map/all_to_all | solution.py:407
  9.4 0.8 copy-start.5
  10.2 0.7 copy-start.6
  17.0 20.1 %all-to-all-start.1 = ((bf16[16,64,256]{2,1,0:T(8,128)(2,1)}), bf16[16,64,256]{2,1,0:T(8,128)(2,1)S(1)}, u32[]{:S(2)}, u32[]{:S(2)}) async-start(bf16[16,64,256]{2,1,0:T(8,128)(2,1)} %bitcast.4), calls=%async_computation.1 | async-start | bytes 1048576 | tf_op jit(solution)/shard_map/all_to_all | solution.py:407
  42.4 1.6 %collective-permute-start = (bf16[4,5,32,256]{3,2,1,0:T(8,128)(2,1)S(1)}, bf16[4,5,32,256]{3,2,1,0:T(8,128)(2,1)S(1)}, u32[]{:S(2)}, u32[]{:S(2)}) collective-permute-start(bf16[4,5,32,256]{3,2,1,0:T(8,128)(2,1)S(1)} %get-tuple-element.32), channel_id=1, source_target_pairs={{0,1},{1,0},{2,3},{3,2},{4,5},{5,4},{6,7},{7,6},{8,9},{9,8},{10,11... | collective-permute-start | bytes 983048 | tf_op jit(solution)/shard_map/ppermute | solution.py:419
  44.1 6.3 %collective-permute-start.1 = (bf16[2,5,32,256]{3,2,1,0:T(8,128)(2,1)S(1)}, bf16[2,5,32,256]{3,2,1,0:T(8,128)(2,1)S(1)}, u32[]{:S(2)}, u32[]{:S(2)}) collective-permute-start(bf16[2,5,32,256]{3,2,1,0:T(8,128)(2,1)S(1)} %get-tuple-element.36), channel_id=1, source_target_pairs={{0,2},{1,3},{2,0},{3,1},{4,6},{5,7},{6,4},{7,5},{8,10},{9,11},{10,... | collective-permute-start | bytes 491528 | tf_op jit(solution)/shard_map/ppermute | solution.py:419
  44.9 20.2 %all-to-all-start.2 = ((bf16[16,64,256]{2,1,0:T(8,128)(2,1)}), bf16[16,64,256]{2,1,0:T(8,128)(2,1)S(1)}, u32[]{:S(2)}, u32[]{:S(2)}) async-start(bf16[16,64,256]{2,1,0:T(8,128)(2,1)} %bitcast.7), calls=%async_computation.2 | async-start | bytes 1048576 | tf_op jit(solution)/shard_map/all_to_all | solution.py:407
  50.4 14.7 %copy-start.7 = (s32[1,256]{1,0:T(1,128)S(1)}, s32[1,256]{1,0:T(1,128)}, u32[]{:S(2)}) copy-start(s32[1,256]{1,0:T(1,128)} %counts.1) | copy-start | bytes 3076
  50.4 10.9 %collective-permute-start.2 = (bf16[1,5,32,256]{3,2,1,0:T(8,128)(2,1)S(1)}, bf16[1,5,32,256]{3,2,1,0:T(8,128)(2,1)S(1)}, u32[]{:S(2)}, u32[]{:S(2)}) collective-permute-start(bf16[1,5,32,256]{3,2,1,0:T(8,128)(2,1)S(1)} %get-tuple-element.38), channel_id=1, source_target_pairs={{0,4},{1,5},{2,6},{3,7},{4,0},{5,1},{6,2},{7,3},{8,12},{9,13},{10,... | collective-permute-start | bytes 245768 | tf_op jit(solution)/shard_map/ppermute | solution.py:419
  61.3 7.9 %collective-permute-start.3 = (bf16[1,5,32,256]{3,2,1,0:T(8,128)(2,1)S(1)}, bf16[1,5,32,256]{3,2,1,0:T(8,128)(2,1)S(1)}, u32[]{:S(2)}, u32[]{:S(2)}) collective-permute-start(bf16[1,5,32,256]{3,2,1,0:T(8,128)(2,1)S(1)} %shard_map.126.a), channel_id=1, source_target_pairs={{0,8},{1,9},{2,10},{3,11},{4,12},{5,13},{6,14},{7,15},{8,0},{9,1},... | collective-permute-start | bytes 245768 | tf_op jit(solution)/shard_map/ppermute | solution.py:419
  69.3 6.2 %collective-permute-start.6 = (bf16[1,5,32,256]{3,2,1,0:T(8,128)(2,1)S(1)}, bf16[1,5,32,256]{3,2,1,0:T(8,128)(2,1)S(1)}, u32[]{:S(2)}, u32[]{:S(2)}) collective-permute-start(bf16[1,5,32,256]{3,2,1,0:T(8,128)(2,1)S(1)} %shard_map.128), channel_id=1, source_target_pairs={{0,6},{1,7},{2,4},{3,5},{4,2},{5,3},{6,0},{7,1},{8,14},{9,15},{10,... | collective-permute-start | bytes 245768 | tf_op jit(solution)/shard_map/ppermute | solution.py:419
  69.8 6.1 %collective-permute-start.5 = (bf16[1,5,32,256]{3,2,1,0:T(8,128)(2,1)S(1)}, bf16[1,5,32,256]{3,2,1,0:T(8,128)(2,1)S(1)}, u32[]{:S(2)}, u32[]{:S(2)}) collective-permute-start(bf16[1,5,32,256]{3,2,1,0:T(8,128)(2,1)S(1)} %shard_map.128), channel_id=1, source_target_pairs={{0,2},{1,3},{2,0},{3,1},{4,6},{5,7},{6,4},{7,5},{8,10},{9,11},{10,... | collective-permute-start | bytes 245768 | tf_op jit(solution)/shard_map/ppermute | solution.py:419
  70.9 5.2 %collective-permute-start.4 = (bf16[1,5,32,256]{3,2,1,0:T(8,128)(2,1)S(1)}, bf16[1,5,32,256]{3,2,1,0:T(8,128)(2,1)S(1)}, u32[]{:S(2)}, u32[]{:S(2)}) collective-permute-start(bf16[1,5,32,256]{3,2,1,0:T(8,128)(2,1)S(1)} %shard_map.128), channel_id=1, source_target_pairs={{0,4},{1,5},{2,6},{3,7},{4,0},{5,1},{6,2},{7,3},{8,12},{9,13},{10,... | collective-permute-start | bytes 245768 | tf_op jit(solution)/shard_map/ppermute | solution.py:419
  76.1 1.7 %collective-permute-start.7 = (bf16[4,5,32,256]{3,2,1,0:T(8,128)(2,1)S(1)}, bf16[4,5,32,256]{3,2,1,0:T(8,128)(2,1)S(1)}, u32[]{:S(2)}, u32[]{:S(2)}) collective-permute-start(bf16[4,5,32,256]{3,2,1,0:T(8,128)(2,1)S(1)} %pad_maximum_fusion.refs_0_), channel_id=1, source_target_pairs={{0,1},{1,0},{2,3},{3,2},{4,5},{5,4},{6,7},{7,6},{8,9},{9,8},{10,11... | collective-permute-start | bytes 983048 | tf_op jit(solution)/shard_map/ppermute | solution.py:419

commit v8 on v7

--- a/solution.py
+++ b/solution.py
@@ -14,7 +14,7 @@
 F32 = jnp.float32
 BF16 = jnp.bfloat16
 VMEM_LIMIT = 32 * 1024 * 1024
-MOST_VMEM = 51 * 1024 * 1024
+MOST_VMEM = 56 * 1024 * 1024
 SMALL = pltpu.CompilerParams(vmem_limit_bytes=8 * 1024 * 1024)
 
 
@@ -71,27 +71,16 @@
     return within + before
 
 
-def means_kernel(
-    counts_h, members_h, raw_h, mean_out, table, counts_v, members, raw, small_sem, raw_sem
-):
-    clusters = counts_v.shape[1]
+def table_kernel(counts_h, members_h, table, counts_v, members, sem):
+    copies = [
+        pltpu.make_async_copy(counts_h, counts_v, sem.at[0]),
+        pltpu.make_async_copy(members_h, members, sem.at[1]),
+    ]
+    for copy in copies:
+        copy.start()
+    for copy in copies:
+        copy.wait()
     groups = members.shape[0]
-    parts = raw_sem.shape[0]
-    part = raw.shape[0] // parts
-    small = [
-        pltpu.make_async_copy(counts_h, counts_v, small_sem.at[0]),
-        pltpu.make_async_copy(members_h, members, small_sem.at[1]),
-    ]
-    large = [
-        pltpu.make_async_copy(
-            raw_h.at[pl.ds(k * part, part)], raw.at[pl.ds(k * part, part)], raw_sem.at[k]
-        )
-        for k in range(parts)
-    ]
-    for copy in small + large:
-        copy.start()
-    for copy in small:
-        copy.wait()
     cluster = position_clusters(counts_v[...], groups)
     rows = members[...]
     high = rows // LANES
@@ -108,6 +97,45 @@
             b_parts.append(ones_where(low[m : m + 1] == low_iota))
         total = total + dot_nt(jnp.concatenate(a_parts, axis=1), jnp.concatenate(b_parts, axis=1))
     table[...] = total
+
+
+def row_table(counts, members):
+    clusters = counts.shape[1]
+    groups = members.shape[1] // LANES
+    return pl.pallas_call(
+        table_kernel,
+        in_specs=[pl.BlockSpec(memory_space=pltpu.HBM)] * 2,
+        out_shape=jax.ShapeDtypeStruct((groups, LANES), F32),
+        scratch_shapes=[
+            pltpu.VMEM((1, clusters), jnp.int32),
+            pltpu.VMEM((groups, LANES), jnp.int32),
+            pltpu.SemaphoreType.DMA((2,)),
+        ],
+        compiler_params=pltpu.CompilerParams(vmem_limit_bytes=MOST_VMEM),
+        cost_estimate=pl.CostEstimate(
+            flops=2 * members.size * clusters * LANES, bytes_accessed=0, transcendentals=0
+        ),
+    )(counts, members.reshape(groups, LANES))
+
+
+def means_kernel(counts_h, table_h, raw_h, mean_out, counts_v, table, raw, small_sem, raw_sem):
+    clusters = counts_v.shape[1]
+    parts = raw_sem.shape[0]
+    part = raw.shape[0] // parts
+    small = [
+        pltpu.make_async_copy(counts_h, counts_v, small_sem.at[0]),
+        pltpu.make_async_copy(table_h, table, small_sem.at[1]),
+    ]
+    large = [
+        pltpu.make_async_copy(
+            raw_h.at[pl.ds(k * part, part)], raw.at[pl.ds(k * part, part)], raw_sem.at[k]
+        )
+        for k in range(parts)
+    ]
+    for copy in small + large:
+        copy.start()
+    for copy in small:
+        copy.wait()
     count_column = column_of(counts_v[...].astype(F32))
     sums = jnp.zeros((clusters, raw.shape[1]), F32)
     for p in range(parts):
@@ -119,21 +147,17 @@
     mean_out[...] = (sums / count_column).astype(BF16)
 
 
-def cluster_means(counts, members, raw_rows):
+def cluster_means(counts, table, raw_rows):
     clusters = counts.shape[1]
     rows, width = raw_rows.shape
-    groups = rows // LANES
     parts = 8
     return pl.pallas_call(
         means_kernel,
         in_specs=[pl.BlockSpec(memory_space=pltpu.HBM)] * 3,
-        out_shape=[
-            jax.ShapeDtypeStruct((clusters, width), BF16),
-            jax.ShapeDtypeStruct((groups, LANES), F32),
-        ],
+        out_shape=jax.ShapeDtypeStruct((clusters, width), BF16),
         scratch_shapes=[
             pltpu.VMEM((1, clusters), jnp.int32),
-            pltpu.VMEM((groups, LANES), jnp.int32),
+            pltpu.VMEM(table.shape, F32),
             pltpu.VMEM((rows, width), BF16),
             pltpu.SemaphoreType.DMA((2,)),
             pltpu.SemaphoreType.DMA((parts,)),
@@ -142,34 +166,51 @@
         cost_estimate=pl.CostEstimate(
             flops=2 * rows * clusters * width, bytes_accessed=2 * rows * width, transcendentals=0
         ),
-    )(counts, members.reshape(groups, LANES), raw_rows)
-
-
-def select_kernel(got, means, onehot_t, sent):
+    )(counts, table, raw_rows)
+
+
+def select_kernel(asked, means_h, onehot_t, sent, means, sem):
+    copy = pltpu.make_async_copy(means_h, means, sem)
+    copy.start()
     clusters = means.shape[0]
-    parity = lax.axis_index("clu") % 2
+    owners = asked.shape[0]
+    me = lax.axis_index("clu")
     half = LANES // 2
-    wanted = lax.rem(got[...], clusters)
-    turned = pltpu.roll(wanted, half, 1)
-    first = jnp.where(parity == 0, wanted, turned)
-    second = jnp.where(parity == 0, turned, wanted)
     left = iota((1, LANES), 1) < half
-    for k in range(got.shape[0] // 2):
-        row = jnp.where(left, first[2 * k : 2 * k + 1], second[2 * k + 1 : 2 * k + 2])
+
+    def wanted(asker):
+        flip = asker ^ me
+        place = (flip & 1) * (owners // 2) + (lax.shift_right_logical(flip, 1) & 3) * (owners // 8)
+        place = place + lax.shift_right_logical(flip, 3)
+        return lax.rem(asked[place, pl.ds(lax.shift_right_logical(me, 1), 1), :], clusters)
+
+    for k in range(owners // 2):
+        first, second = wanted(2 * k), wanted(2 * k + 1)
+        row = jnp.where(
+            me % 2 == 0,
+            jnp.where(left, first, pltpu.roll(second, half, 1)),
+            jnp.where(left, pltpu.roll(first, half, 1), second),
+        )
         onehot_t[:, k * LANES : (k + 1) * LANES] = ones_where(row == iota((clusters, LANES), 0))
+    copy.wait()
     sent[...] = dot_tn(onehot_t[...], means[...]).astype(BF16)
 
 
-def select_rows(got, means, pooled):
+def select_rows(asked, means, pooled):
     clusters, width = means.shape
     return pl.pallas_call(
         select_kernel,
+        in_specs=[
+            pl.BlockSpec(memory_space=pltpu.VMEM),
+            pl.BlockSpec(memory_space=pltpu.HBM),
+        ],
         out_shape=[
             jax.ShapeDtypeStruct((clusters, pooled), BF16),
             jax.ShapeDtypeStruct((pooled, width), BF16),
         ],
-        compiler_params=pltpu.CompilerParams(vmem_limit_bytes=VMEM_LIMIT),
-    )(got, means)
+        scratch_shapes=[pltpu.VMEM((clusters, width), BF16), pltpu.SemaphoreType.DMA],
+        compiler_params=pltpu.CompilerParams(vmem_limit_bytes=MOST_VMEM),
+    )(asked, means)
 
 
 def spread_heads(rows):
@@ -418,11 +459,16 @@
     def exchange(flip, block):
         return lax.ppermute(block, "clu", [(d, d ^ flip) for d in range(owners)])
 
-    pairs = pool.reshape(owners // 2, 1, 1, LANES)
-    asking = jnp.broadcast_to(pairs, (owners // 2, 2, 1, LANES)).reshape(owners, 1, LANES)
-    got = swap(asking).reshape(owners, LANES)
-    means, table = cluster_means(counts, member_rows, raw_rows)
-    onehot_t, sent = select_rows(got, means, pooled)
+    asked = pool.reshape(1, pooled // LANES, LANES)
+    for bit in range(3, bits):
+        asked = jnp.concatenate([asked, exchange(1 << bit, asked)])
+    table = row_table(counts, member_rows)
+    asked, table = lax.optimization_barrier((asked, table))
+    asked = jnp.concatenate([asked] + [exchange(flip, asked) for flip in (2, 4, 6)])
+    means = cluster_means(counts, table, raw_rows)
+    asked, means = lax.optimization_barrier((asked, means))
+    asked = jnp.concatenate([asked, exchange(1, asked)])
+    onehot_t, sent = select_rows(asked, means, pooled)
     raw_pool = swap(sent.reshape(owners, pooled // owners, width)).reshape(pooled, width)
     bias, query_heads, mixed_heads = target_terms(
         scale, picks.T, queries, out_grad, attn_weights, pooled

time: 79.4 us -> 84.1 us (1.059)
  Pallas kernels: 20.3 us -> 25.7 us
  local copies, waits for them, and re-layouts: 2.81 us -> 0.03 us
  other arithmetic: 0.04 us -> 1.37 us
    all_to_all x3 -> x2, starting transfers between devices: 17.3 us -> 9.52 us  [swap(): lax.all_to_all(blocks, 'clu', split_axis=0, concat_axis=0, tiled=True)]
    ppermute x8 -> x13, starting transfers between devices: 9.99 us -> 17.7 us  [exchange(): return lax.ppermute(block, 'clu', [(d, d ^ flip) for d in range(owners)])]
    pallas_call x1 -> x2, Pallas kernels: 1.28 us -> 5.78 us  [the longest x1 2.95 us: select_rows(): pl.pallas_call(select_kernel, in_specs=[pl.BlockSpec(memory_space=pltpu.V...]
    unnamed x16, local copies, waits for them, and re-layouts: 1.46 us -> 0.03 us
    broadcast_in_dim x1 -> x0, local copies, waits for them, and re-layouts: 1.36 us -> none  [local(): jnp.broadcast_to(pairs, (owners // 2, 2, 1, LANES))]
    concatenate x0 -> x3, other arithmetic: none -> 1.33 us  [the longest x1 0.69 us: local(): asked = jnp.concatenate([asked, exchange(1 << bit, asked)])]
    ppermute x8 -> x13, waiting for transfers between devices: 16.8 us -> 17.9 us  [exchange(): return lax.ppermute(block, 'clu', [(d, d ^ flip) for d in range(owners)])]
    pallas_call x1, Pallas kernels: 4.49 us -> 5.4 us  [cluster_means(): pl.pallas_call(means_kernel, in_specs=[pl.BlockSpec(memory_space=pltpu.HB...]
  transfers between devices with their start and end apart: 11 -> 15, of which waited for: 9 -> 9; matrix products, arithmetic and copies ran while one was open for 0% -> 0% of each run, Pallas kernels for 16% -> 19%
where the time goes in v8:
time: 84.1 us; the launch traced here: 83.7 us
  waiting for transfers between devices  28.5 us (34%)
  starting transfers between devices  27.2 us (32%)
  Pallas kernels  25.7 us (31%)
  other arithmetic  1.37 us (2%)
  between operations  0.86 us (1%)
    ppermute x13, waiting for transfers between devices, exchange(): return lax.ppermute(block, 'clu', [(d, d ^ flip) for d in range(owners)])  17.9 us
    ppermute x13, starting transfers between devices, exchange(): return lax.ppermute(block, 'clu', [(d, d ^ flip) for d in range(owners)])  17.7 us
    all_to_all x2, waiting for transfers between devices, swap(): lax.all_to_all(blocks, 'clu', split_axis=0, concat_axis=0, tiled=True)  10.6 us
    all_to_all x2, starting transfers between devices, swap(): lax.all_to_all(blocks, 'clu', split_axis=0, concat_axis=0, tiled=True)  9.52 us
    pallas_call x1, Pallas kernels, cluster_means(): pl.pallas_call(means_kernel, in_specs=[pl.BlockSpec(memory_space=pltpu.HB...  5.4 us
    pallas_call x1, Pallas kernels, attention(): pl.pallas_call(functools.partial(attention_kernel, scale), out_shape=[jax...  5.27 us
    pallas_call x1, Pallas kernels, member_grads(): pl.pallas_call(rows_kernel, out_specs=pl.BlockSpec(memory_space=pltpu.HBM...  4.09 us
    pallas_call x1, Pallas kernels, target_terms(): pl.pallas_call(functools.partial(targets_kernel, scale), out_shape=[jax.S...  3.87 us
  transfers between devices with their start and end apart: 15, of which 9 were waited for; matrix products, arithmetic and copies ran while one was open for 0% of the time, Pallas kernels for 19%

profile of v8, /device:TPU:0, one launch (start us, length us, event | category | flops | bytes accessed | tf_op | source)
XLA Modules:
  0.0 83.7 jit_solution(4492815549509869082)
XLA Ops:
  0.7 4.1 %collective-permute-start = (s32[1,8,128]{2,1,0:T(8,128)}, s32[1,8,128]{2,1,0:T(8,128)S(1)}, u32[]{:S(2)}, u32[]{:S(2)}) collective-permute-start(s32[1,8,128]{2,1,0:T(8,128)} %bitcast.11), channel_id=1, source_target_pairs={{0,8},{1,9},{2,10},{3,11},{4,12},{5,13},{6,14},{7,15},{8,0},{9,1},... | collective-permute-start | bytes 12296 | tf_op jit(solution)/shard_map/ppermute | solution.py:460
  4.8 2.8 %shard_map.120.table_h.table = f32[64,128]{1,0:T(8,128)} custom-call(s32[1,256]{1,0:T(1,128)} %counts.1, s32[64,128]{1,0:T(8,128)} %bitcast.13), custom_call_target="tpu_custom_call" | custom-call | flops 536870912 | tf_op jit(solution)/shard_map/pallas_call | solution.py:105
  7.6 0.7 pad_add_fusion.2
  8.3 2.5 %collective-permute-start.3 = (s32[2,8,128]{2,1,0:T(8,128)S(1)}, s32[2,8,128]{2,1,0:T(8,128)S(1)}, u32[]{:S(2)}, u32[]{:S(2)}) collective-permute-start(s32[2,8,128]{2,1,0:T(8,128)S(1)} %pad_add_fusion.2), channel_id=1, source_target_pairs={{0,6},{1,7},{2,4},{3,5},{4,2},{5,3},{6,0},{7,1},{8,14},{9,15},{10,... | collective-permute-start | bytes 24584 | tf_op jit(solution)/shard_map/ppermute | solution.py:460
  11.8 5.4 %shard_map.121.means_h = bf16[256,256]{1,0:T(8,128)(2,1)} custom-call(s32[1,256]{1,0:T(1,128)} %counts.1, f32[64,128]{1,0:T(8,128)} %shard_map.120.table_h.table, bf16[8192,256]{1,0:T(8,128)(2,1)} %raw_h.1), custom_call_target="tpu_custom_call" | custom-call | flops 1073741824 | bytes 4194304 | tf_op jit(solution)/shard_map/pallas_call | solution.py:154
  17.3 1.2 %collective-permute-done.4 = s32[8,8,128]{2,1,0:T(8,128)S(1)} collective-permute-done((s32[8,8,128]{2,1,0:T(8,128)S(1)}, s32[8,8,128]{2,1,0:T(8,128)S(1)}, u32[]{:S(2)}, u32[]{:S(2)}) %collective-permute-start.4) | collective-permute-done | bytes 32800 | tf_op jit(solution)/shard_map/ppermute | solution.py:460
  19.2 3.0 %shard_map.122 = (bf16[256,1024]{1,0:T(8,128)(2,1)}, bf16[1024,256]{1,0:T(8,128)(2,1)}) custom-call(s32[16,8,128]{2,1,0:T(8,128)} %pad_add_fusion.asked, bf16[256,256]{1,0:T(8,128)(2,1)} %shard_map.121.means_h), custom_call_target="tpu_custom_call" | custom-call | tf_op jit(solution)/shard_map/pallas_call | solution.py:201
  22.1 5.2 %all-to-all-start = ((bf16[16,64,256]{2,1,0:T(8,128)(2,1)}), bf16[16,64,256]{2,1,0:T(8,128)(2,1)S(1)}, u32[]{:S(2)}, u32[]{:S(2)}) async-start(bf16[16,64,256]{2,1,0:T(8,128)(2,1)} %bitcast.10), calls=%async_computation | async-start | bytes 1048576 | tf_op jit(solution)/shard_map/all_to_all | solution.py:448
  27.4 3.9 %shard_map.123 = (f32[1024,128]{1,0:T(8,128)S(1)}, bf16[512,256]{1,0:T(8,128)(2,1)S(1)}, bf16[512,256]{1,0:T(8,128)(2,1)S(1)}) custom-call(s32[100,128]{1,0:T(8,128)S(1)} %bitcast.9, bf16[128,256]{1,0:T(8,128)(2,1)S(1)} %copy-done.2, bf16[128,256]{1,0:T(8,128)(2,1)S(1)} %copy-done.3, bf16[4,256,256]{2,1,0:T(8,128)(2,1)S(1)} %copy-done), custom_call_target="tpu_custom_call" | custom-call | flops 52428800 | bytes 524288 | tf_op jit(solution)/shard_map/pallas_call | solution.py:245
  31.3 10.5 %all-to-all-done = bf16[16,64,256]{2,1,0:T(8,128)(2,1)S(1)} async-done(((bf16[16,64,256]{2,1,0:T(8,128)(2,1)}), bf16[16,64,256]{2,1,0:T(8,128)(2,1)S(1)}, u32[]{:S(2)}, u32[]{:S(2)}) %all-to-all-start) | async-done | bytes 524320 | tf_op jit(solution)/shard_map/all_to_all | solution.py:448
  41.8 5.3 %shard_map.124 = (bf16[1024,256]{1,0:T(8,128)(2,1)}, bf16[128,256]{1,0:T(8,128)(2,1)}, bf16[4,5,32,256]{3,2,1,0:T(8,128)(2,1)S(1)}, bf16[4,5,32,256]{3,2,1,0:T(8,128)(2,1)S(1)}) custom-call(bf16[1024,256]{1,0:T(8,128)(2,1)S(1)} %bitcast.8, bf16[256,256]{1,0:T(8,128)(2,1)S(1)} %copy-done.5, bf16[4,256,256]{2,1,0:T(8,128)(2,1)S(1)} %copy-done, ...), custom_call_target="tpu_custom_call" | custom-call | tf_op jit(solution)/shard_map/pallas_call | solution.py:332
  47.1 1.6 %collective-permute-done.5.got = bf16[4,5,32,256]{3,2,1,0:T(8,128)(2,1)S(1)} collective-permute-done((bf16[4,5,32,256]{3,2,1,0:T(8,128)(2,1)S(1)}, bf16[4,5,32,256]{3,2,1,0:T(8,128)(2,1)S(1)}, u32[]{:S(2)}, u32[]{:S(2)}) %collective-permute-start.5) | collective-permute-done | bytes 327712 | tf_op jit(solution)/shard_map/ppermute | solution.py:460
  48.8 0.9 %collective-permute-start.6 = (bf16[2,5,32,256]{3,2,1,0:T(8,128)(2,1)S(1)}, bf16[2,5,32,256]{3,2,1,0:T(8,128)(2,1)S(1)}, u32[]{:S(2)}, u32[]{:S(2)}) collective-permute-start(bf16[2,5,32,256]{3,2,1,0:T(8,128)(2,1)S(1)} %get-tuple-element.41), channel_id=1, source_target_pairs={{0,2},{1,3},{2,0},{3,1},{4,6},{5,7},{6,4},{7,5},{8,10},{9,11},{10,... | collective-permute-start | bytes 491528 | tf_op jit(solution)/shard_map/ppermute | solution.py:460
  49.7 4.3 %all-to-all-start.1 = ((bf16[16,64,256]{2,1,0:T(8,128)(2,1)}), bf16[16,64,256]{2,1,0:T(8,128)(2,1)S(1)}, u32[]{:S(2)}, u32[]{:S(2)}) async-start(bf16[16,64,256]{2,1,0:T(8,128)(2,1)} %bitcast.5), calls=%async_computation.1 | async-start | bytes 1048576 | tf_op jit(solution)/shard_map/all_to_all | solution.py:448
  54.0 1.1 %collective-permute-done.6.got = bf16[2,5,32,256]{3,2,1,0:T(8,128)(2,1)S(1)} collective-permute-done((bf16[2,5,32,256]{3,2,1,0:T(8,128)(2,1)S(1)}, bf16[2,5,32,256]{3,2,1,0:T(8,128)(2,1)S(1)}, u32[]{:S(2)}, u32[]{:S(2)}) %collective-permute-start.6) | collective-permute-done | bytes 163872 | tf_op jit(solution)/shard_map/ppermute | solution.py:460
  55.2 1.7 %collective-permute-start.7 = (bf16[1,5,32,256]{3,2,1,0:T(8,128)(2,1)S(1)}, bf16[1,5,32,256]{3,2,1,0:T(8,128)(2,1)S(1)}, u32[]{:S(2)}, u32[]{:S(2)}) collective-permute-start(bf16[1,5,32,256]{3,2,1,0:T(8,128)(2,1)S(1)} %get-tuple-element.43), channel_id=1, source_target_pairs={{0,4},{1,5},{2,6},{3,7},{4,0},{5,1},{6,2},{7,3},{8,12},{9,13},{10,... | collective-permute-start | bytes 245768 | tf_op jit(solution)/shard_map/ppermute | solution.py:460
  56.8 9.2 %collective-permute-done.7.b = bf16[1,5,32,256]{3,2,1,0:T(8,128)(2,1)S(1)} collective-permute-done((bf16[1,5,32,256]{3,2,1,0:T(8,128)(2,1)S(1)}, bf16[1,5,32,256]{3,2,1,0:T(8,128)(2,1)S(1)}, u32[]{:S(2)}, u32[]{:S(2)}) %collective-permute-start.7) | collective-permute-done | bytes 81952 | tf_op jit(solution)/shard_map/ppermute | solution.py:460
  66.1 3.8 %collective-permute-start.8 = (bf16[1,5,32,256]{3,2,1,0:T(8,128)(2,1)S(1)}, bf16[1,5,32,256]{3,2,1,0:T(8,128)(2,1)S(1)}, u32[]{:S(2)}, u32[]{:S(2)}) collective-permute-start(bf16[1,5,32,256]{3,2,1,0:T(8,128)(2,1)S(1)} %shard_map.127.a), channel_id=1, source_target_pairs={{0,8},{1,9},{2,10},{3,11},{4,12},{5,13},{6,14},{7,15},{8,0},{9,1},... | collective-permute-start | bytes 245768 | tf_op jit(solution)/shard_map/ppermute | solution.py:460
  69.9 4.1 %shard_map.128 = bf16[8192,256]{1,0:T(8,128)(2,1)} custom-call(s32[1,256]{1,0:T(1,128)S(1)} %copy-done.7, bf16[256,1024]{1,0:T(8,128)(2,1)S(1)} %copy-done.1, f32[64,128]{1,0:T(8,128)S(1)} %copy-done.4, bf16[1024,256]{1,0:T(8,128)(2,1)S(1)} %bitcast.7), custom_call_target="tpu_custom_call" | custom-call | flops 1073741824 | bytes 4194304 | tf_op jit(solution)/shard_map/pallas_call | solution.py:431
  74.5 1.1 %collective-permute-start.10 = (bf16[1,5,32,256]{3,2,1,0:T(8,128)(2,1)S(1)}, bf16[1,5,32,256]{3,2,1,0:T(8,128)(2,1)S(1)}, u32[]{:S(2)}, u32[]{:S(2)}) collective-permute-start(bf16[1,5,32,256]{3,2,1,0:T(8,128)(2,1)S(1)} %shard_map.129), channel_id=1, source_target_pairs={{0,2},{1,3},{2,0},{3,1},{4,6},{5,7},{6,4},{7,5},{8,10},{9,11},{10,... | collective-permute-start | bytes 245768 | tf_op jit(solution)/shard_map/ppermute | solution.py:460
  75.6 2.0 %collective-permute-start.9 = (bf16[1,5,32,256]{3,2,1,0:T(8,128)(2,1)S(1)}, bf16[1,5,32,256]{3,2,1,0:T(8,128)(2,1)S(1)}, u32[]{:S(2)}, u32[]{:S(2)}) collective-permute-start(bf16[1,5,32,256]{3,2,1,0:T(8,128)(2,1)S(1)} %shard_map.129), channel_id=1, source_target_pairs={{0,4},{1,5},{2,6},{3,7},{4,0},{5,1},{6,2},{7,3},{8,12},{9,13},{10,... | collective-permute-start | bytes 245768 | tf_op jit(solution)/shard_map/ppermute | solution.py:460
  77.6 2.6 %collective-permute-done.11 = bf16[1,5,32,256]{3,2,1,0:T(8,128)(2,1)S(1)} collective-permute-done((bf16[1,5,32,256]{3,2,1,0:T(8,128)(2,1)S(1)}, bf16[1,5,32,256]{3,2,1,0:T(8,128)(2,1)S(1)}, u32[]{:S(2)}, u32[]{:S(2)}) %collective-permute-start.11) | collective-permute-done | bytes 81952 | tf_op jit(solution)/shard_map/ppermute | solution.py:460
  80.9 1.6 %collective-permute-done.12.refs_1_ = bf16[4,5,32,256]{3,2,1,0:T(8,128)(2,1)S(1)} collective-permute-done((bf16[4,5,32,256]{3,2,1,0:T(8,128)(2,1)S(1)}, bf16[4,5,32,256]{3,2,1,0:T(8,128)(2,1)S(1)}, u32[]{:S(2)}, u32[]{:S(2)}) %collective-permute-start.12) | collective-permute-done | bytes 327712 | tf_op jit(solution)/shard_map/ppermute | solution.py:460
  82.5 1.1 %shard_map.130 = (f32[4,256,256]{2,1,0:T(8,128)}, f32[256,256]{1,0:T(8,128)}) custom-call(bf16[4,5,32,256]{3,2,1,0:T(8,128)(2,1)S(1)} %pad_maximum_fusion.refs_0_, bf16[4,5,32,256]{3,2,1,0:T(8,128)(2,1)S(1)} %collective-permute-done.12.refs_1_), custom_call_target="tpu_custom_call" | custom-call | tf_op jit(solution)/shard_map/pallas_call | solution.py:393
  (37 shorter events, 3.1 us)
Async XLA Ops:
  0.6 26.7 %copy-start.3 = (bf16[128,256]{1,0:T(8,128)(2,1)S(1)}, bf16[128,256]{1,0:T(8,128)(2,1)}, u32[]{:S(2)}) copy-start(bf16[128,256]{1,0:T(8,128)(2,1)} %out_grad.3) | copy-start | bytes 196612
  0.6 26.7 %copy-start = (bf16[4,256,256]{2,1,0:T(8,128)(2,1)S(1)}, bf16[4,256,256]{2,1,0:T(8,128)(2,1)}, u32[]{:S(2)}) copy-start(bf16[4,256,256]{2,1,0:T(8,128)(2,1)} %weights.3) | copy-start | bytes 1572868
  0.7 26.7 %copy-start.2 = (bf16[128,256]{1,0:T(8,128)(2,1)S(1)}, bf16[128,256]{1,0:T(8,128)(2,1)}, u32[]{:S(2)}) copy-start(bf16[128,256]{1,0:T(8,128)(2,1)} %queries.3) | copy-start | bytes 196612
  0.7 26.7 %copy-start.6 = (s32[128,100]{0,1:T(8,128)S(1)}, s32[128,100]{0,1:T(8,128)}, u32[]{:S(2)}) copy-start(s32[128,100]{0,1:T(8,128)} %param.14) | copy-start | bytes 153604
  0.7 6.9 %collective-permute-start = (s32[1,8,128]{2,1,0:T(8,128)}, s32[1,8,128]{2,1,0:T(8,128)S(1)}, u32[]{:S(2)}, u32[]{:S(2)}) collective-permute-start(s32[1,8,128]{2,1,0:T(8,128)} %bitcast.11), channel_id=1, source_target_pairs={{0,8},{1,9},{2,10},{3,11},{4,12},{5,13},{6,14},{7,15},{8,0},{9,1},... | collective-permute-start | bytes 12296 | tf_op jit(solution)/shard_map/ppermute | solution.py:460
  4.8 37.1 %copy-start.5 = (bf16[256,256]{1,0:T(8,128)(2,1)S(1)}, bf16[256,256]{1,0:T(8,128)(2,1)}, u32[]{:S(2)}) copy-start(bf16[256,256]{1,0:T(8,128)(2,1)} %enc.1) | copy-start | bytes 393220
  8.3 8.9 %collective-permute-start.3 = (s32[2,8,128]{2,1,0:T(8,128)S(1)}, s32[2,8,128]{2,1,0:T(8,128)S(1)}, u32[]{:S(2)}, u32[]{:S(2)}) collective-permute-start(s32[2,8,128]{2,1,0:T(8,128)S(1)} %pad_add_fusion.2), channel_id=1, source_target_pairs={{0,6},{1,7},{2,4},{3,5},{4,2},{5,3},{6,0},{7,1},{8,14},{9,15},{10,... | collective-permute-start | bytes 24584 | tf_op jit(solution)/shard_map/ppermute | solution.py:460
  10.8 6.4 %collective-permute-start.2 = (s32[2,8,128]{2,1,0:T(8,128)S(1)}, s32[2,8,128]{2,1,0:T(8,128)S(1)}, u32[]{:S(2)}, u32[]{:S(2)}) collective-permute-start(s32[2,8,128]{2,1,0:T(8,128)S(1)} %pad_add_fusion.2), channel_id=1, source_target_pairs={{0,4},{1,5},{2,6},{3,7},{4,0},{5,1},{6,2},{7,3},{8,12},{9,13},{10,... | collective-permute-start | bytes 24584 | tf_op jit(solution)/shard_map/ppermute | solution.py:460
  11.3 5.9 %collective-permute-start.1 = (s32[2,8,128]{2,1,0:T(8,128)S(1)}, s32[2,8,128]{2,1,0:T(8,128)S(1)}, u32[]{:S(2)}, u32[]{:S(2)}) collective-permute-start(s32[2,8,128]{2,1,0:T(8,128)S(1)} %pad_add_fusion.2), channel_id=1, source_target_pairs={{0,2},{1,3},{2,0},{3,1},{4,6},{5,7},{6,4},{7,5},{8,10},{9,11},{10,... | collective-permute-start | bytes 24584 | tf_op jit(solution)/shard_map/ppermute | solution.py:460
  17.3 1.3 %collective-permute-start.4 = (s32[8,8,128]{2,1,0:T(8,128)S(1)}, s32[8,8,128]{2,1,0:T(8,128)S(1)}, u32[]{:S(2)}, u32[]{:S(2)}) collective-permute-start(s32[8,8,128]{2,1,0:T(8,128)S(1)} %pad_add_fusion.1), channel_id=1, source_target_pairs={{0,1},{1,0},{2,3},{3,2},{4,5},{5,4},{6,7},{7,6},{8,9},{9,8},{10,11... | collective-permute-start | bytes 98312 | tf_op jit(solution)/shard_map/ppermute | solution.py:460
  22.1 19.7 %all-to-all-start = ((bf16[16,64,256]{2,1,0:T(8,128)(2,1)}), bf16[16,64,256]{2,1,0:T(8,128)(2,1)S(1)}, u32[]{:S(2)}, u32[]{:S(2)}) async-start(bf16[16,64,256]{2,1,0:T(8,128)(2,1)} %bitcast.10), calls=%async_computation | async-start | bytes 1048576 | tf_op jit(solution)/shard_map/all_to_all | solution.py:448
  47.1 1.6 %collective-permute-start.5 = (bf16[4,5,32,256]{3,2,1,0:T(8,128)(2,1)S(1)}, bf16[4,5,32,256]{3,2,1,0:T(8,128)(2,1)S(1)}, u32[]{:S(2)}, u32[]{:S(2)}) collective-permute-start(bf16[4,5,32,256]{3,2,1,0:T(8,128)(2,1)S(1)} %get-tuple-element.37), channel_id=1, source_target_pairs={{0,1},{1,0},{2,3},{3,2},{4,5},{5,4},{6,7},{7,6},{8,9},{9,8},{10,11... | collective-permute-start | bytes 983048 | tf_op jit(solution)/shard_map/ppermute | solution.py:460
  48.8 6.3 %collective-permute-start.6 = (bf16[2,5,32,256]{3,2,1,0:T(8,128)(2,1)S(1)}, bf16[2,5,32,256]{3,2,1,0:T(8,128)(2,1)S(1)}, u32[]{:S(2)}, u32[]{:S(2)}) collective-permute-start(bf16[2,5,32,256]{3,2,1,0:T(8,128)(2,1)S(1)} %get-tuple-element.41), channel_id=1, source_target_pairs={{0,2},{1,3},{2,0},{3,1},{4,6},{5,7},{6,4},{7,5},{8,10},{9,11},{10,... | collective-permute-start | bytes 491528 | tf_op jit(solution)/shard_map/ppermute | solution.py:460
  49.7 20.2 %all-to-all-start.1 = ((bf16[16,64,256]{2,1,0:T(8,128)(2,1)}), bf16[16,64,256]{2,1,0:T(8,128)(2,1)S(1)}, u32[]{:S(2)}, u32[]{:S(2)}) async-start(bf16[16,64,256]{2,1,0:T(8,128)(2,1)} %bitcast.5), calls=%async_computation.1 | async-start | bytes 1048576 | tf_op jit(solution)/shard_map/all_to_all | solution.py:448
  55.1 14.8 %copy-start.1 = (bf16[256,1024]{1,0:T(8,128)(2,1)S(1)}, bf16[256,1024]{1,0:T(8,128)(2,1)}, u32[]{:S(2)}) copy-start(bf16[256,1024]{1,0:T(8,128)(2,1)} %get-tuple-element.44.onehot_t) | copy-start | bytes 1572868
  55.1 14.8 %copy-start.4 = (f32[64,128]{1,0:T(8,128)S(1)}, f32[64,128]{1,0:T(8,128)}, u32[]{:S(2)}) copy-start(f32[64,128]{1,0:T(8,128)} %shard_map.120.table_h.table) | copy-start | bytes 98308
  55.1 14.8 %copy-start.7 = (s32[1,256]{1,0:T(1,128)S(1)}, s32[1,256]{1,0:T(1,128)}, u32[]{:S(2)}) copy-start(s32[1,256]{1,0:T(1,128)} %counts.1) | copy-start | bytes 3076
  55.2 10.9 %collective-permute-start.7 = (bf16[1,5,32,256]{3,2,1,0:T(8,128)(2,1)S(1)}, bf16[1,5,32,256]{3,2,1,0:T(8,128)(2,1)S(1)}, u32[]{:S(2)}, u32[]{:S(2)}) collective-permute-start(bf16[1,5,32,256]{3,2,1,0:T(8,128)(2,1)S(1)} %get-tuple-element.43), channel_id=1, source_target_pairs={{0,4},{1,5},{2,6},{3,7},{4,0},{5,1},{6,2},{7,3},{8,12},{9,13},{10,... | collective-permute-start | bytes 245768 | tf_op jit(solution)/shard_map/ppermute | solution.py:460
  66.1 7.9 %collective-permute-start.8 = (bf16[1,5,32,256]{3,2,1,0:T(8,128)(2,1)S(1)}, bf16[1,5,32,256]{3,2,1,0:T(8,128)(2,1)S(1)}, u32[]{:S(2)}, u32[]{:S(2)}) collective-permute-start(bf16[1,5,32,256]{3,2,1,0:T(8,128)(2,1)S(1)} %shard_map.127.a), channel_id=1, source_target_pairs={{0,8},{1,9},{2,10},{3,11},{4,12},{5,13},{6,14},{7,15},{8,0},{9,1},... | collective-permute-start | bytes 245768 | tf_op jit(solution)/shard_map/ppermute | solution.py:460
  74.0 6.2 %collective-permute-start.11 = (bf16[1,5,32,256]{3,2,1,0:T(8,128)(2,1)S(1)}, bf16[1,5,32,256]{3,2,1,0:T(8,128)(2,1)S(1)}, u32[]{:S(2)}, u32[]{:S(2)}) collective-permute-start(bf16[1,5,32,256]{3,2,1,0:T(8,128)(2,1)S(1)} %shard_map.129), channel_id=1, source_target_pairs={{0,6},{1,7},{2,4},{3,5},{4,2},{5,3},{6,0},{7,1},{8,14},{9,15},{10,... | collective-permute-start | bytes 245768 | tf_op jit(solution)/shard_map/ppermute | solution.py:460
  74.5 6.1 %collective-permute-start.10 = (bf16[1,5,32,256]{3,2,1,0:T(8,128)(2,1)S(1)}, bf16[1,5,32,256]{3,2,1,0:T(8,128)(2,1)S(1)}, u32[]{:S(2)}, u32[]{:S(2)}) collective-permute-start(bf16[1,5,32,256]{3,2,1,0:T(8,128)(2,1)S(1)} %shard_map.129), channel_id=1, source_target_pairs={{0,2},{1,3},{2,0},{3,1},{4,6},{5,7},{6,4},{7,5},{8,10},{9,11},{10,... | collective-permute-start | bytes 245768 | tf_op jit(solution)/shard_map/ppermute | solution.py:460
  75.6 5.1 %collective-permute-start.9 = (bf16[1,5,32,256]{3,2,1,0:T(8,128)(2,1)S(1)}, bf16[1,5,32,256]{3,2,1,0:T(8,128)(2,1)S(1)}, u32[]{:S(2)}, u32[]{:S(2)}) collective-permute-start(bf16[1,5,32,256]{3,2,1,0:T(8,128)(2,1)S(1)} %shard_map.129), channel_id=1, source_target_pairs={{0,4},{1,5},{2,6},{3,7},{4,0},{5,1},{6,2},{7,3},{8,12},{9,13},{10,... | collective-permute-start | bytes 245768 | tf_op jit(solution)/shard_map/ppermute | solution.py:460
  80.8 1.7 %collective-permute-start.12 = (bf16[4,5,32,256]{3,2,1,0:T(8,128)(2,1)S(1)}, bf16[4,5,32,256]{3,2,1,0:T(8,128)(2,1)S(1)}, u32[]{:S(2)}, u32[]{:S(2)}) collective-permute-start(bf16[4,5,32,256]{3,2,1,0:T(8,128)(2,1)S(1)} %pad_maximum_fusion.refs_0_), channel_id=1, source_target_pairs={{0,1},{1,0},{2,3},{3,2},{4,5},{5,4},{6,7},{7,6},{8,9},{9,8},{10,11... | collective-permute-start | bytes 983048 | tf_op jit(solution)/shard_map/ppermute | solution.py:460

commit v9 on v7

--- a/solution.py
+++ b/solution.py
@@ -145,31 +145,55 @@
     )(counts, members.reshape(groups, LANES), raw_rows)
 
 
-def select_kernel(got, means, onehot_t, sent):
+def select_kernel(got, means, onehot_t, keep, give):
     clusters = means.shape[0]
-    parity = lax.axis_index("clu") % 2
+    chips, per_owner, _ = keep.shape
+    me = lax.axis_index("clu")
+    parity = me % 2
     half = LANES // 2
     wanted = lax.rem(got[...], clusters)
     turned = pltpu.roll(wanted, half, 1)
     first = jnp.where(parity == 0, wanted, turned)
     second = jnp.where(parity == 0, turned, wanted)
     left = iota((1, LANES), 1) < half
-    for k in range(got.shape[0] // 2):
+    for k in range(chips):
         row = jnp.where(left, first[2 * k : 2 * k + 1], second[2 * k + 1 : 2 * k + 2])
         onehot_t[:, k * LANES : (k + 1) * LANES] = ones_where(row == iota((clusters, LANES), 0))
-    sent[...] = dot_tn(onehot_t[...], means[...]).astype(BF16)
+    sent = dot_tn(onehot_t[...], means[...]).astype(BF16)
+    for k in range(chips):
+        place = lax.shift_right_logical(me, 1) ^ k
+        even = sent[2 * k * per_owner : (2 * k + 1) * per_owner]
+        odd = sent[(2 * k + 1) * per_owner : (2 * k + 2) * per_owner]
+        keep[place] = jnp.where(parity == 0, even, odd)
+        give[place] = jnp.where(parity == 0, odd, even)
 
 
 def select_rows(got, means, pooled):
     clusters, width = means.shape
+    chips = got.shape[0] // 2
+    half = jax.ShapeDtypeStruct((chips, pooled // chips // 2, width), BF16)
     return pl.pallas_call(
         select_kernel,
-        out_shape=[
-            jax.ShapeDtypeStruct((clusters, pooled), BF16),
-            jax.ShapeDtypeStruct((pooled, width), BF16),
-        ],
+        out_shape=[jax.ShapeDtypeStruct((clusters, pooled), BF16), half, half],
         compiler_params=pltpu.CompilerParams(vmem_limit_bytes=VMEM_LIMIT),
     )(got, means)
+
+
+def pair_kernel(keep, got, *outs):
+    parity = lax.axis_index("clu") % 2
+    per_owner = keep.shape[1]
+    for k, out in enumerate(outs):
+        out[pl.ds(pl.multiple_of(parity * per_owner, per_owner), per_owner), :] = keep[k]
+        out[pl.ds(pl.multiple_of((1 - parity) * per_owner, per_owner), per_owner), :] = got[k]
+
+
+def pair_up(keep, got):
+    chips, per_owner, width = keep.shape
+    return pl.pallas_call(
+        pair_kernel,
+        out_shape=[jax.ShapeDtypeStruct((2 * per_owner, width), BF16)] * chips,
+        compiler_params=SMALL,
+    )(keep, got)
 
 
 def spread_heads(rows):
@@ -189,7 +213,8 @@
 
     def body(b, carry):
         at = pl.multiple_of(b * block, block)
-        slot = iota((block, targets), 0) + at
+        chip = lax.shift_right_logical(lax.axis_index("clu"), 1) ^ b
+        slot = iota((block, targets), 0) + chip * block
         found = jnp.zeros((block, targets), F32)
         for i in range(count):
             found = jnp.where(picks[i : i + 1, :] == slot, 1.0, found)
@@ -226,12 +251,13 @@
     return out
 
 
-def attention_kernel(
-    scale, raw, enc, weights, queries, out_grad, bias, query_heads, mixed_heads, back, grad_query, keep, send, grads
-):
-    pooled, width = raw.shape
+def attention_kernel(scale, chips, *refs):
+    raws = refs[:chips]
+    enc, weights, queries, out_grad, bias, query_heads, mixed_heads = refs[chips : chips + 7]
+    back, grad_query, keep, send, grads = refs[chips + 7 :]
+    per_chip, width = raws[0].shape
     targets = queries.shape[0]
-    raw_pool = raw[...]
+    raw_pool = jnp.concatenate([raw[...] for raw in raws], axis=0)
     emb = dot(raw_pool, enc[...]).astype(BF16)
     key = dot(emb, weights[1]).astype(BF16)
     value = dot(emb, weights[2]).astype(BF16)
@@ -240,40 +266,41 @@
     pair_bias = jnp.concatenate([bias[...], bias[...]], axis=1)
     head_size = width // HEADS
     upper = iota((2 * head_size, targets), 0) < head_size
-    mixed_parts, qproj_parts = [], []
-    key_grad = jnp.zeros((pooled, width), F32)
-    value_grad = jnp.zeros((pooled, width), F32)
+    mixed_parts, qproj_parts, key_parts, value_parts = [], [], [], []
     for pair in range(HEADS // 2):
         rows = slice(pair * 2 * targets, (pair + 1) * 2 * targets)
-        query_pair = query_heads[rows, :]
-        mixed_pair = mixed_heads[rows, :]
-        scores = dot_nt(key, query_pair) + pair_bias
+        wide = slice(pair * 2 * head_size, (pair + 1) * 2 * head_size)
+        query_pair = query_heads[rows, wide]
+        mixed_pair = mixed_heads[rows, wide]
+        scores = dot_nt(key[:, wide], query_pair) + pair_bias
         raised = jnp.exp(scores - jnp.max(scores, axis=0, keepdims=True))
         attend = raised * (1.0 / jnp.sum(raised, axis=0, keepdims=True))
         attend_low = attend.astype(BF16)
-        weighted = attend * dot_nt(value, mixed_pair)
+        weighted = attend * dot_nt(value[:, wide], mixed_pair)
         score_low = (weighted - attend * jnp.sum(weighted, axis=0, keepdims=True)).astype(BF16)
-        value_grad = value_grad + dot(attend_low, mixed_pair)
-        key_grad = key_grad + dot(score_low, query_pair)
-        wide = slice(pair * 2 * head_size, (pair + 1) * 2 * head_size)
+        value_parts.append(dot(attend_low, mixed_pair).astype(BF16))
+        key_parts.append(dot(score_low, query_pair).astype(BF16))
         mixed_both = dot(value_t[wide], attend_low)
         qproj_both = dot(key_t[wide], score_low)
         mixed_parts.append(jnp.where(upper, mixed_both[:, :targets], mixed_both[:, targets:]))
         qproj_parts.append(jnp.where(upper, qproj_both[:, :targets], qproj_both[:, targets:]))
-    mixed_t = jnp.concatenate(mixed_parts, axis=0)
-    qproj_t = jnp.concatenate(qproj_parts, axis=0)
-    grad_qproj = (qproj_t * scale).T.astype(BF16)
+    mixed_t = jnp.concatenate(mixed_parts, axis=0).astype(BF16)
+    grad_qproj = (jnp.concatenate(qproj_parts, axis=0) * scale).T.astype(BF16)
     grad_query[...] = dot_nt(grad_qproj, weights[0]).astype(BF16)
-    key_low = key_grad.astype(BF16)
-    value_low = value_grad.astype(BF16)
+    key_low = jnp.concatenate(key_parts, axis=1)
+    value_low = jnp.concatenate(value_parts, axis=1)
     emb_grad = (dot_nt(key_low, weights[1]) + dot_nt(value_low, weights[2])).astype(BF16)
-    grads[0:width, :] = dot_tn(queries[...], grad_qproj)
-    grads[width : 2 * width, :] = dot_tn(emb, key_low)
-    grads[2 * width : 3 * width, :] = dot_tn(emb, value_low)
-    grads[3 * width : 4 * width, :] = dot(mixed_t.astype(BF16), out_grad[...])
-    grads[4 * width : 5 * width, :] = dot_tn(raw_pool, emb_grad)
-    back[...] = emb_grad
-    core = lax.axis_index("clu") % 2
+    both = dot_tn(emb, jnp.concatenate([key_low, value_low], axis=1))
+    grads[0:width, :] = dot_tn(queries[...], grad_qproj).astype(BF16)
+    grads[width : 2 * width, :] = both[:, :width].astype(BF16)
+    grads[2 * width : 3 * width, :] = both[:, width:].astype(BF16)
+    grads[3 * width : 4 * width, :] = dot(mixed_t, out_grad[...]).astype(BF16)
+    grads[4 * width : 5 * width, :] = dot_tn(raw_pool, emb_grad).astype(BF16)
+    me = lax.axis_index("clu")
+    for k in range(chips):
+        at = pl.multiple_of((lax.shift_right_logical(me, 1) ^ k) * per_chip, per_chip)
+        back[pl.ds(at, per_chip), :] = emb_grad[k * per_chip : (k + 1) * per_chip]
+    core = me % 2
     pieces, _, part, _ = keep.shape
     for q in range(pieces):
         base = 2 * mirrored(q, pieces)
@@ -281,24 +308,24 @@
             at = m * width + base * part
             kept = pl.ds(pl.multiple_of(at + core * part, part), part)
             given = pl.ds(pl.multiple_of(at + (1 - core) * part, part), part)
-            keep[q, m] = grads[kept, :].astype(BF16)
-            send[q, m] = grads[given, :].astype(BF16)
-
-
-def attention(scale, owners, raw_pool, enc, weights, queries, out_grad, bias, query_heads, mixed_heads):
-    pooled, width = raw_pool.shape
+            keep[q, m] = grads[kept, :]
+            send[q, m] = grads[given, :]
+
+
+def attention(scale, owners, raws, enc, weights, queries, out_grad, bias, query_heads, mixed_heads):
+    pooled, width = bias.shape[0], enc.shape[0]
     half = jax.ShapeDtypeStruct((owners // 4, MATRICES, 2 * width // owners, width), BF16)
     return pl.pallas_call(
-        functools.partial(attention_kernel, scale),
+        functools.partial(attention_kernel, scale, len(raws)),
         out_shape=[
             jax.ShapeDtypeStruct((pooled, width), BF16),
             jax.ShapeDtypeStruct(queries.shape, BF16),
             half,
             half,
         ],
-        scratch_shapes=[pltpu.VMEM((MATRICES * width, width), F32)],
+        scratch_shapes=[pltpu.VMEM((MATRICES * width, width), BF16)],
         compiler_params=pltpu.CompilerParams(vmem_limit_bytes=VMEM_LIMIT),
-    )(raw_pool, enc, weights, queries, out_grad, bias, query_heads, mixed_heads)
+    )(*raws, enc, weights, queries, out_grad, bias, query_heads, mixed_heads)
 
 
 def add_low(a, b):
@@ -422,13 +449,15 @@
     asking = jnp.broadcast_to(pairs, (owners // 2, 2, 1, LANES)).reshape(owners, 1, LANES)
     got = swap(asking).reshape(owners, LANES)
     means, table = cluster_means(counts, member_rows, raw_rows)
-    onehot_t, sent = select_rows(got, means, pooled)
-    raw_pool = swap(sent.reshape(owners, pooled // owners, width)).reshape(pooled, width)
+    onehot_t, keep, give = select_rows(got, means, pooled)
+    paired = pair_up(keep, exchange(1, give))
+    far_first = {k: exchange(2 * k, paired[k]) for k in range(owners // 2 - 1, 0, -1)}
+    raws = [paired[0]] + [far_first[k] for k in range(1, owners // 2)]
     bias, query_heads, mixed_heads = target_terms(
         scale, picks.T, queries, out_grad, attn_weights, pooled
     )
     back, grad_query, keep, given = attention(
-        scale, owners, raw_pool, enc_weight, attn_weights, queries, out_grad, bias, query_heads, mixed_heads
+        scale, owners, raws, enc_weight, attn_weights, queries, out_grad, bias, query_heads, mixed_heads
     )
     keep, given = split(1, keep, exchange(1, given), keep.size)
     given, back = lax.optimization_barrier((given, back))

time: 79.4 us -> 78.6 us (0.990)
  starting transfers between devices: 27.3 us -> 34.2 us
  waiting for transfers between devices: 27.7 us -> 21 us
  Pallas kernels: 20.3 us -> 19.4 us
    ppermute x8 -> x16, starting transfers between devices: 9.99 us -> 21.4 us  [exchange(): return lax.ppermute(block, 'clu', [(d, d ^ flip) for d in range(owners)])]
    all_to_all x3 -> x2, waiting for transfers between devices: 10.9 us -> 0.4 us  [swap(): lax.all_to_all(blocks, 'clu', split_axis=0, concat_axis=0, tiled=True)]
    all_to_all x3 -> x2, starting transfers between devices: 17.3 us -> 12.8 us  [swap(): lax.all_to_all(blocks, 'clu', split_axis=0, concat_axis=0, tiled=True)]
    ppermute x8 -> x16, waiting for transfers between devices: 16.8 us -> 20.6 us  [exchange(): return lax.ppermute(block, 'clu', [(d, d ^ flip) for d in range(owners)])]
    pallas_call x1, Pallas kernels: 1.28 us -> 0.48 us  [select_rows(): pl.pallas_call(select_kernel, out_shape=[jax.ShapeDtypeStruct((clusters,...]
    pallas_call x1 -> x2, Pallas kernels: 5.22 us -> 5.15 us  [the longest x1 5.1 us: attention(): pl.pallas_call(functools.partial(attention_kernel, scale, len(raws)), out...]
  transfers between devices with their start and end apart: 11 -> 18, of which waited for: 9 -> 11; matrix products, arithmetic and copies ran while one was open for 0% -> 0% of each run, Pallas kernels for 16% -> 16%
where the time goes in v9:
time: 78.6 us; the launch traced here: 78.2 us
  starting transfers between devices  34.2 us (44%)
  waiting for transfers between devices  21 us (27%)
  Pallas kernels  19.4 us (25%)
  local copies, waits for them, and re-layouts  2.81 us (4%)
  between operations  0.81 us (1%)
    ppermute x16, starting transfers between devices, exchange(): return lax.ppermute(block, 'clu', [(d, d ^ flip) for d in range(owners)])  21.4 us
    ppermute x16, waiting for transfers between devices, exchange(): return lax.ppermute(block, 'clu', [(d, d ^ flip) for d in range(owners)])  20.6 us
    all_to_all x2, starting transfers between devices, swap(): lax.all_to_all(blocks, 'clu', split_axis=0, concat_axis=0, tiled=True)  12.8 us
    pallas_call x1, Pallas kernels, attention(): pl.pallas_call(functools.partial(attention_kernel, scale, len(raws)), out...  5.1 us
    pallas_call x1, Pallas kernels, cluster_means(): pl.pallas_call(means_kernel, in_specs=[pl.BlockSpec(memory_space=pltpu.HB...  4.49 us
    pallas_call x1, Pallas kernels, member_grads(): pl.pallas_call(rows_kernel, out_specs=pl.BlockSpec(memory_space=pltpu.HBM...  4.08 us
    pallas_call x1, Pallas kernels, target_terms(): pl.pallas_call(functools.partial(targets_kernel, scale), out_shape=[jax.S...  3.9 us
  transfers between devices with their start and end apart: 18, of which 11 were waited for; matrix products, arithmetic and copies ran while one was open for 0% of the time, Pallas kernels for 16%

profile of v9, /device:TPU:0, one launch (start us, length us, event | category | flops | bytes accessed | tf_op | source)
XLA Modules:
  0.0 78.2 jit_solution(10712141696051629293)
XLA Ops:
  0.7 1.4 %broadcast_in_dim.10 = s32[8,2,128]{2,1,0:T(2,128)} broadcast(s32[8,128]{1,0:T(8,128)} %bitcast.11), dimensions={0,2} | broadcast | bytes 12288 | tf_op jit(solution)/shard_map/broadcast_in_dim | solution.py:449
  2.0 7.4 %all-to-all-start = ((s32[16,1,128]{2,1,0:T(1,128)}), s32[16,1,128]{2,1,0:T(1,128)S(1)}, u32[]{:S(2)}, u32[]{:S(2)}) async-start(s32[16,1,128]{2,1,0:T(1,128)} %bitcast.1), calls=%async_computation | async-start | bytes 16384 | tf_op jit(solution)/shard_map/all_to_all | solution.py:434
  10.9 4.5 %shard_map.120 = (bf16[256,256]{1,0:T(8,128)(2,1)S(1)}, f32[64,128]{1,0:T(8,128)S(1)}) custom-call(s32[1,256]{1,0:T(1,128)S(1)} %copy-done.6, s32[64,128]{1,0:T(8,128)S(1)} %bitcast.9, bf16[8192,256]{1,0:T(8,128)(2,1)} %raw_h.1), custom_call_target="tpu_custom_call" | custom-call | flops 1073741824 | bytes 4194304 | tf_op jit(solution)/shard_map/pallas_call | solution.py:127
  16.3 1.5 %collective-permute-done.got = bf16[8,64,256]{2,1,0:T(8,128)(2,1)S(1)} collective-permute-done((bf16[8,64,256]{2,1,0:T(8,128)(2,1)S(1)}, bf16[8,64,256]{2,1,0:T(8,128)(2,1)S(1)}, u32[]{:S(2)}, u32[]{:S(2)}) %collective-permute-start) | collective-permute-done | bytes 262176 | tf_op jit(solution)/shard_map/ppermute | solution.py:446
  17.9 1.6 %collective-permute-start.1 = (bf16[128,256]{1,0:T(8,128)(2,1)S(1)}, bf16[128,256]{1,0:T(8,128)(2,1)S(1)}, u32[]{:S(2)}, u32[]{:S(2)}) collective-permute-start(bf16[128,256]{1,0:T(8,128)(2,1)S(1)} %get-tuple-element.38), channel_id=1, source_target_pairs={{0,2},{1,3},{2,0},{3,1},{4,6},{5,7},{6,4},{7,5},{8,10},{9,11},{10,... | collective-permute-start | bytes 196616 | tf_op jit(solution)/shard_map/ppermute | solution.py:446
  19.5 1.5 %collective-permute-start.2 = (bf16[128,256]{1,0:T(8,128)(2,1)S(1)}, bf16[128,256]{1,0:T(8,128)(2,1)S(1)}, u32[]{:S(2)}, u32[]{:S(2)}) collective-permute-start(bf16[128,256]{1,0:T(8,128)(2,1)S(1)} %get-tuple-element.39), channel_id=1, source_target_pairs={{0,4},{1,5},{2,6},{3,7},{4,0},{5,1},{6,2},{7,3},{8,12},{9,13},{10,... | collective-permute-start | bytes 196616 | tf_op jit(solution)/shard_map/ppermute | solution.py:446
  21.5 2.4 %collective-permute-start.4 = (bf16[128,256]{1,0:T(8,128)(2,1)S(1)}, bf16[128,256]{1,0:T(8,128)(2,1)S(1)}, u32[]{:S(2)}, u32[]{:S(2)}) collective-permute-start(bf16[128,256]{1,0:T(8,128)(2,1)S(1)} %get-tuple-element.41), channel_id=1, source_target_pairs={{0,8},{1,9},{2,10},{3,11},{4,12},{5,13},{6,14},{7,15},{8,0},{9,1},... | collective-permute-start | bytes 196616 | tf_op jit(solution)/shard_map/ppermute | solution.py:446
  23.9 1.5 %collective-permute-start.5 = (bf16[128,256]{1,0:T(8,128)(2,1)S(1)}, bf16[128,256]{1,0:T(8,128)(2,1)S(1)}, u32[]{:S(2)}, u32[]{:S(2)}) collective-permute-start(bf16[128,256]{1,0:T(8,128)(2,1)S(1)} %get-tuple-element.42), channel_id=1, source_target_pairs={{0,10},{1,11},{2,8},{3,9},{4,14},{5,15},{6,12},{7,13},{8,2},{9,3},... | collective-permute-start | bytes 196616 | tf_op jit(solution)/shard_map/ppermute | solution.py:446
  25.4 3.3 %collective-permute-start.6 = (bf16[128,256]{1,0:T(8,128)(2,1)S(1)}, bf16[128,256]{1,0:T(8,128)(2,1)S(1)}, u32[]{:S(2)}, u32[]{:S(2)}) collective-permute-start(bf16[128,256]{1,0:T(8,128)(2,1)S(1)} %get-tuple-element.43), channel_id=1, source_target_pairs={{0,12},{1,13},{2,14},{3,15},{4,8},{5,9},{6,10},{7,11},{8,4},{9,5},... | collective-permute-start | bytes 196616 | tf_op jit(solution)/shard_map/ppermute | solution.py:446
  29.1 3.9 %shard_map.123 = (f32[1024,128]{1,0:T(8,128)S(1)}, bf16[512,256]{1,0:T(8,128)(2,1)S(1)}, bf16[512,256]{1,0:T(8,128)(2,1)S(1)}) custom-call(s32[100,128]{1,0:T(8,128)S(1)} %bitcast.8, bf16[128,256]{1,0:T(8,128)(2,1)S(1)} %copy-done.1, bf16[128,256]{1,0:T(8,128)(2,1)S(1)} %copy-done.2, bf16[4,256,256]{2,1,0:T(8,128)(2,1)S(1)} %copy-done), custom_call_target="tpu_custom_call" | custom-call | flops 52428800 | bytes 524288 | tf_op jit(solution)/shard_map/pallas_call | solution.py:229
  33.1 1.2 %collective-permute-done.5.refs_5_ = bf16[128,256]{1,0:T(8,128)(2,1)S(1)} collective-permute-done((bf16[128,256]{1,0:T(8,128)(2,1)S(1)}, bf16[128,256]{1,0:T(8,128)(2,1)S(1)}, u32[]{:S(2)}, u32[]{:S(2)}) %collective-permute-start.5) | collective-permute-done | bytes 65568 | tf_op jit(solution)/shard_map/ppermute | solution.py:446
  34.2 1.5 %collective-permute-done.7.refs_7_ = bf16[128,256]{1,0:T(8,128)(2,1)S(1)} collective-permute-done((bf16[128,256]{1,0:T(8,128)(2,1)S(1)}, bf16[128,256]{1,0:T(8,128)(2,1)S(1)}, u32[]{:S(2)}, u32[]{:S(2)}) %collective-permute-start.7) | collective-permute-done | bytes 65568 | tf_op jit(solution)/shard_map/ppermute | solution.py:446
  35.7 5.1 %shard_map.124 = (bf16[1024,256]{1,0:T(8,128)(2,1)}, bf16[128,256]{1,0:T(8,128)(2,1)}, bf16[4,5,32,256]{3,2,1,0:T(8,128)(2,1)S(1)}, bf16[4,5,32,256]{3,2,1,0:T(8,128)(2,1)S(1)}) custom-call(bf16[128,256]{1,0:T(8,128)(2,1)S(1)} %get-tuple-element.37.refs_0_, bf16[128,256]{1,0:T(8,128)(2,1)S(1)} %collective-permute-done.1.refs_1_, ...), custom_call_target="tpu_custom_call" | custom-call | tf_op jit(solution)/shard_map/pallas_call | solution.py:318
  40.8 1.6 %collective-permute-done.8.got = bf16[4,5,32,256]{3,2,1,0:T(8,128)(2,1)S(1)} collective-permute-done((bf16[4,5,32,256]{3,2,1,0:T(8,128)(2,1)S(1)}, bf16[4,5,32,256]{3,2,1,0:T(8,128)(2,1)S(1)}, u32[]{:S(2)}, u32[]{:S(2)}) %collective-permute-start.8) | collective-permute-done | bytes 327712 | tf_op jit(solution)/shard_map/ppermute | solution.py:446
  43.2 5.4 %all-to-all-start.1 = ((bf16[16,64,256]{2,1,0:T(8,128)(2,1)}), bf16[16,64,256]{2,1,0:T(8,128)(2,1)S(1)}, u32[]{:S(2)}, u32[]{:S(2)}) async-start(bf16[16,64,256]{2,1,0:T(8,128)(2,1)} %bitcast.5), calls=%async_computation.1 | async-start | bytes 1048576 | tf_op jit(solution)/shard_map/all_to_all | solution.py:434
  48.9 2.0 %collective-permute-start.10 = (bf16[1,5,32,256]{3,2,1,0:T(8,128)(2,1)S(1)}, bf16[1,5,32,256]{3,2,1,0:T(8,128)(2,1)S(1)}, u32[]{:S(2)}, u32[]{:S(2)}) collective-permute-start(bf16[1,5,32,256]{3,2,1,0:T(8,128)(2,1)S(1)} %get-tuple-element.56), channel_id=1, source_target_pairs={{0,4},{1,5},{2,6},{3,7},{4,0},{5,1},{6,2},{7,3},{8,12},{9,13},{10,... | collective-permute-start | bytes 245768 | tf_op jit(solution)/shard_map/ppermute | solution.py:446
  50.9 9.7 %collective-permute-done.10.b = bf16[1,5,32,256]{3,2,1,0:T(8,128)(2,1)S(1)} collective-permute-done((bf16[1,5,32,256]{3,2,1,0:T(8,128)(2,1)S(1)}, bf16[1,5,32,256]{3,2,1,0:T(8,128)(2,1)S(1)}, u32[]{:S(2)}, u32[]{:S(2)}) %collective-permute-start.10) | collective-permute-done | bytes 81952 | tf_op jit(solution)/shard_map/ppermute | solution.py:446
  60.7 3.8 %collective-permute-start.11 = (bf16[1,5,32,256]{3,2,1,0:T(8,128)(2,1)S(1)}, bf16[1,5,32,256]{3,2,1,0:T(8,128)(2,1)S(1)}, u32[]{:S(2)}, u32[]{:S(2)}) collective-permute-start(bf16[1,5,32,256]{3,2,1,0:T(8,128)(2,1)S(1)} %shard_map.127.a), channel_id=1, source_target_pairs={{0,8},{1,9},{2,10},{3,11},{4,12},{5,13},{6,14},{7,15},{8,0},{9,1},... | collective-permute-start | bytes 245768 | tf_op jit(solution)/shard_map/ppermute | solution.py:446
  64.5 4.1 %shard_map.128 = bf16[8192,256]{1,0:T(8,128)(2,1)} custom-call(s32[1,256]{1,0:T(1,128)S(1)} %copy-done.7, bf16[256,1024]{1,0:T(8,128)(2,1)S(1)} %get-tuple-element.57.onehot_t, f32[64,128]{1,0:T(8,128)S(1)} %get-tuple-element.58.table, bf16[1024,256]{1,0:T(8,128)(2,1)S(1)} %bitcast.7), custom_call_target="tpu_custom_call" | custom-call | flops 1073741824 | bytes 4194304 | tf_op jit(solution)/shard_map/pallas_call | solution.py:417
  69.1 1.1 %collective-permute-start.13 = (bf16[1,5,32,256]{3,2,1,0:T(8,128)(2,1)S(1)}, bf16[1,5,32,256]{3,2,1,0:T(8,128)(2,1)S(1)}, u32[]{:S(2)}, u32[]{:S(2)}) collective-permute-start(bf16[1,5,32,256]{3,2,1,0:T(8,128)(2,1)S(1)} %shard_map.129), channel_id=1, source_target_pairs={{0,2},{1,3},{2,0},{3,1},{4,6},{5,7},{6,4},{7,5},{8,10},{9,11},{10,... | collective-permute-start | bytes 245768 | tf_op jit(solution)/shard_map/ppermute | solution.py:446
  70.2 1.9 %collective-permute-start.12 = (bf16[1,5,32,256]{3,2,1,0:T(8,128)(2,1)S(1)}, bf16[1,5,32,256]{3,2,1,0:T(8,128)(2,1)S(1)}, u32[]{:S(2)}, u32[]{:S(2)}) collective-permute-start(bf16[1,5,32,256]{3,2,1,0:T(8,128)(2,1)S(1)} %shard_map.129), channel_id=1, source_target_pairs={{0,4},{1,5},{2,6},{3,7},{4,0},{5,1},{6,2},{7,3},{8,12},{9,13},{10,... | collective-permute-start | bytes 245768 | tf_op jit(solution)/shard_map/ppermute | solution.py:446
  72.1 2.6 %collective-permute-done.14 = bf16[1,5,32,256]{3,2,1,0:T(8,128)(2,1)S(1)} collective-permute-done((bf16[1,5,32,256]{3,2,1,0:T(8,128)(2,1)S(1)}, bf16[1,5,32,256]{3,2,1,0:T(8,128)(2,1)S(1)}, u32[]{:S(2)}, u32[]{:S(2)}) %collective-permute-start.14) | collective-permute-done | bytes 81952 | tf_op jit(solution)/shard_map/ppermute | solution.py:446
  75.5 1.6 %collective-permute-done.15.refs_1_ = bf16[4,5,32,256]{3,2,1,0:T(8,128)(2,1)S(1)} collective-permute-done((bf16[4,5,32,256]{3,2,1,0:T(8,128)(2,1)S(1)}, bf16[4,5,32,256]{3,2,1,0:T(8,128)(2,1)S(1)}, u32[]{:S(2)}, u32[]{:S(2)}) %collective-permute-start.15) | collective-permute-done | bytes 327712 | tf_op jit(solution)/shard_map/ppermute | solution.py:446
  77.1 1.1 %shard_map.130 = (f32[4,256,256]{2,1,0:T(8,128)}, f32[256,256]{1,0:T(8,128)}) custom-call(bf16[4,5,32,256]{3,2,1,0:T(8,128)(2,1)S(1)} %pad_maximum_fusion.refs_0_, bf16[4,5,32,256]{3,2,1,0:T(8,128)(2,1)S(1)} %collective-permute-done.15.refs_1_), custom_call_target="tpu_custom_call" | custom-call | tf_op jit(solution)/shard_map/pallas_call | solution.py:379
  (41 shorter events, 5.7 us)
Async XLA Ops:
  0.6 28.5 %copy-start.2 = (bf16[128,256]{1,0:T(8,128)(2,1)S(1)}, bf16[128,256]{1,0:T(8,128)(2,1)}, u32[]{:S(2)}) copy-start(bf16[128,256]{1,0:T(8,128)(2,1)} %refs_11_.1) | copy-start | bytes 196612
  0.6 28.5 %copy-start = (bf16[4,256,256]{2,1,0:T(8,128)(2,1)S(1)}, bf16[4,256,256]{2,1,0:T(8,128)(2,1)}, u32[]{:S(2)}) copy-start(bf16[4,256,256]{2,1,0:T(8,128)(2,1)} %refs_9_.1) | copy-start | bytes 1572868
  0.7 28.5 %copy-start.1 = (bf16[128,256]{1,0:T(8,128)(2,1)S(1)}, bf16[128,256]{1,0:T(8,128)(2,1)}, u32[]{:S(2)}) copy-start(bf16[128,256]{1,0:T(8,128)(2,1)} %refs_10_.1) | copy-start | bytes 196612
  0.7 28.5 %copy-start.4 = (s32[128,100]{0,1:T(8,128)S(1)}, s32[128,100]{0,1:T(8,128)}, u32[]{:S(2)}) copy-start(s32[128,100]{0,1:T(8,128)} %param.14) | copy-start | bytes 153604
  0.7 35.0 %copy-start.3 = (bf16[256,256]{1,0:T(8,128)(2,1)S(1)}, bf16[256,256]{1,0:T(8,128)(2,1)}, u32[]{:S(2)}) copy-start(bf16[256,256]{1,0:T(8,128)(2,1)} %refs_8_.1) | copy-start | bytes 393220
  2.0 13.7 %all-to-all-start = ((s32[16,1,128]{2,1,0:T(1,128)}), s32[16,1,128]{2,1,0:T(1,128)S(1)}, u32[]{:S(2)}, u32[]{:S(2)}) async-start(s32[16,1,128]{2,1,0:T(1,128)} %bitcast.1), calls=%async_computation | async-start | bytes 16384 | tf_op jit(solution)/shard_map/all_to_all | solution.py:434
  16.3 1.6 %collective-permute-start = (bf16[8,64,256]{2,1,0:T(8,128)(2,1)S(1)}, bf16[8,64,256]{2,1,0:T(8,128)(2,1)S(1)}, u32[]{:S(2)}, u32[]{:S(2)}) collective-permute-start(bf16[8,64,256]{2,1,0:T(8,128)(2,1)S(1)} %get-tuple-element.36), channel_id=1, source_target_pairs={{0,1},{1,0},{2,3},{3,2},{4,5},{5,4},{6,7},{7,6},{8,9},{9,8},{10,11... | collective-permute-start | bytes 786440 | tf_op jit(solution)/shard_map/ppermute | solution.py:446
  17.9 7.5 %collective-permute-start.1 = (bf16[128,256]{1,0:T(8,128)(2,1)S(1)}, bf16[128,256]{1,0:T(8,128)(2,1)S(1)}, u32[]{:S(2)}, u32[]{:S(2)}) collective-permute-start(bf16[128,256]{1,0:T(8,128)(2,1)S(1)} %get-tuple-element.38), channel_id=1, source_target_pairs={{0,2},{1,3},{2,0},{3,1},{4,6},{5,7},{6,4},{7,5},{8,10},{9,11},{10,... | collective-permute-start | bytes 196616 | tf_op jit(solution)/shard_map/ppermute | solution.py:446
  19.5 9.1 %collective-permute-start.2 = (bf16[128,256]{1,0:T(8,128)(2,1)S(1)}, bf16[128,256]{1,0:T(8,128)(2,1)S(1)}, u32[]{:S(2)}, u32[]{:S(2)}) collective-permute-start(bf16[128,256]{1,0:T(8,128)(2,1)S(1)} %get-tuple-element.39), channel_id=1, source_target_pairs={{0,4},{1,5},{2,6},{3,7},{4,0},{5,1},{6,2},{7,3},{8,12},{9,13},{10,... | collective-permute-start | bytes 196616 | tf_op jit(solution)/shard_map/ppermute | solution.py:446
  21.0 12.1 %collective-permute-start.3 = (bf16[128,256]{1,0:T(8,128)(2,1)S(1)}, bf16[128,256]{1,0:T(8,128)(2,1)S(1)}, u32[]{:S(2)}, u32[]{:S(2)}) collective-permute-start(bf16[128,256]{1,0:T(8,128)(2,1)S(1)} %get-tuple-element.40), channel_id=1, source_target_pairs={{0,6},{1,7},{2,4},{3,5},{4,2},{5,3},{6,0},{7,1},{8,14},{9,15},{10,... | collective-permute-start | bytes 196616 | tf_op jit(solution)/shard_map/ppermute | solution.py:446
  21.5 11.6 %collective-permute-start.4 = (bf16[128,256]{1,0:T(8,128)(2,1)S(1)}, bf16[128,256]{1,0:T(8,128)(2,1)S(1)}, u32[]{:S(2)}, u32[]{:S(2)}) collective-permute-start(bf16[128,256]{1,0:T(8,128)(2,1)S(1)} %get-tuple-element.41), channel_id=1, source_target_pairs={{0,8},{1,9},{2,10},{3,11},{4,12},{5,13},{6,14},{7,15},{8,0},{9,1},... | collective-permute-start | bytes 196616 | tf_op jit(solution)/shard_map/ppermute | solution.py:446
  23.9 10.3 %collective-permute-start.5 = (bf16[128,256]{1,0:T(8,128)(2,1)S(1)}, bf16[128,256]{1,0:T(8,128)(2,1)S(1)}, u32[]{:S(2)}, u32[]{:S(2)}) collective-permute-start(bf16[128,256]{1,0:T(8,128)(2,1)S(1)} %get-tuple-element.42), channel_id=1, source_target_pairs={{0,10},{1,11},{2,8},{3,9},{4,14},{5,15},{6,12},{7,13},{8,2},{9,3},... | collective-permute-start | bytes 196616 | tf_op jit(solution)/shard_map/ppermute | solution.py:446
  25.4 8.9 %collective-permute-start.6 = (bf16[128,256]{1,0:T(8,128)(2,1)S(1)}, bf16[128,256]{1,0:T(8,128)(2,1)S(1)}, u32[]{:S(2)}, u32[]{:S(2)}) collective-permute-start(bf16[128,256]{1,0:T(8,128)(2,1)S(1)} %get-tuple-element.43), channel_id=1, source_target_pairs={{0,12},{1,13},{2,14},{3,15},{4,8},{5,9},{6,10},{7,11},{8,4},{9,5},... | collective-permute-start | bytes 196616 | tf_op jit(solution)/shard_map/ppermute | solution.py:446
  28.6 7.1 %collective-permute-start.7 = (bf16[128,256]{1,0:T(8,128)(2,1)S(1)}, bf16[128,256]{1,0:T(8,128)(2,1)S(1)}, u32[]{:S(2)}, u32[]{:S(2)}) collective-permute-start(bf16[128,256]{1,0:T(8,128)(2,1)S(1)} %get-tuple-element.44), channel_id=1, source_target_pairs={{0,14},{1,15},{2,12},{3,13},{4,10},{5,11},{6,8},{7,9},{8,6},{9,7},... | collective-permute-start | bytes 196616 | tf_op jit(solution)/shard_map/ppermute | solution.py:446
  40.8 1.6 %collective-permute-start.8 = (bf16[4,5,32,256]{3,2,1,0:T(8,128)(2,1)S(1)}, bf16[4,5,32,256]{3,2,1,0:T(8,128)(2,1)S(1)}, u32[]{:S(2)}, u32[]{:S(2)}) collective-permute-start(bf16[4,5,32,256]{3,2,1,0:T(8,128)(2,1)S(1)} %get-tuple-element.50), channel_id=1, source_target_pairs={{0,1},{1,0},{2,3},{3,2},{4,5},{5,4},{6,7},{7,6},{8,9},{9,8},{10,11... | collective-permute-start | bytes 983048 | tf_op jit(solution)/shard_map/ppermute | solution.py:446
  42.5 6.3 %collective-permute-start.9 = (bf16[2,5,32,256]{3,2,1,0:T(8,128)(2,1)S(1)}, bf16[2,5,32,256]{3,2,1,0:T(8,128)(2,1)S(1)}, u32[]{:S(2)}, u32[]{:S(2)}) collective-permute-start(bf16[2,5,32,256]{3,2,1,0:T(8,128)(2,1)S(1)} %get-tuple-element.54), channel_id=1, source_target_pairs={{0,2},{1,3},{2,0},{3,1},{4,6},{5,7},{6,4},{7,5},{8,10},{9,11},{10,... | collective-permute-start | bytes 491528 | tf_op jit(solution)/shard_map/ppermute | solution.py:446
  43.2 21.3 %all-to-all-start.1 = ((bf16[16,64,256]{2,1,0:T(8,128)(2,1)}), bf16[16,64,256]{2,1,0:T(8,128)(2,1)S(1)}, u32[]{:S(2)}, u32[]{:S(2)}) async-start(bf16[16,64,256]{2,1,0:T(8,128)(2,1)} %bitcast.5), calls=%async_computation.1 | async-start | bytes 1048576 | tf_op jit(solution)/shard_map/all_to_all | solution.py:434
  48.8 15.6 %copy-start.7 = (s32[1,256]{1,0:T(1,128)S(1)}, s32[1,256]{1,0:T(1,128)}, u32[]{:S(2)}) copy-start(s32[1,256]{1,0:T(1,128)} %counts.1) | copy-start | bytes 3076
  48.9 11.8 %collective-permute-start.10 = (bf16[1,5,32,256]{3,2,1,0:T(8,128)(2,1)S(1)}, bf16[1,5,32,256]{3,2,1,0:T(8,128)(2,1)S(1)}, u32[]{:S(2)}, u32[]{:S(2)}) collective-permute-start(bf16[1,5,32,256]{3,2,1,0:T(8,128)(2,1)S(1)} %get-tuple-element.56), channel_id=1, source_target_pairs={{0,4},{1,5},{2,6},{3,7},{4,0},{5,1},{6,2},{7,3},{8,12},{9,13},{10,... | collective-permute-start | bytes 245768 | tf_op jit(solution)/shard_map/ppermute | solution.py:446
  60.7 7.9 %collective-permute-start.11 = (bf16[1,5,32,256]{3,2,1,0:T(8,128)(2,1)S(1)}, bf16[1,5,32,256]{3,2,1,0:T(8,128)(2,1)S(1)}, u32[]{:S(2)}, u32[]{:S(2)}) collective-permute-start(bf16[1,5,32,256]{3,2,1,0:T(8,128)(2,1)S(1)} %shard_map.127.a), channel_id=1, source_target_pairs={{0,8},{1,9},{2,10},{3,11},{4,12},{5,13},{6,14},{7,15},{8,0},{9,1},... | collective-permute-start | bytes 245768 | tf_op jit(solution)/shard_map/ppermute | solution.py:446
  68.6 6.2 %collective-permute-start.14 = (bf16[1,5,32,256]{3,2,1,0:T(8,128)(2,1)S(1)}, bf16[1,5,32,256]{3,2,1,0:T(8,128)(2,1)S(1)}, u32[]{:S(2)}, u32[]{:S(2)}) collective-permute-start(bf16[1,5,32,256]{3,2,1,0:T(8,128)(2,1)S(1)} %shard_map.129), channel_id=1, source_target_pairs={{0,6},{1,7},{2,4},{3,5},{4,2},{5,3},{6,0},{7,1},{8,14},{9,15},{10,... | collective-permute-start | bytes 245768 | tf_op jit(solution)/shard_map/ppermute | solution.py:446
  69.1 6.1 %collective-permute-start.13 = (bf16[1,5,32,256]{3,2,1,0:T(8,128)(2,1)S(1)}, bf16[1,5,32,256]{3,2,1,0:T(8,128)(2,1)S(1)}, u32[]{:S(2)}, u32[]{:S(2)}) collective-permute-start(bf16[1,5,32,256]{3,2,1,0:T(8,128)(2,1)S(1)} %shard_map.129), channel_id=1, source_target_pairs={{0,2},{1,3},{2,0},{3,1},{4,6},{5,7},{6,4},{7,5},{8,10},{9,11},{10,... | collective-permute-start | bytes 245768 | tf_op jit(solution)/shard_map/ppermute | solution.py:446
  70.2 5.2 %collective-permute-start.12 = (bf16[1,5,32,256]{3,2,1,0:T(8,128)(2,1)S(1)}, bf16[1,5,32,256]{3,2,1,0:T(8,128)(2,1)S(1)}, u32[]{:S(2)}, u32[]{:S(2)}) collective-permute-start(bf16[1,5,32,256]{3,2,1,0:T(8,128)(2,1)S(1)} %shard_map.129), channel_id=1, source_target_pairs={{0,4},{1,5},{2,6},{3,7},{4,0},{5,1},{6,2},{7,3},{8,12},{9,13},{10,... | collective-permute-start | bytes 245768 | tf_op jit(solution)/shard_map/ppermute | solution.py:446
  75.4 1.7 %collective-permute-start.15 = (bf16[4,5,32,256]{3,2,1,0:T(8,128)(2,1)S(1)}, bf16[4,5,32,256]{3,2,1,0:T(8,128)(2,1)S(1)}, u32[]{:S(2)}, u32[]{:S(2)}) collective-permute-start(bf16[4,5,32,256]{3,2,1,0:T(8,128)(2,1)S(1)} %pad_maximum_fusion.refs_0_), channel_id=1, source_target_pairs={{0,1},{1,0},{2,3},{3,2},{4,5},{5,4},{6,7},{7,6},{8,9},{9,8},{10,11... | collective-permute-start | bytes 983048 | tf_op jit(solution)/shard_map/ppermute | solution.py:446
  (2 other events, 1.4 us)

commit v10 on v9

--- a/solution.py
+++ b/solution.py
@@ -9,7 +9,6 @@
 
 HEADS = 4
 MATRICES = 5
-WEIGHT = 10**11
 LANES = 128
 F32 = jnp.float32
 BF16 = jnp.bfloat16
@@ -147,7 +146,7 @@
 
 def select_kernel(got, means, onehot_t, keep, give):
     clusters = means.shape[0]
-    chips, per_owner, _ = keep.shape
+    chips = keep.shape[0]
     me = lax.axis_index("clu")
     parity = me % 2
     half = LANES // 2
@@ -158,14 +157,18 @@
     left = iota((1, LANES), 1) < half
     for k in range(chips):
         row = jnp.where(left, first[2 * k : 2 * k + 1], second[2 * k + 1 : 2 * k + 2])
-        onehot_t[:, k * LANES : (k + 1) * LANES] = ones_where(row == iota((clusters, LANES), 0))
-    sent = dot_tn(onehot_t[...], means[...]).astype(BF16)
+        at = pl.multiple_of((lax.shift_right_logical(me, 1) ^ k) * LANES, LANES)
+        onehot_t[:, pl.ds(at, LANES)] = ones_where(row == iota((clusters, LANES), 0))
+    sort_rows(parity, dot_tn(onehot_t[...], means[...]).astype(BF16), keep, give)
+
+
+def sort_rows(parity, rows, keep, give):
+    chips, part, _ = keep.shape
     for k in range(chips):
-        place = lax.shift_right_logical(me, 1) ^ k
-        even = sent[2 * k * per_owner : (2 * k + 1) * per_owner]
-        odd = sent[(2 * k + 1) * per_owner : (2 * k + 2) * per_owner]
-        keep[place] = jnp.where(parity == 0, even, odd)
-        give[place] = jnp.where(parity == 0, odd, even)
+        even = rows[2 * k * part : (2 * k + 1) * part]
+        odd = rows[(2 * k + 1) * part : (2 * k + 2) * part]
+        keep[k] = jnp.where(parity == 0, even, odd)
+        give[k] = jnp.where(parity == 0, odd, even)
 
 
 def select_rows(got, means, pooled):
@@ -254,8 +257,8 @@
 def attention_kernel(scale, chips, *refs):
     raws = refs[:chips]
     enc, weights, queries, out_grad, bias, query_heads, mixed_heads = refs[chips : chips + 7]
-    back, grad_query, keep, send, grads = refs[chips + 7 :]
-    per_chip, width = raws[0].shape
+    keep_rows, send_rows, grad_query, keep, send, grads = refs[chips + 7 :]
+    width = enc.shape[0]
     targets = queries.shape[0]
     raw_pool = jnp.concatenate([raw[...] for raw in raws], axis=0)
     emb = dot(raw_pool, enc[...]).astype(BF16)
@@ -296,11 +299,8 @@
     grads[2 * width : 3 * width, :] = both[:, width:].astype(BF16)
     grads[3 * width : 4 * width, :] = dot(mixed_t, out_grad[...]).astype(BF16)
     grads[4 * width : 5 * width, :] = dot_tn(raw_pool, emb_grad).astype(BF16)
-    me = lax.axis_index("clu")
-    for k in range(chips):
-        at = pl.multiple_of((lax.shift_right_logical(me, 1) ^ k) * per_chip, per_chip)
-        back[pl.ds(at, per_chip), :] = emb_grad[k * per_chip : (k + 1) * per_chip]
-    core = me % 2
+    core = lax.axis_index("clu") % 2
+    sort_rows(core, emb_grad, keep_rows, send_rows)
     pieces, _, part, _ = keep.shape
     for q in range(pieces):
         base = 2 * mirrored(q, pieces)
@@ -313,12 +313,14 @@
 
 
 def attention(scale, owners, raws, enc, weights, queries, out_grad, bias, query_heads, mixed_heads):
-    pooled, width = bias.shape[0], enc.shape[0]
+    width = enc.shape[0]
     half = jax.ShapeDtypeStruct((owners // 4, MATRICES, 2 * width // owners, width), BF16)
+    rows = jax.ShapeDtypeStruct((len(raws), raws[0].shape[0] // 2, width), BF16)
     return pl.pallas_call(
         functools.partial(attention_kernel, scale, len(raws)),
         out_shape=[
-            jax.ShapeDtypeStruct((pooled, width), BF16),
+            rows,
+            rows,
             jax.ShapeDtypeStruct(queries.shape, BF16),
             half,
             half,
@@ -342,13 +344,12 @@
         given[i] = add_low(keep[other], got[other])
 
 
-def split(bit, keep, got, flops):
+def split(bit, keep, got):
     half = jax.ShapeDtypeStruct((keep.shape[0] // 2,) + keep.shape[1:], BF16)
     return pl.pallas_call(
         functools.partial(split_kernel, bit),
         out_shape=[half, half],
         compiler_params=SMALL,
-        cost_estimate=pl.CostEstimate(flops=flops, bytes_accessed=4 * keep.size, transcendentals=0),
     )(keep, got)
 
 
@@ -386,9 +387,10 @@
     )(*[piece for piece, _ in pieces])
 
 
-def rows_kernel(counts, onehot_t, table, back, out, share, filled, sem):
+def rows_kernel(counts, onehot_t, table, *refs):
+    *backs, out, share, filled, sem = refs
     clusters = counts.shape[1]
-    total = dot(onehot_t[...], back[...])
+    total = dot(onehot_t[...], jnp.concatenate([back[...] for back in backs], axis=0))
     share[...] = (total / column_of(counts[...].astype(F32))).astype(BF16)
 
     def block(k):
@@ -411,9 +413,9 @@
     lax.fori_loop(0, blocks, finish, 0)
 
 
-def member_grads(counts, onehot_t, table, back, rows):
+def member_grads(counts, onehot_t, table, backs, rows):
     clusters = counts.shape[1]
-    width = back.shape[1]
+    width = backs[0].shape[1]
     return pl.pallas_call(
         rows_kernel,
         out_specs=pl.BlockSpec(memory_space=pltpu.HBM),
@@ -427,7 +429,7 @@
         cost_estimate=pl.CostEstimate(
             flops=2 * rows * clusters * width, bytes_accessed=2 * rows * width, transcendentals=0
         ),
-    )(counts, onehot_t, table, back)
+    )(counts, onehot_t, table, *backs)
 
 
 def swap(blocks):
@@ -456,26 +458,42 @@
     bias, query_heads, mixed_heads = target_terms(
         scale, picks.T, queries, out_grad, attn_weights, pooled
     )
-    back, grad_query, keep, given = attention(
+    keep_rows, give_rows, grad_query, keep, given = attention(
         scale, owners, raws, enc_weight, attn_weights, queries, out_grad, bias, query_heads, mixed_heads
     )
-    keep, given = split(1, keep, exchange(1, given), keep.size)
-    given, back = lax.optimization_barrier((given, back))
-    got = exchange(2, given)
-    back = swap(back.reshape(owners, pooled // owners, width)).reshape(pooled, width)
-    keep, given = split(2, keep, got, WEIGHT)
-    for bit in range(2, bits - 2):
-        keep, given = split(bit + 1, keep, exchange(1 << bit, given), keep.size)
-    own = sum_rows(keep, exchange(owners // 4, given))
-    got = exchange(owners // 2, own)
-    grad_rows = member_grads(counts, onehot_t, table, back, rows)
-    got, grad_rows = lax.optimization_barrier((got, grad_rows))
+    got, got_rows = exchange(1, given), exchange(1, give_rows)
+    keep, given = split(1, keep, got)
+    paired = pair_up(keep_rows, got_rows)
+    backs = {0: paired[0]}
+    far_first = list(range(owners // 2 - 1, 0, -1))
+    batch = -(-len(far_first) // (bits - 1))
+
+    def beside_rows(flip, block, kept):
+        now = far_first[:batch]
+        del far_first[:batch]
+        block, *rows_now = lax.optimization_barrier((block, *[paired[k] for k in now]))
+        got = exchange(flip, block)
+        passed = [exchange(2 * k, rows_k) for k, rows_k in zip(now, rows_now)]
+        got, kept, *passed = lax.optimization_barrier((got, kept, *passed))
+        backs.update(zip(now, passed))
+        return got, kept
+
+    for bit in range(1, bits - 2):
+        got, keep = beside_rows(1 << bit, given, keep)
+        keep, given = split(bit + 1, keep, got)
+    got, keep = beside_rows(owners // 4, given, keep)
+    own = sum_rows(keep, got)
+    got, own = beside_rows(owners // 2, own, own)
     own = sum_rows(own, got)
     masks = [0]
     for bit in range(bits - 2, 2, -1):
         own = jnp.concatenate([own, exchange(1 << bit, own)])
         masks = masks + [mask ^ (1 << bit) for mask in masks]
-    chip = jnp.concatenate([own] + [exchange(flip, own) for flip in (4, 2, 6)])
+    passed = [exchange(flip, own) for flip in (4, 2, 6)]
+    in_order = [backs[k] for k in range(owners // 2)]
+    grad_rows = member_grads(counts, onehot_t, table, in_order, rows)
+    passed, grad_rows = lax.optimization_barrier((passed, grad_rows))
+    chip = jnp.concatenate([own] + passed)
     masks = [mask ^ flip for flip in (0, 4, 2, 6) for mask in masks]
     beside = exchange(1, chip)
     grad_attn, grad_encoder = place([(chip, masks), (beside, [mask ^ 1 for mask in masks])])

time: 78.6 us -> 82.8 us (1.053)
  starting transfers between devices: 34.2 us -> 37 us
  waiting for transfers between devices: 21 us -> 22.3 us
    ppermute x16 -> x24, starting transfers between devices: 21.4 us -> 29.6 us  [exchange(): return lax.ppermute(block, 'clu', [(d, d ^ flip) for d in range(owners)])]
    all_to_all x2 -> x1, starting transfers between devices: 12.8 us -> 7.39 us  [swap(): lax.all_to_all(blocks, 'clu', split_axis=0, concat_axis=0, tiled=True)]
    ppermute x16 -> x24, waiting for transfers between devices: 20.6 us -> 22 us  [exchange(): return lax.ppermute(block, 'clu', [(d, d ^ flip) for d in range(owners)])]
  transfers between devices with their start and end apart: 18 -> 25, of which waited for: 11 -> 14; matrix products, arithmetic and copies ran while one was open for 0% -> 0% of each run, Pallas kernels for 16% -> 15%
where the time goes in v10:
time: 82.8 us; the launch traced here: 82.5 us
  starting transfers between devices  37 us (45%)
  waiting for transfers between devices  22.3 us (27%)
  Pallas kernels  19.5 us (24%)
  local copies, waits for them, and re-layouts  2.81 us (3%)
  between operations  0.85 us (1%)
    ppermute x24, starting transfers between devices, exchange(): return lax.ppermute(block, 'clu', [(d, d ^ flip) for d in range(owners)])  29.6 us
    ppermute x24, waiting for transfers between devices, exchange(): return lax.ppermute(block, 'clu', [(d, d ^ flip) for d in range(owners)])  22 us
    all_to_all x1, starting transfers between devices, swap(): lax.all_to_all(blocks, 'clu', split_axis=0, concat_axis=0, tiled=True)  7.39 us
    pallas_call x1, Pallas kernels, attention(): pl.pallas_call(functools.partial(attention_kernel, scale, len(raws)), out...  4.91 us
    pallas_call x1, Pallas kernels, cluster_means(): pl.pallas_call(means_kernel, in_specs=[pl.BlockSpec(memory_space=pltpu.HB...  4.5 us
    pallas_call x1, Pallas kernels, member_grads(): pl.pallas_call(rows_kernel, out_specs=pl.BlockSpec(memory_space=pltpu.HBM...  4.09 us
    pallas_call x1, Pallas kernels, target_terms(): pl.pallas_call(functools.partial(targets_kernel, scale), out_shape=[jax.S...  3.9 us
  transfers between devices with their start and end apart: 25, of which 14 were waited for; matrix products, arithmetic and copies ran while one was open for 0% of the time, Pallas kernels for 15%

profile of v10, /device:TPU:0, one launch (start us, length us, event | category | flops | bytes accessed | tf_op | source)
XLA Modules:
  0.0 82.5 jit_solution(3453036370646011730)
XLA Ops:
  2.0 7.4 %all-to-all-start = ((s32[16,1,128]{2,1,0:T(1,128)}), s32[16,1,128]{2,1,0:T(1,128)S(1)}, u32[]{:S(2)}, u32[]{:S(2)}) async-start(s32[16,1,128]{2,1,0:T(1,128)} %bitcast.1), calls=%async_computation | async-start | bytes 16384 | tf_op jit(solution)/shard_map/all_to_all | solution.py:436
  10.9 4.5 %shard_map.120 = (bf16[256,256]{1,0:T(8,128)(2,1)S(1)}, f32[64,128]{1,0:T(8,128)S(1)}) custom-call(s32[1,256]{1,0:T(1,128)S(1)} %copy-done.6, s32[64,128]{1,0:T(8,128)S(1)} %bitcast.6, bf16[8192,256]{1,0:T(8,128)(2,1)} %raw_h.1), custom_call_target="tpu_custom_call" | custom-call | flops 1073741824 | bytes 4194304 | tf_op jit(solution)/shard_map/pallas_call | solution.py:126
  16.5 1.5 %collective-permute-done.got = bf16[8,64,256]{2,1,0:T(8,128)(2,1)S(1)} collective-permute-done((bf16[8,64,256]{2,1,0:T(8,128)(2,1)S(1)}, bf16[8,64,256]{2,1,0:T(8,128)(2,1)S(1)}, u32[]{:S(2)}, u32[]{:S(2)}) %collective-permute-start) | collective-permute-done | bytes 262176 | tf_op jit(solution)/shard_map/ppermute | solution.py:448
  18.1 1.6 %collective-permute-start.1 = (bf16[128,256]{1,0:T(8,128)(2,1)S(1)}, bf16[128,256]{1,0:T(8,128)(2,1)S(1)}, u32[]{:S(2)}, u32[]{:S(2)}) collective-permute-start(bf16[128,256]{1,0:T(8,128)(2,1)S(1)} %get-tuple-element.70), channel_id=1, source_target_pairs={{0,2},{1,3},{2,0},{3,1},{4,6},{5,7},{6,4},{7,5},{8,10},{9,11},{10,... | collective-permute-start | bytes 196616 | tf_op jit(solution)/shard_map/ppermute | solution.py:448
  19.7 1.5 %collective-permute-start.2 = (bf16[128,256]{1,0:T(8,128)(2,1)S(1)}, bf16[128,256]{1,0:T(8,128)(2,1)S(1)}, u32[]{:S(2)}, u32[]{:S(2)}) collective-permute-start(bf16[128,256]{1,0:T(8,128)(2,1)S(1)} %get-tuple-element.71), channel_id=1, source_target_pairs={{0,4},{1,5},{2,6},{3,7},{4,0},{5,1},{6,2},{7,3},{8,12},{9,13},{10,... | collective-permute-start | bytes 196616 | tf_op jit(solution)/shard_map/ppermute | solution.py:448
  21.6 2.5 %collective-permute-start.4 = (bf16[128,256]{1,0:T(8,128)(2,1)S(1)}, bf16[128,256]{1,0:T(8,128)(2,1)S(1)}, u32[]{:S(2)}, u32[]{:S(2)}) collective-permute-start(bf16[128,256]{1,0:T(8,128)(2,1)S(1)} %get-tuple-element.73), channel_id=1, source_target_pairs={{0,8},{1,9},{2,10},{3,11},{4,12},{5,13},{6,14},{7,15},{8,0},{9,1},... | collective-permute-start | bytes 196616 | tf_op jit(solution)/shard_map/ppermute | solution.py:448
  24.1 1.5 %collective-permute-start.5 = (bf16[128,256]{1,0:T(8,128)(2,1)S(1)}, bf16[128,256]{1,0:T(8,128)(2,1)S(1)}, u32[]{:S(2)}, u32[]{:S(2)}) collective-permute-start(bf16[128,256]{1,0:T(8,128)(2,1)S(1)} %get-tuple-element.74), channel_id=1, source_target_pairs={{0,10},{1,11},{2,8},{3,9},{4,14},{5,15},{6,12},{7,13},{8,2},{9,3},... | collective-permute-start | bytes 196616 | tf_op jit(solution)/shard_map/ppermute | solution.py:448
  25.6 3.3 %collective-permute-start.6 = (bf16[128,256]{1,0:T(8,128)(2,1)S(1)}, bf16[128,256]{1,0:T(8,128)(2,1)S(1)}, u32[]{:S(2)}, u32[]{:S(2)}) collective-permute-start(bf16[128,256]{1,0:T(8,128)(2,1)S(1)} %get-tuple-element.75), channel_id=1, source_target_pairs={{0,12},{1,13},{2,14},{3,15},{4,8},{5,9},{6,10},{7,11},{8,4},{9,5},... | collective-permute-start | bytes 196616 | tf_op jit(solution)/shard_map/ppermute | solution.py:448
  29.3 3.9 %shard_map.123 = (f32[1024,128]{1,0:T(8,128)S(1)}, bf16[512,256]{1,0:T(8,128)(2,1)S(1)}, bf16[512,256]{1,0:T(8,128)(2,1)S(1)}) custom-call(s32[100,128]{1,0:T(8,128)S(1)} %bitcast.5, bf16[128,256]{1,0:T(8,128)(2,1)S(1)} %copy-done.1, bf16[128,256]{1,0:T(8,128)(2,1)S(1)} %copy-done.2, bf16[4,256,256]{2,1,0:T(8,128)(2,1)S(1)} %copy-done), custom_call_target="tpu_custom_call" | custom-call | flops 52428800 | bytes 524288 | tf_op jit(solution)/shard_map/pallas_call | solution.py:232
  34.4 1.5 %collective-permute-done.7.refs_7_ = bf16[128,256]{1,0:T(8,128)(2,1)S(1)} collective-permute-done((bf16[128,256]{1,0:T(8,128)(2,1)S(1)}, bf16[128,256]{1,0:T(8,128)(2,1)S(1)}, u32[]{:S(2)}, u32[]{:S(2)}) %collective-permute-start.7) | collective-permute-done | bytes 65568 | tf_op jit(solution)/shard_map/ppermute | solution.py:448
  35.9 4.9 %shard_map.124 = (bf16[8,64,256]{2,1,0:T(8,128)(2,1)S(1)}, bf16[8,64,256]{2,1,0:T(8,128)(2,1)S(1)}, bf16[128,256]{1,0:T(8,128)(2,1)}, bf16[4,5,32,256]{3,2,1,0:T(8,128)(2,1)S(1)}, bf16[4,5,32,256]{3,2,1,0:T(8,128)(2,1)S(1)}) custom-call(bf16[128,256]{1,0:T(8,128)(2,1)S(1)} %get-tuple-element.69.refs_0_, bf16[128,256]{1,0:T(8,128)(2,1)S(1)} %collective-permute-done.1.refs_1_, ...), custom_call_target="tpu_custom_call" | custom-call | tf_op jit(solution)/shard_map/pallas_call | solution.py:319
  41.3 1.5 %collective-permute-done.9.got = bf16[8,64,256]{2,1,0:T(8,128)(2,1)S(1)} collective-permute-done((bf16[8,64,256]{2,1,0:T(8,128)(2,1)S(1)}, bf16[8,64,256]{2,1,0:T(8,128)(2,1)S(1)}, u32[]{:S(2)}, u32[]{:S(2)}) %collective-permute-start.9) | collective-permute-done | bytes 262176 | tf_op jit(solution)/shard_map/ppermute | solution.py:448
  43.6 2.4 %collective-permute-start.11 = (bf16[128,256]{1,0:T(8,128)(2,1)S(1)}, bf16[128,256]{1,0:T(8,128)(2,1)S(1)}, u32[]{:S(2)}, u32[]{:S(2)}) collective-permute-start(bf16[128,256]{1,0:T(8,128)(2,1)S(1)} %get-tuple-element.91), channel_id=1, source_target_pairs={{0,14},{1,15},{2,12},{3,13},{4,10},{5,11},{6,8},{7,9},{8,6},{9,7},... | collective-permute-start | bytes 196616 | tf_op jit(solution)/shard_map/ppermute | solution.py:448
  46.0 2.3 %collective-permute-start.12 = (bf16[128,256]{1,0:T(8,128)(2,1)S(1)}, bf16[128,256]{1,0:T(8,128)(2,1)S(1)}, u32[]{:S(2)}, u32[]{:S(2)}) collective-permute-start(bf16[128,256]{1,0:T(8,128)(2,1)S(1)} %get-tuple-element.92), channel_id=1, source_target_pairs={{0,12},{1,13},{2,14},{3,15},{4,8},{5,9},{6,10},{7,11},{8,4},{9,5},... | collective-permute-start | bytes 196616 | tf_op jit(solution)/shard_map/ppermute | solution.py:448
  50.9 1.8 %collective-permute-done.12.refs_6_ = bf16[128,256]{1,0:T(8,128)(2,1)S(1)} collective-permute-done((bf16[128,256]{1,0:T(8,128)(2,1)S(1)}, bf16[128,256]{1,0:T(8,128)(2,1)S(1)}, u32[]{:S(2)}, u32[]{:S(2)}) %collective-permute-start.12) | collective-permute-done | bytes 65568 | tf_op jit(solution)/shard_map/ppermute | solution.py:448
  52.7 4.5 %collective-permute-done.13.refs_5_ = bf16[128,256]{1,0:T(8,128)(2,1)S(1)} collective-permute-done((bf16[128,256]{1,0:T(8,128)(2,1)S(1)}, bf16[128,256]{1,0:T(8,128)(2,1)S(1)}, u32[]{:S(2)}, u32[]{:S(2)}) %collective-permute-start.13) | collective-permute-done | bytes 65568 | tf_op jit(solution)/shard_map/ppermute | solution.py:448
  57.3 2.4 %collective-permute-start.15 = (bf16[128,256]{1,0:T(8,128)(2,1)S(1)}, bf16[128,256]{1,0:T(8,128)(2,1)S(1)}, u32[]{:S(2)}, u32[]{:S(2)}) collective-permute-start(bf16[128,256]{1,0:T(8,128)(2,1)S(1)} %get-tuple-element.102), channel_id=1, source_target_pairs={{0,8},{1,9},{2,10},{3,11},{4,12},{5,13},{6,14},{7,15},{8,0},{9,1},... | collective-permute-start | bytes 196616 | tf_op jit(solution)/shard_map/ppermute | solution.py:448
  60.4 1.9 %collective-permute-start.17 = (bf16[128,256]{1,0:T(8,128)(2,1)S(1)}, bf16[128,256]{1,0:T(8,128)(2,1)S(1)}, u32[]{:S(2)}, u32[]{:S(2)}) collective-permute-start(bf16[128,256]{1,0:T(8,128)(2,1)S(1)} %get-tuple-element.104), channel_id=1, source_target_pairs={{0,4},{1,5},{2,6},{3,7},{4,0},{5,1},{6,2},{7,3},{8,12},{9,13},{10,... | collective-permute-start | bytes 196616 | tf_op jit(solution)/shard_map/ppermute | solution.py:448
  63.1 2.2 %collective-permute-done.16.refs_3_ = bf16[128,256]{1,0:T(8,128)(2,1)S(1)} collective-permute-done((bf16[128,256]{1,0:T(8,128)(2,1)S(1)}, bf16[128,256]{1,0:T(8,128)(2,1)S(1)}, u32[]{:S(2)}, u32[]{:S(2)}) %collective-permute-start.16) | collective-permute-done | bytes 65568 | tf_op jit(solution)/shard_map/ppermute | solution.py:448
  65.7 1.4 %collective-permute-start.18 = (bf16[1,5,32,256]{3,2,1,0:T(8,128)(2,1)S(1)}, bf16[1,5,32,256]{3,2,1,0:T(8,128)(2,1)S(1)}, u32[]{:S(2)}, u32[]{:S(2)}) collective-permute-start(bf16[1,5,32,256]{3,2,1,0:T(8,128)(2,1)S(1)} %shard_map.128.a), channel_id=1, source_target_pairs={{0,8},{1,9},{2,10},{3,11},{4,12},{5,13},{6,14},{7,15},{8,0},{9,1},... | collective-permute-start | bytes 245768 | tf_op jit(solution)/shard_map/ppermute | solution.py:448
  68.0 3.3 %collective-permute-done.19.refs_1_ = bf16[128,256]{1,0:T(8,128)(2,1)S(1)} collective-permute-done((bf16[128,256]{1,0:T(8,128)(2,1)S(1)}, bf16[128,256]{1,0:T(8,128)(2,1)S(1)}, u32[]{:S(2)}, u32[]{:S(2)}) %collective-permute-start.19) | collective-permute-done | bytes 65568 | tf_op jit(solution)/shard_map/ppermute | solution.py:448
  74.0 1.5 %collective-permute-start.20 = (bf16[1,5,32,256]{3,2,1,0:T(8,128)(2,1)S(1)}, bf16[1,5,32,256]{3,2,1,0:T(8,128)(2,1)S(1)}, u32[]{:S(2)}, u32[]{:S(2)}) collective-permute-start(bf16[1,5,32,256]{3,2,1,0:T(8,128)(2,1)S(1)} %shard_map.129), channel_id=1, source_target_pairs={{0,4},{1,5},{2,6},{3,7},{4,0},{5,1},{6,2},{7,3},{8,12},{9,13},{10,... | collective-permute-start | bytes 245768 | tf_op jit(solution)/shard_map/ppermute | solution.py:448
  75.5 4.1 %shard_map.130 = bf16[8192,256]{1,0:T(8,128)(2,1)} custom-call(s32[1,256]{1,0:T(1,128)S(1)} %copy-done.7, bf16[256,1024]{1,0:T(8,128)(2,1)S(1)} %get-tuple-element.112.onehot_t, f32[64,128]{1,0:T(8,128)S(1)} %get-tuple-element.113.table, bf16[128,256]{1,0:T(8,128)(2,1)S(1)} %get-tuple-element.114.refs_0_, ...), custom_call_target="tpu_custom_call" | custom-call | flops 1073741824 | bytes 4194304 | tf_op jit(solution)/shard_map/pallas_call | solution.py:419
  79.8 1.6 %collective-permute-done.23.refs_1_ = bf16[4,5,32,256]{3,2,1,0:T(8,128)(2,1)S(1)} collective-permute-done((bf16[4,5,32,256]{3,2,1,0:T(8,128)(2,1)S(1)}, bf16[4,5,32,256]{3,2,1,0:T(8,128)(2,1)S(1)}, u32[]{:S(2)}, u32[]{:S(2)}) %collective-permute-start.23) | collective-permute-done | bytes 327712 | tf_op jit(solution)/shard_map/ppermute | solution.py:448
  (56 shorter events, 16.7 us)
Async XLA Ops:
  2.0 13.7 %all-to-all-start = ((s32[16,1,128]{2,1,0:T(1,128)}), s32[16,1,128]{2,1,0:T(1,128)S(1)}, u32[]{:S(2)}, u32[]{:S(2)}) async-start(s32[16,1,128]{2,1,0:T(1,128)} %bitcast.1), calls=%async_computation | async-start | bytes 16384 | tf_op jit(solution)/shard_map/all_to_all | solution.py:436
  18.1 7.5 %collective-permute-start.1 = (bf16[128,256]{1,0:T(8,128)(2,1)S(1)}, bf16[128,256]{1,0:T(8,128)(2,1)S(1)}, u32[]{:S(2)}, u32[]{:S(2)}) collective-permute-start(bf16[128,256]{1,0:T(8,128)(2,1)S(1)} %get-tuple-element.70), channel_id=1, source_target_pairs={{0,2},{1,3},{2,0},{3,1},{4,6},{5,7},{6,4},{7,5},{8,10},{9,11},{10,... | collective-permute-start | bytes 196616 | tf_op jit(solution)/shard_map/ppermute | solution.py:448
  19.7 9.1 %collective-permute-start.2 = (bf16[128,256]{1,0:T(8,128)(2,1)S(1)}, bf16[128,256]{1,0:T(8,128)(2,1)S(1)}, u32[]{:S(2)}, u32[]{:S(2)}) collective-permute-start(bf16[128,256]{1,0:T(8,128)(2,1)S(1)} %get-tuple-element.71), channel_id=1, source_target_pairs={{0,4},{1,5},{2,6},{3,7},{4,0},{5,1},{6,2},{7,3},{8,12},{9,13},{10,... | collective-permute-start | bytes 196616 | tf_op jit(solution)/shard_map/ppermute | solution.py:448
  21.2 12.0 %collective-permute-start.3 = (bf16[128,256]{1,0:T(8,128)(2,1)S(1)}, bf16[128,256]{1,0:T(8,128)(2,1)S(1)}, u32[]{:S(2)}, u32[]{:S(2)}) collective-permute-start(bf16[128,256]{1,0:T(8,128)(2,1)S(1)} %get-tuple-element.72), channel_id=1, source_target_pairs={{0,6},{1,7},{2,4},{3,5},{4,2},{5,3},{6,0},{7,1},{8,14},{9,15},{10,... | collective-permute-start | bytes 196616 | tf_op jit(solution)/shard_map/ppermute | solution.py:448
  21.6 11.6 %collective-permute-start.4 = (bf16[128,256]{1,0:T(8,128)(2,1)S(1)}, bf16[128,256]{1,0:T(8,128)(2,1)S(1)}, u32[]{:S(2)}, u32[]{:S(2)}) collective-permute-start(bf16[128,256]{1,0:T(8,128)(2,1)S(1)} %get-tuple-element.73), channel_id=1, source_target_pairs={{0,8},{1,9},{2,10},{3,11},{4,12},{5,13},{6,14},{7,15},{8,0},{9,1},... | collective-permute-start | bytes 196616 | tf_op jit(solution)/shard_map/ppermute | solution.py:448
  24.1 10.3 %collective-permute-start.5 = (bf16[128,256]{1,0:T(8,128)(2,1)S(1)}, bf16[128,256]{1,0:T(8,128)(2,1)S(1)}, u32[]{:S(2)}, u32[]{:S(2)}) collective-permute-start(bf16[128,256]{1,0:T(8,128)(2,1)S(1)} %get-tuple-element.74), channel_id=1, source_target_pairs={{0,10},{1,11},{2,8},{3,9},{4,14},{5,15},{6,12},{7,13},{8,2},{9,3},... | collective-permute-start | bytes 196616 | tf_op jit(solution)/shard_map/ppermute | solution.py:448
  25.6 8.9 %collective-permute-start.6 = (bf16[128,256]{1,0:T(8,128)(2,1)S(1)}, bf16[128,256]{1,0:T(8,128)(2,1)S(1)}, u32[]{:S(2)}, u32[]{:S(2)}) collective-permute-start(bf16[128,256]{1,0:T(8,128)(2,1)S(1)} %get-tuple-element.75), channel_id=1, source_target_pairs={{0,12},{1,13},{2,14},{3,15},{4,8},{5,9},{6,10},{7,11},{8,4},{9,5},... | collective-permute-start | bytes 196616 | tf_op jit(solution)/shard_map/ppermute | solution.py:448
  28.8 7.1 %collective-permute-start.7 = (bf16[128,256]{1,0:T(8,128)(2,1)S(1)}, bf16[128,256]{1,0:T(8,128)(2,1)S(1)}, u32[]{:S(2)}, u32[]{:S(2)}) collective-permute-start(bf16[128,256]{1,0:T(8,128)(2,1)S(1)} %get-tuple-element.76), channel_id=1, source_target_pairs={{0,14},{1,15},{2,12},{3,13},{4,10},{5,11},{6,8},{7,9},{8,6},{9,7},... | collective-permute-start | bytes 196616 | tf_op jit(solution)/shard_map/ppermute | solution.py:448
  40.8 2.1 %collective-permute-start.8 = (bf16[4,5,32,256]{3,2,1,0:T(8,128)(2,1)S(1)}, bf16[4,5,32,256]{3,2,1,0:T(8,128)(2,1)S(1)}, u32[]{:S(2)}, u32[]{:S(2)}) collective-permute-start(bf16[4,5,32,256]{3,2,1,0:T(8,128)(2,1)S(1)} %get-tuple-element.82), channel_id=1, source_target_pairs={{0,1},{1,0},{2,3},{3,2},{4,5},{5,4},{6,7},{7,6},{8,9},{9,8},{10,11... | collective-permute-start | bytes 983048 | tf_op jit(solution)/shard_map/ppermute | solution.py:448
  40.8 2.0 %collective-permute-start.9 = (bf16[8,64,256]{2,1,0:T(8,128)(2,1)S(1)}, bf16[8,64,256]{2,1,0:T(8,128)(2,1)S(1)}, u32[]{:S(2)}, u32[]{:S(2)}) collective-permute-start(bf16[8,64,256]{2,1,0:T(8,128)(2,1)S(1)} %get-tuple-element.85), channel_id=1, source_target_pairs={{0,1},{1,0},{2,3},{3,2},{4,5},{5,4},{6,7},{7,6},{8,9},{9,8},{10,11... | collective-permute-start | bytes 786440 | tf_op jit(solution)/shard_map/ppermute | solution.py:448
  43.0 14.2 %collective-permute-start.10 = (bf16[2,5,32,256]{3,2,1,0:T(8,128)(2,1)S(1)}, bf16[2,5,32,256]{3,2,1,0:T(8,128)(2,1)S(1)}, u32[]{:S(2)}, u32[]{:S(2)}) collective-permute-start(bf16[2,5,32,256]{3,2,1,0:T(8,128)(2,1)S(1)} %get-tuple-element.89), channel_id=1, source_target_pairs={{0,2},{1,3},{2,0},{3,1},{4,6},{5,7},{6,4},{7,5},{8,10},{9,11},{10,... | collective-permute-start | bytes 491528 | tf_op jit(solution)/shard_map/ppermute | solution.py:448
  43.6 7.3 %collective-permute-start.11 = (bf16[128,256]{1,0:T(8,128)(2,1)S(1)}, bf16[128,256]{1,0:T(8,128)(2,1)S(1)}, u32[]{:S(2)}, u32[]{:S(2)}) collective-permute-start(bf16[128,256]{1,0:T(8,128)(2,1)S(1)} %get-tuple-element.91), channel_id=1, source_target_pairs={{0,14},{1,15},{2,12},{3,13},{4,10},{5,11},{6,8},{7,9},{8,6},{9,7},... | collective-permute-start | bytes 196616 | tf_op jit(solution)/shard_map/ppermute | solution.py:448
  46.0 6.7 %collective-permute-start.12 = (bf16[128,256]{1,0:T(8,128)(2,1)S(1)}, bf16[128,256]{1,0:T(8,128)(2,1)S(1)}, u32[]{:S(2)}, u32[]{:S(2)}) collective-permute-start(bf16[128,256]{1,0:T(8,128)(2,1)S(1)} %get-tuple-element.92), channel_id=1, source_target_pairs={{0,12},{1,13},{2,14},{3,15},{4,8},{5,9},{6,10},{7,11},{8,4},{9,5},... | collective-permute-start | bytes 196616 | tf_op jit(solution)/shard_map/ppermute | solution.py:448
  48.3 8.8 %collective-permute-start.13 = (bf16[128,256]{1,0:T(8,128)(2,1)S(1)}, bf16[128,256]{1,0:T(8,128)(2,1)S(1)}, u32[]{:S(2)}, u32[]{:S(2)}) collective-permute-start(bf16[128,256]{1,0:T(8,128)(2,1)S(1)} %get-tuple-element.93), channel_id=1, source_target_pairs={{0,10},{1,11},{2,8},{3,9},{4,14},{5,15},{6,12},{7,13},{8,2},{9,3},... | collective-permute-start | bytes 196616 | tf_op jit(solution)/shard_map/ppermute | solution.py:448
  57.2 8.4 %collective-permute-start.14 = (bf16[1,5,32,256]{3,2,1,0:T(8,128)(2,1)S(1)}, bf16[1,5,32,256]{3,2,1,0:T(8,128)(2,1)S(1)}, u32[]{:S(2)}, u32[]{:S(2)}) collective-permute-start(bf16[1,5,32,256]{3,2,1,0:T(8,128)(2,1)S(1)} %get-tuple-element.100), channel_id=1, source_target_pairs={{0,4},{1,5},{2,6},{3,7},{4,0},{5,1},{6,2},{7,3},{8,12},{9,13},{10,... | collective-permute-start | bytes 245768 | tf_op jit(solution)/shard_map/ppermute | solution.py:448
  57.3 5.9 %collective-permute-start.15 = (bf16[128,256]{1,0:T(8,128)(2,1)S(1)}, bf16[128,256]{1,0:T(8,128)(2,1)S(1)}, u32[]{:S(2)}, u32[]{:S(2)}) collective-permute-start(bf16[128,256]{1,0:T(8,128)(2,1)S(1)} %get-tuple-element.102), channel_id=1, source_target_pairs={{0,8},{1,9},{2,10},{3,11},{4,12},{5,13},{6,14},{7,15},{8,0},{9,1},... | collective-permute-start | bytes 196616 | tf_op jit(solution)/shard_map/ppermute | solution.py:448
  59.7 5.7 %collective-permute-start.16 = (bf16[128,256]{1,0:T(8,128)(2,1)S(1)}, bf16[128,256]{1,0:T(8,128)(2,1)S(1)}, u32[]{:S(2)}, u32[]{:S(2)}) collective-permute-start(bf16[128,256]{1,0:T(8,128)(2,1)S(1)} %get-tuple-element.103), channel_id=1, source_target_pairs={{0,6},{1,7},{2,4},{3,5},{4,2},{5,3},{6,0},{7,1},{8,14},{9,15},{10,... | collective-permute-start | bytes 196616 | tf_op jit(solution)/shard_map/ppermute | solution.py:448
  60.4 5.2 %collective-permute-start.17 = (bf16[128,256]{1,0:T(8,128)(2,1)S(1)}, bf16[128,256]{1,0:T(8,128)(2,1)S(1)}, u32[]{:S(2)}, u32[]{:S(2)}) collective-permute-start(bf16[128,256]{1,0:T(8,128)(2,1)S(1)} %get-tuple-element.104), channel_id=1, source_target_pairs={{0,4},{1,5},{2,6},{3,7},{4,0},{5,1},{6,2},{7,3},{8,12},{9,13},{10,... | collective-permute-start | bytes 196616 | tf_op jit(solution)/shard_map/ppermute | solution.py:448
  65.7 6.3 %collective-permute-start.18 = (bf16[1,5,32,256]{3,2,1,0:T(8,128)(2,1)S(1)}, bf16[1,5,32,256]{3,2,1,0:T(8,128)(2,1)S(1)}, u32[]{:S(2)}, u32[]{:S(2)}) collective-permute-start(bf16[1,5,32,256]{3,2,1,0:T(8,128)(2,1)S(1)} %shard_map.128.a), channel_id=1, source_target_pairs={{0,8},{1,9},{2,10},{3,11},{4,12},{5,13},{6,14},{7,15},{8,0},{9,1},... | collective-permute-start | bytes 245768 | tf_op jit(solution)/shard_map/ppermute | solution.py:448
  67.1 4.3 %collective-permute-start.19 = (bf16[128,256]{1,0:T(8,128)(2,1)S(1)}, bf16[128,256]{1,0:T(8,128)(2,1)S(1)}, u32[]{:S(2)}, u32[]{:S(2)}) collective-permute-start(bf16[128,256]{1,0:T(8,128)(2,1)S(1)} %get-tuple-element.109), channel_id=1, source_target_pairs={{0,2},{1,3},{2,0},{3,1},{4,6},{5,7},{6,4},{7,5},{8,10},{9,11},{10,... | collective-permute-start | bytes 196616 | tf_op jit(solution)/shard_map/ppermute | solution.py:448
  72.0 7.7 %collective-permute-start.22 = (bf16[1,5,32,256]{3,2,1,0:T(8,128)(2,1)S(1)}, bf16[1,5,32,256]{3,2,1,0:T(8,128)(2,1)S(1)}, u32[]{:S(2)}, u32[]{:S(2)}) collective-permute-start(bf16[1,5,32,256]{3,2,1,0:T(8,128)(2,1)S(1)} %shard_map.129), channel_id=1, source_target_pairs={{0,6},{1,7},{2,4},{3,5},{4,2},{5,3},{6,0},{7,1},{8,14},{9,15},{10,... | collective-permute-start | bytes 245768 | tf_op jit(solution)/shard_map/ppermute | solution.py:448
  73.0 6.6 %collective-permute-start.21 = (bf16[1,5,32,256]{3,2,1,0:T(8,128)(2,1)S(1)}, bf16[1,5,32,256]{3,2,1,0:T(8,128)(2,1)S(1)}, u32[]{:S(2)}, u32[]{:S(2)}) collective-permute-start(bf16[1,5,32,256]{3,2,1,0:T(8,128)(2,1)S(1)} %shard_map.129), channel_id=1, source_target_pairs={{0,2},{1,3},{2,0},{3,1},{4,6},{5,7},{6,4},{7,5},{8,10},{9,11},{10,... | collective-permute-start | bytes 245768 | tf_op jit(solution)/shard_map/ppermute | solution.py:448
  74.0 5.7 %collective-permute-start.20 = (bf16[1,5,32,256]{3,2,1,0:T(8,128)(2,1)S(1)}, bf16[1,5,32,256]{3,2,1,0:T(8,128)(2,1)S(1)}, u32[]{:S(2)}, u32[]{:S(2)}) collective-permute-start(bf16[1,5,32,256]{3,2,1,0:T(8,128)(2,1)S(1)} %shard_map.129), channel_id=1, source_target_pairs={{0,4},{1,5},{2,6},{3,7},{4,0},{5,1},{6,2},{7,3},{8,12},{9,13},{10,... | collective-permute-start | bytes 245768 | tf_op jit(solution)/shard_map/ppermute | solution.py:448
  79.7 1.7 %collective-permute-start.23 = (bf16[4,5,32,256]{3,2,1,0:T(8,128)(2,1)S(1)}, bf16[4,5,32,256]{3,2,1,0:T(8,128)(2,1)S(1)}, u32[]{:S(2)}, u32[]{:S(2)}) collective-permute-start(bf16[4,5,32,256]{3,2,1,0:T(8,128)(2,1)S(1)} %pad_maximum_fusion.refs_0_), channel_id=1, source_target_pairs={{0,1},{1,0},{2,3},{3,2},{4,5},{5,4},{6,7},{7,6},{8,9},{9,8},{10,11... | collective-permute-start | bytes 983048 | tf_op jit(solution)/shard_map/ppermute | solution.py:448
  (9 other events, 217.6 us)

commit v11 on v9

--- a/solution.py
+++ b/solution.py
@@ -145,53 +145,58 @@
     )(counts, members.reshape(groups, LANES), raw_rows)
 
 
-def select_kernel(got, means, onehot_t, keep, give):
+def select_kernel(got, beside, means, onehot_t, keep, give):
     clusters = means.shape[0]
-    chips, per_owner, _ = keep.shape
-    me = lax.axis_index("clu")
-    parity = me % 2
+    parity = lax.axis_index("clu") % 2
     half = LANES // 2
-    wanted = lax.rem(got[...], clusters)
-    turned = pltpu.roll(wanted, half, 1)
-    first = jnp.where(parity == 0, wanted, turned)
-    second = jnp.where(parity == 0, turned, wanted)
-    left = iota((1, LANES), 1) < half
+    even = jnp.where(parity == 0, got[...], beside[...])
+    odd = jnp.where(parity == 0, beside[...], got[...])
+    first = jnp.where(parity == 0, even, pltpu.roll(even, half, 1))
+    second = jnp.where(parity == 0, pltpu.roll(odd, half, 1), odd)
+    wanted = jnp.where(iota(got.shape, 1) < half, first, second)
+    wanted = lax.rem(wanted, clusters)
+    for k in range(got.shape[0]):
+        onehot_t[:, k * LANES : (k + 1) * LANES] = ones_where(
+            wanted[k : k + 1] == iota((clusters, LANES), 0)
+        )
+    sort_rows(parity, dot_tn(onehot_t[...], means[...]).astype(BF16), keep, give)
+
+
+def sort_rows(parity, rows, keep, give):
+    chips, part, _ = keep.shape
     for k in range(chips):
-        row = jnp.where(left, first[2 * k : 2 * k + 1], second[2 * k + 1 : 2 * k + 2])
-        onehot_t[:, k * LANES : (k + 1) * LANES] = ones_where(row == iota((clusters, LANES), 0))
-    sent = dot_tn(onehot_t[...], means[...]).astype(BF16)
-    for k in range(chips):
-        place = lax.shift_right_logical(me, 1) ^ k
-        even = sent[2 * k * per_owner : (2 * k + 1) * per_owner]
-        odd = sent[(2 * k + 1) * per_owner : (2 * k + 2) * per_owner]
-        keep[place] = jnp.where(parity == 0, even, odd)
-        give[place] = jnp.where(parity == 0, odd, even)
-
-
-def select_rows(got, means, pooled):
+        even = rows[2 * k * part : (2 * k + 1) * part]
+        odd = rows[(2 * k + 1) * part : (2 * k + 2) * part]
+        keep[k] = jnp.where(parity == 0, even, odd)
+        give[k] = jnp.where(parity == 0, odd, even)
+
+
+def select_rows(got, beside, means, pooled):
     clusters, width = means.shape
-    chips = got.shape[0] // 2
+    chips = got.shape[0]
     half = jax.ShapeDtypeStruct((chips, pooled // chips // 2, width), BF16)
     return pl.pallas_call(
         select_kernel,
         out_shape=[jax.ShapeDtypeStruct((clusters, pooled), BF16), half, half],
         compiler_params=pltpu.CompilerParams(vmem_limit_bytes=VMEM_LIMIT),
-    )(got, means)
-
-
-def pair_kernel(keep, got, *outs):
+    )(got, beside, means)
+
+
+def pair_kernel(keep, got, out):
     parity = lax.axis_index("clu") % 2
-    per_owner = keep.shape[1]
-    for k, out in enumerate(outs):
-        out[pl.ds(pl.multiple_of(parity * per_owner, per_owner), per_owner), :] = keep[k]
-        out[pl.ds(pl.multiple_of((1 - parity) * per_owner, per_owner), per_owner), :] = got[k]
+    chips, part, _ = keep.shape
+    own = pl.ds(pl.multiple_of(parity * part, part), part)
+    other = pl.ds(pl.multiple_of((1 - parity) * part, part), part)
+    for k in range(chips):
+        out[k, own, :] = keep[k]
+        out[k, other, :] = got[k]
 
 
 def pair_up(keep, got):
-    chips, per_owner, width = keep.shape
+    chips, part, width = keep.shape
     return pl.pallas_call(
         pair_kernel,
-        out_shape=[jax.ShapeDtypeStruct((2 * per_owner, width), BF16)] * chips,
+        out_shape=jax.ShapeDtypeStruct((chips, 2 * part, width), BF16),
         compiler_params=SMALL,
     )(keep, got)
 
@@ -213,8 +218,7 @@
 
     def body(b, carry):
         at = pl.multiple_of(b * block, block)
-        chip = lax.shift_right_logical(lax.axis_index("clu"), 1) ^ b
-        slot = iota((block, targets), 0) + chip * block
+        slot = iota((block, targets), 0) + at
         found = jnp.zeros((block, targets), F32)
         for i in range(count):
             found = jnp.where(picks[i : i + 1, :] == slot, 1.0, found)
@@ -251,13 +255,13 @@
     return out
 
 
-def attention_kernel(scale, chips, *refs):
-    raws = refs[:chips]
-    enc, weights, queries, out_grad, bias, query_heads, mixed_heads = refs[chips : chips + 7]
-    back, grad_query, keep, send, grads = refs[chips + 7 :]
-    per_chip, width = raws[0].shape
+def attention_kernel(
+    scale, raw, enc, weights, queries, out_grad, bias, query_heads, mixed_heads,
+    keep_rows, give_rows, grad_query, keep, send, grads,
+):
+    width = enc.shape[0]
     targets = queries.shape[0]
-    raw_pool = jnp.concatenate([raw[...] for raw in raws], axis=0)
+    raw_pool = raw[...]
     emb = dot(raw_pool, enc[...]).astype(BF16)
     key = dot(emb, weights[1]).astype(BF16)
     value = dot(emb, weights[2]).astype(BF16)
@@ -296,11 +300,8 @@
     grads[2 * width : 3 * width, :] = both[:, width:].astype(BF16)
     grads[3 * width : 4 * width, :] = dot(mixed_t, out_grad[...]).astype(BF16)
     grads[4 * width : 5 * width, :] = dot_tn(raw_pool, emb_grad).astype(BF16)
-    me = lax.axis_index("clu")
-    for k in range(chips):
-        at = pl.multiple_of((lax.shift_right_logical(me, 1) ^ k) * per_chip, per_chip)
-        back[pl.ds(at, per_chip), :] = emb_grad[k * per_chip : (k + 1) * per_chip]
-    core = me % 2
+    core = lax.axis_index("clu") % 2
+    sort_rows(core, emb_grad, keep_rows, give_rows)
     pieces, _, part, _ = keep.shape
     for q in range(pieces):
         base = 2 * mirrored(q, pieces)
@@ -312,20 +313,23 @@
             send[q, m] = grads[given, :]
 
 
-def attention(scale, owners, raws, enc, weights, queries, out_grad, bias, query_heads, mixed_heads):
-    pooled, width = bias.shape[0], enc.shape[0]
+def attention(scale, owners, raw_pool, enc, weights, queries, out_grad, bias, query_heads, mixed_heads):
+    width = enc.shape[0]
     half = jax.ShapeDtypeStruct((owners // 4, MATRICES, 2 * width // owners, width), BF16)
-    return pl.pallas_call(
-        functools.partial(attention_kernel, scale, len(raws)),
+    chips = owners // 2
+    rows = jax.ShapeDtypeStruct((chips, raw_pool.shape[0] // owners, width), BF16)
+    return pl.pallas_call(
+        functools.partial(attention_kernel, scale),
         out_shape=[
-            jax.ShapeDtypeStruct((pooled, width), BF16),
+            rows,
+            rows,
             jax.ShapeDtypeStruct(queries.shape, BF16),
             half,
             half,
         ],
         scratch_shapes=[pltpu.VMEM((MATRICES * width, width), BF16)],
         compiler_params=pltpu.CompilerParams(vmem_limit_bytes=VMEM_LIMIT),
-    )(*raws, enc, weights, queries, out_grad, bias, query_heads, mixed_heads)
+    )(raw_pool, enc, weights, queries, out_grad, bias, query_heads, mixed_heads)
 
 
 def add_low(a, b):
@@ -430,10 +434,6 @@
     )(counts, onehot_t, table, back)
 
 
-def swap(blocks):
-    return lax.all_to_all(blocks, "clu", split_axis=0, concat_axis=0, tiled=True)
-
-
 def local(raw_rows, enc_weight, counts, member_rows, pool, picks, queries, attn_weights, out_grad):
     rows, width = raw_rows.shape
     owners = lax.axis_size("clu")
@@ -445,24 +445,31 @@
     def exchange(flip, block):
         return lax.ppermute(block, "clu", [(d, d ^ flip) for d in range(owners)])
 
-    pairs = pool.reshape(owners // 2, 1, 1, LANES)
-    asking = jnp.broadcast_to(pairs, (owners // 2, 2, 1, LANES)).reshape(owners, 1, LANES)
-    got = swap(asking).reshape(owners, LANES)
+    def swap(blocks):
+        groups = [list(range(core, owners, 2)) for core in range(2)]
+        return lax.all_to_all(
+            blocks, "clu", split_axis=0, concat_axis=0, axis_index_groups=groups, tiled=True
+        )
+
+    chips = owners // 2
+    got = swap(pool.reshape(chips, 1, LANES))
     means, table = cluster_means(counts, member_rows, raw_rows)
-    onehot_t, keep, give = select_rows(got, means, pooled)
-    paired = pair_up(keep, exchange(1, give))
-    far_first = {k: exchange(2 * k, paired[k]) for k in range(owners // 2 - 1, 0, -1)}
-    raws = [paired[0]] + [far_first[k] for k in range(1, owners // 2)]
+    beside = exchange(1, got)
+    got, beside = got.reshape(chips, LANES), beside.reshape(chips, LANES)
+    onehot_t, keep, give = select_rows(got, beside, means, pooled)
+    raw_pool = swap(pair_up(keep, exchange(1, give))).reshape(pooled, width)
     bias, query_heads, mixed_heads = target_terms(
         scale, picks.T, queries, out_grad, attn_weights, pooled
     )
-    back, grad_query, keep, given = attention(
-        scale, owners, raws, enc_weight, attn_weights, queries, out_grad, bias, query_heads, mixed_heads
+    keep_rows, give_rows, grad_query, keep, given = attention(
+        scale, owners, raw_pool, enc_weight, attn_weights, queries, out_grad, bias, query_heads, mixed_heads
     )
-    keep, given = split(1, keep, exchange(1, given), keep.size)
+    got, got_rows = exchange(1, given), exchange(1, give_rows)
+    keep, given = split(1, keep, got, keep.size)
+    back = pair_up(keep_rows, got_rows)
     given, back = lax.optimization_barrier((given, back))
     got = exchange(2, given)
-    back = swap(back.reshape(owners, pooled // owners, width)).reshape(pooled, width)
+    back = swap(back).reshape(pooled, width)
     keep, given = split(2, keep, got, WEIGHT)
     for bit in range(2, bits - 2):
         keep, given = split(bit + 1, keep, exchange(1 << bit, given), keep.size)

time: 78.6 us -> 84.1 us (1.070)
  starting transfers between devices: 34.2 us -> 18.4 us
  blocking collectives: 0 us -> 13.8 us
  waiting for transfers between devices: 21 us -> 28.3 us
  Pallas kernels: 19.4 us -> 20.8 us
  local copies, waits for them, and re-layouts: 2.81 us -> 1.46 us
    all_to_all x0 -> x1, blocking collectives: none -> 13.8 us  [swap(): lax.all_to_all(blocks, 'clu', split_axis=0, concat_axis=0, axis_index_gro...]
    all_to_all x2, waiting for transfers between devices: 0.4 us -> 11.3 us  [swap(): lax.all_to_all(blocks, 'clu', split_axis=0, concat_axis=0, axis_index_gro...]
    ppermute x16 -> x11, starting transfers between devices: 21.4 us -> 11.4 us  [exchange(): return lax.ppermute(block, 'clu', [(d, d ^ flip) for d in range(owners)])]
    all_to_all x2, starting transfers between devices: 12.8 us -> 6.99 us  [swap(): lax.all_to_all(blocks, 'clu', split_axis=0, concat_axis=0, axis_index_gro...]
    ppermute x16 -> x11, waiting for transfers between devices: 20.6 us -> 17 us  [exchange(): return lax.ppermute(block, 'clu', [(d, d ^ flip) for d in range(owners)])]
    pallas_call x2 -> x3, Pallas kernels: 5.15 us -> 6.58 us  [the longest x1 4.9 us: attention(): pl.pallas_call(functools.partial(attention_kernel, scale), out_shape=[row...]
    broadcast_in_dim x1 -> x0, local copies, waits for them, and re-layouts: 1.36 us -> none  [local(): jnp.broadcast_to(pairs, (owners // 2, 2, 1, LANES))]
  transfers between devices with their start and end apart: 18 -> 13, of which waited for: 11 -> 9; matrix products, arithmetic and copies ran while one was open for 0% -> 0% of each run, Pallas kernels for 16% -> 16%
where the time goes in v11:
time: 84.1 us; the launch traced here: 83.7 us
  waiting for transfers between devices  28.3 us (34%)
  Pallas kernels  20.8 us (25%)
  starting transfers between devices  18.4 us (22%)
  blocking collectives  13.8 us (16%)
  local copies, waits for them, and re-layouts  1.46 us (2%)
    ppermute x11, waiting for transfers between devices, exchange(): return lax.ppermute(block, 'clu', [(d, d ^ flip) for d in range(owners)])  17 us
    all_to_all x1, blocking collectives, swap(): lax.all_to_all(blocks, 'clu', split_axis=0, concat_axis=0, axis_index_gro...  13.8 us
    ppermute x11, starting transfers between devices, exchange(): return lax.ppermute(block, 'clu', [(d, d ^ flip) for d in range(owners)])  11.4 us
    all_to_all x2, waiting for transfers between devices, swap(): lax.all_to_all(blocks, 'clu', split_axis=0, concat_axis=0, axis_index_gro...  11.3 us
    all_to_all x2, starting transfers between devices, swap(): lax.all_to_all(blocks, 'clu', split_axis=0, concat_axis=0, axis_index_gro...  6.99 us
    pallas_call x1, Pallas kernels, attention(): pl.pallas_call(functools.partial(attention_kernel, scale), out_shape=[row...  4.9 us
    pallas_call x1, Pallas kernels, cluster_means(): pl.pallas_call(means_kernel, in_specs=[pl.BlockSpec(memory_space=pltpu.HB...  4.49 us
    pallas_call x1, Pallas kernels, member_grads(): pl.pallas_call(rows_kernel, out_specs=pl.BlockSpec(memory_space=pltpu.HBM...  4.08 us
  transfers between devices with their start and end apart: 13, of which 9 were waited for; matrix products, arithmetic and copies ran while one was open for 0% of the time, Pallas kernels for 16%

profile of v11, /device:TPU:0, one launch (start us, length us, event | category | flops | bytes accessed | tf_op | source)
XLA Modules:
  0.0 83.7 jit_solution(8191640974085879471)
XLA Ops:
  0.7 13.8 %all_to_all.15 = s32[8,1,128]{2,1,0:T(1,128)S(1)} all-to-all(s32[8,1,128]{2,1,0:T(1,128)} %bitcast.15), channel_id=1, replica_groups={{0,2,4,6,8,10,12,14},{1,3,5,7,9,11,13,15},{16,18,20,22,24,26,28,30},{17..., dimensions={0} | all-to-all | bytes 8192 | tf_op jit(solution)/shard_map/all_to_all | solution.py:450
  14.5 0.8 copy-done.5
  15.3 0.7 copy-done.6
  15.9 4.5 %shard_map.120 = (bf16[256,256]{1,0:T(8,128)(2,1)S(1)}, f32[64,128]{1,0:T(8,128)S(1)}) custom-call(s32[1,256]{1,0:T(1,128)S(1)} %copy-done.6, s32[64,128]{1,0:T(8,128)S(1)} %bitcast.11, bf16[8192,256]{1,0:T(8,128)(2,1)} %raw_h.1), custom_call_target="tpu_custom_call" | custom-call | flops 1073741824 | bytes 4194304 | tf_op jit(solution)/shard_map/pallas_call | solution.py:127
  21.5 1.2 %collective-permute-done.1.got = bf16[8,64,256]{2,1,0:T(8,128)(2,1)S(1)} collective-permute-done((bf16[8,64,256]{2,1,0:T(8,128)(2,1)S(1)}, bf16[8,64,256]{2,1,0:T(8,128)(2,1)S(1)}, u32[]{:S(2)}, u32[]{:S(2)}) %collective-permute-start.1) | collective-permute-done | bytes 262176 | tf_op jit(solution)/shard_map/ppermute | solution.py:446
  22.7 0.8 %shard_map.122 = bf16[8,128,256]{2,1,0:T(8,128)(2,1)} custom-call(bf16[8,64,256]{2,1,0:T(8,128)(2,1)S(1)} %get-tuple-element.28.keep, bf16[8,64,256]{2,1,0:T(8,128)(2,1)S(1)} %collective-permute-done.1.got), custom_call_target="tpu_custom_call" | custom-call | tf_op jit(solution)/shard_map/pallas_call | solution.py:197
  23.5 3.5 %all-to-all-start.1 = ((bf16[8,128,256]{2,1,0:T(8,128)(2,1)}), bf16[8,128,256]{2,1,0:T(8,128)(2,1)S(1)}, u32[]{:S(2)}, u32[]{:S(2)}) async-start(bf16[8,128,256]{2,1,0:T(8,128)(2,1)} %shard_map.122), calls=%async_computation.1 | async-start | bytes 1048576 | tf_op jit(solution)/shard_map/all_to_all | solution.py:450
  27.1 3.9 %shard_map.123 = (f32[1024,128]{1,0:T(8,128)S(1)}, bf16[512,256]{1,0:T(8,128)(2,1)S(1)}, bf16[512,256]{1,0:T(8,128)(2,1)S(1)}) custom-call(s32[100,128]{1,0:T(8,128)S(1)} %bitcast.10, bf16[128,256]{1,0:T(8,128)(2,1)S(1)} %copy-done.1, bf16[128,256]{1,0:T(8,128)(2,1)S(1)} %copy-done.2, bf16[4,256,256]{2,1,0:T(8,128)(2,1)S(1)} %copy-done), custom_call_target="tpu_custom_call" | custom-call | flops 52428800 | bytes 524288 | tf_op jit(solution)/shard_map/pallas_call | solution.py:233
  30.9 11.3 %all-to-all-done.1 = bf16[8,128,256]{2,1,0:T(8,128)(2,1)S(1)} async-done(((bf16[8,128,256]{2,1,0:T(8,128)(2,1)}), bf16[8,128,256]{2,1,0:T(8,128)(2,1)S(1)}, u32[]{:S(2)}, u32[]{:S(2)}) %all-to-all-start.1) | async-done | bytes 524320 | tf_op jit(solution)/shard_map/all_to_all | solution.py:450
  42.2 4.9 %shard_map.124 = (bf16[8,64,256]{2,1,0:T(8,128)(2,1)S(1)}, bf16[8,64,256]{2,1,0:T(8,128)(2,1)S(1)}, bf16[128,256]{1,0:T(8,128)(2,1)}, bf16[4,5,32,256]{3,2,1,0:T(8,128)(2,1)S(1)}, bf16[4,5,32,256]{3,2,1,0:T(8,128)(2,1)S(1)}) custom-call(bf16[1024,256]{1,0:T(8,128)(2,1)S(1)} %bitcast.9, bf16[256,256]{1,0:T(8,128)(2,1)S(1)} %copy-done.3, ...), custom_call_target="tpu_custom_call" | custom-call | tf_op jit(solution)/shard_map/pallas_call | solution.py:321
  47.7 1.5 %collective-permute-done.3.got = bf16[8,64,256]{2,1,0:T(8,128)(2,1)S(1)} collective-permute-done((bf16[8,64,256]{2,1,0:T(8,128)(2,1)S(1)}, bf16[8,64,256]{2,1,0:T(8,128)(2,1)S(1)}, u32[]{:S(2)}, u32[]{:S(2)}) %collective-permute-start.3) | collective-permute-done | bytes 262176 | tf_op jit(solution)/shard_map/ppermute | solution.py:446
  49.2 0.8 %shard_map.126 = bf16[8,128,256]{2,1,0:T(8,128)(2,1)} custom-call(bf16[8,64,256]{2,1,0:T(8,128)(2,1)S(1)} %get-tuple-element.38.keep, bf16[8,64,256]{2,1,0:T(8,128)(2,1)S(1)} %collective-permute-done.3.got), custom_call_target="tpu_custom_call" | custom-call | tf_op jit(solution)/shard_map/pallas_call | solution.py:197
  50.1 1.5 %collective-permute-start.4 = (bf16[2,5,32,256]{3,2,1,0:T(8,128)(2,1)S(1)}, bf16[2,5,32,256]{3,2,1,0:T(8,128)(2,1)S(1)}, u32[]{:S(2)}, u32[]{:S(2)}) collective-permute-start(bf16[2,5,32,256]{3,2,1,0:T(8,128)(2,1)S(1)} %get-tuple-element.40), channel_id=1, source_target_pairs={{0,2},{1,3},{2,0},{3,1},{4,6},{5,7},{6,4},{7,5},{8,10},{9,11},{10,... | collective-permute-start | bytes 491528 | tf_op jit(solution)/shard_map/ppermute | solution.py:446
  51.6 3.5 %all-to-all-start.2 = ((bf16[8,128,256]{2,1,0:T(8,128)(2,1)}), bf16[8,128,256]{2,1,0:T(8,128)(2,1)S(1)}, u32[]{:S(2)}, u32[]{:S(2)}) async-start(bf16[8,128,256]{2,1,0:T(8,128)(2,1)} %shard_map.126), calls=%async_computation.2 | async-start | bytes 1048576 | tf_op jit(solution)/shard_map/all_to_all | solution.py:450
  55.1 1.3 %collective-permute-done.4.got = bf16[2,5,32,256]{3,2,1,0:T(8,128)(2,1)S(1)} collective-permute-done((bf16[2,5,32,256]{3,2,1,0:T(8,128)(2,1)S(1)}, bf16[2,5,32,256]{3,2,1,0:T(8,128)(2,1)S(1)}, u32[]{:S(2)}, u32[]{:S(2)}) %collective-permute-start.4) | collective-permute-done | bytes 163872 | tf_op jit(solution)/shard_map/ppermute | solution.py:446
  56.4 0.7 collective-permute-start.5
  57.2 8.7 %collective-permute-done.5.b = bf16[1,5,32,256]{3,2,1,0:T(8,128)(2,1)S(1)} collective-permute-done((bf16[1,5,32,256]{3,2,1,0:T(8,128)(2,1)S(1)}, bf16[1,5,32,256]{3,2,1,0:T(8,128)(2,1)S(1)}, u32[]{:S(2)}, u32[]{:S(2)}) %collective-permute-start.5) | collective-permute-done | bytes 81952 | tf_op jit(solution)/shard_map/ppermute | solution.py:446
  65.9 4.4 %collective-permute-start.6 = (bf16[1,5,32,256]{3,2,1,0:T(8,128)(2,1)S(1)}, bf16[1,5,32,256]{3,2,1,0:T(8,128)(2,1)S(1)}, u32[]{:S(2)}, u32[]{:S(2)}) collective-permute-start(bf16[1,5,32,256]{3,2,1,0:T(8,128)(2,1)S(1)} %shard_map.128.a), channel_id=1, source_target_pairs={{0,8},{1,9},{2,10},{3,11},{4,12},{5,13},{6,14},{7,15},{8,0},{9,1},... | collective-permute-start | bytes 245768 | tf_op jit(solution)/shard_map/ppermute | solution.py:446
  70.3 4.1 %shard_map.129 = bf16[8192,256]{1,0:T(8,128)(2,1)} custom-call(s32[1,256]{1,0:T(1,128)S(1)} %copy-done.7, bf16[256,1024]{1,0:T(8,128)(2,1)S(1)} %get-tuple-element.43.onehot_t, f32[64,128]{1,0:T(8,128)S(1)} %get-tuple-element.44.table, bf16[1024,256]{1,0:T(8,128)(2,1)S(1)} %bitcast.8), custom_call_target="tpu_custom_call" | custom-call | flops 1073741824 | bytes 4194304 | tf_op jit(solution)/shard_map/pallas_call | solution.py:421
  75.0 1.3 %collective-permute-start.8 = (bf16[1,5,32,256]{3,2,1,0:T(8,128)(2,1)S(1)}, bf16[1,5,32,256]{3,2,1,0:T(8,128)(2,1)S(1)}, u32[]{:S(2)}, u32[]{:S(2)}) collective-permute-start(bf16[1,5,32,256]{3,2,1,0:T(8,128)(2,1)S(1)} %shard_map.130), channel_id=1, source_target_pairs={{0,2},{1,3},{2,0},{3,1},{4,6},{5,7},{6,4},{7,5},{8,10},{9,11},{10,... | collective-permute-start | bytes 245768 | tf_op jit(solution)/shard_map/ppermute | solution.py:446
  76.3 1.8 %collective-permute-start.7 = (bf16[1,5,32,256]{3,2,1,0:T(8,128)(2,1)S(1)}, bf16[1,5,32,256]{3,2,1,0:T(8,128)(2,1)S(1)}, u32[]{:S(2)}, u32[]{:S(2)}) collective-permute-start(bf16[1,5,32,256]{3,2,1,0:T(8,128)(2,1)S(1)} %shard_map.130), channel_id=1, source_target_pairs={{0,4},{1,5},{2,6},{3,7},{4,0},{5,1},{6,2},{7,3},{8,12},{9,13},{10,... | collective-permute-start | bytes 245768 | tf_op jit(solution)/shard_map/ppermute | solution.py:446
  78.0 2.0 %collective-permute-done.9 = bf16[1,5,32,256]{3,2,1,0:T(8,128)(2,1)S(1)} collective-permute-done((bf16[1,5,32,256]{3,2,1,0:T(8,128)(2,1)S(1)}, bf16[1,5,32,256]{3,2,1,0:T(8,128)(2,1)S(1)}, u32[]{:S(2)}, u32[]{:S(2)}) %collective-permute-start.9) | collective-permute-done | bytes 81952 | tf_op jit(solution)/shard_map/ppermute | solution.py:446
  80.9 1.6 %collective-permute-done.10.refs_1_ = bf16[4,5,32,256]{3,2,1,0:T(8,128)(2,1)S(1)} collective-permute-done((bf16[4,5,32,256]{3,2,1,0:T(8,128)(2,1)S(1)}, bf16[4,5,32,256]{3,2,1,0:T(8,128)(2,1)S(1)}, u32[]{:S(2)}, u32[]{:S(2)}) %collective-permute-start.10) | collective-permute-done | bytes 327712 | tf_op jit(solution)/shard_map/ppermute | solution.py:446
  82.5 1.1 %shard_map.131 = (f32[4,256,256]{2,1,0:T(8,128)}, f32[256,256]{1,0:T(8,128)}) custom-call(bf16[4,5,32,256]{3,2,1,0:T(8,128)(2,1)S(1)} %pad_maximum_fusion.refs_0_, bf16[4,5,32,256]{3,2,1,0:T(8,128)(2,1)S(1)} %collective-permute-done.10.refs_1_), custom_call_target="tpu_custom_call" | custom-call | tf_op jit(solution)/shard_map/pallas_call | solution.py:383
  (32 shorter events, 3.2 us)
Async XLA Ops:
  0.6 26.4 %copy-start.2 = (bf16[128,256]{1,0:T(8,128)(2,1)S(1)}, bf16[128,256]{1,0:T(8,128)(2,1)}, u32[]{:S(2)}) copy-start(bf16[128,256]{1,0:T(8,128)(2,1)} %out_grad.3) | copy-start | bytes 196612
  0.6 26.4 %copy-start = (bf16[4,256,256]{2,1,0:T(8,128)(2,1)S(1)}, bf16[4,256,256]{2,1,0:T(8,128)(2,1)}, u32[]{:S(2)}) copy-start(bf16[4,256,256]{2,1,0:T(8,128)(2,1)} %weights.3) | copy-start | bytes 1572868
  0.7 26.4 %copy-start.1 = (bf16[128,256]{1,0:T(8,128)(2,1)S(1)}, bf16[128,256]{1,0:T(8,128)(2,1)}, u32[]{:S(2)}) copy-start(bf16[128,256]{1,0:T(8,128)(2,1)} %queries.3) | copy-start | bytes 196612
  0.7 26.4 %copy-start.4 = (s32[128,100]{0,1:T(8,128)S(1)}, s32[128,100]{0,1:T(8,128)}, u32[]{:S(2)}) copy-start(s32[128,100]{0,1:T(8,128)} %param.14) | copy-start | bytes 153604
  0.7 41.6 %copy-start.3 = (bf16[256,256]{1,0:T(8,128)(2,1)S(1)}, bf16[256,256]{1,0:T(8,128)(2,1)}, u32[]{:S(2)}) copy-start(bf16[256,256]{1,0:T(8,128)(2,1)} %enc.1) | copy-start | bytes 393220
  14.5 5.9 %collective-permute-start = (s32[8,1,128]{2,0,1:T(8,128)S(1)}, s32[8,1,128]{2,0,1:T(8,128)S(1)}, u32[]{:S(2)}, u32[]{:S(2)}) collective-permute-start(s32[8,1,128]{2,0,1:T(8,128)S(1)} %bitcast.12), channel_id=1, source_target_pairs={{0,1},{1,0},{2,3},{3,2},{4,5},{5,4},{6,7},{7,6},{8,9},{9,8},{10,11... | collective-permute-start | bytes 12296 | tf_op jit(solution)/shard_map/ppermute | solution.py:446
  14.5 0.8 copy-start.5
  15.3 0.7 copy-start.6
  20.9 1.7 %collective-permute-start.1 = (bf16[8,64,256]{2,1,0:T(8,128)(2,1)S(1)}, bf16[8,64,256]{2,1,0:T(8,128)(2,1)S(1)}, u32[]{:S(2)}, u32[]{:S(2)}) collective-permute-start(bf16[8,64,256]{2,1,0:T(8,128)(2,1)S(1)} %get-tuple-element.29), channel_id=1, source_target_pairs={{0,1},{1,0},{2,3},{3,2},{4,5},{5,4},{6,7},{7,6},{8,9},{9,8},{10,11... | collective-permute-start | bytes 786440 | tf_op jit(solution)/shard_map/ppermute | solution.py:446
  23.5 18.7 %all-to-all-start.1 = ((bf16[8,128,256]{2,1,0:T(8,128)(2,1)}), bf16[8,128,256]{2,1,0:T(8,128)(2,1)S(1)}, u32[]{:S(2)}, u32[]{:S(2)}) async-start(bf16[8,128,256]{2,1,0:T(8,128)(2,1)} %shard_map.122), calls=%async_computation.1 | async-start | bytes 1048576 | tf_op jit(solution)/shard_map/all_to_all | solution.py:450
  47.2 2.8 %collective-permute-start.2 = (bf16[4,5,32,256]{3,2,1,0:T(8,128)(2,1)S(1)}, bf16[4,5,32,256]{3,2,1,0:T(8,128)(2,1)S(1)}, u32[]{:S(2)}, u32[]{:S(2)}) collective-permute-start(bf16[4,5,32,256]{3,2,1,0:T(8,128)(2,1)S(1)} %get-tuple-element.35), channel_id=1, source_target_pairs={{0,1},{1,0},{2,3},{3,2},{4,5},{5,4},{6,7},{7,6},{8,9},{9,8},{10,11... | collective-permute-start | bytes 983048 | tf_op jit(solution)/shard_map/ppermute | solution.py:446
  47.2 2.0 %collective-permute-start.3 = (bf16[8,64,256]{2,1,0:T(8,128)(2,1)S(1)}, bf16[8,64,256]{2,1,0:T(8,128)(2,1)S(1)}, u32[]{:S(2)}, u32[]{:S(2)}) collective-permute-start(bf16[8,64,256]{2,1,0:T(8,128)(2,1)S(1)} %get-tuple-element.39), channel_id=1, source_target_pairs={{0,1},{1,0},{2,3},{3,2},{4,5},{5,4},{6,7},{7,6},{8,9},{9,8},{10,11... | collective-permute-start | bytes 786440 | tf_op jit(solution)/shard_map/ppermute | solution.py:446
  50.1 6.3 %collective-permute-start.4 = (bf16[2,5,32,256]{3,2,1,0:T(8,128)(2,1)S(1)}, bf16[2,5,32,256]{3,2,1,0:T(8,128)(2,1)S(1)}, u32[]{:S(2)}, u32[]{:S(2)}) collective-permute-start(bf16[2,5,32,256]{3,2,1,0:T(8,128)(2,1)S(1)} %get-tuple-element.40), channel_id=1, source_target_pairs={{0,2},{1,3},{2,0},{3,1},{4,6},{5,7},{6,4},{7,5},{8,10},{9,11},{10,... | collective-permute-start | bytes 491528 | tf_op jit(solution)/shard_map/ppermute | solution.py:446
  51.6 18.7 %all-to-all-start.2 = ((bf16[8,128,256]{2,1,0:T(8,128)(2,1)}), bf16[8,128,256]{2,1,0:T(8,128)(2,1)S(1)}, u32[]{:S(2)}, u32[]{:S(2)}) async-start(bf16[8,128,256]{2,1,0:T(8,128)(2,1)} %shard_map.126), calls=%async_computation.2 | async-start | bytes 1048576 | tf_op jit(solution)/shard_map/all_to_all | solution.py:450
  56.4 14.0 %copy-start.7 = (s32[1,256]{1,0:T(1,128)S(1)}, s32[1,256]{1,0:T(1,128)}, u32[]{:S(2)}) copy-start(s32[1,256]{1,0:T(1,128)} %counts.1) | copy-start | bytes 3076
  56.4 9.4 %collective-permute-start.5 = (bf16[1,5,32,256]{3,2,1,0:T(8,128)(2,1)S(1)}, bf16[1,5,32,256]{3,2,1,0:T(8,128)(2,1)S(1)}, u32[]{:S(2)}, u32[]{:S(2)}) collective-permute-start(bf16[1,5,32,256]{3,2,1,0:T(8,128)(2,1)S(1)} %get-tuple-element.42), channel_id=1, source_target_pairs={{0,4},{1,5},{2,6},{3,7},{4,0},{5,1},{6,2},{7,3},{8,12},{9,13},{10,... | collective-permute-start | bytes 245768 | tf_op jit(solution)/shard_map/ppermute | solution.py:446
  65.9 8.5 %collective-permute-start.6 = (bf16[1,5,32,256]{3,2,1,0:T(8,128)(2,1)S(1)}, bf16[1,5,32,256]{3,2,1,0:T(8,128)(2,1)S(1)}, u32[]{:S(2)}, u32[]{:S(2)}) collective-permute-start(bf16[1,5,32,256]{3,2,1,0:T(8,128)(2,1)S(1)} %shard_map.128.a), channel_id=1, source_target_pairs={{0,8},{1,9},{2,10},{3,11},{4,12},{5,13},{6,14},{7,15},{8,0},{9,1},... | collective-permute-start | bytes 245768 | tf_op jit(solution)/shard_map/ppermute | solution.py:446
  74.5 5.5 %collective-permute-start.9 = (bf16[1,5,32,256]{3,2,1,0:T(8,128)(2,1)S(1)}, bf16[1,5,32,256]{3,2,1,0:T(8,128)(2,1)S(1)}, u32[]{:S(2)}, u32[]{:S(2)}) collective-permute-start(bf16[1,5,32,256]{3,2,1,0:T(8,128)(2,1)S(1)} %shard_map.130), channel_id=1, source_target_pairs={{0,6},{1,7},{2,4},{3,5},{4,2},{5,3},{6,0},{7,1},{8,14},{9,15},{10,... | collective-permute-start | bytes 245768 | tf_op jit(solution)/shard_map/ppermute | solution.py:446
  75.0 5.3 %collective-permute-start.8 = (bf16[1,5,32,256]{3,2,1,0:T(8,128)(2,1)S(1)}, bf16[1,5,32,256]{3,2,1,0:T(8,128)(2,1)S(1)}, u32[]{:S(2)}, u32[]{:S(2)}) collective-permute-start(bf16[1,5,32,256]{3,2,1,0:T(8,128)(2,1)S(1)} %shard_map.130), channel_id=1, source_target_pairs={{0,2},{1,3},{2,0},{3,1},{4,6},{5,7},{6,4},{7,5},{8,10},{9,11},{10,... | collective-permute-start | bytes 245768 | tf_op jit(solution)/shard_map/ppermute | solution.py:446
  76.3 4.5 %collective-permute-start.7 = (bf16[1,5,32,256]{3,2,1,0:T(8,128)(2,1)S(1)}, bf16[1,5,32,256]{3,2,1,0:T(8,128)(2,1)S(1)}, u32[]{:S(2)}, u32[]{:S(2)}) collective-permute-start(bf16[1,5,32,256]{3,2,1,0:T(8,128)(2,1)S(1)} %shard_map.130), channel_id=1, source_target_pairs={{0,4},{1,5},{2,6},{3,7},{4,0},{5,1},{6,2},{7,3},{8,12},{9,13},{10,... | collective-permute-start | bytes 245768 | tf_op jit(solution)/shard_map/ppermute | solution.py:446
  80.8 1.7 %collective-permute-start.10 = (bf16[4,5,32,256]{3,2,1,0:T(8,128)(2,1)S(1)}, bf16[4,5,32,256]{3,2,1,0:T(8,128)(2,1)S(1)}, u32[]{:S(2)}, u32[]{:S(2)}) collective-permute-start(bf16[4,5,32,256]{3,2,1,0:T(8,128)(2,1)S(1)} %pad_maximum_fusion.refs_0_), channel_id=1, source_target_pairs={{0,1},{1,0},{2,3},{3,2},{4,5},{5,4},{6,7},{7,6},{8,9},{9,8},{10,11... | collective-permute-start | bytes 983048 | tf_op jit(solution)/shard_map/ppermute | solution.py:446

commit v12 on v9

--- a/solution.py
+++ b/solution.py
@@ -251,11 +251,31 @@
     return out
 
 
+def chip_order_kernel(keep, got, out):
+    me = lax.axis_index("clu")
+    chips, part, _ = keep.shape
+    own = pl.ds(pl.multiple_of(me % 2 * part, part), part)
+    other = pl.ds(pl.multiple_of((1 - me % 2) * part, part), part)
+    for k in range(chips):
+        place = lax.shift_right_logical(me, 1) ^ k
+        out[place, own, :] = keep[k]
+        out[place, other, :] = got[k]
+
+
+def chip_order(keep, got):
+    chips, part, width = keep.shape
+    return pl.pallas_call(
+        chip_order_kernel,
+        out_shape=jax.ShapeDtypeStruct((chips, 2 * part, width), BF16),
+        compiler_params=SMALL,
+    )(keep, got)
+
+
 def attention_kernel(scale, chips, *refs):
     raws = refs[:chips]
     enc, weights, queries, out_grad, bias, query_heads, mixed_heads = refs[chips : chips + 7]
-    back, grad_query, keep, send, grads = refs[chips + 7 :]
-    per_chip, width = raws[0].shape
+    keep_rows, give_rows, grad_query, keep, send, grads = refs[chips + 7 :]
+    width = enc.shape[0]
     targets = queries.shape[0]
     raw_pool = jnp.concatenate([raw[...] for raw in raws], axis=0)
     emb = dot(raw_pool, enc[...]).astype(BF16)
@@ -296,11 +316,13 @@
     grads[2 * width : 3 * width, :] = both[:, width:].astype(BF16)
     grads[3 * width : 4 * width, :] = dot(mixed_t, out_grad[...]).astype(BF16)
     grads[4 * width : 5 * width, :] = dot_tn(raw_pool, emb_grad).astype(BF16)
-    me = lax.axis_index("clu")
+    core = lax.axis_index("clu") % 2
+    half = keep_rows.shape[1]
     for k in range(chips):
-        at = pl.multiple_of((lax.shift_right_logical(me, 1) ^ k) * per_chip, per_chip)
-        back[pl.ds(at, per_chip), :] = emb_grad[k * per_chip : (k + 1) * per_chip]
-    core = me % 2
+        even = emb_grad[2 * k * half : (2 * k + 1) * half]
+        odd = emb_grad[(2 * k + 1) * half : (2 * k + 2) * half]
+        keep_rows[k] = jnp.where(core == 0, even, odd)
+        give_rows[k] = jnp.where(core == 0, odd, even)
     pieces, _, part, _ = keep.shape
     for q in range(pieces):
         base = 2 * mirrored(q, pieces)
@@ -313,12 +335,14 @@
 
 
 def attention(scale, owners, raws, enc, weights, queries, out_grad, bias, query_heads, mixed_heads):
-    pooled, width = bias.shape[0], enc.shape[0]
+    width = enc.shape[0]
     half = jax.ShapeDtypeStruct((owners // 4, MATRICES, 2 * width // owners, width), BF16)
+    rows = jax.ShapeDtypeStruct((len(raws), raws[0].shape[0] // 2, width), BF16)
     return pl.pallas_call(
         functools.partial(attention_kernel, scale, len(raws)),
         out_shape=[
-            jax.ShapeDtypeStruct((pooled, width), BF16),
+            rows,
+            rows,
             jax.ShapeDtypeStruct(queries.shape, BF16),
             half,
             half,
@@ -362,28 +386,41 @@
     )(a, b)
 
 
-def place_kernel(masks, *refs):
-    *sources, attn, enc = refs
-    _, matrices, part, _ = sources[0].shape
+def place_kernel(masks, held, *refs):
+    attn, enc, wide, sem = refs[-4:]
+    pieces, matrices, part, _ = held.shape
     place_of = lax.rem(lax.axis_index("clu"), enc.shape[0] // part)
-    for source, flips in zip(sources, masks):
-        for k, flip in enumerate(flips):
-            rows = pl.ds(pl.multiple_of((place_of ^ flip) * part, part), part)
-            for m in range(matrices - 1):
-                attn[m, rows, :] = source[k, m].astype(F32)
-            enc[rows, :] = source[k, matrices - 1].astype(F32)
-
-
-def place(pieces):
-    width = pieces[0][0].shape[3]
-    return pl.pallas_call(
-        functools.partial(place_kernel, [flips for _, flips in pieces]),
+    copies = []
+    for k, flip in zip(range(pieces), masks):
+        rows = pl.ds(pl.multiple_of((place_of ^ flip) * part, part), part)
+        for m in range(matrices):
+            wide[k, m] = held[k, m].astype(F32)
+            target = attn.at[m, rows] if m < matrices - 1 else enc.at[rows]
+            copies.append(pltpu.make_async_copy(wide.at[k, m], target, sem.at[k, m]))
+            copies[-1].start()
+    for copy in copies:
+        copy.wait()
+
+
+def place(masks, held, filled=()):
+    pieces, matrices, _, width = held.shape
+    return pl.pallas_call(
+        functools.partial(place_kernel, masks),
+        in_specs=[pl.BlockSpec(memory_space=pltpu.VMEM)]
+        + [pl.BlockSpec(memory_space=pl.ANY)] * len(filled),
+        out_specs=[pl.BlockSpec(memory_space=pl.ANY)] * 2,
         out_shape=[
-            jax.ShapeDtypeStruct((MATRICES - 1, width, width), F32),
+            jax.ShapeDtypeStruct((matrices - 1, width, width), F32),
             jax.ShapeDtypeStruct((width, width), F32),
         ],
+        scratch_shapes=[
+            pltpu.VMEM(held.shape, F32),
+            pltpu.SemaphoreType.DMA((pieces, matrices)),
+        ],
+        input_output_aliases={1 + k: k for k in range(len(filled))},
         compiler_params=SMALL,
-    )(*[piece for piece, _ in pieces])
+        cost_estimate=pl.CostEstimate(flops=0, bytes_accessed=4 * held.size, transcendentals=0),
+    )(held, *filled)
 
 
 def rows_kernel(counts, onehot_t, table, back, out, share, filled, sem):
@@ -456,13 +493,18 @@
     bias, query_heads, mixed_heads = target_terms(
         scale, picks.T, queries, out_grad, attn_weights, pooled
     )
-    back, grad_query, keep, given = attention(
+    keep_rows, give_rows, grad_query, keep, given = attention(
         scale, owners, raws, enc_weight, attn_weights, queries, out_grad, bias, query_heads, mixed_heads
     )
-    keep, given = split(1, keep, exchange(1, given), keep.size)
+    got, got_rows = exchange(1, given), exchange(1, give_rows)
+    keep, given = split(1, keep, got, keep.size)
+    back = chip_order(keep_rows, got_rows)
     given, back = lax.optimization_barrier((given, back))
     got = exchange(2, given)
-    back = swap(back.reshape(owners, pooled // owners, width)).reshape(pooled, width)
+    parities = [list(range(core, owners, 2)) for core in range(2)]
+    back = lax.all_to_all(
+        back, "clu", split_axis=0, concat_axis=0, axis_index_groups=parities, tiled=True
+    ).reshape(pooled, width)
     keep, given = split(2, keep, got, WEIGHT)
     for bit in range(2, bits - 2):
         keep, given = split(bit + 1, keep, exchange(1 << bit, given), keep.size)
@@ -478,7 +520,8 @@
     chip = jnp.concatenate([own] + [exchange(flip, own) for flip in (4, 2, 6)])
     masks = [mask ^ flip for flip in (0, 4, 2, 6) for mask in masks]
     beside = exchange(1, chip)
-    grad_attn, grad_encoder = place([(chip, masks), (beside, [mask ^ 1 for mask in masks])])
+    placed = place(masks, chip)
+    grad_attn, grad_encoder = place([mask ^ 1 for mask in masks], beside, placed)
     return grad_query, grad_rows, grad_attn, grad_encoder
 
 

time: 78.6 us -> 78.1 us (level)
  waiting for transfers between devices: 21 us -> 18 us
  Pallas kernels: 19.4 us -> 20.9 us
  starting transfers between devices: 34.2 us -> 35.2 us
    all_to_all x2 -> x1, starting transfers between devices: 12.8 us -> 7.39 us  [swap(): lax.all_to_all(blocks, 'clu', split_axis=0, concat_axis=0, tiled=True)]
    all_to_all x0 -> x1, starting transfers between devices: none -> 5.3 us  [local(): lax.all_to_all(back, 'clu', split_axis=0, concat_axis=0, axis_index_group...]
    ppermute x16 -> x17, waiting for transfers between devices: 20.6 us -> 17.6 us  [exchange(): return lax.ppermute(block, 'clu', [(d, d ^ flip) for d in range(owners)])]
    pallas_call x1 -> x3, Pallas kernels: 1.14 us -> 2.84 us  [the longest x2 2 us: place(): pl.pallas_call(functools.partial(place_kernel, masks), in_specs=[pl.Block...]
    ppermute x16 -> x17, starting transfers between devices: 21.4 us -> 22.5 us  [exchange(): return lax.ppermute(block, 'clu', [(d, d ^ flip) for d in range(owners)])]
  transfers between devices with their start and end apart: 18 -> 19, of which waited for: 11 -> 11; matrix products, arithmetic and copies ran while one was open for 0% -> 0% of each run, Pallas kernels for 16% -> 18%
where the time goes in v12:
time: 78.1 us; the launch traced here: 77.7 us
  starting transfers between devices  35.2 us (45%)
  Pallas kernels  20.9 us (27%)
  waiting for transfers between devices  18 us (23%)
  local copies, waits for them, and re-layouts  2.81 us (4%)
  between operations  0.81 us (1%)
    ppermute x17, starting transfers between devices, exchange(): return lax.ppermute(block, 'clu', [(d, d ^ flip) for d in range(owners)])  22.5 us
    ppermute x17, waiting for transfers between devices, exchange(): return lax.ppermute(block, 'clu', [(d, d ^ flip) for d in range(owners)])  17.6 us
    all_to_all x1, starting transfers between devices, swap(): lax.all_to_all(blocks, 'clu', split_axis=0, concat_axis=0, tiled=True)  7.39 us
    all_to_all x1, starting transfers between devices, local(): lax.all_to_all(back, 'clu', split_axis=0, concat_axis=0, axis_index_group...  5.3 us
    pallas_call x1, Pallas kernels, attention(): pl.pallas_call(functools.partial(attention_kernel, scale, len(raws)), out...  4.91 us
    pallas_call x1, Pallas kernels, cluster_means(): pl.pallas_call(means_kernel, in_specs=[pl.BlockSpec(memory_space=pltpu.HB...  4.49 us
    pallas_call x1, Pallas kernels, member_grads(): pl.pallas_call(rows_kernel, out_specs=pl.BlockSpec(memory_space=pltpu.HBM...  4.08 us
    pallas_call x1, Pallas kernels, target_terms(): pl.pallas_call(functools.partial(targets_kernel, scale), out_shape=[jax.S...  3.9 us
  transfers between devices with their start and end apart: 19, of which 11 were waited for; matrix products, arithmetic and copies ran while one was open for 0% of the time, Pallas kernels for 18%

profile of v12, /device:TPU:0, one launch (start us, length us, event | category | flops | bytes accessed | tf_op | source)
XLA Modules:
  0.0 77.7 jit_solution(392210840371542638)
XLA Ops:
  0.7 1.4 %broadcast_in_dim.10 = s32[8,2,128]{2,1,0:T(2,128)} broadcast(s32[8,128]{1,0:T(8,128)} %bitcast.10), dimensions={0,2} | broadcast | bytes 12288 | tf_op jit(solution)/shard_map/broadcast_in_dim | solution.py:486
  2.0 7.4 %all-to-all-start = ((s32[16,1,128]{2,1,0:T(1,128)}), s32[16,1,128]{2,1,0:T(1,128)S(1)}, u32[]{:S(2)}, u32[]{:S(2)}) async-start(s32[16,1,128]{2,1,0:T(1,128)} %bitcast.1), calls=%async_computation | async-start | bytes 16384 | tf_op jit(solution)/shard_map/all_to_all | solution.py:471
  10.9 4.5 %shard_map.120 = (bf16[256,256]{1,0:T(8,128)(2,1)S(1)}, f32[64,128]{1,0:T(8,128)S(1)}) custom-call(s32[1,256]{1,0:T(1,128)S(1)} %copy-done.6, s32[64,128]{1,0:T(8,128)S(1)} %bitcast.8, bf16[8192,256]{1,0:T(8,128)(2,1)} %raw_h.1), custom_call_target="tpu_custom_call" | custom-call | flops 1073741824 | bytes 4194304 | tf_op jit(solution)/shard_map/pallas_call | solution.py:127
  16.3 1.5 %collective-permute-done.got = bf16[8,64,256]{2,1,0:T(8,128)(2,1)S(1)} collective-permute-done((bf16[8,64,256]{2,1,0:T(8,128)(2,1)S(1)}, bf16[8,64,256]{2,1,0:T(8,128)(2,1)S(1)}, u32[]{:S(2)}, u32[]{:S(2)}) %collective-permute-start) | collective-permute-done | bytes 262176 | tf_op jit(solution)/shard_map/ppermute | solution.py:483
  17.9 1.6 %collective-permute-start.1 = (bf16[128,256]{1,0:T(8,128)(2,1)S(1)}, bf16[128,256]{1,0:T(8,128)(2,1)S(1)}, u32[]{:S(2)}, u32[]{:S(2)}) collective-permute-start(bf16[128,256]{1,0:T(8,128)(2,1)S(1)} %get-tuple-element.41), channel_id=1, source_target_pairs={{0,2},{1,3},{2,0},{3,1},{4,6},{5,7},{6,4},{7,5},{8,10},{9,11},{10,... | collective-permute-start | bytes 196616 | tf_op jit(solution)/shard_map/ppermute | solution.py:483
  19.5 1.5 %collective-permute-start.2 = (bf16[128,256]{1,0:T(8,128)(2,1)S(1)}, bf16[128,256]{1,0:T(8,128)(2,1)S(1)}, u32[]{:S(2)}, u32[]{:S(2)}) collective-permute-start(bf16[128,256]{1,0:T(8,128)(2,1)S(1)} %get-tuple-element.42), channel_id=1, source_target_pairs={{0,4},{1,5},{2,6},{3,7},{4,0},{5,1},{6,2},{7,3},{8,12},{9,13},{10,... | collective-permute-start | bytes 196616 | tf_op jit(solution)/shard_map/ppermute | solution.py:483
  21.5 2.4 %collective-permute-start.4 = (bf16[128,256]{1,0:T(8,128)(2,1)S(1)}, bf16[128,256]{1,0:T(8,128)(2,1)S(1)}, u32[]{:S(2)}, u32[]{:S(2)}) collective-permute-start(bf16[128,256]{1,0:T(8,128)(2,1)S(1)} %get-tuple-element.44), channel_id=1, source_target_pairs={{0,8},{1,9},{2,10},{3,11},{4,12},{5,13},{6,14},{7,15},{8,0},{9,1},... | collective-permute-start | bytes 196616 | tf_op jit(solution)/shard_map/ppermute | solution.py:483
  23.9 1.5 %collective-permute-start.5 = (bf16[128,256]{1,0:T(8,128)(2,1)S(1)}, bf16[128,256]{1,0:T(8,128)(2,1)S(1)}, u32[]{:S(2)}, u32[]{:S(2)}) collective-permute-start(bf16[128,256]{1,0:T(8,128)(2,1)S(1)} %get-tuple-element.45), channel_id=1, source_target_pairs={{0,10},{1,11},{2,8},{3,9},{4,14},{5,15},{6,12},{7,13},{8,2},{9,3},... | collective-permute-start | bytes 196616 | tf_op jit(solution)/shard_map/ppermute | solution.py:483
  25.4 3.3 %collective-permute-start.6 = (bf16[128,256]{1,0:T(8,128)(2,1)S(1)}, bf16[128,256]{1,0:T(8,128)(2,1)S(1)}, u32[]{:S(2)}, u32[]{:S(2)}) collective-permute-start(bf16[128,256]{1,0:T(8,128)(2,1)S(1)} %get-tuple-element.46), channel_id=1, source_target_pairs={{0,12},{1,13},{2,14},{3,15},{4,8},{5,9},{6,10},{7,11},{8,4},{9,5},... | collective-permute-start | bytes 196616 | tf_op jit(solution)/shard_map/ppermute | solution.py:483
  29.1 3.9 %shard_map.123 = (f32[1024,128]{1,0:T(8,128)S(1)}, bf16[512,256]{1,0:T(8,128)(2,1)S(1)}, bf16[512,256]{1,0:T(8,128)(2,1)S(1)}) custom-call(s32[100,128]{1,0:T(8,128)S(1)} %bitcast.7, bf16[128,256]{1,0:T(8,128)(2,1)S(1)} %copy-done.1, bf16[128,256]{1,0:T(8,128)(2,1)S(1)} %copy-done.2, bf16[4,256,256]{2,1,0:T(8,128)(2,1)S(1)} %copy-done), custom_call_target="tpu_custom_call" | custom-call | flops 52428800 | bytes 524288 | tf_op jit(solution)/shard_map/pallas_call | solution.py:229
  33.1 1.2 %collective-permute-done.5.refs_5_ = bf16[128,256]{1,0:T(8,128)(2,1)S(1)} collective-permute-done((bf16[128,256]{1,0:T(8,128)(2,1)S(1)}, bf16[128,256]{1,0:T(8,128)(2,1)S(1)}, u32[]{:S(2)}, u32[]{:S(2)}) %collective-permute-start.5) | collective-permute-done | bytes 65568 | tf_op jit(solution)/shard_map/ppermute | solution.py:483
  34.2 1.5 %collective-permute-done.7.refs_7_ = bf16[128,256]{1,0:T(8,128)(2,1)S(1)} collective-permute-done((bf16[128,256]{1,0:T(8,128)(2,1)S(1)}, bf16[128,256]{1,0:T(8,128)(2,1)S(1)}, u32[]{:S(2)}, u32[]{:S(2)}) %collective-permute-start.7) | collective-permute-done | bytes 65568 | tf_op jit(solution)/shard_map/ppermute | solution.py:483
  35.7 4.9 %shard_map.124 = (bf16[8,64,256]{2,1,0:T(8,128)(2,1)S(1)}, bf16[8,64,256]{2,1,0:T(8,128)(2,1)S(1)}, bf16[128,256]{1,0:T(8,128)(2,1)}, bf16[4,5,32,256]{3,2,1,0:T(8,128)(2,1)S(1)}, bf16[4,5,32,256]{3,2,1,0:T(8,128)(2,1)S(1)}) custom-call(bf16[128,256]{1,0:T(8,128)(2,1)S(1)} %get-tuple-element.40.refs_0_, bf16[128,256]{1,0:T(8,128)(2,1)S(1)} %collective-permute-done.1.refs_1_, ...), custom_call_target="tpu_custom_call" | custom-call | tf_op jit(solution)/shard_map/pallas_call | solution.py:341
  41.1 1.5 %collective-permute-done.9.got = bf16[8,64,256]{2,1,0:T(8,128)(2,1)S(1)} collective-permute-done((bf16[8,64,256]{2,1,0:T(8,128)(2,1)S(1)}, bf16[8,64,256]{2,1,0:T(8,128)(2,1)S(1)}, u32[]{:S(2)}, u32[]{:S(2)}) %collective-permute-start.9) | collective-permute-done | bytes 262176 | tf_op jit(solution)/shard_map/ppermute | solution.py:483
  44.2 5.3 %all-to-all-start.1 = ((bf16[8,128,256]{2,1,0:T(8,128)(2,1)}), bf16[8,128,256]{2,1,0:T(8,128)(2,1)S(1)}, u32[]{:S(2)}, u32[]{:S(2)}) async-start(bf16[8,128,256]{2,1,0:T(8,128)(2,1)} %shard_map.126), calls=%async_computation.1 | async-start | bytes 1048576 | tf_op jit(solution)/shard_map/all_to_all | solution.py:505
  49.9 2.0 %collective-permute-start.11 = (bf16[1,5,32,256]{3,2,1,0:T(8,128)(2,1)S(1)}, bf16[1,5,32,256]{3,2,1,0:T(8,128)(2,1)S(1)}, u32[]{:S(2)}, u32[]{:S(2)}) collective-permute-start(bf16[1,5,32,256]{3,2,1,0:T(8,128)(2,1)S(1)} %get-tuple-element.60), channel_id=1, source_target_pairs={{0,4},{1,5},{2,6},{3,7},{4,0},{5,1},{6,2},{7,3},{8,12},{9,13},{10,... | collective-permute-start | bytes 245768 | tf_op jit(solution)/shard_map/ppermute | solution.py:483
  51.9 8.2 %collective-permute-done.11.b = bf16[1,5,32,256]{3,2,1,0:T(8,128)(2,1)S(1)} collective-permute-done((bf16[1,5,32,256]{3,2,1,0:T(8,128)(2,1)S(1)}, bf16[1,5,32,256]{3,2,1,0:T(8,128)(2,1)S(1)}, u32[]{:S(2)}, u32[]{:S(2)}) %collective-permute-start.11) | collective-permute-done | bytes 81952 | tf_op jit(solution)/shard_map/ppermute | solution.py:483
  60.1 4.4 %collective-permute-start.12 = (bf16[1,5,32,256]{3,2,1,0:T(8,128)(2,1)S(1)}, bf16[1,5,32,256]{3,2,1,0:T(8,128)(2,1)S(1)}, u32[]{:S(2)}, u32[]{:S(2)}) collective-permute-start(bf16[1,5,32,256]{3,2,1,0:T(8,128)(2,1)S(1)} %shard_map.128.a), channel_id=1, source_target_pairs={{0,8},{1,9},{2,10},{3,11},{4,12},{5,13},{6,14},{7,15},{8,0},{9,1},... | collective-permute-start | bytes 245768 | tf_op jit(solution)/shard_map/ppermute | solution.py:483
  64.5 4.1 %shard_map.129 = bf16[8192,256]{1,0:T(8,128)(2,1)} custom-call(s32[1,256]{1,0:T(1,128)S(1)} %copy-done.7, bf16[256,1024]{1,0:T(8,128)(2,1)S(1)} %get-tuple-element.61.onehot_t, f32[64,128]{1,0:T(8,128)S(1)} %get-tuple-element.62.table, bf16[1024,256]{1,0:T(8,128)(2,1)S(1)} %bitcast.6), custom_call_target="tpu_custom_call" | custom-call | flops 1073741824 | bytes 4194304 | tf_op jit(solution)/shard_map/pallas_call | solution.py:454
  69.2 1.2 %collective-permute-start.14 = (bf16[1,5,32,256]{3,2,1,0:T(8,128)(2,1)S(1)}, bf16[1,5,32,256]{3,2,1,0:T(8,128)(2,1)S(1)}, u32[]{:S(2)}, u32[]{:S(2)}) collective-permute-start(bf16[1,5,32,256]{3,2,1,0:T(8,128)(2,1)S(1)} %shard_map.130), channel_id=1, source_target_pairs={{0,2},{1,3},{2,0},{3,1},{4,6},{5,7},{6,4},{7,5},{8,10},{9,11},{10,... | collective-permute-start | bytes 245768 | tf_op jit(solution)/shard_map/ppermute | solution.py:483
  70.4 1.8 %collective-permute-start.13 = (bf16[1,5,32,256]{3,2,1,0:T(8,128)(2,1)S(1)}, bf16[1,5,32,256]{3,2,1,0:T(8,128)(2,1)S(1)}, u32[]{:S(2)}, u32[]{:S(2)}) collective-permute-start(bf16[1,5,32,256]{3,2,1,0:T(8,128)(2,1)S(1)} %shard_map.130), channel_id=1, source_target_pairs={{0,4},{1,5},{2,6},{3,7},{4,0},{5,1},{6,2},{7,3},{8,12},{9,13},{10,... | collective-permute-start | bytes 245768 | tf_op jit(solution)/shard_map/ppermute | solution.py:483
  72.2 2.0 %collective-permute-done.15 = bf16[1,5,32,256]{3,2,1,0:T(8,128)(2,1)S(1)} collective-permute-done((bf16[1,5,32,256]{3,2,1,0:T(8,128)(2,1)S(1)}, bf16[1,5,32,256]{3,2,1,0:T(8,128)(2,1)S(1)}, u32[]{:S(2)}, u32[]{:S(2)}) %collective-permute-start.15) | collective-permute-done | bytes 81952 | tf_op jit(solution)/shard_map/ppermute | solution.py:483
  75.1 1.0 %shard_map.131 = (f32[4,256,256]{2,1,0:T(8,128)}, f32[256,256]{1,0:T(8,128)}) custom-call(bf16[4,5,32,256]{3,2,1,0:T(8,128)(2,1)S(1)} %pad_maximum_fusion.held), custom_call_target="tpu_custom_call" | custom-call | bytes 655360 | tf_op jit(solution)/shard_map/pallas_call | solution.py:407
  76.7 1.0 %shard_map.132 = (f32[4,256,256]{2,1,0:T(8,128)}, f32[256,256]{1,0:T(8,128)}) custom-call(bf16[4,5,32,256]{3,2,1,0:T(8,128)(2,1)S(1)} %collective-permute-done.16.held, f32[4,256,256]{2,1,0:T(8,128)} %get-tuple-element.66.refs_0_, f32[256,256]{1,0:T(8,128)} %get-tuple-element.67.refs_1_), custom_call_target="tpu_custom_call", output_to_operand_aliasing={{0}: (1, {}), {1}: (2, {})} | custom-call | bytes 655360 | tf_op jit(solution)/shard_map/pallas_call | solution.py:407
  (45 shorter events, 8.1 us)
Async XLA Ops:
  0.6 28.5 %copy-start.2 = (bf16[128,256]{1,0:T(8,128)(2,1)S(1)}, bf16[128,256]{1,0:T(8,128)(2,1)}, u32[]{:S(2)}) copy-start(bf16[128,256]{1,0:T(8,128)(2,1)} %refs_11_.1) | copy-start | bytes 196612
  0.6 28.5 %copy-start = (bf16[4,256,256]{2,1,0:T(8,128)(2,1)S(1)}, bf16[4,256,256]{2,1,0:T(8,128)(2,1)}, u32[]{:S(2)}) copy-start(bf16[4,256,256]{2,1,0:T(8,128)(2,1)} %refs_9_.1) | copy-start | bytes 1572868
  0.7 28.5 %copy-start.1 = (bf16[128,256]{1,0:T(8,128)(2,1)S(1)}, bf16[128,256]{1,0:T(8,128)(2,1)}, u32[]{:S(2)}) copy-start(bf16[128,256]{1,0:T(8,128)(2,1)} %refs_10_.1) | copy-start | bytes 196612
  0.7 28.5 %copy-start.4 = (s32[128,100]{0,1:T(8,128)S(1)}, s32[128,100]{0,1:T(8,128)}, u32[]{:S(2)}) copy-start(s32[128,100]{0,1:T(8,128)} %param.14) | copy-start | bytes 153604
  0.7 35.0 %copy-start.3 = (bf16[256,256]{1,0:T(8,128)(2,1)S(1)}, bf16[256,256]{1,0:T(8,128)(2,1)}, u32[]{:S(2)}) copy-start(bf16[256,256]{1,0:T(8,128)(2,1)} %refs_8_.1) | copy-start | bytes 393220
  2.0 13.7 %all-to-all-start = ((s32[16,1,128]{2,1,0:T(1,128)}), s32[16,1,128]{2,1,0:T(1,128)S(1)}, u32[]{:S(2)}, u32[]{:S(2)}) async-start(s32[16,1,128]{2,1,0:T(1,128)} %bitcast.1), calls=%async_computation | async-start | bytes 16384 | tf_op jit(solution)/shard_map/all_to_all | solution.py:471
  16.3 1.6 %collective-permute-start = (bf16[8,64,256]{2,1,0:T(8,128)(2,1)S(1)}, bf16[8,64,256]{2,1,0:T(8,128)(2,1)S(1)}, u32[]{:S(2)}, u32[]{:S(2)}) collective-permute-start(bf16[8,64,256]{2,1,0:T(8,128)(2,1)S(1)} %get-tuple-element.39), channel_id=1, source_target_pairs={{0,1},{1,0},{2,3},{3,2},{4,5},{5,4},{6,7},{7,6},{8,9},{9,8},{10,11... | collective-permute-start | bytes 786440 | tf_op jit(solution)/shard_map/ppermute | solution.py:483
  17.9 7.5 %collective-permute-start.1 = (bf16[128,256]{1,0:T(8,128)(2,1)S(1)}, bf16[128,256]{1,0:T(8,128)(2,1)S(1)}, u32[]{:S(2)}, u32[]{:S(2)}) collective-permute-start(bf16[128,256]{1,0:T(8,128)(2,1)S(1)} %get-tuple-element.41), channel_id=1, source_target_pairs={{0,2},{1,3},{2,0},{3,1},{4,6},{5,7},{6,4},{7,5},{8,10},{9,11},{10,... | collective-permute-start | bytes 196616 | tf_op jit(solution)/shard_map/ppermute | solution.py:483
  19.5 9.1 %collective-permute-start.2 = (bf16[128,256]{1,0:T(8,128)(2,1)S(1)}, bf16[128,256]{1,0:T(8,128)(2,1)S(1)}, u32[]{:S(2)}, u32[]{:S(2)}) collective-permute-start(bf16[128,256]{1,0:T(8,128)(2,1)S(1)} %get-tuple-element.42), channel_id=1, source_target_pairs={{0,4},{1,5},{2,6},{3,7},{4,0},{5,1},{6,2},{7,3},{8,12},{9,13},{10,... | collective-permute-start | bytes 196616 | tf_op jit(solution)/shard_map/ppermute | solution.py:483
  21.0 12.1 %collective-permute-start.3 = (bf16[128,256]{1,0:T(8,128)(2,1)S(1)}, bf16[128,256]{1,0:T(8,128)(2,1)S(1)}, u32[]{:S(2)}, u32[]{:S(2)}) collective-permute-start(bf16[128,256]{1,0:T(8,128)(2,1)S(1)} %get-tuple-element.43), channel_id=1, source_target_pairs={{0,6},{1,7},{2,4},{3,5},{4,2},{5,3},{6,0},{7,1},{8,14},{9,15},{10,... | collective-permute-start | bytes 196616 | tf_op jit(solution)/shard_map/ppermute | solution.py:483
  21.5 11.6 %collective-permute-start.4 = (bf16[128,256]{1,0:T(8,128)(2,1)S(1)}, bf16[128,256]{1,0:T(8,128)(2,1)S(1)}, u32[]{:S(2)}, u32[]{:S(2)}) collective-permute-start(bf16[128,256]{1,0:T(8,128)(2,1)S(1)} %get-tuple-element.44), channel_id=1, source_target_pairs={{0,8},{1,9},{2,10},{3,11},{4,12},{5,13},{6,14},{7,15},{8,0},{9,1},... | collective-permute-start | bytes 196616 | tf_op jit(solution)/shard_map/ppermute | solution.py:483
  23.9 10.3 %collective-permute-start.5 = (bf16[128,256]{1,0:T(8,128)(2,1)S(1)}, bf16[128,256]{1,0:T(8,128)(2,1)S(1)}, u32[]{:S(2)}, u32[]{:S(2)}) collective-permute-start(bf16[128,256]{1,0:T(8,128)(2,1)S(1)} %get-tuple-element.45), channel_id=1, source_target_pairs={{0,10},{1,11},{2,8},{3,9},{4,14},{5,15},{6,12},{7,13},{8,2},{9,3},... | collective-permute-start | bytes 196616 | tf_op jit(solution)/shard_map/ppermute | solution.py:483
  25.4 8.9 %collective-permute-start.6 = (bf16[128,256]{1,0:T(8,128)(2,1)S(1)}, bf16[128,256]{1,0:T(8,128)(2,1)S(1)}, u32[]{:S(2)}, u32[]{:S(2)}) collective-permute-start(bf16[128,256]{1,0:T(8,128)(2,1)S(1)} %get-tuple-element.46), channel_id=1, source_target_pairs={{0,12},{1,13},{2,14},{3,15},{4,8},{5,9},{6,10},{7,11},{8,4},{9,5},... | collective-permute-start | bytes 196616 | tf_op jit(solution)/shard_map/ppermute | solution.py:483
  28.6 7.1 %collective-permute-start.7 = (bf16[128,256]{1,0:T(8,128)(2,1)S(1)}, bf16[128,256]{1,0:T(8,128)(2,1)S(1)}, u32[]{:S(2)}, u32[]{:S(2)}) collective-permute-start(bf16[128,256]{1,0:T(8,128)(2,1)S(1)} %get-tuple-element.47), channel_id=1, source_target_pairs={{0,14},{1,15},{2,12},{3,13},{4,10},{5,11},{6,8},{7,9},{8,6},{9,7},... | collective-permute-start | bytes 196616 | tf_op jit(solution)/shard_map/ppermute | solution.py:483
  40.6 2.8 %collective-permute-start.8 = (bf16[4,5,32,256]{3,2,1,0:T(8,128)(2,1)S(1)}, bf16[4,5,32,256]{3,2,1,0:T(8,128)(2,1)S(1)}, u32[]{:S(2)}, u32[]{:S(2)}) collective-permute-start(bf16[4,5,32,256]{3,2,1,0:T(8,128)(2,1)S(1)} %get-tuple-element.53), channel_id=1, source_target_pairs={{0,1},{1,0},{2,3},{3,2},{4,5},{5,4},{6,7},{7,6},{8,9},{9,8},{10,11... | collective-permute-start | bytes 983048 | tf_op jit(solution)/shard_map/ppermute | solution.py:483
  40.6 2.0 %collective-permute-start.9 = (bf16[8,64,256]{2,1,0:T(8,128)(2,1)S(1)}, bf16[8,64,256]{2,1,0:T(8,128)(2,1)S(1)}, u32[]{:S(2)}, u32[]{:S(2)}) collective-permute-start(bf16[8,64,256]{2,1,0:T(8,128)(2,1)S(1)} %get-tuple-element.57), channel_id=1, source_target_pairs={{0,1},{1,0},{2,3},{3,2},{4,5},{5,4},{6,7},{7,6},{8,9},{9,8},{10,11... | collective-permute-start | bytes 786440 | tf_op jit(solution)/shard_map/ppermute | solution.py:483
  43.5 6.3 %collective-permute-start.10 = (bf16[2,5,32,256]{3,2,1,0:T(8,128)(2,1)S(1)}, bf16[2,5,32,256]{3,2,1,0:T(8,128)(2,1)S(1)}, u32[]{:S(2)}, u32[]{:S(2)}) collective-permute-start(bf16[2,5,32,256]{3,2,1,0:T(8,128)(2,1)S(1)} %get-tuple-element.58), channel_id=1, source_target_pairs={{0,2},{1,3},{2,0},{3,1},{4,6},{5,7},{6,4},{7,5},{8,10},{9,11},{10,... | collective-permute-start | bytes 491528 | tf_op jit(solution)/shard_map/ppermute | solution.py:483
  44.2 20.4 %all-to-all-start.1 = ((bf16[8,128,256]{2,1,0:T(8,128)(2,1)}), bf16[8,128,256]{2,1,0:T(8,128)(2,1)S(1)}, u32[]{:S(2)}, u32[]{:S(2)}) async-start(bf16[8,128,256]{2,1,0:T(8,128)(2,1)} %shard_map.126), calls=%async_computation.1 | async-start | bytes 1048576 | tf_op jit(solution)/shard_map/all_to_all | solution.py:505
  49.9 10.2 %collective-permute-start.11 = (bf16[1,5,32,256]{3,2,1,0:T(8,128)(2,1)S(1)}, bf16[1,5,32,256]{3,2,1,0:T(8,128)(2,1)S(1)}, u32[]{:S(2)}, u32[]{:S(2)}) collective-permute-start(bf16[1,5,32,256]{3,2,1,0:T(8,128)(2,1)S(1)} %get-tuple-element.60), channel_id=1, source_target_pairs={{0,4},{1,5},{2,6},{3,7},{4,0},{5,1},{6,2},{7,3},{8,12},{9,13},{10,... | collective-permute-start | bytes 245768 | tf_op jit(solution)/shard_map/ppermute | solution.py:483
  60.1 8.5 %collective-permute-start.12 = (bf16[1,5,32,256]{3,2,1,0:T(8,128)(2,1)S(1)}, bf16[1,5,32,256]{3,2,1,0:T(8,128)(2,1)S(1)}, u32[]{:S(2)}, u32[]{:S(2)}) collective-permute-start(bf16[1,5,32,256]{3,2,1,0:T(8,128)(2,1)S(1)} %shard_map.128.a), channel_id=1, source_target_pairs={{0,8},{1,9},{2,10},{3,11},{4,12},{5,13},{6,14},{7,15},{8,0},{9,1},... | collective-permute-start | bytes 245768 | tf_op jit(solution)/shard_map/ppermute | solution.py:483
  68.7 5.5 %collective-permute-start.15 = (bf16[1,5,32,256]{3,2,1,0:T(8,128)(2,1)S(1)}, bf16[1,5,32,256]{3,2,1,0:T(8,128)(2,1)S(1)}, u32[]{:S(2)}, u32[]{:S(2)}) collective-permute-start(bf16[1,5,32,256]{3,2,1,0:T(8,128)(2,1)S(1)} %shard_map.130), channel_id=1, source_target_pairs={{0,6},{1,7},{2,4},{3,5},{4,2},{5,3},{6,0},{7,1},{8,14},{9,15},{10,... | collective-permute-start | bytes 245768 | tf_op jit(solution)/shard_map/ppermute | solution.py:483
  69.2 5.3 %collective-permute-start.14 = (bf16[1,5,32,256]{3,2,1,0:T(8,128)(2,1)S(1)}, bf16[1,5,32,256]{3,2,1,0:T(8,128)(2,1)S(1)}, u32[]{:S(2)}, u32[]{:S(2)}) collective-permute-start(bf16[1,5,32,256]{3,2,1,0:T(8,128)(2,1)S(1)} %shard_map.130), channel_id=1, source_target_pairs={{0,2},{1,3},{2,0},{3,1},{4,6},{5,7},{6,4},{7,5},{8,10},{9,11},{10,... | collective-permute-start | bytes 245768 | tf_op jit(solution)/shard_map/ppermute | solution.py:483
  70.4 4.6 %collective-permute-start.13 = (bf16[1,5,32,256]{3,2,1,0:T(8,128)(2,1)S(1)}, bf16[1,5,32,256]{3,2,1,0:T(8,128)(2,1)S(1)}, u32[]{:S(2)}, u32[]{:S(2)}) collective-permute-start(bf16[1,5,32,256]{3,2,1,0:T(8,128)(2,1)S(1)} %shard_map.130), channel_id=1, source_target_pairs={{0,4},{1,5},{2,6},{3,7},{4,0},{5,1},{6,2},{7,3},{8,12},{9,13},{10,... | collective-permute-start | bytes 245768 | tf_op jit(solution)/shard_map/ppermute | solution.py:483
  75.1 1.7 %collective-permute-start.16 = (bf16[4,5,32,256]{3,2,1,0:T(8,128)(2,1)S(1)}, bf16[4,5,32,256]{3,2,1,0:T(8,128)(2,1)S(1)}, u32[]{:S(2)}, u32[]{:S(2)}) collective-permute-start(bf16[4,5,32,256]{3,2,1,0:T(8,128)(2,1)S(1)} %pad_maximum_fusion.held), channel_id=1, source_target_pairs={{0,1},{1,0},{2,3},{3,2},{4,5},{5,4},{6,7},{7,6},{8,9},{9,8},{10,11... | collective-permute-start | bytes 983048 | tf_op jit(solution)/shard_map/ppermute | solution.py:483
  (3 other events, 16.1 us)

commit v13 on v12

--- a/solution.py
+++ b/solution.py
@@ -423,19 +423,19 @@
     )(held, *filled)
 
 
-def rows_kernel(counts, onehot_t, table, back, out, share, filled, sem):
-    clusters = counts.shape[1]
-    total = dot(onehot_t[...], back[...])
-    share[...] = (total / column_of(counts[...].astype(F32))).astype(BF16)
+def fill_rows(first, table, share, out, filled, sem):
+    clusters = share.shape[0]
+    blocks = filled.shape[0] // 256
 
     def block(k):
-        rows = pl.ds(pl.multiple_of(k * 256, 256), 256)
-        return pltpu.make_async_copy(filled.at[rows], out.at[rows], sem.at[k])
+        held = pl.ds(pl.multiple_of(k * 256, 256), 256)
+        rows = pl.ds(pl.multiple_of((first + k) * 256, 256), 256)
+        return pltpu.make_async_copy(filled.at[held], out.at[rows], sem.at[k])
 
     def fill(k, carry):
-        onehot = member_onehot(table, k * 2, clusters)
-        rows = pl.ds(pl.multiple_of(k * 256, 256), 256)
-        filled[rows, :] = dot_tn(onehot, share[...]).astype(BF16)
+        onehot = member_onehot(table, (first + k) * 2, clusters)
+        held = pl.ds(pl.multiple_of(k * 256, 256), 256)
+        filled[held, :] = dot_tn(onehot, share[...]).astype(BF16)
         block(k).start()
         return carry
 
@@ -443,28 +443,68 @@
         block(k).wait()
         return carry
 
-    blocks = out.shape[0] // 256
     lax.fori_loop(0, blocks, fill, 0, unroll=4)
     lax.fori_loop(0, blocks, finish, 0)
 
 
-def member_grads(counts, onehot_t, table, back, rows):
+def early_rows_kernel(counts, onehot_t, table, back, out, share, filled, sem):
+    total = dot(onehot_t[...], back[...])
+    share[...] = (total / column_of(counts[...].astype(F32))).astype(BF16)
+    fill_rows(0, table, share, out, filled, sem)
+
+
+def late_rows_kernel(first, table, share, early, out, filled, sem):
+    del early
+    fill_rows(first, table, share, out, filled, sem)
+
+
+def rows_cost(rows, clusters, width):
+    return pl.CostEstimate(
+        flops=2 * rows * clusters * width, bytes_accessed=2 * rows * width, transcendentals=0
+    )
+
+
+def early_rows(counts, onehot_t, table, back, rows, count):
     clusters = counts.shape[1]
     width = back.shape[1]
     return pl.pallas_call(
-        rows_kernel,
-        out_specs=pl.BlockSpec(memory_space=pltpu.HBM),
+        early_rows_kernel,
+        out_specs=[
+            pl.BlockSpec(memory_space=pl.ANY),
+            pl.BlockSpec(memory_space=pltpu.VMEM),
+        ],
+        out_shape=[
+            jax.ShapeDtypeStruct((rows, width), BF16),
+            jax.ShapeDtypeStruct((clusters, width), BF16),
+        ],
+        scratch_shapes=[
+            pltpu.VMEM((count, width), BF16),
+            pltpu.SemaphoreType.DMA((count // 256,)),
+        ],
+        compiler_params=pltpu.CompilerParams(vmem_limit_bytes=VMEM_LIMIT),
+        cost_estimate=rows_cost(count, clusters, width),
+    )(counts, onehot_t, table, back)
+
+
+def late_rows(table, share, early, first):
+    rows, width = early.shape
+    return pl.pallas_call(
+        functools.partial(late_rows_kernel, first // 256),
+        in_specs=[
+            pl.BlockSpec(memory_space=pltpu.VMEM),
+            pl.BlockSpec(memory_space=pltpu.VMEM),
+            pl.BlockSpec(memory_space=pl.ANY),
+        ],
+        out_specs=pl.BlockSpec(memory_space=pl.ANY),
         out_shape=jax.ShapeDtypeStruct((rows, width), BF16),
         scratch_shapes=[
-            pltpu.VMEM((clusters, width), BF16),
-            pltpu.VMEM((rows, width), BF16),
-            pltpu.SemaphoreType.DMA((rows // 256,)),
-        ],
+            pltpu.VMEM((rows - first, width), BF16),
+            pltpu.SemaphoreType.DMA(((rows - first) // 256,)),
+        ],
+        input_output_aliases={2: 0},
         compiler_params=pltpu.CompilerParams(vmem_limit_bytes=VMEM_LIMIT),
-        cost_estimate=pl.CostEstimate(
-            flops=2 * rows * clusters * width, bytes_accessed=2 * rows * width, transcendentals=0
-        ),
-    )(counts, onehot_t, table, back)
+        cost_estimate=rows_cost(rows - first, share.shape[0], width),
+    )(table, share, early)
 
 
 def swap(blocks):
@@ -510,14 +550,17 @@
         keep, given = split(bit + 1, keep, exchange(1 << bit, given), keep.size)
     own = sum_rows(keep, exchange(owners // 4, given))
     got = exchange(owners // 2, own)
-    grad_rows = member_grads(counts, onehot_t, table, back, rows)
-    got, grad_rows = lax.optimization_barrier((got, grad_rows))
+    early, share = early_rows(counts, onehot_t, table, back, rows, rows // 2)
+    got, share = lax.optimization_barrier((got, share))
     own = sum_rows(own, got)
     masks = [0]
     for bit in range(bits - 2, 2, -1):
         own = jnp.concatenate([own, exchange(1 << bit, own)])
         masks = masks + [mask ^ (1 << bit) for mask in masks]
-    chip = jnp.concatenate([own] + [exchange(flip, own) for flip in (4, 2, 6)])
+    passed = [exchange(flip, own) for flip in (4, 2, 6)]
+    grad_rows = late_rows(table, share, early, rows // 2)
+    passed, grad_rows = lax.optimization_barrier((passed, grad_rows))
+    chip = jnp.concatenate([own] + passed)
     masks = [mask ^ flip for flip in (0, 4, 2, 6) for mask in masks]
     beside = exchange(1, chip)
     placed = place(masks, chip)

time: 78.1 us -> 77.3 us (0.990)
  waiting for transfers between devices: 18 us -> 16.4 us
    ppermute x17, waiting for transfers between devices: 17.6 us -> 16 us  [exchange(): return lax.ppermute(block, 'clu', [(d, d ^ flip) for d in range(owners)])]
    pallas_call x1 -> x2, Pallas kernels: 4.08 us -> 4.8 us  [the longest x1 2.55 us: early_rows(): pl.pallas_call(early_rows_kernel, out_specs=[pl.BlockSpec(memory_space=pl...]
  transfers between devices with their start and end apart: 19 -> 19, of which waited for: 11 -> 10; matrix products, arithmetic and copies ran while one was open for 0% -> 0% of each run, Pallas kernels for 18% -> 20%
where the time goes in v13:
time: 77.3 us; the launch traced here: 76.9 us
  starting transfers between devices  35.2 us (46%)
  Pallas kernels  21.6 us (28%)
  waiting for transfers between devices  16.4 us (21%)
  local copies, waits for them, and re-layouts  2.81 us (4%)
  between operations  0.81 us (1%)
    ppermute x17, starting transfers between devices, exchange(): return lax.ppermute(block, 'clu', [(d, d ^ flip) for d in range(owners)])  22.5 us
    ppermute x17, waiting for transfers between devices, exchange(): return lax.ppermute(block, 'clu', [(d, d ^ flip) for d in range(owners)])  16 us
    all_to_all x1, starting transfers between devices, swap(): lax.all_to_all(blocks, 'clu', split_axis=0, concat_axis=0, tiled=True)  7.39 us
    all_to_all x1, starting transfers between devices, local(): lax.all_to_all(back, 'clu', split_axis=0, concat_axis=0, axis_index_group...  5.3 us
    pallas_call x1, Pallas kernels, attention(): pl.pallas_call(functools.partial(attention_kernel, scale, len(raws)), out...  4.9 us
    pallas_call x1, Pallas kernels, cluster_means(): pl.pallas_call(means_kernel, in_specs=[pl.BlockSpec(memory_space=pltpu.HB...  4.49 us
    pallas_call x1, Pallas kernels, target_terms(): pl.pallas_call(functools.partial(targets_kernel, scale), out_shape=[jax.S...  3.9 us
    pallas_call x1, Pallas kernels, early_rows(): pl.pallas_call(early_rows_kernel, out_specs=[pl.BlockSpec(memory_space=pl...  2.55 us
  transfers between devices with their start and end apart: 19, of which 10 were waited for; matrix products, arithmetic and copies ran while one was open for 0% of the time, Pallas kernels for 20%

profile of v13, /device:TPU:0, one launch (start us, length us, event | category | flops | bytes accessed | tf_op | source)
XLA Modules:
  0.0 76.9 jit_solution(17545723728067706206)
XLA Ops:
  0.7 1.4 %broadcast_in_dim.10 = s32[8,2,128]{2,1,0:T(2,128)} broadcast(s32[8,128]{1,0:T(8,128)} %bitcast.10), dimensions={0,2} | broadcast | bytes 12288 | tf_op jit(solution)/shard_map/broadcast_in_dim | solution.py:526
  2.0 7.4 %all-to-all-start = ((s32[16,1,128]{2,1,0:T(1,128)}), s32[16,1,128]{2,1,0:T(1,128)S(1)}, u32[]{:S(2)}, u32[]{:S(2)}) async-start(s32[16,1,128]{2,1,0:T(1,128)} %bitcast.1), calls=%async_computation | async-start | bytes 16384 | tf_op jit(solution)/shard_map/all_to_all | solution.py:511
  10.9 4.5 %shard_map.120 = (bf16[256,256]{1,0:T(8,128)(2,1)S(1)}, f32[64,128]{1,0:T(8,128)S(1)}) custom-call(s32[1,256]{1,0:T(1,128)S(1)} %copy-done.6, s32[64,128]{1,0:T(8,128)S(1)} %bitcast.8, bf16[8192,256]{1,0:T(8,128)(2,1)} %raw_h.1), custom_call_target="tpu_custom_call" | custom-call | flops 1073741824 | bytes 4194304 | tf_op jit(solution)/shard_map/pallas_call | solution.py:127
  16.3 1.5 %collective-permute-done.got = bf16[8,64,256]{2,1,0:T(8,128)(2,1)S(1)} collective-permute-done((bf16[8,64,256]{2,1,0:T(8,128)(2,1)S(1)}, bf16[8,64,256]{2,1,0:T(8,128)(2,1)S(1)}, u32[]{:S(2)}, u32[]{:S(2)}) %collective-permute-start) | collective-permute-done | bytes 262176 | tf_op jit(solution)/shard_map/ppermute | solution.py:523
  17.9 1.6 %collective-permute-start.1 = (bf16[128,256]{1,0:T(8,128)(2,1)S(1)}, bf16[128,256]{1,0:T(8,128)(2,1)S(1)}, u32[]{:S(2)}, u32[]{:S(2)}) collective-permute-start(bf16[128,256]{1,0:T(8,128)(2,1)S(1)} %get-tuple-element.47), channel_id=1, source_target_pairs={{0,2},{1,3},{2,0},{3,1},{4,6},{5,7},{6,4},{7,5},{8,10},{9,11},{10,... | collective-permute-start | bytes 196616 | tf_op jit(solution)/shard_map/ppermute | solution.py:523
  19.5 1.5 %collective-permute-start.2 = (bf16[128,256]{1,0:T(8,128)(2,1)S(1)}, bf16[128,256]{1,0:T(8,128)(2,1)S(1)}, u32[]{:S(2)}, u32[]{:S(2)}) collective-permute-start(bf16[128,256]{1,0:T(8,128)(2,1)S(1)} %get-tuple-element.48), channel_id=1, source_target_pairs={{0,4},{1,5},{2,6},{3,7},{4,0},{5,1},{6,2},{7,3},{8,12},{9,13},{10,... | collective-permute-start | bytes 196616 | tf_op jit(solution)/shard_map/ppermute | solution.py:523
  21.5 2.4 %collective-permute-start.4 = (bf16[128,256]{1,0:T(8,128)(2,1)S(1)}, bf16[128,256]{1,0:T(8,128)(2,1)S(1)}, u32[]{:S(2)}, u32[]{:S(2)}) collective-permute-start(bf16[128,256]{1,0:T(8,128)(2,1)S(1)} %get-tuple-element.50), channel_id=1, source_target_pairs={{0,8},{1,9},{2,10},{3,11},{4,12},{5,13},{6,14},{7,15},{8,0},{9,1},... | collective-permute-start | bytes 196616 | tf_op jit(solution)/shard_map/ppermute | solution.py:523
  23.9 1.5 %collective-permute-start.5 = (bf16[128,256]{1,0:T(8,128)(2,1)S(1)}, bf16[128,256]{1,0:T(8,128)(2,1)S(1)}, u32[]{:S(2)}, u32[]{:S(2)}) collective-permute-start(bf16[128,256]{1,0:T(8,128)(2,1)S(1)} %get-tuple-element.51), channel_id=1, source_target_pairs={{0,10},{1,11},{2,8},{3,9},{4,14},{5,15},{6,12},{7,13},{8,2},{9,3},... | collective-permute-start | bytes 196616 | tf_op jit(solution)/shard_map/ppermute | solution.py:523
  25.4 3.3 %collective-permute-start.6 = (bf16[128,256]{1,0:T(8,128)(2,1)S(1)}, bf16[128,256]{1,0:T(8,128)(2,1)S(1)}, u32[]{:S(2)}, u32[]{:S(2)}) collective-permute-start(bf16[128,256]{1,0:T(8,128)(2,1)S(1)} %get-tuple-element.52), channel_id=1, source_target_pairs={{0,12},{1,13},{2,14},{3,15},{4,8},{5,9},{6,10},{7,11},{8,4},{9,5},... | collective-permute-start | bytes 196616 | tf_op jit(solution)/shard_map/ppermute | solution.py:523
  29.1 3.9 %shard_map.123 = (f32[1024,128]{1,0:T(8,128)S(1)}, bf16[512,256]{1,0:T(8,128)(2,1)S(1)}, bf16[512,256]{1,0:T(8,128)(2,1)S(1)}) custom-call(s32[100,128]{1,0:T(8,128)S(1)} %bitcast.7, bf16[128,256]{1,0:T(8,128)(2,1)S(1)} %copy-done.1, bf16[128,256]{1,0:T(8,128)(2,1)S(1)} %copy-done.2, bf16[4,256,256]{2,1,0:T(8,128)(2,1)S(1)} %copy-done), custom_call_target="tpu_custom_call" | custom-call | flops 52428800 | bytes 524288 | tf_op jit(solution)/shard_map/pallas_call | solution.py:229
  33.1 1.2 %collective-permute-done.5.refs_5_ = bf16[128,256]{1,0:T(8,128)(2,1)S(1)} collective-permute-done((bf16[128,256]{1,0:T(8,128)(2,1)S(1)}, bf16[128,256]{1,0:T(8,128)(2,1)S(1)}, u32[]{:S(2)}, u32[]{:S(2)}) %collective-permute-start.5) | collective-permute-done | bytes 65568 | tf_op jit(solution)/shard_map/ppermute | solution.py:523
  34.2 1.5 %collective-permute-done.7.refs_7_ = bf16[128,256]{1,0:T(8,128)(2,1)S(1)} collective-permute-done((bf16[128,256]{1,0:T(8,128)(2,1)S(1)}, bf16[128,256]{1,0:T(8,128)(2,1)S(1)}, u32[]{:S(2)}, u32[]{:S(2)}) %collective-permute-start.7) | collective-permute-done | bytes 65568 | tf_op jit(solution)/shard_map/ppermute | solution.py:523
  35.7 4.9 %shard_map.124 = (bf16[8,64,256]{2,1,0:T(8,128)(2,1)S(1)}, bf16[8,64,256]{2,1,0:T(8,128)(2,1)S(1)}, bf16[128,256]{1,0:T(8,128)(2,1)}, bf16[4,5,32,256]{3,2,1,0:T(8,128)(2,1)S(1)}, bf16[4,5,32,256]{3,2,1,0:T(8,128)(2,1)S(1)}) custom-call(bf16[128,256]{1,0:T(8,128)(2,1)S(1)} %get-tuple-element.46.refs_0_, bf16[128,256]{1,0:T(8,128)(2,1)S(1)} %collective-permute-done.1.refs_1_, ...), custom_call_target="tpu_custom_call" | custom-call | tf_op jit(solution)/shard_map/pallas_call | solution.py:341
  41.1 1.5 %collective-permute-done.9.got = bf16[8,64,256]{2,1,0:T(8,128)(2,1)S(1)} collective-permute-done((bf16[8,64,256]{2,1,0:T(8,128)(2,1)S(1)}, bf16[8,64,256]{2,1,0:T(8,128)(2,1)S(1)}, u32[]{:S(2)}, u32[]{:S(2)}) %collective-permute-start.9) | collective-permute-done | bytes 262176 | tf_op jit(solution)/shard_map/ppermute | solution.py:523
  44.2 5.3 %all-to-all-start.1 = ((bf16[8,128,256]{2,1,0:T(8,128)(2,1)}), bf16[8,128,256]{2,1,0:T(8,128)(2,1)S(1)}, u32[]{:S(2)}, u32[]{:S(2)}) async-start(bf16[8,128,256]{2,1,0:T(8,128)(2,1)} %shard_map.126), calls=%async_computation.1 | async-start | bytes 1048576 | tf_op jit(solution)/shard_map/all_to_all | solution.py:545
  49.9 2.0 %collective-permute-start.11 = (bf16[1,5,32,256]{3,2,1,0:T(8,128)(2,1)S(1)}, bf16[1,5,32,256]{3,2,1,0:T(8,128)(2,1)S(1)}, u32[]{:S(2)}, u32[]{:S(2)}) collective-permute-start(bf16[1,5,32,256]{3,2,1,0:T(8,128)(2,1)S(1)} %get-tuple-element.66), channel_id=1, source_target_pairs={{0,4},{1,5},{2,6},{3,7},{4,0},{5,1},{6,2},{7,3},{8,12},{9,13},{10,... | collective-permute-start | bytes 245768 | tf_op jit(solution)/shard_map/ppermute | solution.py:523
  51.9 8.2 %collective-permute-done.11.b = bf16[1,5,32,256]{3,2,1,0:T(8,128)(2,1)S(1)} collective-permute-done((bf16[1,5,32,256]{3,2,1,0:T(8,128)(2,1)S(1)}, bf16[1,5,32,256]{3,2,1,0:T(8,128)(2,1)S(1)}, u32[]{:S(2)}, u32[]{:S(2)}) %collective-permute-start.11) | collective-permute-done | bytes 81952 | tf_op jit(solution)/shard_map/ppermute | solution.py:523
  60.1 4.4 %collective-permute-start.12 = (bf16[1,5,32,256]{3,2,1,0:T(8,128)(2,1)S(1)}, bf16[1,5,32,256]{3,2,1,0:T(8,128)(2,1)S(1)}, u32[]{:S(2)}, u32[]{:S(2)}) collective-permute-start(bf16[1,5,32,256]{3,2,1,0:T(8,128)(2,1)S(1)} %shard_map.128.a), channel_id=1, source_target_pairs={{0,8},{1,9},{2,10},{3,11},{4,12},{5,13},{6,14},{7,15},{8,0},{9,1},... | collective-permute-start | bytes 245768 | tf_op jit(solution)/shard_map/ppermute | solution.py:523
  64.5 2.5 %shard_map.129 = (bf16[8192,256]{1,0:T(8,128)(2,1)}, bf16[256,256]{1,0:T(8,128)(2,1)S(1)}) custom-call(s32[1,256]{1,0:T(1,128)S(1)} %copy-done.7, bf16[256,1024]{1,0:T(8,128)(2,1)S(1)} %get-tuple-element.67.onehot_t, f32[64,128]{1,0:T(8,128)S(1)} %get-tuple-element.68.table, bf16[1024,256]{1,0:T(8,128)(2,1)S(1)} %bitcast.6), custom_call_target="tpu_custom_call" | custom-call | flops 536870912 | bytes 2097152 | tf_op jit(solution)/shard_map/pallas_call | solution.py:470
  67.9 1.3 %collective-permute-start.15 = (bf16[1,5,32,256]{3,2,1,0:T(8,128)(2,1)S(1)}, bf16[1,5,32,256]{3,2,1,0:T(8,128)(2,1)S(1)}, u32[]{:S(2)}, u32[]{:S(2)}) collective-permute-start(bf16[1,5,32,256]{3,2,1,0:T(8,128)(2,1)S(1)} %shard_map.130), channel_id=1, source_target_pairs={{0,6},{1,7},{2,4},{3,5},{4,2},{5,3},{6,0},{7,1},{8,14},{9,15},{10,... | collective-permute-start | bytes 245768 | tf_op jit(solution)/shard_map/ppermute | solution.py:523
  69.5 1.9 %collective-permute-start.13 = (bf16[1,5,32,256]{3,2,1,0:T(8,128)(2,1)S(1)}, bf16[1,5,32,256]{3,2,1,0:T(8,128)(2,1)S(1)}, u32[]{:S(2)}, u32[]{:S(2)}) collective-permute-start(bf16[1,5,32,256]{3,2,1,0:T(8,128)(2,1)S(1)} %shard_map.130), channel_id=1, source_target_pairs={{0,4},{1,5},{2,6},{3,7},{4,0},{5,1},{6,2},{7,3},{8,12},{9,13},{10,... | collective-permute-start | bytes 245768 | tf_op jit(solution)/shard_map/ppermute | solution.py:523
  71.4 2.3 %shard_map.131 = bf16[8192,256]{1,0:T(8,128)(2,1)} custom-call(f32[64,128]{1,0:T(8,128)S(1)} %get-tuple-element.68.table, bf16[256,256]{1,0:T(8,128)(2,1)S(1)} %get-tuple-element.72.share, bf16[8192,256]{1,0:T(8,128)(2,1)} %get-tuple-element.73.early), custom_call_target="tpu_custom_call", output_to_operand_aliasing={{}: (2, {})} | custom-call | flops 536870912 | bytes 2097152 | tf_op jit(solution)/shard_map/pallas_call | solution.py:491
  74.3 1.0 %shard_map.132 = (f32[4,256,256]{2,1,0:T(8,128)}, f32[256,256]{1,0:T(8,128)}) custom-call(bf16[4,5,32,256]{3,2,1,0:T(8,128)(2,1)S(1)} %pad_maximum_fusion.held), custom_call_target="tpu_custom_call" | custom-call | bytes 655360 | tf_op jit(solution)/shard_map/pallas_call | solution.py:407
  75.9 1.0 %shard_map.133 = (f32[4,256,256]{2,1,0:T(8,128)}, f32[256,256]{1,0:T(8,128)}) custom-call(bf16[4,5,32,256]{3,2,1,0:T(8,128)(2,1)S(1)} %collective-permute-done.16.held, f32[4,256,256]{2,1,0:T(8,128)} %get-tuple-element.78.refs_0_, f32[256,256]{1,0:T(8,128)} %get-tuple-element.79.refs_1_), custom_call_target="tpu_custom_call", output_to_operand_aliasing={{0}: (1, {}), {1}: (2, {})} | custom-call | bytes 655360 | tf_op jit(solution)/shard_map/pallas_call | solution.py:407
  (46 shorter events, 8.3 us)
Async XLA Ops:
  0.6 28.5 %copy-start.2 = (bf16[128,256]{1,0:T(8,128)(2,1)S(1)}, bf16[128,256]{1,0:T(8,128)(2,1)}, u32[]{:S(2)}) copy-start(bf16[128,256]{1,0:T(8,128)(2,1)} %refs_11_.1) | copy-start | bytes 196612
  0.6 28.5 %copy-start = (bf16[4,256,256]{2,1,0:T(8,128)(2,1)S(1)}, bf16[4,256,256]{2,1,0:T(8,128)(2,1)}, u32[]{:S(2)}) copy-start(bf16[4,256,256]{2,1,0:T(8,128)(2,1)} %refs_9_.1) | copy-start | bytes 1572868
  0.7 28.5 %copy-start.1 = (bf16[128,256]{1,0:T(8,128)(2,1)S(1)}, bf16[128,256]{1,0:T(8,128)(2,1)}, u32[]{:S(2)}) copy-start(bf16[128,256]{1,0:T(8,128)(2,1)} %refs_10_.1) | copy-start | bytes 196612
  0.7 28.5 %copy-start.4 = (s32[128,100]{0,1:T(8,128)S(1)}, s32[128,100]{0,1:T(8,128)}, u32[]{:S(2)}) copy-start(s32[128,100]{0,1:T(8,128)} %param.14) | copy-start | bytes 153604
  0.7 35.0 %copy-start.3 = (bf16[256,256]{1,0:T(8,128)(2,1)S(1)}, bf16[256,256]{1,0:T(8,128)(2,1)}, u32[]{:S(2)}) copy-start(bf16[256,256]{1,0:T(8,128)(2,1)} %refs_8_.1) | copy-start | bytes 393220
  2.0 13.7 %all-to-all-start = ((s32[16,1,128]{2,1,0:T(1,128)}), s32[16,1,128]{2,1,0:T(1,128)S(1)}, u32[]{:S(2)}, u32[]{:S(2)}) async-start(s32[16,1,128]{2,1,0:T(1,128)} %bitcast.1), calls=%async_computation | async-start | bytes 16384 | tf_op jit(solution)/shard_map/all_to_all | solution.py:511
  16.3 1.6 %collective-permute-start = (bf16[8,64,256]{2,1,0:T(8,128)(2,1)S(1)}, bf16[8,64,256]{2,1,0:T(8,128)(2,1)S(1)}, u32[]{:S(2)}, u32[]{:S(2)}) collective-permute-start(bf16[8,64,256]{2,1,0:T(8,128)(2,1)S(1)} %get-tuple-element.45), channel_id=1, source_target_pairs={{0,1},{1,0},{2,3},{3,2},{4,5},{5,4},{6,7},{7,6},{8,9},{9,8},{10,11... | collective-permute-start | bytes 786440 | tf_op jit(solution)/shard_map/ppermute | solution.py:523
  17.9 7.5 %collective-permute-start.1 = (bf16[128,256]{1,0:T(8,128)(2,1)S(1)}, bf16[128,256]{1,0:T(8,128)(2,1)S(1)}, u32[]{:S(2)}, u32[]{:S(2)}) collective-permute-start(bf16[128,256]{1,0:T(8,128)(2,1)S(1)} %get-tuple-element.47), channel_id=1, source_target_pairs={{0,2},{1,3},{2,0},{3,1},{4,6},{5,7},{6,4},{7,5},{8,10},{9,11},{10,... | collective-permute-start | bytes 196616 | tf_op jit(solution)/shard_map/ppermute | solution.py:523
  19.5 9.1 %collective-permute-start.2 = (bf16[128,256]{1,0:T(8,128)(2,1)S(1)}, bf16[128,256]{1,0:T(8,128)(2,1)S(1)}, u32[]{:S(2)}, u32[]{:S(2)}) collective-permute-start(bf16[128,256]{1,0:T(8,128)(2,1)S(1)} %get-tuple-element.48), channel_id=1, source_target_pairs={{0,4},{1,5},{2,6},{3,7},{4,0},{5,1},{6,2},{7,3},{8,12},{9,13},{10,... | collective-permute-start | bytes 196616 | tf_op jit(solution)/shard_map/ppermute | solution.py:523
  21.0 12.1 %collective-permute-start.3 = (bf16[128,256]{1,0:T(8,128)(2,1)S(1)}, bf16[128,256]{1,0:T(8,128)(2,1)S(1)}, u32[]{:S(2)}, u32[]{:S(2)}) collective-permute-start(bf16[128,256]{1,0:T(8,128)(2,1)S(1)} %get-tuple-element.49), channel_id=1, source_target_pairs={{0,6},{1,7},{2,4},{3,5},{4,2},{5,3},{6,0},{7,1},{8,14},{9,15},{10,... | collective-permute-start | bytes 196616 | tf_op jit(solution)/shard_map/ppermute | solution.py:523
  21.5 11.6 %collective-permute-start.4 = (bf16[128,256]{1,0:T(8,128)(2,1)S(1)}, bf16[128,256]{1,0:T(8,128)(2,1)S(1)}, u32[]{:S(2)}, u32[]{:S(2)}) collective-permute-start(bf16[128,256]{1,0:T(8,128)(2,1)S(1)} %get-tuple-element.50), channel_id=1, source_target_pairs={{0,8},{1,9},{2,10},{3,11},{4,12},{5,13},{6,14},{7,15},{8,0},{9,1},... | collective-permute-start | bytes 196616 | tf_op jit(solution)/shard_map/ppermute | solution.py:523
  23.9 10.3 %collective-permute-start.5 = (bf16[128,256]{1,0:T(8,128)(2,1)S(1)}, bf16[128,256]{1,0:T(8,128)(2,1)S(1)}, u32[]{:S(2)}, u32[]{:S(2)}) collective-permute-start(bf16[128,256]{1,0:T(8,128)(2,1)S(1)} %get-tuple-element.51), channel_id=1, source_target_pairs={{0,10},{1,11},{2,8},{3,9},{4,14},{5,15},{6,12},{7,13},{8,2},{9,3},... | collective-permute-start | bytes 196616 | tf_op jit(solution)/shard_map/ppermute | solution.py:523
  25.4 8.9 %collective-permute-start.6 = (bf16[128,256]{1,0:T(8,128)(2,1)S(1)}, bf16[128,256]{1,0:T(8,128)(2,1)S(1)}, u32[]{:S(2)}, u32[]{:S(2)}) collective-permute-start(bf16[128,256]{1,0:T(8,128)(2,1)S(1)} %get-tuple-element.52), channel_id=1, source_target_pairs={{0,12},{1,13},{2,14},{3,15},{4,8},{5,9},{6,10},{7,11},{8,4},{9,5},... | collective-permute-start | bytes 196616 | tf_op jit(solution)/shard_map/ppermute | solution.py:523
  28.6 7.1 %collective-permute-start.7 = (bf16[128,256]{1,0:T(8,128)(2,1)S(1)}, bf16[128,256]{1,0:T(8,128)(2,1)S(1)}, u32[]{:S(2)}, u32[]{:S(2)}) collective-permute-start(bf16[128,256]{1,0:T(8,128)(2,1)S(1)} %get-tuple-element.53), channel_id=1, source_target_pairs={{0,14},{1,15},{2,12},{3,13},{4,10},{5,11},{6,8},{7,9},{8,6},{9,7},... | collective-permute-start | bytes 196616 | tf_op jit(solution)/shard_map/ppermute | solution.py:523
  40.6 2.8 %collective-permute-start.8 = (bf16[4,5,32,256]{3,2,1,0:T(8,128)(2,1)S(1)}, bf16[4,5,32,256]{3,2,1,0:T(8,128)(2,1)S(1)}, u32[]{:S(2)}, u32[]{:S(2)}) collective-permute-start(bf16[4,5,32,256]{3,2,1,0:T(8,128)(2,1)S(1)} %get-tuple-element.59), channel_id=1, source_target_pairs={{0,1},{1,0},{2,3},{3,2},{4,5},{5,4},{6,7},{7,6},{8,9},{9,8},{10,11... | collective-permute-start | bytes 983048 | tf_op jit(solution)/shard_map/ppermute | solution.py:523
  40.6 2.0 %collective-permute-start.9 = (bf16[8,64,256]{2,1,0:T(8,128)(2,1)S(1)}, bf16[8,64,256]{2,1,0:T(8,128)(2,1)S(1)}, u32[]{:S(2)}, u32[]{:S(2)}) collective-permute-start(bf16[8,64,256]{2,1,0:T(8,128)(2,1)S(1)} %get-tuple-element.63), channel_id=1, source_target_pairs={{0,1},{1,0},{2,3},{3,2},{4,5},{5,4},{6,7},{7,6},{8,9},{9,8},{10,11... | collective-permute-start | bytes 786440 | tf_op jit(solution)/shard_map/ppermute | solution.py:523
  43.5 6.3 %collective-permute-start.10 = (bf16[2,5,32,256]{3,2,1,0:T(8,128)(2,1)S(1)}, bf16[2,5,32,256]{3,2,1,0:T(8,128)(2,1)S(1)}, u32[]{:S(2)}, u32[]{:S(2)}) collective-permute-start(bf16[2,5,32,256]{3,2,1,0:T(8,128)(2,1)S(1)} %get-tuple-element.64), channel_id=1, source_target_pairs={{0,2},{1,3},{2,0},{3,1},{4,6},{5,7},{6,4},{7,5},{8,10},{9,11},{10,... | collective-permute-start | bytes 491528 | tf_op jit(solution)/shard_map/ppermute | solution.py:523
  44.2 20.4 %all-to-all-start.1 = ((bf16[8,128,256]{2,1,0:T(8,128)(2,1)}), bf16[8,128,256]{2,1,0:T(8,128)(2,1)S(1)}, u32[]{:S(2)}, u32[]{:S(2)}) async-start(bf16[8,128,256]{2,1,0:T(8,128)(2,1)} %shard_map.126), calls=%async_computation.1 | async-start | bytes 1048576 | tf_op jit(solution)/shard_map/all_to_all | solution.py:545
  49.9 10.2 %collective-permute-start.11 = (bf16[1,5,32,256]{3,2,1,0:T(8,128)(2,1)S(1)}, bf16[1,5,32,256]{3,2,1,0:T(8,128)(2,1)S(1)}, u32[]{:S(2)}, u32[]{:S(2)}) collective-permute-start(bf16[1,5,32,256]{3,2,1,0:T(8,128)(2,1)S(1)} %get-tuple-element.66), channel_id=1, source_target_pairs={{0,4},{1,5},{2,6},{3,7},{4,0},{5,1},{6,2},{7,3},{8,12},{9,13},{10,... | collective-permute-start | bytes 245768 | tf_op jit(solution)/shard_map/ppermute | solution.py:523
  60.1 7.7 %collective-permute-start.12 = (bf16[1,5,32,256]{3,2,1,0:T(8,128)(2,1)S(1)}, bf16[1,5,32,256]{3,2,1,0:T(8,128)(2,1)S(1)}, u32[]{:S(2)}, u32[]{:S(2)}) collective-permute-start(bf16[1,5,32,256]{3,2,1,0:T(8,128)(2,1)S(1)} %shard_map.128.a), channel_id=1, source_target_pairs={{0,8},{1,9},{2,10},{3,11},{4,12},{5,13},{6,14},{7,15},{8,0},{9,1},... | collective-permute-start | bytes 245768 | tf_op jit(solution)/shard_map/ppermute | solution.py:523
  67.9 5.8 %collective-permute-start.15 = (bf16[1,5,32,256]{3,2,1,0:T(8,128)(2,1)S(1)}, bf16[1,5,32,256]{3,2,1,0:T(8,128)(2,1)S(1)}, u32[]{:S(2)}, u32[]{:S(2)}) collective-permute-start(bf16[1,5,32,256]{3,2,1,0:T(8,128)(2,1)S(1)} %shard_map.130), channel_id=1, source_target_pairs={{0,6},{1,7},{2,4},{3,5},{4,2},{5,3},{6,0},{7,1},{8,14},{9,15},{10,... | collective-permute-start | bytes 245768 | tf_op jit(solution)/shard_map/ppermute | solution.py:523
  69.2 5.0 %collective-permute-start.14 = (bf16[1,5,32,256]{3,2,1,0:T(8,128)(2,1)S(1)}, bf16[1,5,32,256]{3,2,1,0:T(8,128)(2,1)S(1)}, u32[]{:S(2)}, u32[]{:S(2)}) collective-permute-start(bf16[1,5,32,256]{3,2,1,0:T(8,128)(2,1)S(1)} %shard_map.130), channel_id=1, source_target_pairs={{0,2},{1,3},{2,0},{3,1},{4,6},{5,7},{6,4},{7,5},{8,10},{9,11},{10,... | collective-permute-start | bytes 245768 | tf_op jit(solution)/shard_map/ppermute | solution.py:523
  69.5 4.7 %collective-permute-start.13 = (bf16[1,5,32,256]{3,2,1,0:T(8,128)(2,1)S(1)}, bf16[1,5,32,256]{3,2,1,0:T(8,128)(2,1)S(1)}, u32[]{:S(2)}, u32[]{:S(2)}) collective-permute-start(bf16[1,5,32,256]{3,2,1,0:T(8,128)(2,1)S(1)} %shard_map.130), channel_id=1, source_target_pairs={{0,4},{1,5},{2,6},{3,7},{4,0},{5,1},{6,2},{7,3},{8,12},{9,13},{10,... | collective-permute-start | bytes 245768 | tf_op jit(solution)/shard_map/ppermute | solution.py:523
  74.2 1.7 %collective-permute-start.16 = (bf16[4,5,32,256]{3,2,1,0:T(8,128)(2,1)S(1)}, bf16[4,5,32,256]{3,2,1,0:T(8,128)(2,1)S(1)}, u32[]{:S(2)}, u32[]{:S(2)}) collective-permute-start(bf16[4,5,32,256]{3,2,1,0:T(8,128)(2,1)S(1)} %pad_maximum_fusion.held), channel_id=1, source_target_pairs={{0,1},{1,0},{2,3},{3,2},{4,5},{5,4},{6,7},{7,6},{8,9},{9,8},{10,11... | collective-permute-start | bytes 983048 | tf_op jit(solution)/shard_map/ppermute | solution.py:523
  (3 other events, 16.1 us)
